TPU v7x, 32 devices: a whole 2x2x4 slice. The times are simulated.
32 devices in a mesh: rep: 8 (over y, x, core), shard: 4 (over z).
Axes of the slice: x: 2, y: 2, z: 4, core: 2. Of those that a mesh axis runs over, the one named last changes fastest.
Arguments:
- tokens: bfloat16 [8192, 1024], P(('rep', 'shard')), may hold values from -6 to 6
- cotangent: bfloat16 [8192, 1024], P(('rep', 'shard')), may hold values from -6 to 6
- segment_ids: int32 [8192], P(('rep', 'shard')), may hold values from 0 to 6, as said below
- routes: int32 [8192, 8], P(('rep', 'shard')), may hold values from 0 to 15, all different within a row; in each aligned block of 256 rows (0 to 255, 256 to 511, ...) at most 160 rows name the same one
- attn_gain: bfloat16 [1024], P('shard'), may hold values from 0.5 to 1.5
- query_weight: bfloat16 [1024, 1024], P('shard'), may hold values from -0.1875 to 0.1875
- key_matrix: bfloat16 [1024, 512], P('shard'), may hold values from -0.1875 to 0.1875
- value_weight: bfloat16 [1024, 512], P('shard'), may hold values from -0.1875 to 0.1875
- out_weight: bfloat16 [1024, 1024], P(None, 'shard'), may hold values from -0.75 to 0.75
- ffn_gain: bfloat16 [1024], P('shard'), may hold values from 0.5 to 1.5
- router_weight: bfloat16 [1024, 16], P('shard'), may hold values from -0.09375 to 0.09375
- gate_weight: bfloat16 [16, 1024, 512], P(None, 'shard'), may hold values from -0.1875 to 0.1875
- up_weight: bfloat16 [16, 1024, 512], P(None, 'shard'), may hold values from -0.1875 to 0.1875
- down_weight: bfloat16 [16, 512, 1024], P(None, 'shard'), may hold values from -1 to 1
Outputs:
- output: bfloat16 [8192, 1024], P(('rep', 'shard'))
- input_grad: float32 [8192, 1024], P(('rep', 'shard'))
- attn_gain_grad: float32 [1024], P('shard')
- query_weight_grad: float32 [1024, 1024], P('shard')
- key_weight_grad: float32 [1024, 512], P('shard')
- value_weight_grad: float32 [1024, 512], P('shard')
- out_weight_grad: float32 [1024, 1024], P(None, 'shard')
- ffn_gain_grad: float32 [1024], P('shard')
- router_weight_grad: float32 [1024, 16], P('shard')
- gate_weight_grad: float32 [16, 1024, 512], P(None, 'shard')
- up_weight_grad: float32 [16, 1024, 512], P(None, 'shard')
- down_weight_grad: float32 [16, 512, 1024], P(None, 'shard')
Inputs may be any that keep to these rules, and one draw needn't show every extreme that they name: `segment_ids`: within each packed sequence of 1024 tokens the ids start at 0, never fall, and end at 6. `routes`: each row names 8 different experts. Among the rows of one device no expert is named more than 160 times, and in every draw some expert is named exactly 160 times by the rows of some device.
All inputs are finite; a program needn't handle non-finite values.
Results may differ from a plain program's by a relative error of at most 0.022.
Values may be sent and summed in bfloat16 or wider, within the bound.
No kernel may reach another device: no remote copies, remote signals or barrier semaphores. Data moves between devices by JAX's collectives and lax.ppermute only.
A program may use at most 320 MiB of HBM per device.

v0:
```python
import jax
import jax.numpy as jnp
from jax import lax
from jax.sharding import PartitionSpec as P

QUERY_HEADS = 16
KEY_VALUE_HEADS = 8
HEAD_SIZE = 64
CAP = 160


eps_norm = 1e-06
score_scale = 0.125
rope_base = 10000.0
masked_score = -1e30


def trig_tables(token_positions, half_size):
    frequency = rope_base ** (-jnp.arange(half_size, dtype=jnp.float32) / half_size)
    angles = token_positions.astype(jnp.float32)[:, None] * frequency[None, :]
    return (jnp.cos(angles)[:, None, :], jnp.sin(angles)[:, None, :])


def apply_rotary(values, rotary_tables, head_count, inverse):
    cosine, sine_table = rotary_tables
    if inverse:
        sine_table = -sine_table
    row_count = values.shape[0]
    shaped = values.reshape(row_count, head_count, -1)
    half_size = shaped.shape[2] // 2
    first_half = shaped[:, :, :half_size]
    second_half = shaped[:, :, half_size:]
    turned = jnp.concatenate(
        [
            first_half * cosine - second_half * sine_table,
            second_half * cosine + first_half * sine_table,
        ],
        axis=-1,
    )
    return turned.reshape(row_count, -1)


def norm_forward(values, gain_vec):
    inverse_rms = lax.rsqrt(jnp.mean(values * values, axis=-1, keepdims=True) + eps_norm)
    scaled = values * inverse_rms
    return (scaled, inverse_rms, (scaled * gain_vec.astype(jnp.float32)).astype(jnp.bfloat16))


def norm_backward(grad_in, scaled, inverse_rms, gain_vec):
    gain_grad = jnp.sum(grad_in * scaled, axis=0)
    weighted = grad_in * gain_vec.astype(jnp.float32)
    return (
        gain_grad,
        inverse_rms * (weighted - scaled * jnp.mean(weighted * scaled, axis=-1, keepdims=True)),
    )


def head_scores(query_head, key_head, allowed):
    scores = (
        jnp.einsum("bgd,sd->gbs", query_head, key_head, preferred_element_type=jnp.float32)
        * score_scale
    )
    return jnp.where(allowed[None, :, :], scores, masked_score)


def expert_acts(buffer, gate_full, up_full):
    gate_act = jnp.einsum("ecd,edf->ecf", buffer, gate_full, preferred_element_type=jnp.float32)
    up_act = jnp.einsum("ecd,edf->ecf", buffer, up_full, preferred_element_type=jnp.float32)
    sigmoid_gate = jax.nn.sigmoid(gate_act)
    activated = gate_act * sigmoid_gate
    inner_act = (activated * up_act).astype(jnp.bfloat16)
    return (gate_act, up_act, sigmoid_gate, activated, inner_act)


def expert_apply(inner_act, down_full):
    return jnp.einsum(
        "ecf,efd->ecd", inner_act, down_full, preferred_element_type=jnp.float32
    ).astype(jnp.bfloat16)


def expert_grads(buffer, slot_grads, acts, gate_full, up_full, down_full):
    gate_act, up_act, sigmoid_gate, activated, inner_act = acts
    inner_grad = jnp.einsum(
        "ecd,efd->ecf", slot_grads, down_full, preferred_element_type=jnp.float32
    )
    down_grad = jnp.einsum(
        "ecf,ecd->efd", inner_act, slot_grads, preferred_element_type=jnp.float32
    )
    gate_grad = (
        inner_grad * up_act * sigmoid_gate * (1.0 + gate_act * (1.0 - sigmoid_gate))
    ).astype(jnp.bfloat16)
    up_grad = (inner_grad * activated).astype(jnp.bfloat16)
    gate_wgrad = jnp.einsum("ecd,ecf->edf", buffer, gate_grad, preferred_element_type=jnp.float32)
    up_wgrad = jnp.einsum("ecd,ecf->edf", buffer, up_grad, preferred_element_type=jnp.float32)
    buffer_grad = jnp.einsum(
        "ecf,edf->ecd", gate_grad, gate_full, preferred_element_type=jnp.float32
    )
    buffer_grad = buffer_grad + jnp.einsum(
        "ecf,edf->ecd", up_grad, up_full, preferred_element_type=jnp.float32
    )
    return (buffer_grad, gate_wgrad, up_wgrad, down_grad)


def per_device(
    tokens,
    cotangent,
    segment_ids,
    routes,
    attn_gain,
    query_weight,
    key_matrix,
    value_weight,
    out_weight,
    ffn_gain,
    router_weight,
    gate_weight,
    up_weight,
    down_weight,
):
    dense_owned = (
        attn_gain,
        query_weight,
        key_matrix,
        value_weight,
        out_weight,
        ffn_gain,
        router_weight,
    )
    dense_weights = (
        lax.all_gather(dense_owned[0], "shard", axis=0, tiled=True),
        lax.all_gather(dense_owned[1], "shard", axis=0, tiled=True),
        lax.all_gather(dense_owned[2], "shard", axis=0, tiled=True),
        lax.all_gather(dense_owned[3], "shard", axis=0, tiled=True),
        lax.all_gather(dense_owned[4], "shard", axis=1, tiled=True),
        lax.all_gather(dense_owned[5], "shard", axis=0, tiled=True),
        lax.all_gather(dense_owned[6], "shard", axis=0, tiled=True),
    )
    tok_rows = tokens.shape[0]
    feat_width = tokens.shape[1]
    experts = gate_weight.shape[0]
    pick_count = routes.shape[1]
    first_row = lax.axis_index("shard") * tok_rows
    token_positions = first_row + jnp.arange(tok_rows, dtype=jnp.int32)
    rotary_tables = trig_tables(token_positions, HEAD_SIZE // 2)
    block_rows = min(tok_rows, 512)
    blocks = tok_rows // block_rows

    def to_blocks(stacked):
        return stacked.reshape((blocks, block_rows) + stacked.shape[1:])

    def head_major(input_rows):
        return jnp.transpose(
            input_rows.reshape(
                input_rows.shape[0], KEY_VALUE_HEADS, QUERY_HEADS // KEY_VALUE_HEADS, HEAD_SIZE
            ),
            (1, 0, 2, 3),
        )

    input_f32 = tokens.astype(jnp.float32)
    scaled1, inverse1, normalized_input = norm_forward(input_f32, dense_weights[0])
    query_rows = apply_rotary(
        jnp.dot(normalized_input, dense_weights[1], preferred_element_type=jnp.float32),
        rotary_tables,
        QUERY_HEADS,
        False,
    ).astype(jnp.bfloat16)
    projected_keys = apply_rotary(
        jnp.dot(normalized_input, dense_weights[2], preferred_element_type=jnp.float32),
        rotary_tables,
        KEY_VALUE_HEADS,
        False,
    ).astype(jnp.bfloat16)
    projected_values = jnp.dot(
        normalized_input, dense_weights[3], preferred_element_type=jnp.float32
    ).astype(jnp.bfloat16)
    gathered_key_rows, gathered_value_rows, key_segs = (
        lax.all_gather(projected_keys, "shard", axis=0, tiled=True),
        lax.all_gather(projected_values, "shard", axis=0, tiled=True),
        lax.all_gather(segment_ids, "shard", axis=0, tiled=True),
    )
    sequence_length = gathered_key_rows.shape[0]
    key_head_count = jnp.transpose(
        gathered_key_rows.reshape(sequence_length, KEY_VALUE_HEADS, HEAD_SIZE), (1, 0, 2)
    )
    value_head_count = jnp.transpose(
        gathered_value_rows.reshape(sequence_length, KEY_VALUE_HEADS, HEAD_SIZE), (1, 0, 2)
    )
    key_pos = jnp.arange(sequence_length, dtype=jnp.int32)

    def block_mask(seg_block, pos_block):
        return (seg_block[:, None] == key_segs[None, :]) & (key_pos[None, :] <= pos_block[:, None])

    def attend(block_args):
        query_block_rows, seg_block, pos_block = block_args
        allowed = block_mask(seg_block, pos_block)

        def one_head(head_args):
            query_head, key_head, value_head = head_args
            scores = head_scores(query_head, key_head, allowed)
            top_score = jnp.max(scores, axis=-1, keepdims=True)
            log_total = top_score + jnp.log(
                jnp.sum(jnp.exp(scores - top_score), axis=-1, keepdims=True)
            )
            weights = jnp.where(allowed[None, :, :], jnp.exp(scores - log_total), 0.0).astype(
                jnp.bfloat16
            )
            mixed_head = jnp.einsum(
                "gbs,sd->bgd", weights, value_head, preferred_element_type=jnp.float32
            )
            return (mixed_head, log_total)

        mixed_heads, log_total = lax.map(
            one_head, (head_major(query_block_rows), key_head_count, value_head_count)
        )
        return (
            jnp.transpose(mixed_heads, (1, 0, 2, 3)).reshape(query_block_rows.shape[0], -1),
            log_total,
        )

    mixed_rows, log_blocks = lax.map(
        attend, (to_blocks(query_rows), to_blocks(segment_ids), to_blocks(token_positions))
    )
    attended = mixed_rows.reshape(tok_rows, -1).astype(jnp.bfloat16)
    hidden = input_f32 + jnp.dot(attended, dense_weights[4], preferred_element_type=jnp.float32)
    scaled2, inverse2, normed2 = norm_forward(hidden, dense_weights[5])
    logits = jnp.dot(normed2, dense_weights[6], preferred_element_type=jnp.float32)
    expert_ids = jnp.arange(experts, dtype=jnp.int32)
    onehot = routes[:, :, None] == expert_ids[None, None, :]
    chosen = jnp.sum(jnp.where(onehot, logits[:, None, :], 0.0), axis=-1)
    gate_values = jax.nn.softmax(chosen, axis=-1)
    flat_onehot = onehot.reshape(-1, experts).astype(jnp.int32)
    earlier = jnp.cumsum(flat_onehot, axis=0) - flat_onehot
    slot_ids = jnp.sum(earlier * flat_onehot, axis=1)
    places = routes.reshape(-1) * CAP + slot_ids
    buffer = (
        jnp.zeros((experts * CAP, feat_width), jnp.bfloat16)
        .at[places]
        .set(jnp.repeat(normed2, pick_count, axis=0))
    )
    buffer = buffer.reshape(experts, CAP, feat_width)
    expert_full = (
        lax.all_gather(gate_weight, "shard", axis=1, tiled=True),
        lax.all_gather(up_weight, "shard", axis=1, tiled=True),
        lax.all_gather(down_weight, "shard", axis=1, tiled=True),
    )
    kept_acts = expert_acts(buffer, expert_full[0], expert_full[1])
    expert_out = expert_apply(kept_acts[4], expert_full[2])
    picked = (
        expert_out.reshape(experts * CAP, feat_width)[places]
        .reshape(tok_rows, pick_count, feat_width)
        .astype(jnp.float32)
    )
    expert_mix = jnp.sum(gate_values[:, :, None] * picked, axis=1)
    output = (hidden + expert_mix).astype(jnp.bfloat16)
    dense_weights = (
        lax.all_gather(dense_owned[0], "shard", axis=0, tiled=True),
        lax.all_gather(dense_owned[1], "shard", axis=0, tiled=True),
        lax.all_gather(dense_owned[2], "shard", axis=0, tiled=True),
        lax.all_gather(dense_owned[3], "shard", axis=0, tiled=True),
        lax.all_gather(dense_owned[4], "shard", axis=1, tiled=True),
        lax.all_gather(dense_owned[5], "shard", axis=0, tiled=True),
        lax.all_gather(dense_owned[6], "shard", axis=0, tiled=True),
    )
    out_grad = cotangent.astype(jnp.float32)
    gate_grads = jnp.sum(picked * out_grad[:, None, :], axis=-1)
    slot_grads = (
        (gate_values[:, :, None] * out_grad[:, None, :])
        .astype(jnp.bfloat16)
        .reshape(-1, feat_width)
    )
    expert_grad = jnp.zeros((experts * CAP, feat_width), jnp.bfloat16).at[places].set(slot_grads)
    expert_grad = expert_grad.reshape(experts, CAP, feat_width)
    buffer_grad, gate_wgrad, up_wgrad, down_wgrad = expert_grads(
        buffer, expert_grad, kept_acts, expert_full[0], expert_full[1], expert_full[2]
    )
    owned_experts = (
        lax.psum_scatter(
            gate_wgrad.astype(jnp.bfloat16), "shard", scatter_dimension=1, tiled=True
        ).astype(jnp.float32),
        lax.psum_scatter(
            up_wgrad.astype(jnp.bfloat16), "shard", scatter_dimension=1, tiled=True
        ).astype(jnp.float32),
        lax.psum_scatter(
            down_wgrad.astype(jnp.bfloat16), "shard", scatter_dimension=1, tiled=True
        ).astype(jnp.float32),
    )
    buffer_grad = buffer_grad.reshape(experts * CAP, feat_width)
    select_grad = gate_values * (
        gate_grads - jnp.sum(gate_values * gate_grads, axis=-1, keepdims=True)
    )
    logit_grads = jnp.sum(jnp.where(onehot, select_grad[:, :, None], 0.0), axis=1)
    router_grad = jnp.dot(
        normed2.astype(jnp.float32).T, logit_grads, precision=lax.Precision.HIGHEST
    )
    normed2_grad = jnp.sum(buffer_grad[places].reshape(tok_rows, pick_count, feat_width), axis=1)
    normed2_grad = normed2_grad + jnp.dot(
        logit_grads, dense_weights[6].astype(jnp.float32).T, precision=lax.Precision.HIGHEST
    )
    ffn_gain_grad, hidden_part = norm_backward(normed2_grad, scaled2, inverse2, dense_weights[5])
    hidden_grad = out_grad + hidden_part
    attn_out_grad = hidden_grad.astype(jnp.bfloat16)
    out_weight_grad = jnp.dot(attended.T, attn_out_grad, preferred_element_type=jnp.float32)
    attended_grad = jnp.dot(
        attn_out_grad, dense_weights[4].T, preferred_element_type=jnp.float32
    ).astype(jnp.bfloat16)

    def attend_back(kv_carry, block_args):
        key_total, value_total = kv_carry
        query_block_rows, seg_block, pos_block, grad_block, log_total = block_args
        allowed = block_mask(seg_block, pos_block)

        def one_head_back(head_args):
            query_head, key_head, value_head, grad_head, head_log = head_args
            scores = head_scores(query_head, key_head, allowed)
            weights = jnp.where(allowed[None, :, :], jnp.exp(scores - head_log), 0.0)
            weight_grad = jnp.einsum(
                "bgd,sd->gbs", grad_head, value_head, preferred_element_type=jnp.float32
            )
            score_grad = (
                weights * (weight_grad - jnp.sum(weights * weight_grad, axis=-1, keepdims=True))
            ).astype(jnp.bfloat16)
            query_grad = (
                jnp.einsum("gbs,sd->bgd", score_grad, key_head, preferred_element_type=jnp.float32)
                * score_scale
            )
            key_grad = (
                jnp.einsum(
                    "gbs,bgd->sd", score_grad, query_head, preferred_element_type=jnp.float32
                )
                * score_scale
            )
            value_grad = jnp.einsum(
                "gbs,bgd->sd",
                weights.astype(jnp.bfloat16),
                grad_head,
                preferred_element_type=jnp.float32,
            )
            return (query_grad, key_grad, value_grad)

        query_grad, key_grad, value_grad = lax.map(
            one_head_back,
            (
                head_major(query_block_rows),
                key_head_count,
                value_head_count,
                head_major(grad_block),
                log_total,
            ),
        )
        query_rows_grad = jnp.transpose(query_grad, (1, 0, 2, 3)).reshape(
            query_block_rows.shape[0], -1
        )
        return ((key_total + key_grad, value_total + value_grad), query_rows_grad)

    empty_key_value = jnp.zeros((KEY_VALUE_HEADS, sequence_length, HEAD_SIZE), jnp.float32)
    kv_sums, query_grads = lax.scan(
        attend_back,
        (empty_key_value, empty_key_value),
        (
            to_blocks(query_rows),
            to_blocks(segment_ids),
            to_blocks(token_positions),
            to_blocks(attended_grad),
            log_blocks,
        ),
    )
    key_value_width = projected_values.shape[1]
    kv_total = jnp.concatenate(
        [
            jnp.transpose(kv_sums[0], (1, 0, 2)).reshape(sequence_length, -1),
            jnp.transpose(kv_sums[1], (1, 0, 2)).reshape(sequence_length, -1),
        ],
        axis=1,
    )
    local_key_value = lax.psum_scatter(
        kv_total.astype(jnp.bfloat16), "shard", scatter_dimension=0, tiled=True
    ).astype(jnp.float32)
    query_grad0 = apply_rotary(
        query_grads.reshape(tok_rows, -1), rotary_tables, QUERY_HEADS, True
    ).astype(jnp.bfloat16)
    key_gradient_zero = apply_rotary(
        local_key_value[:, :key_value_width], rotary_tables, KEY_VALUE_HEADS, True
    ).astype(jnp.bfloat16)
    value_grad0 = local_key_value[:, key_value_width:].astype(jnp.bfloat16)
    query_weight_grad = jnp.dot(normalized_input.T, query_grad0, preferred_element_type=jnp.float32)
    key_weight_grad = jnp.dot(
        normalized_input.T, key_gradient_zero, preferred_element_type=jnp.float32
    )
    value_weight_grad = jnp.dot(normalized_input.T, value_grad0, preferred_element_type=jnp.float32)
    normed_grad = jnp.dot(query_grad0, dense_weights[1].T, preferred_element_type=jnp.float32)
    normed_grad = normed_grad + jnp.dot(
        key_gradient_zero, dense_weights[2].T, preferred_element_type=jnp.float32
    )
    normed_grad = normed_grad + jnp.dot(
        value_grad0, dense_weights[3].T, preferred_element_type=jnp.float32
    )
    attn_gain_grad, input_part = norm_backward(normed_grad, scaled1, inverse1, dense_weights[0])
    input_grad = hidden_grad + input_part
    dense_grads = (
        attn_gain_grad,
        query_weight_grad,
        key_weight_grad,
        value_weight_grad,
        out_weight_grad,
        ffn_gain_grad,
        router_grad,
    )
    owned_dense = (
        lax.psum_scatter(
            dense_grads[0].astype(jnp.bfloat16), "shard", scatter_dimension=0, tiled=True
        ).astype(jnp.float32),
        lax.psum_scatter(
            dense_grads[1].astype(jnp.bfloat16), "shard", scatter_dimension=0, tiled=True
        ).astype(jnp.float32),
        lax.psum_scatter(
            dense_grads[2].astype(jnp.bfloat16), "shard", scatter_dimension=0, tiled=True
        ).astype(jnp.float32),
        lax.psum_scatter(
            dense_grads[3].astype(jnp.bfloat16), "shard", scatter_dimension=0, tiled=True
        ).astype(jnp.float32),
        lax.psum_scatter(
            dense_grads[4].astype(jnp.bfloat16), "shard", scatter_dimension=1, tiled=True
        ).astype(jnp.float32),
        lax.psum_scatter(
            dense_grads[5].astype(jnp.bfloat16), "shard", scatter_dimension=0, tiled=True
        ).astype(jnp.float32),
        lax.psum_scatter(
            dense_grads[6].astype(jnp.bfloat16), "shard", scatter_dimension=0, tiled=True
        ).astype(jnp.float32),
    )
    owned_all = (
        owned_dense[0],
        owned_dense[1],
        owned_dense[2],
        owned_dense[3],
        owned_dense[4],
        owned_dense[5],
        owned_dense[6],
        owned_experts[0],
        owned_experts[1],
        owned_experts[2],
    )
    replica_parts = (
        lax.psum_scatter(owned_all[0], "rep", scatter_dimension=0, tiled=True),
        lax.psum_scatter(owned_all[1], "rep", scatter_dimension=0, tiled=True),
        lax.psum_scatter(owned_all[2], "rep", scatter_dimension=0, tiled=True),
        lax.psum_scatter(owned_all[3], "rep", scatter_dimension=0, tiled=True),
        lax.psum_scatter(owned_all[4], "rep", scatter_dimension=1, tiled=True),
        lax.psum_scatter(owned_all[5], "rep", scatter_dimension=0, tiled=True),
        lax.psum_scatter(owned_all[6], "rep", scatter_dimension=0, tiled=True),
        lax.psum_scatter(owned_all[7], "rep", scatter_dimension=1, tiled=True),
        lax.psum_scatter(owned_all[8], "rep", scatter_dimension=1, tiled=True),
        lax.psum_scatter(owned_all[9], "rep", scatter_dimension=2, tiled=True),
    )
    summed = (
        lax.all_gather(replica_parts[0].astype(jnp.bfloat16), "rep", axis=0, tiled=True).astype(
            jnp.float32
        ),
        lax.all_gather(replica_parts[1].astype(jnp.bfloat16), "rep", axis=0, tiled=True).astype(
            jnp.float32
        ),
        lax.all_gather(replica_parts[2].astype(jnp.bfloat16), "rep", axis=0, tiled=True).astype(
            jnp.float32
        ),
        lax.all_gather(replica_parts[3].astype(jnp.bfloat16), "rep", axis=0, tiled=True).astype(
            jnp.float32
        ),
        lax.all_gather(replica_parts[4].astype(jnp.bfloat16), "rep", axis=1, tiled=True).astype(
            jnp.float32
        ),
        lax.all_gather(replica_parts[5].astype(jnp.bfloat16), "rep", axis=0, tiled=True).astype(
            jnp.float32
        ),
        lax.all_gather(replica_parts[6].astype(jnp.bfloat16), "rep", axis=0, tiled=True).astype(
            jnp.float32
        ),
        lax.all_gather(replica_parts[7].astype(jnp.bfloat16), "rep", axis=1, tiled=True).astype(
            jnp.float32
        ),
        lax.all_gather(replica_parts[8].astype(jnp.bfloat16), "rep", axis=1, tiled=True).astype(
            jnp.float32
        ),
        lax.all_gather(replica_parts[9].astype(jnp.bfloat16), "rep", axis=2, tiled=True).astype(
            jnp.float32
        ),
    )
    return (
        output,
        input_grad,
        summed[0],
        summed[1],
        summed[2],
        summed[3],
        summed[4],
        summed[5],
        summed[6],
        summed[7],
        summed[8],
        summed[9],
    )


def solution(mesh):
    placed = (
        P(("rep", "shard"), None),
        P(("rep", "shard"), None),
        P(("rep", "shard")),
        P(("rep", "shard"), None),
        P("shard"),
        P("shard", None),
        P("shard", None),
        P("shard", None),
        P(None, "shard"),
        P("shard"),
        P("shard", None),
        P(None, "shard", None),
        P(None, "shard", None),
        P(None, "shard", None),
    )
    return jax.shard_map(
        per_device,
        mesh=mesh,
        in_specs=placed,
        out_specs=(
            P(("rep", "shard"), None),
            P(("rep", "shard"), None),
            P("shard"),
            P("shard", None),
            P("shard", None),
            P("shard", None),
            P(None, "shard"),
            P("shard"),
            P("shard", None),
            P(None, "shard", None),
            P(None, "shard", None),
            P(None, "shard", None),
        ),
        check_vma=False,
    )
```

profile of v0, /device:TPU:0, one launch (start us, length us, event | category | flops | bytes accessed | tf_op | source)
XLA Modules:
  0.0 2800.6 jit_solution(398512938006360574)
XLA Ops:
  9.4 12.6 all-gather
  23.2 17.1 all-gather.17.cloned.1.call-done
  44.4 24.9 all-gather.21.cloned.1.call-done
  75.3 9.5 all-gather.2
  98.2 13.1 all_gather.85
  113.1 32.9 %all-gather.25.cloned.1.call-done = bf16[1024,1024]{1,0:T(8,128)(2,1)} async-done(((bf16[256,1024]{1,0:T(8,128)(2,1)}), bf16[1024,1024]{1,0:T(8,128)(2,1)}) %all-gather.25.cloned.1.call-update) | async-done | bytes 2097168 | tf_op jit(solution)/shard_map/all_gather | solution.py:131
  149.6 27.6 all-gather.23.cloned.1.call-done
  177.2 19.7 while.50
  196.8 26.3 all-gather.27.cloned.1.call-done
  227.3 13.2 scatter_custom_fusion
  240.6 13.8 scatter_custom_fusion.1
  254.4 255.4 %all-gather.31.cloned.1.call-done = bf16[16,1024,512]{2,1,0:T(8,128)(2,1)} async-done(((bf16[16,256,512]{2,1,0:T(8,128)(2,1)}), bf16[16,1024,512]{2,1,0:T(8,128)(2,1)}) %all-gather.31.cloned.1.call-update) | async-done | bytes 16777232 | tf_op jit(solution)/shard_map/all_gather | solution.py:243
  509.8 13.4 fusion.100
  523.2 273.2 %all-gather.29.cloned.1.call-done = bf16[16,1024,512]{2,1,0:T(8,128)(2,1)} async-done(((bf16[16,256,512]{2,1,0:T(8,128)(2,1)}), bf16[16,1024,512]{2,1,0:T(8,128)(2,1)}) %all-gather.29.cloned.1.call-update) | async-done | bytes 16777232 | tf_op jit(solution)/shard_map/all_gather | solution.py:242
  796.3 13.4 fusion.99
  809.7 273.2 %all-gather.33.cloned.1.call-done = bf16[16,512,1024]{2,1,0:T(8,128)(2,1)} async-done(((bf16[16,128,1024]{2,1,0:T(8,128)(2,1)}), bf16[16,512,1024]{2,1,0:T(8,128)(2,1)}) %all-gather.33.cloned.1.call-update) | async-done | bytes 16777232 | tf_op jit(solution)/shard_map/all_gather | solution.py:244
  1082.9 16.1 multiply_convert_fusion
  1099.0 11.8 convolution_convert_fusion.3
  1110.8 14.1 gather_fusion
  1131.2 12.3 fusion.101
  1143.6 14.1 convolution_add_fusion
  1157.7 15.6 gather_fusion.1
  1185.0 69.2 %while.51 = (s32[]{:T(128)}, f32[8,256,2,64]{1,3,2,0:T(8,128)}, bf16[8,1024,64]{1,2,0:T(8,128)(2,1)}, bf16[8,1024,64]{1,2,0:T(8,128)(2,1)}, bf16[8,1024,64]{1,2,...) while((s32[]{:T(128)}, f32[8,256,2,64]{1,3,2,0:T(8,128)}, ...), condition=%wide.region_22.23_spmd.clone.clone, body=%wide.region_20.22_spmd.clone.sunk.clone | while | flops 341671424 | bytes 17585272 | solution.py:340
  1257.3 11.1 convolution_convert_fusion
  1268.4 11.7 convolution_convert_fusion.2
  1280.2 11.1 convolution_convert_fusion.1
  1304.8 276.8 %reduce-scatter.48.cloned.1.call-done = bf16[16,128,1024]{2,1,0:T(8,128)(2,1)} async-done(((bf16[16,512,1024]{2,1,0:T(8,128)(2,1)}), bf16[16,128,1024]{2,1,0:T(8,128)(2,1)}) %reduce-scatter.48.cloned.1.call-update) | async-done | bytes 4194320 | tf_op jit(solution)/shard_map/reduce_scatter | solution.py:283
  1581.7 283.2 %reduce-scatter.40.cloned.1.call-done = bf16[16,256,512]{2,1,0:T(8,128)(2,1)} async-done(((bf16[16,1024,512]{2,1,0:T(8,128)(2,1)}), bf16[16,256,512]{2,1,0:T(8,128)(2,1)}) %reduce-scatter.40.cloned.1.call-update) | async-done | bytes 4194320 | tf_op jit(solution)/shard_map/reduce_scatter | solution.py:277
  1864.9 283.5 %reduce-scatter.44.cloned.1.call-done = bf16[16,256,512]{2,1,0:T(8,128)(2,1)} async-done(((bf16[16,1024,512]{2,1,0:T(8,128)(2,1)}), bf16[16,256,512]{2,1,0:T(8,128)(2,1)}) %reduce-scatter.44.cloned.1.call-update) | async-done | bytes 4194320 | tf_op jit(solution)/shard_map/reduce_scatter | solution.py:280
  2148.5 22.2 reduce-scatter.38.cloned.1.call-done
  2172.2 43.4 %reduce-scatter.24.cloned.1.call-done = bf16[256,1024]{1,0:T(8,128)(2,1)} async-done(((bf16[1024,1024]{1,0:T(8,128)(2,1)}), bf16[256,1024]{1,0:T(8,128)(2,1)}) %reduce-scatter.24.cloned.1.call-update) | async-done | bytes 524304 | tf_op jit(solution)/shard_map/reduce_scatter | solution.py:412
  2215.7 45.9 %reduce-scatter.36.cloned.1.call-done = bf16[1024,256]{1,0:T(8,128)(2,1)} async-done(((bf16[1024,1024]{1,0:T(8,128)(2,1)}), bf16[1024,256]{1,0:T(8,128)(2,1)}) %reduce-scatter.36.cloned.1.call-update) | async-done | bytes 524304 | tf_op jit(solution)/shard_map/reduce_scatter | solution.py:421
  2263.8 27.0 reduce-scatter.28.cloned.1.call-done
  2290.9 28.5 %reduce-scatter.32.cloned.1.call-done = bf16[256,512]{1,0:T(8,128)(2,1)} async-done(((bf16[1024,512]{1,0:T(8,128)(2,1)}), bf16[256,512]{1,0:T(8,128)(2,1)}) %reduce-scatter.32.cloned.1.call-update) | async-done | bytes 262160 | tf_op jit(solution)/shard_map/reduce_scatter | solution.py:418
  2319.5 53.7 %reduce-scatter.50.cloned.1.call-done = bf16[16,128,128]{2,1,0:T(8,128)(2,1)} async-done(((bf16[16,128,1024]{2,1,0:T(8,128)(2,1)}), bf16[16,128,128]{2,1,0:T(8,128)(2,1)}) %reduce-scatter.50.cloned.1.call-update) | async-done | bytes 524304 | tf_op jit(solution)/shard_map/reduce_scatter | solution.py:453
  2373.2 54.5 %reduce-scatter.42.cloned.1.call-done = bf16[16,32,512]{2,1,0:T(8,128)(2,1)} async-done(((bf16[16,256,512]{2,1,0:T(8,128)(2,1)}), bf16[16,32,512]{2,1,0:T(8,128)(2,1)}) %reduce-scatter.42.cloned.1.call-update) | async-done | bytes 524304 | tf_op jit(solution)/shard_map/reduce_scatter | solution.py:451
  2427.8 55.0 %reduce-scatter.46.cloned.1.call-done = bf16[16,32,512]{2,1,0:T(8,128)(2,1)} async-done(((bf16[16,256,512]{2,1,0:T(8,128)(2,1)}), bf16[16,32,512]{2,1,0:T(8,128)(2,1)}) %reduce-scatter.46.cloned.1.call-update) | async-done | bytes 524304 | tf_op jit(solution)/shard_map/reduce_scatter | solution.py:452
  2488.3 31.4 %reduce-scatter.54.cloned.1.call-done = f32[32,16]{1,0:T(8,128)} async-done(((f32[256,16]{1,0:T(8,128)}), f32[32,16]{1,0:T(8,128)}) %reduce-scatter.54.cloned.1.call-update) | async-done | bytes 2064
  2534.3 11.7 all-reduce.8
  2546.0 11.9 all-reduce.6
  2558.5 11.8 all-reduce.7
  2582.9 14.0 reduce-scatter.52.cloned.1.call-done
  2597.9 9.8 all_gather.93
  2608.8 24.8 reduce-scatter.30.cloned.1.call-done
  2643.7 26.7 reduce-scatter.34.cloned.1.call-done
  2680.5 29.1 %all-gather.39.cloned.1.call-done = bf16[16,128,1024]{2,1,0:T(8,128)(2,1)} async-done(((bf16[16,128,128]{2,1,0:T(8,128)(2,1)}), bf16[16,128,1024]{2,1,0:T(8,128)(2,1)}) %all-gather.39.cloned.1.call-update) | async-done | bytes 4194320 | tf_op jit(solution)/shard_map/all_gather | solution.py:483
  2716.3 32.0 %all-gather.35.cloned.1.call-done = bf16[16,256,512]{2,1,0:T(8,128)(2,1)} async-done(((bf16[16,32,512]{2,1,0:T(8,128)(2,1)}), bf16[16,256,512]{2,1,0:T(8,128)(2,1)}) %all-gather.35.cloned.1.call-update) | async-done | bytes 4194320 | tf_op jit(solution)/shard_map/all_gather | solution.py:477
  2755.0 31.9 %all-gather.37.cloned.1.call-done = bf16[16,256,512]{2,1,0:T(8,128)(2,1)} async-done(((bf16[16,32,512]{2,1,0:T(8,128)(2,1)}), bf16[16,256,512]{2,1,0:T(8,128)(2,1)}) %all-gather.37.cloned.1.call-update) | async-done | bytes 4194320 | tf_op jit(solution)/shard_map/all_gather | solution.py:480
  (328 shorter events, 236.9 us)
Async XLA Ops:
  7.2 62.1 %copy-start = (bf16[256,1024]{1,0:T(8,128)(2,1)S(1)}, bf16[256,1024]{1,0:T(8,128)(2,1)}, u32[]{:S(2)}) copy-start(bf16[256,1024]{1,0:T(8,128)(2,1)} %param.18) | copy-start | bytes 1572868
  7.2 33.1 %all-gather.17.cloned.1.call-start = ((), (), s32[]{:S(2)}) async-start(), calls=%async_computation.17 | async-start | bytes 1310720 | tf_op jit(solution)/shard_map/all_gather | solution.py:133
  7.9 61.4 %all-gather.21.cloned.1.call-start = ((), (), s32[]{:S(2)}) async-start(), calls=%async_computation.19 | async-start | bytes 1310720 | tf_op jit(solution)/shard_map/all_gather | solution.py:132
  8.7 102.9 %all-gather.19.cloned.1.call-start = ((), (), s32[]{:S(2)}) async-start(), calls=%async_computation.18 | async-start | bytes 1310720 | tf_op jit(solution)/shard_map/all_gather | solution.py:178
  22.0 124.0 %copy-start.19 = (f32[4,1,256]{2,1,0:T(1,128)}, f32[4,1,256]{2,1,0:T(1,128)S(1)}, u32[]{:S(2)}) copy-start(f32[4,1,256]{2,1,0:T(1,128)S(1)} %convert_element_type.300) | copy-start | bytes 12292
  23.2 122.7 %copy-start.23 = (f32[256]{0:T(256)}, f32[256]{0:T(256)S(1)}, u32[]{:S(2)}) copy-start(f32[256]{0:T(256)S(1)} %add_rsqrt_fusion.1) | copy-start | bytes 3076
  42.9 103.0 %all-gather.25.cloned.1.call-start = ((), (), s32[]{:S(2)}) async-start(), calls=%async_computation.21 | async-start | bytes 2621440 | tf_op jit(solution)/shard_map/all_gather | solution.py:131
  43.5 133.6 %all-gather.23.cloned.1.call-start = ((), (), s32[]{:S(2)}) async-start(), calls=%async_computation.20 | async-start | bytes 1310720 | tf_op jit(solution)/shard_map/all_gather | solution.py:177
  44.4 104.1 %copy-start.16 = (f32[256,32]{0,1:T(8,128)}, f32[256,32]{0,1:T(8,128)S(1)}, u32[]{:S(2)}) copy-start(f32[256,32]{0,1:T(8,128)S(1)} %get-tuple-element.353) | copy-start | bytes 98308
  71.9 151.2 %all-gather.27.cloned.1.call-start = ((), (), s32[]{:S(2)}) async-start(), calls=%async_computation.22 | async-start | bytes 2621440 | tf_op jit(solution)/shard_map/all_gather | solution.py:134
  72.5 437.3 %all-gather.31.cloned.1.call-start = ((), (), s32[]{:S(2)}) async-start(), calls=%async_computation.24 | async-start | bytes 20971520 | tf_op jit(solution)/shard_map/all_gather | solution.py:243
  73.3 16.9 copy-start.14
  73.3 723.0 %all-gather.29.cloned.1.call-start = ((), (), s32[]{:S(2)}) async-start(), calls=%async_computation.23 | async-start | bytes 20971520 | tf_op jit(solution)/shard_map/all_gather | solution.py:242
  74.0 16.3 copy-start.22
  74.1 24.1 copy-start.25
  74.1 1008.8 %all-gather.33.cloned.1.call-start = ((), (), s32[]{:S(2)}) async-start(), calls=%async_computation.25 | async-start | bytes 20971520 | tf_op jit(solution)/shard_map/all_gather | solution.py:244
  74.8 1224.6 %reduce-scatter.22.cloned.1.call-start = ((), (), s32[]{:S(2)}) async-start(), calls=%async_computation.26 | async-start | bytes 2621440 | tf_op jit(solution)/shard_map/reduce_scatter | solution.py:375
  90.3 150.2 %copy-start.6 = (f32[256,1024]{1,0:T(8,128)}, f32[256,1024]{1,0:T(8,128)S(1)}, u32[]{:S(2)}) copy-start(f32[256,1024]{1,0:T(8,128)S(1)} %convert_element_type.251) | copy-start | bytes 3145732
  196.8 43.7 %copy-start.10 = (bf16[8,256,2,64]{1,3,2,0:T(8,128)(2,1)}, bf16[8,256,2,64]{1,3,2,0:T(8,128)(2,1)S(1)}, u32[]{:S(2)}) copy-start(bf16[8,256,2,64]{1,3,2,0:T(8,128)(2,1)S(1)} %get-tuple-element.173) | copy-start | bytes 1572868
  196.8 43.7 %copy-start.13 = (bf16[8,1024,64]{1,2,0:T(8,128)(2,1)}, bf16[8,1024,64]{1,2,0:T(8,128)(2,1)S(1)}, u32[]{:S(2)}) copy-start(bf16[8,1024,64]{1,2,0:T(8,128)(2,1)S(1)} %get-tuple-element.685) | copy-start | bytes 3145732
  226.7 27.7 copy-start.8
  1173.2 5.8 copy-start.3
  1173.3 6.8 copy-start.12
  1173.3 6.8 copy-start.15
  1257.2 324.4 %reduce-scatter.48.cloned.1.call-start = ((), (), s32[]{:S(2)}) async-start(), calls=%async_computation.41 | async-start | bytes 20971520 | tf_op jit(solution)/shard_map/reduce_scatter | solution.py:283
  1268.4 596.5 %reduce-scatter.40.cloned.1.call-start = ((), (), s32[]{:S(2)}) async-start(), calls=%async_computation.35 | async-start | bytes 20971520 | tf_op jit(solution)/shard_map/reduce_scatter | solution.py:277
  1280.1 868.3 %reduce-scatter.44.cloned.1.call-start = ((), (), s32[]{:S(2)}) async-start(), calls=%async_computation.38 | async-start | bytes 20971520 | tf_op jit(solution)/shard_map/reduce_scatter | solution.py:280
  1291.3 3.3 copy-start.20
  1291.3 879.4 %reduce-scatter.38.cloned.1.call-start = ((), (), s32[]{:S(2)}) async-start(), calls=%async_computation.34 | async-start | bytes 40960 | tf_op jit(solution)/shard_map/reduce_scatter | solution.py:427
  1292.0 4.8 copy-start.5
  1292.1 4.8 copy-start.11
  1294.5 921.1 %reduce-scatter.24.cloned.1.call-start = ((), (), s32[]{:S(2)}) async-start(), calls=%async_computation.27 | async-start | bytes 2621440 | tf_op jit(solution)/shard_map/reduce_scatter | solution.py:412
  1296.8 964.7 %reduce-scatter.36.cloned.1.call-start = ((), (), s32[]{:S(2)}) async-start(), calls=%async_computation.33 | async-start | bytes 2621440 | tf_op jit(solution)/shard_map/reduce_scatter | solution.py:421
  1299.0 991.9 %reduce-scatter.28.cloned.1.call-start = ((), (), s32[]{:S(2)}) async-start(), calls=%async_computation.29 | async-start | bytes 1310720 | tf_op jit(solution)/shard_map/reduce_scatter | solution.py:415
  1302.2 1017.2 %reduce-scatter.32.cloned.1.call-start = ((), (), s32[]{:S(2)}) async-start(), calls=%async_computation.31 | async-start | bytes 1310720 | tf_op jit(solution)/shard_map/reduce_scatter | solution.py:418
  1304.7 1068.4 %reduce-scatter.50.cloned.1.call-start = ((), (), s32[]{:S(2)}) async-start(), calls=%async_computation.42 | async-start | bytes 4718592 | tf_op jit(solution)/shard_map/reduce_scatter | solution.py:453
  1581.6 846.1 %reduce-scatter.42.cloned.1.call-start = ((), (), s32[]{:S(2)}) async-start(), calls=%async_computation.36 | async-start | bytes 4718592 | tf_op jit(solution)/shard_map/reduce_scatter | solution.py:451
  1864.9 617.9 %reduce-scatter.46.cloned.1.call-start = ((), (), s32[]{:S(2)}) async-start(), calls=%async_computation.39 | async-start | bytes 4718592 | tf_op jit(solution)/shard_map/reduce_scatter | solution.py:452
  2148.4 334.4 %copy-start.28 = (u32[32]{0:T(128)S(1)}, u32[32]{0:T(128)}, u32[]{:S(2)}) copy-start(u32[32]{0:T(128)} %constant.133) | copy-start | bytes 388
  2148.4 335.0 %copy-start.26 = (u32[32]{0:T(128)S(1)}, u32[32]{0:T(128)}, u32[]{:S(2)}) copy-start(u32[32]{0:T(128)} %constant.121) | copy-start | bytes 388
  2148.4 371.3 %reduce-scatter.54.cloned.1.call-start = ((), (), s32[]{:S(2)}) async-start(), calls=%async_computation.45 | async-start | bytes 147456
  2172.2 400.5 %reduce-scatter.26.cloned.1.call-start = ((), (), s32[]{:S(2)}) async-start(), calls=%async_computation.28 | async-start | bytes 589824 | tf_op jit(solution)/shard_map/reduce_scatter | solution.py:445
  2215.6 381.3 %reduce-scatter.52.cloned.1.call-start = ((), (), s32[]{:S(2)}) async-start(), calls=%async_computation.44 | async-start | bytes 1179648
  2263.8 369.8 %reduce-scatter.30.cloned.1.call-start = ((), (), s32[]{:S(2)}) async-start(), calls=%async_computation.30 | async-start | bytes 294912 | tf_op jit(solution)/shard_map/reduce_scatter | solution.py:446
  2290.9 379.5 %reduce-scatter.34.cloned.1.call-start = ((), (), s32[]{:S(2)}) async-start(), calls=%async_computation.32 | async-start | bytes 294912 | tf_op jit(solution)/shard_map/reduce_scatter | solution.py:447
  2319.4 390.2 %all-gather.39.cloned.1.call-start = ((), (), s32[]{:S(2)}) async-start(), calls=%async_computation.43 | async-start | bytes 4718592 | tf_op jit(solution)/shard_map/all_gather | solution.py:483
  2373.2 375.1 %all-gather.35.cloned.1.call-start = ((), (), s32[]{:S(2)}) async-start(), calls=%async_computation.37 | async-start | bytes 4718592 | tf_op jit(solution)/shard_map/all_gather | solution.py:477
  2427.7 359.2 %all-gather.37.cloned.1.call-start = ((), (), s32[]{:S(2)}) async-start(), calls=%async_computation.40 | async-start | bytes 4718592 | tf_op jit(solution)/shard_map/all_gather | solution.py:480
  (10 other events, 19.2 us)
Sparse Core Ops, SparseCore 0:
  9.6 30.6 all-gather.16
  41.9 27.3 all-gather.20
  71.4 27.5 all-gather.18
  100.4 45.4 all-gather.24
  147.9 29.1 all-gather.22
  178.6 44.5 all-gather.26
  224.7 285.0 all-gather.30
  511.3 284.9 all-gather.28
  797.9 284.9 all-gather.32
  1257.3 42.0 reduce-scatter.21
  1301.9 279.6 reduce-scatter.47
  1583.8 281.0 reduce-scatter.39
  1867.3 281.0 reduce-scatter.43
  2151.1 19.6 reduce-scatter.37
  2173.5 42.0 reduce-scatter.23
  2218.3 43.1 reduce-scatter.35
  2264.4 26.4 reduce-scatter.27
  2293.6 25.7 reduce-scatter.31
  2323.1 49.9 reduce-scatter.49
  2376.3 51.3 reduce-scatter.41
  2431.4 51.2 reduce-scatter.45
  2486.3 33.3 reduce-scatter.53
  2523.1 34.1 reduce-scatter.25
  2560.9 36.0 reduce-scatter.51
  2600.0 33.5 reduce-scatter.29
  2636.8 33.5 reduce-scatter.33
  2672.1 37.4 all-gather.38
  2711.5 36.7 all-gather.34
  2750.2 36.7 all-gather.36
where the time goes:
time: 2810 us; the launch traced here: 2800 us
  waiting for transfers between devices  2300 us (82%)
  matrix products  221 us (8%)
  blocking collectives  125 us (4%)
  other arithmetic  76.6 us (3%)
  local copies, waits for them, and re-layouts  59.4 us (2%)
    reduce_scatter x1, waiting for transfers between devices, per_device(): lax.psum_scatter(up_wgrad.astype(jnp.bfloat16), 'shard', scatter_dimensio...  283 us
    reduce_scatter x1, waiting for transfers between devices, per_device(): lax.psum_scatter(gate_wgrad.astype(jnp.bfloat16), 'shard', scatter_dimens...  283 us
    reduce_scatter x1, waiting for transfers between devices, per_device(): lax.psum_scatter(down_wgrad.astype(jnp.bfloat16), 'shard', scatter_dimens...  277 us
    all_gather x1, waiting for transfers between devices, per_device(): lax.all_gather(down_weight, 'shard', axis=1, tiled=True)  273 us
    all_gather x1, waiting for transfers between devices, per_device(): lax.all_gather(gate_weight, 'shard', axis=1, tiled=True)  273 us
    all_gather x1, waiting for transfers between devices, per_device(): lax.all_gather(up_weight, 'shard', axis=1, tiled=True)  255 us
  transfers between devices with their start and end apart: 29, of which 27 were waited for; matrix products, arithmetic and copies ran while one was open for 6% of the time, Pallas kernels for 0%

commit v1 on v0

v1 whole, which is shorter than its diff:
```python
import functools
import math

import jax
import jax.numpy as jnp
from jax import lax
from jax.experimental import pallas as pl
from jax.experimental.pallas import tpu as pltpu
from jax.sharding import Mesh
from jax.sharding import PartitionSpec as P

QUERY_HEADS = 16
KEY_VALUE_HEADS = 8
HEAD = 64
LANES = 128

EPS = 1e-06
ROPE_BASE = 10000.0
MASKED = -1e30
F32 = jnp.float32
BF16 = jnp.bfloat16
NT = (((1,), (1,)), ((), ()))
TN = (((0,), (0,)), ((), ()))
VMEM_LIMIT = 60 * 1024 * 1024


def dot(a, b):
    return jnp.dot(a, b, preferred_element_type=F32)


def dot_nt(a, b):
    return lax.dot_general(a, b, NT, preferred_element_type=F32)


def dot_tn(a, b):
    return lax.dot_general(a, b, TN, preferred_element_type=F32)


def split_hi_lo(value):
    high = value.astype(BF16)
    return high, (value - high.astype(F32)).astype(BF16)


def inverse_rms(value):
    return lax.rsqrt(jnp.mean(value * value, axis=-1, keepdims=True) + EPS)


def swap_halves(value):
    width = value.shape[1]
    lane = lax.broadcasted_iota(jnp.int32, value.shape, 1)
    up = pltpu.roll(value, width - HEAD // 2, 1)
    down = pltpu.roll(value, HEAD // 2, 1)
    return jnp.where(lane % HEAD < HEAD // 2, up, down)


def rotate(value, cosine, sine):
    copies = value.shape[1] // LANES
    cosine = jnp.concatenate([cosine] * copies, axis=1)
    sine = jnp.concatenate([sine] * copies, axis=1)
    return value * cosine + swap_halves(value) * sine


def allowed_pairs(seg_col, seg_row, row0, count):
    rows = seg_col.shape[0]
    row = row0 + lax.broadcasted_iota(jnp.int32, (rows, count), 0)
    col = lax.broadcasted_iota(jnp.int32, (rows, count), 1)
    return (seg_col == seg_row) & (col <= row)


def front_kernel(
    block, heads, kv_heads, x_ref, gain_ref, w_ref, cos_ref, sin_ref, segc_ref, segr_ref,
    normed_ref, q_ref, k_ref, v_ref, att_ref, lse_ref, out_s,
):
    seq = x_ref.shape[0]
    blocks = seq // block
    group = heads // kv_heads
    qw, kw = heads * HEAD, kv_heads * HEAD

    def project(i, carry):
        rows = pl.ds(pl.multiple_of(i * block, block), block)
        x = x_ref[rows, :].astype(F32)
        normed = (x * inverse_rms(x) * gain_ref[...]).astype(BF16)
        normed_ref[rows, :] = normed
        qkv = dot(normed, w_ref[...])
        turned = rotate(qkv[:, : qw + kw], cos_ref[rows, :], sin_ref[rows, :])
        for h in range(heads):
            q_ref[h, rows, :] = turned[:, h * HEAD : (h + 1) * HEAD].astype(BF16)
        for h in range(kv_heads):
            k_ref[h, rows, :] = turned[:, qw + h * HEAD : qw + (h + 1) * HEAD].astype(BF16)
            v_ref[h, rows, :] = qkv[:, qw + kw + h * HEAD : qw + kw + (h + 1) * HEAD].astype(BF16)
        return carry

    lax.fori_loop(0, blocks, project, 0)

    def one_head(h, carry):
        kv = h // group
        for i in range(blocks):
            count = (i + 1) * block
            rows = slice(i * block, (i + 1) * block)
            q = q_ref[h, rows, :] * jnp.asarray(0.125, BF16)
            k = k_ref[kv, :count, :]
            v = v_ref[kv, :count, :]
            allowed = allowed_pairs(segc_ref[rows, :], segr_ref[:, :count], i * block, count)
            s = jnp.where(allowed, dot_nt(q, k), MASKED)
            top = jnp.max(s, axis=-1, keepdims=True)
            e = jnp.exp(s - top)
            total = jnp.sum(e, axis=-1, keepdims=True)
            lse_ref[h, rows, :] = top + jnp.log(total)
            p = (e * (1.0 / total)).astype(BF16)
            out_s[h, rows, :] = dot(p, v)
        return carry

    lax.fori_loop(0, heads, one_head, 0)
    for h in range(heads):
        att_ref[:, h * HEAD : (h + 1) * HEAD] = out_s[h].astype(BF16)


def back_kernel(
    block, heads, kv_heads, q_ref, k_ref, v_ref, do_ref, lse_ref, segc_ref, segr_ref, x_ref,
    normed_ref, w_ref, cos_ref, sin_ref, ng_ref, dw_ref, gain_ref, do_s, dq_s, dk_s, dv_s, raw_s, g_s,
):
    seq = x_ref.shape[0]
    blocks = seq // block
    group = heads // kv_heads
    qw, kw = heads * HEAD, kv_heads * HEAD
    for h in range(heads):
        do_s[h] = do_ref[:, h * HEAD : (h + 1) * HEAD]
    dk_s[...] = jnp.zeros_like(dk_s)
    dv_s[...] = jnp.zeros_like(dv_s)

    def one_head(h, carry):
        kv = h // group
        for i in range(blocks):
            count = (i + 1) * block
            rows = slice(i * block, (i + 1) * block)
            q = q_ref[h, rows, :] * jnp.asarray(0.125, BF16)
            k = k_ref[kv, :count, :]
            v = v_ref[kv, :count, :]
            do = do_s[h, rows, :]
            allowed = allowed_pairs(segc_ref[rows, :], segr_ref[:, :count], i * block, count)
            s = jnp.where(allowed, dot_nt(q, k), MASKED)
            prob = jnp.exp(s - lse_ref[h, rows, :])
            grad = dot_nt(do, v)
            inner = jnp.sum(prob * grad, axis=-1, keepdims=True)
            ds = (prob * (grad - inner)).astype(BF16)
            dq_s[h, rows, :] = dot(ds, k) * 0.125
            dk_s[kv, :count, :] += dot_tn(ds, q)
            dv_s[kv, :count, :] += dot_tn(prob.astype(BF16), do)
        return carry

    lax.fori_loop(0, heads, one_head, 0)
    for h in range(heads):
        raw_s[:, h * HEAD : (h + 1) * HEAD] = dq_s[h]
    for h in range(kv_heads):
        raw_s[:, qw + h * HEAD : qw + (h + 1) * HEAD] = dk_s[h]
        raw_s[:, qw + kw + h * HEAD : qw + kw + (h + 1) * HEAD] = dv_s[h]
    gain_ref[...] = jnp.zeros_like(gain_ref)

    def finish(i, carry):
        rows = pl.ds(pl.multiple_of(i * block, block), block)
        g_s[rows, : qw + kw] = rotate(raw_s[rows, : qw + kw], cos_ref[rows, :], -sin_ref[rows, :]).astype(BF16)
        g_s[rows, qw + kw :] = raw_s[rows, qw + kw :].astype(BF16)
        ng = dot_nt(g_s[rows, :], w_ref[...])
        x = x_ref[rows, :].astype(F32)
        gain_ref[...] += jnp.sum(ng * (x * inverse_rms(x)), axis=0, keepdims=True)
        ng_ref[rows, :] = ng.astype(BF16)
        return carry

    lax.fori_loop(0, blocks, finish, 0)
    width = normed_ref.shape[1]
    for c in range(0, width, 256):
        dw_ref[c : c + 256, :] = dot_tn(normed_ref[:, c : c + 256], g_s[...]).astype(BF16)


def softmax_gates(logits, mask):
    shown = jnp.where(mask > 0.0, logits, MASKED)
    e = jnp.where(mask > 0.0, jnp.exp(shown - jnp.max(shown, axis=-1, keepdims=True)), 0.0)
    return e * (1.0 / jnp.sum(e, axis=-1, keepdims=True))


def mid_kernel(x_ref, att_ref, ow_ref, gain_ref, router_ref, mask_ref, hidden_ref, normed_ref, gates_ref):
    parts, width = ow_ref.shape[0], ow_ref.shape[2]
    depth = att_ref.shape[2]
    for j in range(parts):
        cols = slice(j * width, (j + 1) * width)
        total = x_ref[:, cols].astype(F32)
        for i in range(att_ref.shape[0]):
            total = total + dot(att_ref[i], ow_ref[j, i * depth : (i + 1) * depth, :])
        hidden_ref[:, cols] = total
    hidden = hidden_ref[...]
    normed = (hidden * inverse_rms(hidden) * gain_ref[...]).astype(BF16)
    normed_ref[...] = normed
    gates_ref[...] = softmax_gates(dot(normed, router_ref[...]), mask_ref[...])


def mid_back_kernel(
    hidden_ref, nb_ref, dy_ref, gates_ref, mix_ref, normed_ref, router_ref, gain_ref, ow_ref, att_ref,
    hg_ref, ag_ref, owg_ref, fg_ref, rg_ref, aog_s,
):
    gates = gates_ref[...]
    mix = mix_ref[...]
    lg = gates * (mix - jnp.sum(gates * mix, axis=-1, keepdims=True))
    high, low = split_hi_lo(lg)
    normed = normed_ref[...]
    rg_ref[...] = dot_tn(high, normed) + dot_tn(low, normed)
    router = router_ref[...]
    ng = nb_ref[...].astype(F32) + dot_nt(high, router) + dot_nt(low, router)
    hidden = hidden_ref[...]
    inv = inverse_rms(hidden)
    scaled = hidden * inv
    fg_ref[...] = jnp.sum(ng * scaled, axis=0, keepdims=True)
    w = ng * gain_ref[...]
    hg = dy_ref[...].astype(F32) + inv * (w - scaled * jnp.mean(w * scaled, axis=-1, keepdims=True))
    hg_ref[...] = hg
    aog_s[...] = hg.astype(BF16)
    parts, width = ow_ref.shape[0], ow_ref.shape[2]
    groups, _, depth = att_ref.shape
    for i in range(groups):
        rows = slice(i * depth, (i + 1) * depth)
        total = dot_nt(aog_s[:, 0:width], ow_ref[0, rows, :])
        for j in range(1, parts):
            total = total + dot_nt(aog_s[:, j * width : (j + 1) * width], ow_ref[j, rows, :])
        ag_ref[i] = total.astype(BF16)
        for j in range(parts):
            owg_ref[j, rows, :] = dot_tn(att_ref[i], aog_s[:, j * width : (j + 1) * width]).astype(BF16)


def expert_kernel(
    experts, parts, place_ref, n2_ref, dy_ref, mask_ref, router_ref, *refs
):
    weights = refs[: 3 * parts]
    moe_ref, nb_ref, mix_ref, inner_ref, gg_ref, ug_ref = refs[3 * parts : 3 * parts + 6]
    wg_s, wu_s, wd_s, sems = refs[3 * parts + 6 :]
    z = place_ref[0]
    first = place_ref[1]

    @pl.when(pl.program_id(0) == 0)
    def load():
        copies = []
        for m, target in enumerate((wg_s, wu_s, wd_s)):
            for k in range(parts):
                source = weights[m * parts + k]
                size = source.shape[1]
                chunk = lax.rem(z - k + parts, parts)
                at = pl.ds(pl.multiple_of(chunk * size, size), size)
                copies.append(pltpu.make_async_copy(source, target.at[:, at, :], sems.at[m * parts + k]))
        for copy in copies:
            copy.start()
        for copy in copies:
            copy.wait()

    x = n2_ref[...]
    dy = dy_ref[...].astype(F32)
    gates = softmax_gates(dot(x, router_ref[...]), mask_ref[...])
    lane = lax.broadcasted_iota(jnp.int32, gates.shape, 1)
    moe = nb = mix_out = None
    for e in range(experts):
        g = jnp.sum(jnp.where(lane == first + e, gates, 0.0), axis=-1, keepdims=True)
        ga = dot(x, wg_s[e])
        ua = dot(x, wu_s[e])
        sg = jax.nn.sigmoid(ga)
        act = ga * sg
        inner = (act * ua).astype(BF16)
        inner_ref[e] = inner
        eo = dot(inner, wd_s[e]).astype(BF16).astype(F32)
        mix = jnp.sum(dy * eo, axis=-1, keepdims=True)
        part = g * eo
        moe = part if moe is None else moe + part
        row = jnp.where(lane == e, mix, 0.0) + jnp.where(lane == experts + e, g, 0.0)
        mix_out = row if mix_out is None else mix_out + row
        ig = dot_nt((g * dy).astype(BF16), wd_s[e])
        gg = (ig * ua * sg * (1.0 + ga * (1.0 - sg))).astype(BF16)
        ug = (ig * act).astype(BF16)
        gg_ref[e] = gg
        ug_ref[e] = ug
        back = dot_nt(gg, wg_s[e]) + dot_nt(ug, wu_s[e])
        nb = back if nb is None else nb + back
    moe_ref[...] = moe.astype(BF16)
    nb_ref[...] = nb.astype(BF16)
    mix_ref[...] = mix_out


def expert_grad_kernel(
    experts, parts, place_ref, n2_ref, dy_ref, mix_ref, inner_ref, gg_ref, ug_ref,
    dg_ref, du_ref, dd_ref, g_s, u_s, d_s,
):
    e, step = pl.program_id(0), pl.program_id(1)

    @pl.when(step == 0)
    def clear():
        g_s[...] = jnp.zeros_like(g_s)
        u_s[...] = jnp.zeros_like(u_s)
        d_s[...] = jnp.zeros_like(d_s)

    x = n2_ref[...]
    mix = mix_ref[...]
    lane = lax.broadcasted_iota(jnp.int32, mix.shape, 1)
    g = jnp.sum(jnp.where(lane == experts + e, mix, 0.0), axis=-1, keepdims=True)
    og = (g * dy_ref[...].astype(F32)).astype(BF16)
    g_s[...] += dot_tn(x, gg_ref[0])
    u_s[...] += dot_tn(x, ug_ref[0])
    d_s[...] += dot_tn(inner_ref[0], og)

    @pl.when(step == pl.num_programs(1) - 1)
    def store():
        z = place_ref[0]
        for total, out in ((g_s, dg_ref), (u_s, du_ref), (d_s, dd_ref)):
            size = out.shape[2]
            for k in range(parts):
                chunk = lax.rem(z - k + parts, parts)
                out[k, 0] = total[pl.ds(pl.multiple_of(chunk * size, size), size), :].astype(BF16)


def sds(shape, dtype):
    return jax.ShapeDtypeStruct(shape, dtype)


def params():
    return pltpu.CompilerParams(vmem_limit_bytes=VMEM_LIMIT)


def per_device(
    hi, ep, n, tokens, cotangent, segment_ids, routes, attn_gain, query_weight, key_matrix, value_weight,
    out_weight, ffn_gain, router_weight, gate_weight, up_weight, down_weight,
):
    rows, width = tokens.shape
    seq = rows * n
    experts = gate_weight.shape[0]
    own = experts // ep
    heads, kv_heads = QUERY_HEADS // n, KEY_VALUE_HEADS // n
    qw, kw = heads * HEAD, kv_heads * HEAD
    cols = qw + 2 * kw
    slab = width // n
    ff = gate_weight.shape[2]
    z = lax.axis_index("shard").astype(jnp.int32)
    r = lax.axis_index("ep").astype(jnp.int32)
    place = jnp.stack([z, r * own])
    ring = [(i, (i + 1) % n) for i in range(n)]
    everyone = ("hi", "ep", "shard")

    x_all = lax.all_gather(tokens, "shard", axis=0, tiled=True)
    by_dest = jnp.concatenate(
        [
            query_weight.reshape(slab, n, qw),
            key_matrix.reshape(slab, n, kw),
            value_weight.reshape(slab, n, kw),
        ],
        axis=2,
    ).transpose(1, 0, 2)
    w_qkv = lax.all_to_all(by_dest, "shard", 0, 0).reshape(width, cols)

    pack = jnp.concatenate(
        [
            attn_gain[None],
            ffn_gain[None],
            segment_ids.astype(BF16)[None],
            router_weight.T,
        ],
        axis=0,
    )
    packs = lax.all_gather(pack, "shard", axis=0, tiled=False)
    gain1 = packs[:, 0, :].reshape(1, width).astype(F32)
    gain2 = packs[:, 1, :].reshape(1, width).astype(F32)
    segments = packs[:, 2, :].reshape(seq).astype(F32)
    seg_col, seg_row = segments[:, None], segments[None, :]
    router = jnp.pad(packs[:, 3:, :].transpose(0, 2, 1).reshape(width, experts), ((0, 0), (0, LANES - experts)))
    ids = jnp.arange(experts, dtype=jnp.int32)
    routed = jnp.any(routes[:, :, None] == ids[None, None, :], axis=1)
    mask_own = jnp.pad(routed.astype(F32), ((0, 0), (0, LANES - experts)))
    mask_all = lax.all_gather(routed.T.astype(BF16), "ep", axis=0, tiled=False)
    mask_all = mask_all.transpose(0, 2, 1).reshape(ep * rows, experts).astype(F32)
    mask_all = jnp.pad(mask_all, ((0, 0), (0, LANES - experts)))

    positions = jnp.arange(seq, dtype=jnp.int32).astype(F32)
    frequency = ROPE_BASE ** (-jnp.arange(HEAD // 2, dtype=F32) / (HEAD // 2))
    angles = positions[:, None] * frequency[None, :]
    cosine, sine = jnp.cos(angles), jnp.sin(angles)
    cosine = jnp.concatenate([cosine] * 4, axis=1)
    sine = jnp.concatenate([-sine, sine] * 2, axis=1)

    normed, q, k, v, att, lse = pl.pallas_call(
        functools.partial(front_kernel, rows, heads, kv_heads),
        out_shape=(
            sds((seq, width), BF16),
            sds((heads, seq, HEAD), BF16),
            sds((kv_heads, seq, HEAD), BF16),
            sds((kv_heads, seq, HEAD), BF16),
            sds((seq, qw), BF16),
            sds((heads, seq, 1), F32),
        ),
        scratch_shapes=[pltpu.VMEM((heads, seq, HEAD), F32)],
        compiler_params=params(),
        name="front",
    )(x_all, gain1, w_qkv, cosine, sine, seg_col, seg_row)

    ow = lax.all_gather(out_weight, "shard", axis=0, tiled=False)
    dy_all = lax.all_gather(cotangent, "ep", axis=0, tiled=True)
    att = lax.all_to_all(att.reshape(n, rows, qw), "shard", 0, 0)

    mine = [lax.dynamic_slice_in_dim(w, r * own, own, axis=0) for w in (gate_weight, up_weight, down_weight)]
    mine, x_all = lax.optimization_barrier((mine, x_all))
    slabs = []
    for w in mine:
        slabs.append(w)
        for _ in range(n - 1):
            w = lax.ppermute(w, "shard", ring)
            slabs.append(w)

    hidden, normed2, gates_own = pl.pallas_call(
        mid_kernel,
        out_shape=(sds((rows, width), F32), sds((rows, width), BF16), sds((rows, LANES), F32)),
        compiler_params=params(),
        name="mid",
    )(tokens, att, ow, gain2, router, mask_own)

    n2_all = lax.all_gather(normed2, "ep", axis=0, tiled=True)
    total = ep * rows
    block = 512
    moe, nb, mix, inner, gg, ug = pl.pallas_call(
        functools.partial(expert_kernel, own, n),
        grid=(total // block,),
        in_specs=[
            pl.BlockSpec(memory_space=pltpu.SMEM),
            pl.BlockSpec((block, width), lambda i: (i, 0)),
            pl.BlockSpec((block, width), lambda i: (i, 0)),
            pl.BlockSpec((block, LANES), lambda i: (i, 0)),
            pl.BlockSpec((width, LANES), lambda i: (0, 0)),
        ]
        + [pl.BlockSpec(memory_space=pl.ANY)] * (3 * n),
        out_specs=(
            pl.BlockSpec((block, width), lambda i: (i, 0)),
            pl.BlockSpec((block, width), lambda i: (i, 0)),
            pl.BlockSpec((block, LANES), lambda i: (i, 0)),
            pl.BlockSpec((own, block, ff), lambda i: (0, i, 0)),
            pl.BlockSpec((own, block, ff), lambda i: (0, i, 0)),
            pl.BlockSpec((own, block, ff), lambda i: (0, i, 0)),
        ),
        out_shape=(
            sds((total, width), BF16),
            sds((total, width), BF16),
            sds((total, LANES), F32),
            sds((own, total, ff), BF16),
            sds((own, total, ff), BF16),
            sds((own, total, ff), BF16),
        ),
        scratch_shapes=[
            pltpu.VMEM((own, width, ff), BF16),
            pltpu.VMEM((own, width, ff), BF16),
            pltpu.VMEM((own, ff, width), BF16),
            pltpu.SemaphoreType.DMA((3 * n,)),
        ],
        compiler_params=params(),
        name="experts",
    )(place, n2_all, dy_all, mask_all, router, *slabs)

    nb_own = lax.psum_scatter(nb, "ep", scatter_dimension=0, tiled=True)
    mix_sent = mix[:, :own].reshape(ep, rows, own).transpose(0, 2, 1)
    mix_own = lax.all_to_all(mix_sent, "ep", 0, 0).reshape(experts, rows).T
    mix_own = jnp.pad(mix_own, ((0, 0), (0, LANES - experts)))

    ff_slab = ff // n
    dg, du, dd = pl.pallas_call(
        functools.partial(expert_grad_kernel, own, n),
        grid=(own, total // block),
        in_specs=[
            pl.BlockSpec(memory_space=pltpu.SMEM),
            pl.BlockSpec((block, width), lambda e, i: (i, 0)),
            pl.BlockSpec((block, width), lambda e, i: (i, 0)),
            pl.BlockSpec((block, LANES), lambda e, i: (i, 0)),
            pl.BlockSpec((1, block, ff), lambda e, i: (e, i, 0)),
            pl.BlockSpec((1, block, ff), lambda e, i: (e, i, 0)),
            pl.BlockSpec((1, block, ff), lambda e, i: (e, i, 0)),
        ],
        out_specs=(
            pl.BlockSpec((n, 1, slab, ff), lambda e, i: (0, e, 0, 0)),
            pl.BlockSpec((n, 1, slab, ff), lambda e, i: (0, e, 0, 0)),
            pl.BlockSpec((n, 1, ff_slab, width), lambda e, i: (0, e, 0, 0)),
        ),
        out_shape=(
            sds((n, own, slab, ff), BF16),
            sds((n, own, slab, ff), BF16),
            sds((n, own, ff_slab, width), BF16),
        ),
        scratch_shapes=[
            pltpu.VMEM((width, ff), F32),
            pltpu.VMEM((width, ff), F32),
            pltpu.VMEM((ff, width), F32),
        ],
        compiler_params=params(),
        name="expert_grads",
    )(place, n2_all, dy_all, mix, inner, gg, ug)

    hidden_grad, att_grad, ow_grad, ffn_grad, router_grad = pl.pallas_call(
        mid_back_kernel,
        out_shape=(
            sds((rows, width), F32),
            sds((n, rows, qw), BF16),
            sds((n, n * qw, slab), BF16),
            sds((1, width), F32),
            sds((LANES, width), F32),
        ),
        scratch_shapes=[pltpu.VMEM((rows, width), BF16)],
        compiler_params=params(),
        name="mid_back",
    )(hidden, nb_own, cotangent, gates_own, mix_own, normed2, router, gain2, ow, att)

    att_grad = lax.all_to_all(att_grad, "shard", 0, 0).reshape(seq, qw)
    ng, qkv_grad, gain_grad = pl.pallas_call(
        functools.partial(back_kernel, rows, heads, kv_heads),
        out_shape=(sds((seq, width), BF16), sds((width, cols), BF16), sds((1, width), F32)),
        scratch_shapes=[
            pltpu.VMEM((heads, seq, HEAD), BF16),
            pltpu.VMEM((heads, seq, HEAD), F32),
            pltpu.VMEM((kv_heads, seq, HEAD), F32),
            pltpu.VMEM((kv_heads, seq, HEAD), F32),
            pltpu.VMEM((seq, cols), F32),
            pltpu.VMEM((seq, cols), BF16),
        ],
        compiler_params=params(),
        name="back",
    )(q, k, v, att_grad, lse, seg_col, seg_row, x_all, normed, w_qkv, cosine, sine)

    ng_own = lax.psum_scatter(ng, "shard", scatter_dimension=0, tiled=True).astype(F32)
    moe_own = lax.psum_scatter(moe, "ep", scatter_dimension=0, tiled=True)
    output = (hidden + moe_own.astype(F32)).astype(BF16)

    x = tokens.astype(F32)
    inv = inverse_rms(x)
    scaled = x * inv
    w1 = ng_own * gain1
    input_grad = hidden_grad + inv * (w1 - scaled * jnp.mean(w1 * scaled, axis=-1, keepdims=True))

    def expert_sum(parts):
        part = parts[1]
        for step in list(range(2, n)) + [0]:
            part = lax.ppermute(part, "shard", ring).astype(F32) + parts[step].astype(F32)
            if step:
                part = part.astype(BF16)
        if hi > 1:
            part = lax.psum(part, "hi")
        return lax.all_gather(part.astype(BF16), "ep", axis=0, tiled=True).astype(F32)

    gate_grad, up_grad, down_grad = expert_sum(dg), expert_sum(du), expert_sum(dd)

    qkv_part = lax.psum_scatter(qkv_grad.reshape(n, slab, cols), "ep", scatter_dimension=1, tiled=True)
    qkv_part = lax.all_to_all(qkv_part, "shard", 0, 0)
    ow_part = lax.psum_scatter(ow_grad, "ep", scatter_dimension=1, tiled=True)
    ow_part = jnp.sum(lax.all_to_all(ow_part, "shard", 0, 0).astype(F32), axis=0)
    if hi > 1:
        qkv_part = lax.psum(qkv_part.astype(F32), "hi").astype(BF16)
        ow_part = lax.psum(ow_part, "hi")
    qkv_full = lax.all_gather(qkv_part, "ep", axis=1, tiled=True).astype(F32)
    ow_full = lax.all_gather(ow_part.astype(BF16), "ep", axis=0, tiled=True).astype(F32)

    def columns(part):
        return part.transpose(1, 0, 2).reshape(slab, -1)

    small = lax.psum(jnp.concatenate([gain_grad, ffn_grad, router_grad[:experts]], axis=0), everyone)
    small = lax.dynamic_slice_in_dim(small, z * slab, slab, axis=1)
    return (
        output,
        input_grad,
        small[0],
        columns(qkv_full[:, :, :qw]),
        columns(qkv_full[:, :, qw : qw + kw]),
        columns(qkv_full[:, :, qw + kw :]),
        ow_full,
        small[1],
        small[2:].T,
        gate_grad,
        up_grad,
        down_grad,
    )


def solution(mesh):
    rep, n = mesh.shape["rep"], mesh.shape["shard"]
    ep = math.gcd(rep, 8)
    hi = rep // ep
    split = Mesh(mesh.devices.reshape(hi, ep, n), ("hi", "ep", "shard"))
    rows = ("hi", "ep", "shard")
    placed = (
        P(rows, None),
        P(rows, None),
        P(rows),
        P(rows, None),
        P("shard"),
        P("shard", None),
        P("shard", None),
        P("shard", None),
        P(None, "shard"),
        P("shard"),
        P("shard", None),
        P(None, "shard", None),
        P(None, "shard", None),
        P(None, "shard", None),
    )
    return jax.shard_map(
        functools.partial(per_device, hi, ep, n),
        mesh=split,
        in_specs=placed,
        out_specs=(
            P(rows, None),
            P(rows, None),
            P("shard"),
            P("shard", None),
            P("shard", None),
            P("shard", None),
            P(None, "shard"),
            P("shard"),
            P("shard", None),
            P(None, "shard", None),
            P(None, "shard", None),
            P(None, "shard", None),
        ),
        check_vma=False,
    )
```

time: 2810 us -> 854 us (0.30)
  waiting for transfers between devices: 2300 us -> 533 us
  matrix products: 221 us -> 0 us
  Pallas kernels: 0 us -> 109 us
  local copies, waits for them, and re-layouts: 59.4 us -> 18.1 us
  other arithmetic: 76.6 us -> 44.7 us
    reduce_scatter x15 -> x5, waiting for transfers between devices: 1230 us -> 80.8 us  [the longest x1 41.6 us: per_device(): lax.psum_scatter(ng, 'shard', scatter_dimension=0, tiled=True).astype(F32)]
    all_gather x12 -> x8, waiting for transfers between devices: 1020 us -> 143 us  [the longest x3 102 us: expert_sum(): lax.all_gather(part.astype(BF16), 'ep', axis=0, tiled=True).astype(F32)]
    dot_general x80 -> x0, matrix products: 221 us -> none  [the longest x16 25.1 us: head_scores(): jnp.einsum('bgd,sd->gbs', query_head, key_head, preferred_element_type=jn...]
    ppermute x0 -> x18, waiting for transfers between devices: none -> 210 us  [the longest x9 118 us: expert_sum(): lax.ppermute(part, 'shard', ring).astype(F32) + parts[step].astype(F32)]
    pallas_call x0 -> x6, Pallas kernels: none -> 109 us  [the longest x1 38.8 us: per_device(): pl.pallas_call(functools.partial(expert_kernel, own, n), grid=(total // b...]
    psum x0 -> x1, waiting for transfers between devices: none -> 95.2 us  [per_device(): lax.psum(jnp.concatenate([gain_grad, ffn_grad, router_grad[:experts]], ax...]
    unnamed x31 -> x14, waiting for transfers between devices: 50.3 us -> 4.1 us
    all_to_all x0 -> x3, blocking collectives: none -> 39.3 us  [the longest x1 19.2 us: per_device(): att_grad = lax.all_to_all(att_grad, 'shard', 0, 0).reshape(seq, qw)]
  transfers between devices with their start and end apart: 29 -> 35, of which waited for: 27 -> 25; matrix products, arithmetic and copies ran while one was open for 6% -> 7% of each run, Pallas kernels for 0% -> 5%
where the time goes in v1:
time: 854 us; the launch traced here: 852 us
  waiting for transfers between devices  533 us (62%)
  blocking collectives  116 us (14%)
  Pallas kernels  109 us (13%)
  other arithmetic  44.7 us (5%)
  local copies, waits for them, and re-layouts  18.1 us (2%)
  starting transfers between devices  16.7 us (2%)
  between operations  14.5 us (2%)
    ppermute x9, waiting for transfers between devices, expert_sum(): lax.ppermute(part, 'shard', ring).astype(F32) + parts[step].astype(F32)  118 us
    all_gather x3, waiting for transfers between devices, expert_sum(): lax.all_gather(part.astype(BF16), 'ep', axis=0, tiled=True).astype(F32)  102 us
    psum x1, waiting for transfers between devices, per_device(): lax.psum(jnp.concatenate([gain_grad, ffn_grad, router_grad[:experts]], ax...  95.2 us
    ppermute x9, waiting for transfers between devices, per_device(): w = lax.ppermute(w, 'shard', ring)  92 us
    all_gather x1, blocking collectives, per_device(): packs = lax.all_gather(pack, 'shard', axis=0, tiled=False)  57.5 us
    reduce_scatter x1, waiting for transfers between devices, per_device(): lax.psum_scatter(ng, 'shard', scatter_dimension=0, tiled=True).astype(F32)  41.6 us
    reduce_scatter x1, waiting for transfers between devices, per_device(): nb_own = lax.psum_scatter(nb, 'ep', scatter_dimension=0, tiled=True)  39.1 us
    pallas_call x1, Pallas kernels, per_device(): pl.pallas_call(functools.partial(expert_kernel, own, n), grid=(total // b...  38.8 us
  transfers between devices with their start and end apart: 35, of which 25 were waited for; matrix products, arithmetic and copies ran while one was open for 7% of the time, Pallas kernels for 5%

profile of v1, /device:TPU:0, one launch (start us, length us, event | category | flops | bytes accessed | tf_op | source)
XLA Modules:
  0.0 852.4 jit_solution(6505040437126188008)
XLA Ops:
  11.8 6.3 all-to-all-start
  18.2 57.5 %all-gather.3 = bf16[4,19,256]{2,1,0:T(8,128)(2,1)S(1)} all-gather(bf16[1,19,256]{2,1,0:T(8,128)(2,1)S(1)} %maximum_bitcast_fusion.1), channel_id=2, replica_groups=mesh['rep'=8,'shard'=4] {'shard'}, dimensions={0}, use_global_device_ids=true | all-gather | bytes 48640 | tf_op jit(solution)/shard_map/all_gather | solution.py:361
  77.3 1.9 fusion.16
  82.0 16.3 %front.1 = (bf16[1024,1024]{1,0:T(8,128)(2,1)}, bf16[4,1024,64]{2,1,0:T(8,128)(2,1)}, bf16[2,1024,64]{2,1,0:T(8,128)(2,1)}, bf16[2,1024,64]{2,1,0:T(8,128)(2,1)}...) custom-call(bf16[1024,1024]{1,0:T(8,128)(2,1)} %all-gather.13.cloned.1.call-done.x_ref, f32[1,1024]{1,0:T(1,128)} %bitcast.115, ...), custom_call_target="tpu_custom_call" | custom-call | tf_op jit(solution)/shard_map/front/pallas_call | solution.py:381
  98.4 3.5 all-to-all-start.1
  104.3 32.3 %all-gather.27.cloned.1.call-done = bf16[4096,256]{1,0:T(8,128)(2,1)} async-done(((bf16[1024,256]{1,0:T(8,128)(2,1)}), bf16[4096,256]{1,0:T(8,128)(2,1)}) %all-gather.27.cloned.1.call-update) | async-done | bytes 2097168 | tf_op jit(solution)/shard_map/all_gather | solution.py:396
  137.4 3.8 mid.1
  144.0 2.0 collective-permute-start.6
  146.0 14.5 %collective-permute-done.refs_1_ = bf16[2,256,512]{2,1,0:T(8,128)(2,1)S(1)} collective-permute-done((bf16[2,256,512]{2,1,0:T(8,128)(2,1)S(1)}, bf16[2,256,512]{2,1,0:T(8,128)(2,1)S(1)}, u32[]{:S(2)}, u32[]{:S(2)}) %collective-permute-start) | collective-permute-done | bytes 524320 | tf_op jit(solution)/shard_map/ppermute | solution.py:406
  160.6 11.2 %collective-permute-done.3.refs_5_ = bf16[2,256,512]{2,1,0:T(8,128)(2,1)S(1)} collective-permute-done((bf16[2,256,512]{2,1,0:T(8,128)(2,1)S(1)}, bf16[2,256,512]{2,1,0:T(8,128)(2,1)S(1)}, u32[]{:S(2)}, u32[]{:S(2)}) %collective-permute-start.3) | collective-permute-done | bytes 524320 | tf_op jit(solution)/shard_map/ppermute | solution.py:406
  171.8 11.2 %collective-permute-done.6.refs_9_ = bf16[2,128,1024]{2,1,0:T(8,128)(2,1)S(1)} collective-permute-done((bf16[2,128,1024]{2,1,0:T(8,128)(2,1)S(1)}, bf16[2,128,1024]{2,1,0:T(8,128)(2,1)S(1)}, u32[]{:S(2)}, u32[]{:S(2)}) %collective-permute-start.6) | collective-permute-done | bytes 524320 | tf_op jit(solution)/shard_map/ppermute | solution.py:406
  183.1 11.3 %collective-permute-done.1.refs_2_ = bf16[2,256,512]{2,1,0:T(8,128)(2,1)} collective-permute-done((bf16[2,256,512]{2,1,0:T(8,128)(2,1)S(1)}, bf16[2,256,512]{2,1,0:T(8,128)(2,1)}, u32[]{:S(2)}, u32[]{:S(2)}) %collective-permute-start.1) | collective-permute-done | bytes 524320 | tf_op jit(solution)/shard_map/ppermute | solution.py:406
  194.4 11.2 %collective-permute-done.4.refs_6_ = bf16[2,256,512]{2,1,0:T(8,128)(2,1)} collective-permute-done((bf16[2,256,512]{2,1,0:T(8,128)(2,1)S(1)}, bf16[2,256,512]{2,1,0:T(8,128)(2,1)}, u32[]{:S(2)}, u32[]{:S(2)}) %collective-permute-start.4) | collective-permute-done | bytes 524320 | tf_op jit(solution)/shard_map/ppermute | solution.py:406
  205.6 11.2 %collective-permute-done.7.refs_10_ = bf16[2,128,1024]{2,1,0:T(8,128)(2,1)} collective-permute-done((bf16[2,128,1024]{2,1,0:T(8,128)(2,1)S(1)}, bf16[2,128,1024]{2,1,0:T(8,128)(2,1)}, u32[]{:S(2)}, u32[]{:S(2)}) %collective-permute-start.7) | collective-permute-done | bytes 524320 | tf_op jit(solution)/shard_map/ppermute | solution.py:406
  216.9 9.3 %all-gather.2 = bf16[128,256]{1,0:T(8,128)(2,1)S(1)} all-gather(bf16[16,256]{1,0:T(8,128)(2,1)S(1)} %convert_bitcast_fusion), channel_id=4, replica_groups=mesh['rep'=8,'shard'=4] {'rep'}, dimensions={0}, use_global_device_ids=true | all-gather | bytes 73728 | tf_op jit(solution)/shard_map/all_gather | solution.py:370
  228.1 11.2 %collective-permute-done.5.refs_7_ = bf16[2,256,512]{2,1,0:T(8,128)(2,1)} collective-permute-done((bf16[2,256,512]{2,1,0:T(8,128)(2,1)}, bf16[2,256,512]{2,1,0:T(8,128)(2,1)}, u32[]{:S(2)}, u32[]{:S(2)}) %collective-permute-start.5) | collective-permute-done | bytes 524320 | tf_op jit(solution)/shard_map/ppermute | solution.py:406
  239.3 10.0 %collective-permute-done.8.refs_11_ = bf16[2,128,1024]{2,1,0:T(8,128)(2,1)} collective-permute-done((bf16[2,128,1024]{2,1,0:T(8,128)(2,1)}, bf16[2,128,1024]{2,1,0:T(8,128)(2,1)}, u32[]{:S(2)}, u32[]{:S(2)}) %collective-permute-start.8) | collective-permute-done | bytes 524320 | tf_op jit(solution)/shard_map/ppermute | solution.py:406
  249.4 38.8 %experts.1 = (bf16[2048,1024]{1,0:T(8,128)(2,1)}, bf16[2048,1024]{1,0:T(8,128)(2,1)}, f32[2048,128]{1,0:T(8,128)}, bf16[2,2048,512]{2,1,0:T(8,128)(2,1)}, bf16[2...) custom-call(s32[2]{0:T(128)} %pad_add_fusion.place_ref, bf16[2048,1024]{1,0:T(8,128)(2,1)} %all-gather.15.cloned.1.call-done.n2_ref, ...), custom_call_target="tpu_custom_call" | custom-call | tf_op jit(solution)/shard_map/experts/pallas_call | solution.py:419
  289.7 8.3 all_to_all.30
  298.8 39.1 %reduce-scatter.8.cloned.1.call-done.nb_ref = bf16[256,1024]{1,0:T(8,128)(2,1)} async-done(((bf16[2048,1024]{1,0:T(8,128)(2,1)}), bf16[256,1024]{1,0:T(8,128)(2,1)}) %reduce-scatter.8.cloned.1.call-update) | async-done | bytes 524304 | tf_op jit(solution)/shard_map/reduce_scatter | solution.py:456
  337.9 6.3 mid_back.1
  344.2 19.2 %all_to_all.31 = bf16[4,256,256]{2,1,0:T(8,128)(2,1)} all-to-all(bf16[4,256,256]{2,1,0:T(8,128)(2,1)} %get-tuple-element.56), channel_id=1, replica_groups=mesh['rep'=8,'shard'=4] {'shard'}, dimensions={0} | all-to-all | bytes 1048576 | tf_op jit(solution)/shard_map/all_to_all | solution.py:507
  363.4 22.2 %back.1 = (bf16[1024,1024]{1,0:T(8,128)(2,1)}, bf16[1024,512]{1,0:T(8,128)(2,1)}, f32[1,1024]{1,0:T(1,128)}) custom-call(bf16[4,1024,64]{2,1,0:T(8,128)(2,1)} %get-tuple-element.53.q_ref, bf16[2,1024,64]{2,1,0:T(8,128)(2,1)} %get-tuple-element.54.k_ref, bf16[2,1024,64]{2,1,0:T(8,128)(2,1)} %get-tuple-element.55.v_ref, bf16[1024,256]{1,0:T(8,128)(2,1)} %bitcast.105, ...), custom_call_target="tpu_custom_call" | custom-call | tf_op jit(solution)/shard_map/back/pallas_call | solution.py:508
  387.2 22.0 %expert_grads.1 = (bf16[4,2,256,512]{3,2,1,0:T(8,128)(2,1)}, bf16[4,2,256,512]{3,2,1,0:T(8,128)(2,1)}, bf16[4,2,128,1024]{3,2,1,0:T(8,128)(2,1)}) custom-call(s32[2]{0:T(128)} %pad_add_fusion.place_ref, bf16[2048,1024]{1,0:T(8,128)(2,1)} %all-gather.15.cloned.1.call-done.n2_ref, bf16[2048,1024]{1,0:T(8,128)(2,1)} %all-gather.17.cloned.1.call-done.dy_ref, ...), custom_call_target="tpu_custom_call" | custom-call | tf_op jit(solution)/shard_map/expert_grads/pallas_call | solution.py:462
  410.3 14.1 %collective-permute-done.9 = bf16[2,256,512]{2,1,0:T(8,128)(2,1)S(1)} collective-permute-done((bf16[2,256,512]{2,1,0:T(8,128)(2,1)S(1)}, bf16[2,256,512]{2,1,0:T(8,128)(2,1)S(1)}, u32[]{:S(2)}, u32[]{:S(2)}) %collective-permute-start.9) | collective-permute-done | bytes 524320 | tf_op jit(solution)/shard_map/ppermute | solution.py:536
  425.7 13.2 %collective-permute-done.10 = bf16[2,256,512]{2,1,0:T(8,128)(2,1)S(1)} collective-permute-done((bf16[2,256,512]{2,1,0:T(8,128)(2,1)S(1)}, bf16[2,256,512]{2,1,0:T(8,128)(2,1)S(1)}, u32[]{:S(2)}, u32[]{:S(2)}) %collective-permute-start.10) | collective-permute-done | bytes 524320 | tf_op jit(solution)/shard_map/ppermute | solution.py:536
  441.8 10.7 %collective-permute-done.11 = bf16[2,256,512]{2,1,0:T(8,128)(2,1)S(1)} collective-permute-done((bf16[2,256,512]{2,1,0:T(8,128)(2,1)S(1)}, bf16[2,256,512]{2,1,0:T(8,128)(2,1)S(1)}, u32[]{:S(2)}, u32[]{:S(2)}) %collective-permute-start.11) | collective-permute-done | bytes 524320 | tf_op jit(solution)/shard_map/ppermute | solution.py:536
  452.5 2.0 fusion.13
  454.7 11.9 %collective-permute-done.12 = bf16[2,256,512]{2,1,0:T(8,128)(2,1)S(1)} collective-permute-done((bf16[2,256,512]{2,1,0:T(8,128)(2,1)S(1)}, bf16[2,256,512]{2,1,0:T(8,128)(2,1)S(1)}, u32[]{:S(2)}, u32[]{:S(2)}) %collective-permute-start.12) | collective-permute-done | bytes 524320 | tf_op jit(solution)/shard_map/ppermute | solution.py:536
  466.8 12.6 %collective-permute-done.13 = bf16[2,256,512]{2,1,0:T(8,128)(2,1)S(1)} collective-permute-done((bf16[2,256,512]{2,1,0:T(8,128)(2,1)S(1)}, bf16[2,256,512]{2,1,0:T(8,128)(2,1)S(1)}, u32[]{:S(2)}, u32[]{:S(2)}) %collective-permute-start.13) | collective-permute-done | bytes 524320 | tf_op jit(solution)/shard_map/ppermute | solution.py:536
  479.5 12.7 %collective-permute-done.14 = bf16[2,256,512]{2,1,0:T(8,128)(2,1)S(1)} collective-permute-done((bf16[2,256,512]{2,1,0:T(8,128)(2,1)S(1)}, bf16[2,256,512]{2,1,0:T(8,128)(2,1)S(1)}, u32[]{:S(2)}, u32[]{:S(2)}) %collective-permute-start.14) | collective-permute-done | bytes 524320 | tf_op jit(solution)/shard_map/ppermute | solution.py:536
  493.4 14.7 %collective-permute-done.15 = bf16[2,128,1024]{2,1,0:T(8,128)(2,1)S(1)} collective-permute-done((bf16[2,128,1024]{2,1,0:T(8,128)(2,1)S(1)}, bf16[2,128,1024]{2,1,0:T(8,128)(2,1)S(1)}, u32[]{:S(2)}, u32[]{:S(2)}) %collective-permute-start.15) | collective-permute-done | bytes 524320 | tf_op jit(solution)/shard_map/ppermute | solution.py:536
  508.3 15.8 %collective-permute-done.16 = bf16[2,128,1024]{2,1,0:T(8,128)(2,1)S(1)} collective-permute-done((bf16[2,128,1024]{2,1,0:T(8,128)(2,1)S(1)}, bf16[2,128,1024]{2,1,0:T(8,128)(2,1)S(1)}, u32[]{:S(2)}, u32[]{:S(2)}) %collective-permute-start.16) | collective-permute-done | bytes 524320 | tf_op jit(solution)/shard_map/ppermute | solution.py:536
  524.4 11.8 %collective-permute-done.17 = bf16[2,128,1024]{2,1,0:T(8,128)(2,1)S(1)} collective-permute-done((bf16[2,128,1024]{2,1,0:T(8,128)(2,1)S(1)}, bf16[2,128,1024]{2,1,0:T(8,128)(2,1)S(1)}, u32[]{:S(2)}, u32[]{:S(2)}) %collective-permute-start.17) | collective-permute-done | bytes 524320 | tf_op jit(solution)/shard_map/ppermute | solution.py:536
  537.3 11.8 %all_to_all.32 = bf16[4,32,512]{2,1,0:T(8,128)(2,1)} all-to-all(bf16[4,32,512]{2,1,0:T(8,128)(2,1)} %reduce-scatter.12.cloned.1.call-done), channel_id=1, replica_groups=mesh['rep'=8,'shard'=4] {'shard'}, dimensions={0} | all-to-all | bytes 262144 | tf_op jit(solution)/shard_map/all_to_all | solution.py:546
  550.0 3.7 all-to-all-start.5
  553.7 2.0 add_convert_fusion
  555.7 95.2 %all-reduce.6.cloned.1.call-done = f32[18,1024]{1,0:T(8,128)} async-done(((f32[18,1024]{1,0:T(8,128)}), f32[18,1024]{1,0:T(8,128)}) %all-reduce.6.cloned.1.call-update) | async-done | bytes 73744 | tf_op jit(solution)/shard_map/psum | solution.py:558
  653.7 37.2 %all-gather.21.cloned.1.call-done = bf16[16,256,512]{2,1,0:T(8,128)(2,1)} async-done(((bf16[2,256,512]{2,1,0:T(8,128)(2,1)}), bf16[16,256,512]{2,1,0:T(8,128)(2,1)}) %all-gather.21.cloned.1.call-update) | async-done | bytes 4194320 | tf_op jit(solution)/shard_map/all_gather | solution.py:541
  690.9 6.7 convert_element_type.252
  697.7 32.6 %all-gather.23.cloned.1.call-done = bf16[16,256,512]{2,1,0:T(8,128)(2,1)} async-done(((bf16[2,256,512]{2,1,0:T(8,128)(2,1)}), bf16[16,256,512]{2,1,0:T(8,128)(2,1)}) %all-gather.23.cloned.1.call-update) | async-done | bytes 4194320 | tf_op jit(solution)/shard_map/all_gather | solution.py:541
  730.3 6.7 convert_element_type.265
  737.0 32.5 %all-gather.25.cloned.1.call-done = bf16[16,128,1024]{2,1,0:T(8,128)(2,1)} async-done(((bf16[2,128,1024]{2,1,0:T(8,128)(2,1)}), bf16[16,128,1024]{2,1,0:T(8,128)(2,1)}) %all-gather.25.cloned.1.call-update) | async-done | bytes 4194320 | tf_op jit(solution)/shard_map/all_gather | solution.py:541
  769.5 6.7 convert_element_type.278
  776.2 10.2 %all_gather.56 = bf16[1024,256]{1,0:T(8,128)(2,1)S(1)} all-gather(bf16[128,256]{1,0:T(8,128)(2,1)S(1)} %reduce_sum.32), channel_id=1, replica_groups=mesh['rep'=8,'shard'=4] {'rep'}, dimensions={0}, use_global_device_ids=true | all-gather | bytes 589824 | tf_op jit(solution)/shard_map/all_gather | solution.py:553
  787.5 8.5 all-gather.19.cloned.1.call-done
  800.5 41.6 %reduce-scatter.10.cloned.1.call-done = bf16[256,1024]{1,0:T(8,128)(2,1)} async-done(((bf16[1024,1024]{1,0:T(8,128)(2,1)}), bf16[256,1024]{1,0:T(8,128)(2,1)}) %reduce-scatter.10.cloned.1.call-update) | async-done | bytes 524304 | tf_op jit(solution)/shard_map/reduce_scatter | solution.py:523
  843.5 2.3 fusion.5
  (166 shorter events, 39.8 us)
Async XLA Ops:
  7.2 73.9 %all-gather.13.cloned.1.call-start = ((), (), s32[]{:S(2)}) async-start(), calls=%async_computation.11 | async-start | bytes 2621440 | tf_op jit(solution)/shard_map/all_gather | solution.py:341
  7.9 128.6 %all-gather.27.cloned.1.call-start = ((), (), s32[]{:S(2)}) async-start(), calls=%async_computation.24 | async-start | bytes 2621440 | tf_op jit(solution)/shard_map/all_gather | solution.py:396
  8.7 240.6 %all-gather.17.cloned.1.call-start = ((), (), s32[]{:S(2)}) async-start(), calls=%async_computation.13 | async-start | bytes 4718592 | tf_op jit(solution)/shard_map/all_gather | solution.py:397
  11.8 69.3 %all-to-all-start = ((bf16[4,256,512]{2,1,0:T(8,128)(2,1)}), bf16[4,256,512]{2,1,0:T(8,128)(2,1)S(1)}, u32[]{:S(2)}, u32[]{:S(2)}) async-start(bf16[4,256,512]{2,1,0:T(8,128)(2,1)} %maximum_bitcast_fusion), calls=%async_computation | async-start | bytes 2097152 | tf_op jit(solution)/shard_map/all_to_all | solution.py:350
  98.4 38.2 %all-to-all-start.1 = ((bf16[4,256,256]{2,1,0:T(8,128)(2,1)}), bf16[4,256,256]{2,1,0:T(8,128)(2,1)S(1)}, u32[]{:S(2)}, u32[]{:S(2)}) async-start(bf16[4,256,256]{2,1,0:T(8,128)(2,1)} %bitcast.112), calls=%async_computation.1 | async-start | bytes 1048576 | tf_op jit(solution)/shard_map/all_to_all | solution.py:398
  101.8 147.5 %all-gather.15.cloned.1.call-start = ((), (), s32[]{:S(2)}) async-start(), calls=%async_computation.12 | async-start | bytes 4718592 | tf_op jit(solution)/shard_map/all_gather | solution.py:416
  141.2 196.7 %reduce-scatter.8.cloned.1.call-start = ((), (), s32[]{:S(2)}) async-start(), calls=%async_computation.15 | async-start | bytes 4718592 | tf_op jit(solution)/shard_map/reduce_scatter | solution.py:456
  142.4 85.8 %copy-start.12 = (bf16[2,128,1024]{2,1,0:T(8,128)(2,1)}, bf16[2,128,1024]{2,1,0:T(8,128)(2,1)S(1)}, u32[]{:S(2)}) copy-start(bf16[2,128,1024]{2,1,0:T(8,128)(2,1)S(1)} %constant_dynamic-slice_fusion.1.refs_8_) | copy-start | bytes 1572868
  143.9 105.5 %copy-start.10 = (bf16[2,256,512]{2,1,0:T(8,128)(2,1)}, bf16[2,256,512]{2,1,0:T(8,128)(2,1)S(1)}, u32[]{:S(2)}) copy-start(bf16[2,256,512]{2,1,0:T(8,128)(2,1)S(1)} %get-tuple-element.46.refs_4_) | copy-start | bytes 1572868
  143.9 105.4 %copy-start.11 = (bf16[2,256,512]{2,1,0:T(8,128)(2,1)}, bf16[2,256,512]{2,1,0:T(8,128)(2,1)S(1)}, u32[]{:S(2)}) copy-start(bf16[2,256,512]{2,1,0:T(8,128)(2,1)S(1)} %get-tuple-element.45.refs_0_) | copy-start | bytes 1572868
  143.9 16.7 %collective-permute-start = (bf16[2,256,512]{2,1,0:T(8,128)(2,1)S(1)}, bf16[2,256,512]{2,1,0:T(8,128)(2,1)S(1)}, u32[]{:S(2)}, u32[]{:S(2)}) collective-permute-start(bf16[2,256,512]{2,1,0:T(8,128)(2,1)S(1)} %get-tuple-element.45.refs_0_), channel_id=1, source_target_pairs={{0,1},{1,2},{2,3},{3,0},{4,5},{5,6},{6,7},{7,4},{8,9},{9,10},{10,1... | collective-permute-start | bytes 1572872 | tf_op jit(solution)/shard_map/ppermute | solution.py:406
  144.0 27.8 %collective-permute-start.3 = (bf16[2,256,512]{2,1,0:T(8,128)(2,1)S(1)}, bf16[2,256,512]{2,1,0:T(8,128)(2,1)S(1)}, u32[]{:S(2)}, u32[]{:S(2)}) collective-permute-start(bf16[2,256,512]{2,1,0:T(8,128)(2,1)S(1)} %get-tuple-element.46.refs_4_), channel_id=1, source_target_pairs={{0,1},{1,2},{2,3},{3,0},{4,5},{5,6},{6,7},{7,4},{8,9},{9,10},{10,1... | collective-permute-start | bytes 1572872 | tf_op jit(solution)/shard_map/ppermute | solution.py:406
  144.0 39.0 %collective-permute-start.6 = (bf16[2,128,1024]{2,1,0:T(8,128)(2,1)S(1)}, bf16[2,128,1024]{2,1,0:T(8,128)(2,1)S(1)}, u32[]{:S(2)}, u32[]{:S(2)}) collective-permute-start(bf16[2,128,1024]{2,1,0:T(8,128)(2,1)S(1)} %constant_dynamic-slice_fusion.1.refs_8_), channel_id=1, source_target_pairs={{0,1},{1,2},{2,3},{3,0},{4,5},{5,6},{6,7},{7,4},{8,9},{9,10},{10,1... | collective-permute-start | bytes 1572872 | tf_op jit(solution)/shard_map/ppermute | solution.py:406
  160.6 88.8 %copy-start.14 = (bf16[2,256,512]{2,1,0:T(8,128)(2,1)}, bf16[2,256,512]{2,1,0:T(8,128)(2,1)S(1)}, u32[]{:S(2)}) copy-start(bf16[2,256,512]{2,1,0:T(8,128)(2,1)S(1)} %collective-permute-done.refs_1_) | copy-start | bytes 1572868
  160.6 33.8 %collective-permute-start.1 = (bf16[2,256,512]{2,1,0:T(8,128)(2,1)S(1)}, bf16[2,256,512]{2,1,0:T(8,128)(2,1)}, u32[]{:S(2)}, u32[]{:S(2)}) collective-permute-start(bf16[2,256,512]{2,1,0:T(8,128)(2,1)S(1)} %collective-permute-done.refs_1_), channel_id=1, source_target_pairs={{0,1},{1,2},{2,3},{3,0},{4,5},{5,6},{6,7},{7,4},{8,9},{9,10},{10,1... | collective-permute-start | bytes 1572872 | tf_op jit(solution)/shard_map/ppermute | solution.py:406
  171.8 77.5 %copy-start.15 = (bf16[2,256,512]{2,1,0:T(8,128)(2,1)}, bf16[2,256,512]{2,1,0:T(8,128)(2,1)S(1)}, u32[]{:S(2)}) copy-start(bf16[2,256,512]{2,1,0:T(8,128)(2,1)S(1)} %collective-permute-done.3.refs_5_) | copy-start | bytes 1572868
  171.8 33.8 %collective-permute-start.4 = (bf16[2,256,512]{2,1,0:T(8,128)(2,1)S(1)}, bf16[2,256,512]{2,1,0:T(8,128)(2,1)}, u32[]{:S(2)}, u32[]{:S(2)}) collective-permute-start(bf16[2,256,512]{2,1,0:T(8,128)(2,1)S(1)} %collective-permute-done.3.refs_5_), channel_id=1, source_target_pairs={{0,1},{1,2},{2,3},{3,0},{4,5},{5,6},{6,7},{7,4},{8,9},{9,10},{10,1... | collective-permute-start | bytes 1572872 | tf_op jit(solution)/shard_map/ppermute | solution.py:406
  183.1 43.1 %copy-start.16 = (bf16[2,128,1024]{2,1,0:T(8,128)(2,1)}, bf16[2,128,1024]{2,1,0:T(8,128)(2,1)S(1)}, u32[]{:S(2)}) copy-start(bf16[2,128,1024]{2,1,0:T(8,128)(2,1)S(1)} %collective-permute-done.6.refs_9_) | copy-start | bytes 1572868
  183.1 33.8 %collective-permute-start.7 = (bf16[2,128,1024]{2,1,0:T(8,128)(2,1)S(1)}, bf16[2,128,1024]{2,1,0:T(8,128)(2,1)}, u32[]{:S(2)}, u32[]{:S(2)}) collective-permute-start(bf16[2,128,1024]{2,1,0:T(8,128)(2,1)S(1)} %collective-permute-done.6.refs_9_), channel_id=1, source_target_pairs={{0,1},{1,2},{2,3},{3,0},{4,5},{5,6},{6,7},{7,4},{8,9},{9,10},{10,1... | collective-permute-start | bytes 1572872 | tf_op jit(solution)/shard_map/ppermute | solution.py:406
  194.4 33.7 %collective-permute-start.2 = (bf16[2,256,512]{2,1,0:T(8,128)(2,1)}, bf16[2,256,512]{2,1,0:T(8,128)(2,1)}, u32[]{:S(2)}, u32[]{:S(2)}) collective-permute-start(bf16[2,256,512]{2,1,0:T(8,128)(2,1)} %collective-permute-done.1.refs_2_), channel_id=1, source_target_pairs={{0,1},{1,2},{2,3},{3,0},{4,5},{5,6},{6,7},{7,4},{8,9},{9,10},{10,1... | collective-permute-start | bytes 1572872 | tf_op jit(solution)/shard_map/ppermute | solution.py:406
  205.6 33.7 %collective-permute-start.5 = (bf16[2,256,512]{2,1,0:T(8,128)(2,1)}, bf16[2,256,512]{2,1,0:T(8,128)(2,1)}, u32[]{:S(2)}, u32[]{:S(2)}) collective-permute-start(bf16[2,256,512]{2,1,0:T(8,128)(2,1)} %collective-permute-done.4.refs_6_), channel_id=1, source_target_pairs={{0,1},{1,2},{2,3},{3,0},{4,5},{5,6},{6,7},{7,4},{8,9},{9,10},{10,1... | collective-permute-start | bytes 1572872 | tf_op jit(solution)/shard_map/ppermute | solution.py:406
  216.9 32.5 %collective-permute-start.8 = (bf16[2,128,1024]{2,1,0:T(8,128)(2,1)}, bf16[2,128,1024]{2,1,0:T(8,128)(2,1)}, u32[]{:S(2)}, u32[]{:S(2)}) collective-permute-start(bf16[2,128,1024]{2,1,0:T(8,128)(2,1)} %collective-permute-done.7.refs_10_), channel_id=1, source_target_pairs={{0,1},{1,2},{2,3},{3,0},{4,5},{5,6},{6,7},{7,4},{8,9},{9,10},{10,1... | collective-permute-start | bytes 1572872 | tf_op jit(solution)/shard_map/ppermute | solution.py:406
  288.2 249.1 %reduce-scatter.12.cloned.1.call-start = ((), (), s32[]{:S(2)}) async-start(), calls=%async_computation.18 | async-start | bytes 1179648 | tf_op jit(solution)/shard_map/reduce_scatter | solution.py:545
  385.6 164.4 %reduce-scatter.14.cloned.1.call-start = ((), (), s32[]{:S(2)}) async-start(), calls=%async_computation.20 | async-start | bytes 2359296 | tf_op jit(solution)/shard_map/reduce_scatter | solution.py:547
  386.4 167.3 %reduce-scatter.6.cloned.1.call-start = ((), (), s32[]{:S(2)}) async-start(), calls=%async_computation.14 | async-start | bytes 4718592 | tf_op jit(solution)/shard_map/reduce_scatter | solution.py:524
  387.1 263.8 %all-reduce.6.cloned.1.call-start = ((), (), s32[]{:S(2)}) async-start(), calls=%async_computation.17 | async-start | bytes 196608 | tf_op jit(solution)/shard_map/psum | solution.py:558
  409.2 31.9 %copy-start.22 = (f32[1,1024]{1,0:T(1,128)S(1)}, f32[1,1024]{1,0:T(1,128)}, u32[]{:S(2)}) copy-start(f32[1,1024]{1,0:T(1,128)} %get-tuple-element.62) | copy-start | bytes 12292
  409.2 31.9 %copy-start.23 = (f32[1,1024]{1,0:T(1,128)S(1)}, f32[1,1024]{1,0:T(1,128)}, u32[]{:S(2)}) copy-start(f32[1,1024]{1,0:T(1,128)} %get-tuple-element.61) | copy-start | bytes 12292
  410.3 14.2 %collective-permute-start.9 = (bf16[2,256,512]{2,1,0:T(8,128)(2,1)S(1)}, bf16[2,256,512]{2,1,0:T(8,128)(2,1)S(1)}, u32[]{:S(2)}, u32[]{:S(2)}) collective-permute-start(bf16[2,256,512]{2,1,0:T(8,128)(2,1)S(1)} %slice_bitcast_fusion.5), channel_id=1, source_target_pairs={{0,1},{1,2},{2,3},{3,0},{4,5},{5,6},{6,7},{7,4},{8,9},{9,10},{10,1... | collective-permute-start | bytes 1572872 | tf_op jit(solution)/shard_map/ppermute | solution.py:536
  425.6 28.9 %copy-start.8 = (bf16[4,2,256,512]{3,2,1,0:T(8,128)(2,1)S(1)}, bf16[4,2,256,512]{3,2,1,0:T(8,128)(2,1)}, u32[]{:S(2)}) copy-start(bf16[4,2,256,512]{3,2,1,0:T(8,128)(2,1)} %get-tuple-element.70) | copy-start | bytes 6291460
  425.6 13.3 %collective-permute-start.10 = (bf16[2,256,512]{2,1,0:T(8,128)(2,1)S(1)}, bf16[2,256,512]{2,1,0:T(8,128)(2,1)S(1)}, u32[]{:S(2)}, u32[]{:S(2)}) collective-permute-start(bf16[2,256,512]{2,1,0:T(8,128)(2,1)S(1)} %fusion.15), channel_id=1, source_target_pairs={{0,1},{1,2},{2,3},{3,0},{4,5},{5,6},{6,7},{7,4},{8,9},{9,10},{10,1... | collective-permute-start | bytes 1572872 | tf_op jit(solution)/shard_map/ppermute | solution.py:536
  440.1 12.4 %collective-permute-start.11 = (bf16[2,256,512]{2,1,0:T(8,128)(2,1)S(1)}, bf16[2,256,512]{2,1,0:T(8,128)(2,1)S(1)}, u32[]{:S(2)}, u32[]{:S(2)}) collective-permute-start(bf16[2,256,512]{2,1,0:T(8,128)(2,1)S(1)} %fusion.14), channel_id=1, source_target_pairs={{0,1},{1,2},{2,3},{3,0},{4,5},{5,6},{6,7},{7,4},{8,9},{9,10},{10,1... | collective-permute-start | bytes 1572872 | tf_op jit(solution)/shard_map/ppermute | solution.py:536
  441.7 249.2 %all-gather.21.cloned.1.call-start = ((), (), s32[]{:S(2)}) async-start(), calls=%async_computation.21 | async-start | bytes 4718592 | tf_op jit(solution)/shard_map/all_gather | solution.py:541
  454.5 275.8 %all-gather.23.cloned.1.call-start = ((), (), s32[]{:S(2)}) async-start(), calls=%async_computation.22 | async-start | bytes 4718592 | tf_op jit(solution)/shard_map/all_gather | solution.py:541
  454.6 11.9 %collective-permute-start.12 = (bf16[2,256,512]{2,1,0:T(8,128)(2,1)S(1)}, bf16[2,256,512]{2,1,0:T(8,128)(2,1)S(1)}, u32[]{:S(2)}, u32[]{:S(2)}) collective-permute-start(bf16[2,256,512]{2,1,0:T(8,128)(2,1)S(1)} %slice_bitcast_fusion.4), channel_id=1, source_target_pairs={{0,1},{1,2},{2,3},{3,0},{4,5},{5,6},{6,7},{7,4},{8,9},{9,10},{10,1... | collective-permute-start | bytes 1572872 | tf_op jit(solution)/shard_map/ppermute | solution.py:536
  466.7 26.6 %copy-start.7 = (bf16[4,2,128,1024]{3,2,1,0:T(8,128)(2,1)S(1)}, bf16[4,2,128,1024]{3,2,1,0:T(8,128)(2,1)}, u32[]{:S(2)}) copy-start(bf16[4,2,128,1024]{3,2,1,0:T(8,128)(2,1)} %get-tuple-element.71) | copy-start | bytes 6291460
  466.7 12.6 %collective-permute-start.13 = (bf16[2,256,512]{2,1,0:T(8,128)(2,1)S(1)}, bf16[2,256,512]{2,1,0:T(8,128)(2,1)S(1)}, u32[]{:S(2)}, u32[]{:S(2)}) collective-permute-start(bf16[2,256,512]{2,1,0:T(8,128)(2,1)S(1)} %fusion.12), channel_id=1, source_target_pairs={{0,1},{1,2},{2,3},{3,0},{4,5},{5,6},{6,7},{7,4},{8,9},{9,10},{10,1... | collective-permute-start | bytes 1572872 | tf_op jit(solution)/shard_map/ppermute | solution.py:536
  479.5 12.8 %collective-permute-start.14 = (bf16[2,256,512]{2,1,0:T(8,128)(2,1)S(1)}, bf16[2,256,512]{2,1,0:T(8,128)(2,1)S(1)}, u32[]{:S(2)}, u32[]{:S(2)}) collective-permute-start(bf16[2,256,512]{2,1,0:T(8,128)(2,1)S(1)} %fusion.11), channel_id=1, source_target_pairs={{0,1},{1,2},{2,3},{3,0},{4,5},{5,6},{6,7},{7,4},{8,9},{9,10},{10,1... | collective-permute-start | bytes 1572872 | tf_op jit(solution)/shard_map/ppermute | solution.py:536
  493.2 276.3 %all-gather.25.cloned.1.call-start = ((), (), s32[]{:S(2)}) async-start(), calls=%async_computation.23 | async-start | bytes 4718592 | tf_op jit(solution)/shard_map/all_gather | solution.py:541
  493.3 14.7 %collective-permute-start.15 = (bf16[2,128,1024]{2,1,0:T(8,128)(2,1)S(1)}, bf16[2,128,1024]{2,1,0:T(8,128)(2,1)S(1)}, u32[]{:S(2)}, u32[]{:S(2)}) collective-permute-start(bf16[2,128,1024]{2,1,0:T(8,128)(2,1)S(1)} %slice_bitcast_fusion.3), channel_id=1, source_target_pairs={{0,1},{1,2},{2,3},{3,0},{4,5},{5,6},{6,7},{7,4},{8,9},{9,10},{10,1... | collective-permute-start | bytes 1572872 | tf_op jit(solution)/shard_map/ppermute | solution.py:536
  508.2 15.9 %collective-permute-start.16 = (bf16[2,128,1024]{2,1,0:T(8,128)(2,1)S(1)}, bf16[2,128,1024]{2,1,0:T(8,128)(2,1)S(1)}, u32[]{:S(2)}, u32[]{:S(2)}) collective-permute-start(bf16[2,128,1024]{2,1,0:T(8,128)(2,1)S(1)} %fusion.9), channel_id=1, source_target_pairs={{0,1},{1,2},{2,3},{3,0},{4,5},{5,6},{6,7},{7,4},{8,9},{9,10},{10,1... | collective-permute-start | bytes 1572872 | tf_op jit(solution)/shard_map/ppermute | solution.py:536
  524.3 25.4 %copy-start.2 = (bf16[256,1024]{1,0:T(8,128)(2,1)S(1)}, bf16[256,1024]{1,0:T(8,128)(2,1)}, u32[]{:S(2)}) copy-start(bf16[256,1024]{1,0:T(8,128)(2,1)} %x_ref.1) | copy-start | bytes 1572868
  524.3 11.9 %collective-permute-start.17 = (bf16[2,128,1024]{2,1,0:T(8,128)(2,1)S(1)}, bf16[2,128,1024]{2,1,0:T(8,128)(2,1)S(1)}, u32[]{:S(2)}, u32[]{:S(2)}) collective-permute-start(bf16[2,128,1024]{2,1,0:T(8,128)(2,1)S(1)} %fusion.8), channel_id=1, source_target_pairs={{0,1},{1,2},{2,3},{3,0},{4,5},{5,6},{6,7},{7,4},{8,9},{9,10},{10,1... | collective-permute-start | bytes 1572872 | tf_op jit(solution)/shard_map/ppermute | solution.py:536
  537.3 258.7 %all-gather.19.cloned.1.call-start = ((), (), s32[]{:S(2)}) async-start(), calls=%async_computation.19 | async-start | bytes 1179648 | tf_op jit(solution)/shard_map/all_gather | solution.py:552
  549.2 292.9 %reduce-scatter.10.cloned.1.call-start = ((), (), s32[]{:S(2)}) async-start(), calls=%async_computation.16 | async-start | bytes 2621440 | tf_op jit(solution)/shard_map/reduce_scatter | solution.py:523
  550.0 226.2 %all-to-all-start.5 = ((bf16[4,128,256]{2,1,0:T(8,128)(2,1)}), bf16[4,128,256]{2,1,0:T(8,128)(2,1)S(1)}, u32[]{:S(2)}, u32[]{:S(2)}) async-start(bf16[4,128,256]{2,1,0:T(8,128)(2,1)} %reduce-scatter.14.cloned.1.call-done), calls=%async_computation.10 | async-start | bytes 524288 | tf_op jit(solution)/shard_map/all_to_all | solution.py:548
  798.7 43.4 %copy-start.18 = (f32[4,1,256]{2,1,0:T(1,128)S(1)}, f32[4,1,256]{2,1,0:T(1,128)}, u32[]{:S(2)}) copy-start(f32[4,1,256]{2,1,0:T(1,128)} %get-tuple-element.78) | copy-start | bytes 12292
  798.8 44.8 %copy-start.13 = (f32[256,1024]{1,0:T(8,128)S(1)}, f32[256,1024]{1,0:T(8,128)}, u32[]{:S(2)}) copy-start(f32[256,1024]{1,0:T(8,128)} %get-tuple-element.52) | copy-start | bytes 3145732
  (14 other events, 110.0 us)
Sparse Core Ops, SparseCore 0:
  9.6 69.0 all-gather.12
  80.3 56.2 all-gather.26
  138.5 35.3 all-gather.16
  175.6 36.7 all-gather.14
  288.3 49.5 reduce-scatter.7
  385.7 34.1 reduce-scatter.11
  424.1 41.1 reduce-scatter.13
  469.3 51.3 reduce-scatter.5
  527.7 123.0 all-reduce.5
  653.3 37.5 all-gather.20
  693.6 36.7 all-gather.22
  732.8 36.7 all-gather.24
  771.6 24.3 all-gather.18
  798.2 43.8 reduce-scatter.9

commit v2 on v1

v2 whole, which is shorter than its diff:
```python
import functools
import math

import jax
import jax.numpy as jnp
from jax import lax
from jax.experimental import pallas as pl
from jax.experimental.pallas import tpu as pltpu
from jax.sharding import Mesh
from jax.sharding import PartitionSpec as P

QUERY_HEADS = 16
KEY_VALUE_HEADS = 8
HEAD = 64
LANES = 128
MIX_LOW = 64

EPS = 1e-06
ROPE_BASE = 10000.0
MASKED = -1e30
F32 = jnp.float32
BF16 = jnp.bfloat16
NT = (((1,), (1,)), ((), ()))
TN = (((0,), (0,)), ((), ()))
VMEM_LIMIT = 60 * 1024 * 1024


def dot(a, b):
    return jnp.dot(a, b, preferred_element_type=F32)


def dot_nt(a, b):
    return lax.dot_general(a, b, NT, preferred_element_type=F32)


def dot_tn(a, b):
    return lax.dot_general(a, b, TN, preferred_element_type=F32)


def split_hi_lo(value):
    high = value.astype(BF16)
    return high, (value - high.astype(F32)).astype(BF16)


def inverse_rms(value):
    return lax.rsqrt(jnp.mean(value * value, axis=-1, keepdims=True) + EPS)


def swap_halves(value):
    width = value.shape[1]
    lane = lax.broadcasted_iota(jnp.int32, value.shape, 1)
    up = pltpu.roll(value, width - HEAD // 2, 1)
    down = pltpu.roll(value, HEAD // 2, 1)
    return jnp.where(lane % HEAD < HEAD // 2, up, down)


def rotate(value, cosine, sine):
    copies = value.shape[1] // LANES
    cosine = jnp.concatenate([cosine] * copies, axis=1)
    sine = jnp.concatenate([sine] * copies, axis=1)
    return value * cosine + swap_halves(value) * sine


def allowed_pairs(seg_col, seg_row, row0, count):
    rows = seg_col.shape[0]
    row = row0 + lax.broadcasted_iota(jnp.int32, (rows, count), 0)
    col = lax.broadcasted_iota(jnp.int32, (rows, count), 1)
    return (seg_col == seg_row) & (col <= row)


def ring_chunk(z, k, parts):
    return lax.rem(z - k + parts, parts)


def chunk_of(index, size):
    return pl.ds(pl.multiple_of(index * size, size), size)


def front_kernel(
    block, heads, kv_heads, parts, place_ref, *refs
):
    chunks = refs[:parts]
    (gain_ref, wrel_ref, cos_ref, sin_ref, segc_ref, segr_ref,
     x_ref, w_ref, normed_ref, q_ref, k_ref, v_ref, att_ref, lse_ref, out_s, sems) = refs[parts:]
    seq = x_ref.shape[0]
    blocks = seq // block
    group = heads // kv_heads
    qw, kw = heads * HEAD, kv_heads * HEAD
    z = place_ref[0]
    slab = wrel_ref.shape[1]
    copies = []
    for i in range(parts):
        at = chunk_of(ring_chunk(z, i, parts), block)
        copies.append(pltpu.make_async_copy(chunks[i], x_ref.at[at, :], sems.at[i]))
    for copy in copies:
        copy.start()
    for i in range(parts):
        w_ref[chunk_of(ring_chunk(z, i, parts), slab), :] = wrel_ref[i]
    for copy in copies:
        copy.wait()

    def project(i, carry):
        rows = pl.ds(pl.multiple_of(i * block, block), block)
        x = x_ref[rows, :].astype(F32)
        normed = (x * inverse_rms(x) * gain_ref[...]).astype(BF16)
        normed_ref[rows, :] = normed
        qkv = dot(normed, w_ref[...])
        turned = rotate(qkv[:, : qw + kw], cos_ref[rows, :], sin_ref[rows, :])
        for h in range(heads):
            q_ref[h, rows, :] = turned[:, h * HEAD : (h + 1) * HEAD].astype(BF16)
        for h in range(kv_heads):
            k_ref[h, rows, :] = turned[:, qw + h * HEAD : qw + (h + 1) * HEAD].astype(BF16)
            v_ref[h, rows, :] = qkv[:, qw + kw + h * HEAD : qw + kw + (h + 1) * HEAD].astype(BF16)
        return carry

    lax.fori_loop(0, blocks, project, 0)

    def one_head(h, carry):
        kv = h // group
        for i in range(blocks):
            count = (i + 1) * block
            rows = slice(i * block, (i + 1) * block)
            q = q_ref[h, rows, :] * jnp.asarray(0.125, BF16)
            k = k_ref[kv, :count, :]
            v = v_ref[kv, :count, :]
            allowed = allowed_pairs(segc_ref[rows, :], segr_ref[:, :count], i * block, count)
            s = jnp.where(allowed, dot_nt(q, k), MASKED)
            top = jnp.max(s, axis=-1, keepdims=True)
            e = jnp.exp(s - top)
            total = jnp.sum(e, axis=-1, keepdims=True)
            lse_ref[h, rows, :] = top + jnp.log(total)
            p = (e * (1.0 / total)).astype(BF16)
            out_s[h, rows, :] = dot(p, v)
        return carry

    lax.fori_loop(0, heads, one_head, 0)
    for h in range(heads):
        att_ref[:, h * HEAD : (h + 1) * HEAD] = out_s[h].astype(BF16)


def back_kernel(
    block, heads, kv_heads, place_ref, q_ref, k_ref, v_ref, do_ref, lse_ref, segc_ref, segr_ref, x_ref,
    normed_ref, w_ref, cos_ref, sin_ref, ng_ref, dw_ref, gain_ref, do_s, dq_s, dk_s, dv_s, raw_s, g_s,
):
    seq = x_ref.shape[0]
    blocks = seq // block
    group = heads // kv_heads
    qw, kw = heads * HEAD, kv_heads * HEAD
    for h in range(heads):
        do_s[h] = do_ref[:, h * HEAD : (h + 1) * HEAD]
    dk_s[...] = jnp.zeros_like(dk_s)
    dv_s[...] = jnp.zeros_like(dv_s)

    def one_head(h, carry):
        kv = h // group
        for i in range(blocks):
            count = (i + 1) * block
            rows = slice(i * block, (i + 1) * block)
            q = q_ref[h, rows, :] * jnp.asarray(0.125, BF16)
            k = k_ref[kv, :count, :]
            v = v_ref[kv, :count, :]
            do = do_s[h, rows, :]
            allowed = allowed_pairs(segc_ref[rows, :], segr_ref[:, :count], i * block, count)
            s = jnp.where(allowed, dot_nt(q, k), MASKED)
            prob = jnp.exp(s - lse_ref[h, rows, :])
            grad = dot_nt(do, v)
            inner = jnp.sum(prob * grad, axis=-1, keepdims=True)
            ds = (prob * (grad - inner)).astype(BF16)
            dq_s[h, rows, :] = dot(ds, k) * 0.125
            dk_s[kv, :count, :] += dot_tn(ds, q)
            dv_s[kv, :count, :] += dot_tn(prob.astype(BF16), do)
        return carry

    lax.fori_loop(0, heads, one_head, 0)
    for h in range(heads):
        raw_s[:, h * HEAD : (h + 1) * HEAD] = dq_s[h]
    for h in range(kv_heads):
        raw_s[:, qw + h * HEAD : qw + (h + 1) * HEAD] = dk_s[h]
        raw_s[:, qw + kw + h * HEAD : qw + kw + (h + 1) * HEAD] = dv_s[h]
    gain_ref[...] = jnp.zeros_like(gain_ref)

    def finish(i, carry):
        rows = pl.ds(pl.multiple_of(i * block, block), block)
        g_s[rows, : qw + kw] = rotate(raw_s[rows, : qw + kw], cos_ref[rows, :], -sin_ref[rows, :]).astype(BF16)
        g_s[rows, qw + kw :] = raw_s[rows, qw + kw :].astype(BF16)
        ng = dot_nt(g_s[rows, :], w_ref[...])
        x = x_ref[rows, :].astype(F32)
        gain_ref[...] += jnp.sum(ng * (x * inverse_rms(x)), axis=0, keepdims=True)
        ng_ref[ring_chunk(place_ref[0], i, blocks)] = ng.astype(BF16)
        return carry

    lax.fori_loop(0, blocks, finish, 0)
    width = normed_ref.shape[1]
    for c in range(0, width, 256):
        dw_ref[c : c + 256, :] = dot_tn(normed_ref[:, c : c + 256], g_s[...]).astype(BF16)


def softmax_gates(logits, mask):
    shown = jnp.where(mask > 0.0, logits, MASKED)
    e = jnp.where(mask > 0.0, jnp.exp(shown - jnp.max(shown, axis=-1, keepdims=True)), 0.0)
    return e * (1.0 / jnp.sum(e, axis=-1, keepdims=True))


def mid_kernel(place_ref, x_ref, att_ref, ow_ref, gain_ref, router_ref, mask_ref, hidden_ref, normed_ref, gates_ref):
    parts, width = ow_ref.shape[0], ow_ref.shape[2]
    depth = att_ref.shape[2]
    for j in range(parts):
        cols = chunk_of(ring_chunk(place_ref[0], j, parts), width)
        total = x_ref[:, cols].astype(F32)
        for i in range(att_ref.shape[0]):
            total = total + dot(att_ref[i], ow_ref[j, i * depth : (i + 1) * depth, :])
        hidden_ref[:, cols] = total
    hidden = hidden_ref[...]
    normed = (hidden * inverse_rms(hidden) * gain_ref[...]).astype(BF16)
    normed_ref[...] = normed
    gates_ref[...] = softmax_gates(dot(normed, router_ref[...]), mask_ref[...])


def mid_back_kernel(
    place_ref, hidden_ref, nb_ref, dy_ref, gates_ref, normed_ref, router_ref, gain_ref, ow_ref, att_ref,
    hg_ref, ag_ref, owg_ref, fg_ref, rg_ref, aog_s,
):
    gates = gates_ref[...]
    width_all = hidden_ref.shape[1]
    mix = nb_ref[:, width_all:].astype(F32)
    mix = mix + pltpu.roll(mix, LANES - MIX_LOW, 1)
    lg = gates * (mix - jnp.sum(gates * mix, axis=-1, keepdims=True))
    high, low = split_hi_lo(lg)
    normed = normed_ref[...]
    rg_ref[...] = dot_tn(high, normed) + dot_tn(low, normed)
    router = router_ref[...]
    ng = nb_ref[:, :width_all].astype(F32) + dot_nt(high, router) + dot_nt(low, router)
    hidden = hidden_ref[...]
    inv = inverse_rms(hidden)
    scaled = hidden * inv
    fg_ref[...] = jnp.sum(ng * scaled, axis=0, keepdims=True)
    w = ng * gain_ref[...]
    hg = dy_ref[...].astype(F32) + inv * (w - scaled * jnp.mean(w * scaled, axis=-1, keepdims=True))
    hg_ref[...] = hg
    aog_s[...] = hg.astype(BF16)
    parts, width = ow_ref.shape[0], ow_ref.shape[2]
    groups, _, depth = att_ref.shape
    for i in range(groups):
        rows = slice(i * depth, (i + 1) * depth)
        total = None
        for j in range(parts):
            chunk = ring_chunk(place_ref[0], j, parts)
            part = dot_nt(aog_s[:, chunk_of(chunk, width)], ow_ref[j, rows, :])
            total = part if total is None else total + part
        ag_ref[i] = total.astype(BF16)
        for j in range(parts):
            owg_ref[j, rows, :] = dot_tn(att_ref[i], aog_s[:, j * width : (j + 1) * width]).astype(BF16)


def expert_kernel(
    experts, parts, place_ref, n2_ref, dy_ref, mask_ref, router_ref, *refs
):
    weights = refs[: 3 * parts]
    moe_ref, nb_ref, g_ref, inner_ref, gg_ref, ug_ref = refs[3 * parts : 3 * parts + 6]
    wg_s, wu_s, wd_s, sems = refs[3 * parts + 6 :]
    z = place_ref[0]
    first = place_ref[1]

    @pl.when(pl.program_id(0) == 0)
    def load():
        copies = []
        for m, target in enumerate((wg_s, wu_s, wd_s)):
            for k in range(parts):
                source = weights[m * parts + k]
                size = source.shape[1]
                at = chunk_of(ring_chunk(z, k, parts), size)
                copies.append(pltpu.make_async_copy(source, target.at[:, at, :], sems.at[m * parts + k]))
        for copy in copies:
            copy.start()
        for copy in copies:
            copy.wait()

    x = n2_ref[...]
    dy = dy_ref[...].astype(F32)
    gates = softmax_gates(dot(x, router_ref[...]), mask_ref[...])
    lane = lax.broadcasted_iota(jnp.int32, gates.shape, 1)
    moe = nb = mix_out = None
    for e in range(experts):
        g = jnp.sum(jnp.where(lane == first + e, gates, 0.0), axis=-1, keepdims=True)
        ga = dot(x, wg_s[e])
        ua = dot(x, wu_s[e])
        sg = jax.nn.sigmoid(ga)
        act = ga * sg
        inner = (act * ua).astype(BF16)
        inner_ref[e] = inner
        eo = dot(inner, wd_s[e]).astype(BF16).astype(F32)
        mix = jnp.sum(dy * eo, axis=-1, keepdims=True)
        part = g * eo
        moe = part if moe is None else moe + part
        high, low = split_hi_lo(mix)
        row = jnp.where(lane == first + e, high.astype(F32), 0.0)
        row = row + jnp.where(lane == MIX_LOW + first + e, low.astype(F32), 0.0)
        mix_out = row if mix_out is None else mix_out + row
        g_ref[...] = jnp.where(lane == e, g, g_ref[...] if e else 0.0)
        ig = dot_nt((g * dy).astype(BF16), wd_s[e])
        gg = (ig * ua * sg * (1.0 + ga * (1.0 - sg))).astype(BF16)
        ug = (ig * act).astype(BF16)
        gg_ref[e] = gg
        ug_ref[e] = ug
        back = dot_nt(gg, wg_s[e]) + dot_nt(ug, wu_s[e])
        nb = back if nb is None else nb + back
    moe_ref[...] = moe.astype(BF16)
    width = n2_ref.shape[1]
    nb_ref[:, :width] = nb.astype(BF16)
    nb_ref[:, width:] = mix_out.astype(BF16)


def expert_grad_kernel(experts, parts, half, place_ref, *refs):
    halves = (refs[:6], refs[6:12])
    dg_ref, du_ref, dd_ref, g_s, u_s, d_s = refs[12:]
    e, step = pl.program_id(0), pl.program_id(1)

    @pl.when(step == 0)
    def clear():
        g_s[...] = jnp.zeros_like(g_s)
        u_s[...] = jnp.zeros_like(u_s)
        d_s[...] = jnp.zeros_like(d_s)

    def add(n2_ref, dy_ref, g_ref, inner_ref, gg_ref, ug_ref):
        x = n2_ref[...]
        lane = lax.broadcasted_iota(jnp.int32, g_ref.shape, 1)
        g = jnp.sum(jnp.where(lane == e, g_ref[...], 0.0), axis=-1, keepdims=True)
        og = (g * dy_ref[...].astype(F32)).astype(BF16)
        g_s[...] += dot_tn(x, gg_ref[0])
        u_s[...] += dot_tn(x, ug_ref[0])
        d_s[...] += dot_tn(inner_ref[0], og)

    pl.when(step < half)(lambda: add(*halves[0]))
    pl.when(step >= half)(lambda: add(*halves[1]))

    @pl.when(step == pl.num_programs(1) - 1)
    def store():
        z = place_ref[0]
        for total, out in ((g_s, dg_ref), (u_s, du_ref), (d_s, dd_ref)):
            size = out.shape[2]
            for k in range(parts):
                out[k, 0] = total[chunk_of(ring_chunk(z, k, parts), size), :].astype(BF16)


def sds(shape, dtype):
    return jax.ShapeDtypeStruct(shape, dtype)


def params():
    return pltpu.CompilerParams(vmem_limit_bytes=VMEM_LIMIT)


def cost(flops, traffic):
    return pl.CostEstimate(flops=int(flops), bytes_accessed=int(traffic), transcendentals=0)


def per_device(
    hi, yx, n, tokens, cotangent, segment_ids, routes, attn_gain, query_weight, key_matrix, value_weight,
    out_weight, ffn_gain, router_weight, gate_weight, up_weight, down_weight,
):
    rows, width = tokens.shape
    seq = rows * n
    experts = gate_weight.shape[0]
    ep = yx * 2
    own = experts // ep
    heads, kv_heads = QUERY_HEADS // n, KEY_VALUE_HEADS // n
    qw, kw = heads * HEAD, kv_heads * HEAD
    cols = qw + 2 * kw
    slab = width // n
    ff = gate_weight.shape[2]
    z = lax.axis_index("shard").astype(jnp.int32)
    core = lax.axis_index("cr").astype(jnp.int32)
    r = lax.axis_index("yx").astype(jnp.int32) * 2 + core
    place = jnp.stack([z, r * own])
    plane = ("yx", "cr")
    smem = pl.BlockSpec(memory_space=pltpu.SMEM)
    vmem = pl.BlockSpec(memory_space=pltpu.VMEM)
    hbm = pl.BlockSpec(memory_space=pl.ANY)

    def shift(value, k=1):
        return lax.ppermute(value, "shard", [(i, (i + k) % n) for i in range(n)])

    def swap(value):
        return lax.ppermute(value, "cr", [(0, 1), (1, 0)])

    def pick(value, index, axis):
        return lax.dynamic_index_in_dim(value, index, axis, keepdims=False)

    def absolute(parts):
        stacked = jnp.stack(parts)
        return jnp.stack([pick(stacked, lax.rem(z - j + n, n), 0) for j in range(n)])

    pack = jnp.concatenate(
        [attn_gain[None], ffn_gain[None], segment_ids.astype(BF16)[None], router_weight.T], axis=0
    )
    packs = absolute([pack] + [shift(pack, k) for k in range(1, n)])
    gain1 = packs[:, 0, :].reshape(1, width).astype(F32)
    gain2 = packs[:, 1, :].reshape(1, width).astype(F32)
    segments = packs[:, 2, :].reshape(seq).astype(F32)
    seg_col, seg_row = segments[:, None], segments[None, :]
    router = jnp.pad(packs[:, 3:, :].transpose(0, 2, 1).reshape(width, experts), ((0, 0), (0, LANES - experts)))

    part_rows = slab // ep
    by_dest = jnp.concatenate(
        [
            lax.dynamic_slice_in_dim(w, r * part_rows, part_rows, axis=0).reshape(part_rows, n, -1)
            for w in (query_weight, key_matrix, value_weight)
        ],
        axis=2,
    )
    w_rel = jnp.stack(
        [pick(by_dest, z, 1)] + [shift(pick(by_dest, lax.rem(z + k, n), 1), k) for k in range(1, n)]
    )
    w_rel = lax.all_gather(w_rel, plane, axis=1, tiled=True)
    ow_rows = out_weight.shape[0] // ep
    ow_mine = lax.dynamic_slice_in_dim(out_weight, r * ow_rows, ow_rows, axis=0)
    ow = jnp.stack([ow_mine] + [shift(ow_mine, k) for k in range(1, n)])
    ow = lax.all_gather(ow, plane, axis=1, tiled=True)

    chunks = [tokens]
    for _ in range(n - 1):
        chunks.append(shift(chunks[-1]))

    ids = jnp.arange(experts, dtype=jnp.int32)
    routed = jnp.any(routes[:, :, None] == ids[None, None, :], axis=1)
    mask_own = jnp.pad(routed.astype(F32), ((0, 0), (0, LANES - experts)))
    mask_all = lax.all_gather(routed.T.astype(BF16), plane, axis=0, tiled=False).reshape(yx, 2, experts, rows)

    def mask_of(which):
        mask = pick(mask_all, which, 1).transpose(0, 2, 1).reshape(yx * rows, experts).astype(F32)
        return jnp.pad(mask, ((0, 0), (0, LANES - experts)))

    positions = jnp.arange(seq, dtype=jnp.int32).astype(F32)
    frequency = ROPE_BASE ** (-jnp.arange(HEAD // 2, dtype=F32) / (HEAD // 2))
    angles = positions[:, None] * frequency[None, :]
    cosine, sine = jnp.cos(angles), jnp.sin(angles)
    cosine = jnp.concatenate([cosine] * 4, axis=1)
    sine = jnp.concatenate([-sine, sine] * 2, axis=1)

    mine = [lax.dynamic_slice_in_dim(w, r * own, own, axis=0) for w in (gate_weight, up_weight, down_weight)]
    mine, chunks = lax.optimization_barrier((mine, chunks))
    slabs = []
    for w in mine:
        slabs.append(w)
        for _ in range(n - 1):
            w = shift(w)
            slabs.append(w)

    x_all, w_qkv, normed, q, k, v, att, lse = pl.pallas_call(
        functools.partial(front_kernel, rows, heads, kv_heads, n),
        in_specs=[smem] + [hbm] * n + [vmem] * 6,
        out_shape=(
            sds((seq, width), BF16),
            sds((width, cols), BF16),
            sds((seq, width), BF16),
            sds((heads, seq, HEAD), BF16),
            sds((kv_heads, seq, HEAD), BF16),
            sds((kv_heads, seq, HEAD), BF16),
            sds((seq, qw), BF16),
            sds((heads, seq, 1), F32),
        ),
        scratch_shapes=[pltpu.VMEM((heads, seq, HEAD), F32), pltpu.SemaphoreType.DMA((n,))],
        compiler_params=params(),
        cost_estimate=cost(2 * seq * width * cols, 60e6),
        name="front",
    )(place, *chunks, gain1, w_rel, cosine, sine, seg_col, seg_row)

    att = lax.all_to_all(att.reshape(n, rows, qw), "shard", 0, 0)
    hidden, normed2, gates_own = pl.pallas_call(
        mid_kernel,
        in_specs=[smem] + [vmem] * 6,
        out_shape=(sds((rows, width), F32), sds((rows, width), BF16), sds((rows, LANES), F32)),
        compiler_params=params(),
        cost_estimate=cost(2 * rows * width * width, 14e6),
        name="mid",
    )(place, tokens, att, ow, gain2, router, mask_own)

    dy_mine = lax.all_gather(cotangent, "yx", axis=0, tiled=True)
    dy_mate = swap(dy_mine)
    n2_mine = lax.all_gather(normed2, "yx", axis=0, tiled=True)
    n2_mate = swap(n2_mine)

    total = yx * rows
    block = min(512, total)
    steps = total // block

    def run_experts(n2, dy, mask):
        return pl.pallas_call(
            functools.partial(expert_kernel, own, n),
            grid=(steps,),
            in_specs=[
                smem,
                pl.BlockSpec((block, width), lambda i: (i, 0)),
                pl.BlockSpec((block, width), lambda i: (i, 0)),
                pl.BlockSpec((block, LANES), lambda i: (i, 0)),
                pl.BlockSpec((width, LANES), lambda i: (0, 0)),
            ]
            + [hbm] * (3 * n),
            out_specs=(
                pl.BlockSpec((block, width), lambda i: (i, 0)),
                pl.BlockSpec((block, width + LANES), lambda i: (i, 0)),
                pl.BlockSpec((block, LANES), lambda i: (i, 0)),
                pl.BlockSpec((own, block, ff), lambda i: (0, i, 0)),
                pl.BlockSpec((own, block, ff), lambda i: (0, i, 0)),
                pl.BlockSpec((own, block, ff), lambda i: (0, i, 0)),
            ),
            out_shape=(
                sds((total, width), BF16),
                sds((total, width + LANES), BF16),
                sds((total, LANES), F32),
                sds((own, total, ff), BF16),
                sds((own, total, ff), BF16),
                sds((own, total, ff), BF16),
            ),
            scratch_shapes=[
                pltpu.VMEM((own, width, ff), BF16),
                pltpu.VMEM((own, width, ff), BF16),
                pltpu.VMEM((own, ff, width), BF16),
                pltpu.SemaphoreType.DMA((3 * n,)),
            ],
            compiler_params=params(),
            cost_estimate=cost(12 * own * total * width * ff, 70e6),
            name="experts",
        )(place, n2, dy, mask, router, *slabs)

    moe_mate, nb_mate, *saved_mate = run_experts(n2_mate, dy_mate, mask_of(1 - core))
    nb_got = swap(nb_mate)
    moe_got = swap(moe_mate)
    moe, nb, *saved_mine = run_experts(n2_mine, dy_mine, mask_of(core))

    def plus(one, other):
        return (one.astype(F32) + other.astype(F32)).astype(BF16)

    nb_own = lax.psum_scatter(plus(nb, nb_got), "yx", scatter_dimension=0, tiled=True)
    moe_own = lax.psum_scatter(plus(moe, moe_got), "yx", scatter_dimension=0, tiled=True)

    ff_slab = ff // n

    def half_specs(at):
        return [
            pl.BlockSpec((block, width), lambda e, i: (at(i), 0)),
            pl.BlockSpec((block, width), lambda e, i: (at(i), 0)),
            pl.BlockSpec((block, LANES), lambda e, i: (at(i), 0)),
            pl.BlockSpec((1, block, ff), lambda e, i: (e, at(i), 0)),
            pl.BlockSpec((1, block, ff), lambda e, i: (e, at(i), 0)),
            pl.BlockSpec((1, block, ff), lambda e, i: (e, at(i), 0)),
        ]

    dg, du, dd = pl.pallas_call(
        functools.partial(expert_grad_kernel, own, n, steps),
        grid=(own, 2 * steps),
        in_specs=[smem]
        + half_specs(lambda i: jnp.minimum(i, steps - 1))
        + half_specs(lambda i: jnp.maximum(i - steps, 0)),
        out_specs=(
            pl.BlockSpec((n, 1, slab, ff), lambda e, i: (0, e, 0, 0)),
            pl.BlockSpec((n, 1, slab, ff), lambda e, i: (0, e, 0, 0)),
            pl.BlockSpec((n, 1, ff_slab, width), lambda e, i: (0, e, 0, 0)),
        ),
        out_shape=(
            sds((n, own, slab, ff), BF16),
            sds((n, own, slab, ff), BF16),
            sds((n, own, ff_slab, width), BF16),
        ),
        scratch_shapes=[
            pltpu.VMEM((width, ff), F32),
            pltpu.VMEM((width, ff), F32),
            pltpu.VMEM((ff, width), F32),
        ],
        compiler_params=params(),
        cost_estimate=cost(6 * own * 2 * total * width * ff, 80e6),
        name="expert_grads",
    )(place, n2_mate, dy_mate, *saved_mate, n2_mine, dy_mine, *saved_mine)

    def ring_sum(parts):
        part = parts[1]
        for step in list(range(2, n)) + [0]:
            part = shift(part).astype(F32) + parts[step].astype(F32)
            if step:
                part = part.astype(BF16)
        return part

    def expert_sum(parts):
        part = ring_sum(parts)
        if hi > 1:
            part = lax.psum(part, "hi")
        mine = lax.all_gather(part.astype(BF16), "yx", axis=0, tiled=False)
        mate = swap(mine)
        even, odd = jnp.where(core == 0, mine, mate), jnp.where(core == 0, mate, mine)
        return jnp.stack([even, odd], axis=1).reshape((experts,) + part.shape[1:]).astype(F32)

    gate_grad, up_grad, down_grad = expert_sum(dg), expert_sum(du), expert_sum(dd)

    hidden_grad, att_grad, ow_grad, ffn_grad, router_grad = pl.pallas_call(
        mid_back_kernel,
        in_specs=[smem] + [vmem] * 9,
        out_shape=(
            sds((rows, width), F32),
            sds((n, rows, qw), BF16),
            sds((n, n * qw, slab), BF16),
            sds((1, width), F32),
            sds((LANES, width), F32),
        ),
        scratch_shapes=[pltpu.VMEM((rows, width), BF16)],
        compiler_params=params(),
        cost_estimate=cost(4 * rows * width * width, 20e6),
        name="mid_back",
    )(place, hidden, nb_own, cotangent, gates_own, normed2, router, gain2, ow, att)

    att_grad = lax.all_to_all(att_grad, "shard", 0, 0).reshape(seq, qw)
    ng, qkv_grad, gain_grad = pl.pallas_call(
        functools.partial(back_kernel, rows, heads, kv_heads),
        in_specs=[smem] + [vmem] * 12,
        out_shape=(sds((n, rows, width), BF16), sds((width, cols), BF16), sds((1, width), F32)),
        scratch_shapes=[
            pltpu.VMEM((heads, seq, HEAD), BF16),
            pltpu.VMEM((heads, seq, HEAD), F32),
            pltpu.VMEM((kv_heads, seq, HEAD), F32),
            pltpu.VMEM((kv_heads, seq, HEAD), F32),
            pltpu.VMEM((seq, cols), F32),
            pltpu.VMEM((seq, cols), BF16),
        ],
        compiler_params=params(),
        cost_estimate=cost(4 * seq * width * cols, 80e6),
        name="back",
    )(place, q, k, v, att_grad, lse, seg_col, seg_row, x_all, normed, w_qkv, cosine, sine)

    ng_own = ring_sum(ng)
    output = (hidden + moe_own.astype(F32)).astype(BF16)

    x = tokens.astype(F32)
    inv = inverse_rms(x)
    scaled = x * inv
    w1 = ng_own * gain1
    input_grad = hidden_grad + inv * (w1 - scaled * jnp.mean(w1 * scaled, axis=-1, keepdims=True))

    kvw = 2 * kw
    small = jnp.concatenate([gain_grad, ffn_grad, router_grad[:experts]], axis=0)
    small_rows = 16
    small = jnp.pad(small, ((0, ep * small_rows - small.shape[0]), (0, 0)))
    small = small.reshape(ep, small_rows, n, slab).transpose(2, 0, 1, 3).astype(BF16)
    qkv_rows = qkv_grad.reshape(n, ep, part_rows, cols)
    wide = max(slab, qw, kvw)

    def widen(part):
        return jnp.pad(part, ((0, 0),) * 3 + ((0, wide - part.shape[3]),))

    pieces = [widen(ow_grad.reshape(n, ep, ow_rows, slab)), widen(small), widen(qkv_rows[..., :qw]), widen(qkv_rows[..., qw:])]
    dense = jnp.concatenate(pieces, axis=2)
    dense = dense.reshape(n, yx, 2, dense.shape[2], wide).transpose(2, 1, 0, 3, 4)
    dense = plus(pick(dense, core, 0), swap(pick(dense, 1 - core, 0)))
    piece = dense.shape[1:]
    dense = lax.psum_scatter(dense.reshape(-1, wide), "yx", scatter_dimension=0, tiled=True).reshape(piece)
    if hi > 1:
        dense = lax.psum(dense.astype(F32), "hi").astype(BF16)
    dense = lax.all_to_all(dense, "shard", 0, 0)
    cut = ow_rows + small_rows
    summed = jnp.sum(dense[:, :cut].astype(F32), axis=0).astype(BF16)
    kept = dense[:, cut:].reshape(n * 2 * part_rows, wide)
    full = lax.all_gather(jnp.concatenate([summed, kept], axis=0), plane, axis=0, tiled=False)
    ow_full = full[:, :ow_rows, :slab].reshape(-1, slab).astype(F32)
    small_full = full[:, ow_rows:cut, :slab].reshape(-1, slab).astype(F32)
    kept = full[:, cut:].reshape(ep, n, 2, part_rows, wide)

    def columns(which, start, size):
        part = kept[:, :, which, :, start : start + size]
        return part.transpose(0, 2, 1, 3).reshape(slab, n * size).astype(F32)

    return (
        output,
        input_grad,
        small_full[0],
        columns(0, 0, qw),
        columns(1, 0, kw),
        columns(1, kw, kw),
        ow_full,
        small_full[1],
        small_full[2 : 2 + experts].T,
        gate_grad,
        up_grad,
        down_grad,
    )


def solution(mesh):
    rep, n = mesh.shape["rep"], mesh.shape["shard"]
    yx = math.gcd(rep // 2, 4)
    hi = rep // (2 * yx)
    split = Mesh(mesh.devices.reshape(hi, yx, 2, n), ("hi", "yx", "cr", "shard"))
    rows = ("hi", "yx", "cr", "shard")
    placed = (
        P(rows, None),
        P(rows, None),
        P(rows),
        P(rows, None),
        P("shard"),
        P("shard", None),
        P("shard", None),
        P("shard", None),
        P(None, "shard"),
        P("shard"),
        P("shard", None),
        P(None, "shard", None),
        P(None, "shard", None),
        P(None, "shard", None),
    )
    return jax.shard_map(
        functools.partial(per_device, hi, yx, n),
        mesh=split,
        in_specs=placed,
        out_specs=(
            P(rows, None),
            P(rows, None),
            P("shard"),
            P("shard", None),
            P("shard", None),
            P("shard", None),
            P(None, "shard"),
            P("shard"),
            P("shard", None),
            P(None, "shard", None),
            P(None, "shard", None),
            P(None, "shard", None),
        ),
        check_vma=False,
    )
```

time: 854 us -> 654 us (0.77)
  waiting for transfers between devices: 533 us -> 383 us
  blocking collectives: 116 us -> 9.36 us
  local copies, waits for them, and re-layouts: 18.1 us -> 37.5 us
  starting transfers between devices: 16.7 us -> 34.4 us
  Pallas kernels: 109 us -> 121 us
    all_gather x8, waiting for transfers between devices: 143 us -> 44.2 us  [the longest x1 37.6 us: per_device(): n2_mine = lax.all_gather(normed2, 'yx', axis=0, tiled=True)]
    psum x1 -> x0, waiting for transfers between devices: 95.2 us -> none  [per_device(): lax.psum(jnp.concatenate([gain_grad, ffn_grad, router_grad[:experts]], ax...]
    all_gather x3 -> x1, blocking collectives: 77 us -> 9.36 us  [per_device(): lax.all_gather(routed.T.astype(BF16), plane, axis=0, tiled=False)]
    ppermute x18 -> x41, waiting for transfers between devices: 210 us -> 262 us  [the longest x33 254 us: shift(): return lax.ppermute(value, 'shard', [(i, (i + k) % n) for i in range(n)])]
    reduce_scatter x5 -> x3, waiting for transfers between devices: 80.8 us -> 38.7 us  [the longest x1 33.7 us: per_device(): lax.psum_scatter(dense.reshape(-1, wide), 'yx', scatter_dimension=0, tile...]
    all_to_all x3 -> x0, blocking collectives: 39.3 us -> none  [the longest x1 19.2 us: per_device(): att_grad = lax.all_to_all(att_grad, 'shard', 0, 0).reshape(seq, qw)]
    all_to_all x2, waiting for transfers between devices: 0.01 us -> 29.4 us  [the longest x1 15.9 us: per_device(): dense = lax.all_to_all(dense, 'shard', 0, 0)]
    ppermute x18 -> x41, starting transfers between devices: 2.68 us -> 22.5 us  [the longest x33 21.5 us: shift(): return lax.ppermute(value, 'shard', [(i, (i + k) % n) for i in range(n)])]
  transfers between devices with their start and end apart: 35 -> 55, of which waited for: 25 -> 38; matrix products, arithmetic and copies ran while one was open for 7% -> 10% of each run, Pallas kernels for 5% -> 15%
where the time goes in v2:
time: 654 us; the launch traced here: 645 us
  waiting for transfers between devices  383 us (59%)
  Pallas kernels  121 us (19%)
  other arithmetic  43.6 us (7%)
  local copies, waits for them, and re-layouts  37.5 us (6%)
  starting transfers between devices  34.4 us (5%)
  between operations  15.1 us (2%)
  blocking collectives  9.36 us (1%)
    ppermute x33, waiting for transfers between devices, shift(): return lax.ppermute(value, 'shard', [(i, (i + k) % n) for i in range(n)])  254 us
    pallas_call x2, Pallas kernels, run_experts(): pl.pallas_call(functools.partial(expert_kernel, own, n), grid=(steps,), i...  46.4 us
    all_gather x1, waiting for transfers between devices, per_device(): n2_mine = lax.all_gather(normed2, 'yx', axis=0, tiled=True)  37.6 us
    reduce_scatter x1, waiting for transfers between devices, per_device(): lax.psum_scatter(dense.reshape(-1, wide), 'yx', scatter_dimension=0, tile...  33.7 us
    pallas_call x1, Pallas kernels, per_device(): pl.pallas_call(functools.partial(expert_grad_kernel, own, n, steps), grid...  24.2 us
    pallas_call x1, Pallas kernels, per_device(): pl.pallas_call(functools.partial(back_kernel, rows, heads, kv_heads), in_...  22.1 us
    ppermute x33, starting transfers between devices, shift(): return lax.ppermute(value, 'shard', [(i, (i + k) % n) for i in range(n)])  21.5 us
    pallas_call x1, Pallas kernels, per_device(): pl.pallas_call(functools.partial(front_kernel, rows, heads, kv_heads, n),...  18.2 us
  transfers between devices with their start and end apart: 55, of which 38 were waited for; matrix products, arithmetic and copies ran while one was open for 10% of the time, Pallas kernels for 15%

profile of v2, /device:TPU:0, one launch (start us, length us, event | category | flops | bytes accessed | tf_op | source)
XLA Modules:
  0.0 644.8 jit_solution(8164715495386103798)
XLA Ops:
  9.5 5.1 collective-permute-start.8
  30.4 3.8 collective-permute-start.5
  36.2 7.7 %collective-permute-done.refs_1_ = bf16[256,1024]{1,0:T(8,128)(2,1)S(1)} collective-permute-done((bf16[256,1024]{1,0:T(8,128)(2,1)S(1)}, bf16[256,1024]{1,0:T(8,128)(2,1)S(1)}, u32[]{:S(2)}, u32[]{:S(2)}) %collective-permute-start) | collective-permute-done | bytes 524320 | tf_op jit(solution)/shard_map/ppermute | solution.py:381
  47.7 8.3 %collective-permute-done.1.refs_2_ = bf16[256,1024]{1,0:T(8,128)(2,1)S(1)} collective-permute-done((bf16[256,1024]{1,0:T(8,128)(2,1)S(1)}, bf16[256,1024]{1,0:T(8,128)(2,1)S(1)}, u32[]{:S(2)}, u32[]{:S(2)}) %collective-permute-start.1) | collective-permute-done | bytes 524320 | tf_op jit(solution)/shard_map/ppermute | solution.py:381
  59.6 7.4 %collective-permute-done.2.refs_3_ = bf16[256,1024]{1,0:T(8,128)(2,1)S(1)} collective-permute-done((bf16[256,1024]{1,0:T(8,128)(2,1)S(1)}, bf16[256,1024]{1,0:T(8,128)(2,1)S(1)}, u32[]{:S(2)}, u32[]{:S(2)}) %collective-permute-start.2) | collective-permute-done | bytes 524320 | tf_op jit(solution)/shard_map/ppermute | solution.py:381
  67.8 18.2 %front.1 = (bf16[1024,1024]{1,0:T(8,128)(2,1)}, bf16[1024,512]{1,0:T(8,128)(2,1)}, bf16[1024,1024]{1,0:T(8,128)(2,1)}, bf16[4,1024,64]{2,1,0:T(8,128)(2,1)}, bf1...) custom-call(s32[2]{0:T(128)} %pad_add_fusion.place_ref, ...), custom_call_target="tpu_custom_call" | custom-call | flops 1073741824 | bytes 60000000 | tf_op jit(solution)/shard_map/front/pallas_call | solution.py:449
  86.0 3.5 all-to-all-start
  91.9 7.8 %all-to-all-done.att_ref = bf16[4,256,256]{2,1,0:T(8,128)(2,1)S(1)} async-done(((bf16[4,256,256]{2,1,0:T(8,128)(2,1)}), bf16[4,256,256]{2,1,0:T(8,128)(2,1)S(1)}, u32[]{:S(2)}, u32[]{:S(2)}) %all-to-all-start) | async-done | bytes 524320 | tf_op jit(solution)/shard_map/all_to_all | solution.py:468
  100.5 4.0 mid.1
  104.6 6.6 %all-gather.20.cloned.1.call-done.dy_ref.refs_7_ = bf16[1024,1024]{1,0:T(8,128)(2,1)} async-done(((bf16[256,1024]{1,0:T(8,128)(2,1)}), bf16[1024,1024]{1,0:T(8,128)(2,1)}) %all-gather.20.cloned.1.call-update) | async-done | bytes 2097168 | tf_op jit(solution)/shard_map/all_gather | solution.py:478
  111.2 37.6 %all-gather.18.cloned.1.call-done.n2_ref.refs_6_ = bf16[1024,1024]{1,0:T(8,128)(2,1)} async-done(((bf16[256,1024]{1,0:T(8,128)(2,1)}), bf16[1024,1024]{1,0:T(8,128)(2,1)}) %all-gather.18.cloned.1.call-update) | async-done | bytes 2097168 | tf_op jit(solution)/shard_map/all_gather | solution.py:480
  153.3 12.1 %collective-permute-done.12.refs_1_ = bf16[2,256,512]{2,1,0:T(8,128)(2,1)S(1)} collective-permute-done((bf16[2,256,512]{2,1,0:T(8,128)(2,1)S(1)}, bf16[2,256,512]{2,1,0:T(8,128)(2,1)S(1)}, u32[]{:S(2)}, u32[]{:S(2)}) %collective-permute-start.12) | collective-permute-done | bytes 524320 | tf_op jit(solution)/shard_map/ppermute | solution.py:381
  165.3 11.2 %collective-permute-done.15.refs_5_ = bf16[2,256,512]{2,1,0:T(8,128)(2,1)S(1)} collective-permute-done((bf16[2,256,512]{2,1,0:T(8,128)(2,1)S(1)}, bf16[2,256,512]{2,1,0:T(8,128)(2,1)S(1)}, u32[]{:S(2)}, u32[]{:S(2)}) %collective-permute-start.15) | collective-permute-done | bytes 524320 | tf_op jit(solution)/shard_map/ppermute | solution.py:381
  176.6 11.2 %collective-permute-done.18.refs_9_ = bf16[2,128,1024]{2,1,0:T(8,128)(2,1)S(1)} collective-permute-done((bf16[2,128,1024]{2,1,0:T(8,128)(2,1)S(1)}, bf16[2,128,1024]{2,1,0:T(8,128)(2,1)S(1)}, u32[]{:S(2)}, u32[]{:S(2)}) %collective-permute-start.18) | collective-permute-done | bytes 524320 | tf_op jit(solution)/shard_map/ppermute | solution.py:381
  187.8 11.2 %collective-permute-done.13.refs_2_ = bf16[2,256,512]{2,1,0:T(8,128)(2,1)S(1)} collective-permute-done((bf16[2,256,512]{2,1,0:T(8,128)(2,1)S(1)}, bf16[2,256,512]{2,1,0:T(8,128)(2,1)S(1)}, u32[]{:S(2)}, u32[]{:S(2)}) %collective-permute-start.13) | collective-permute-done | bytes 524320 | tf_op jit(solution)/shard_map/ppermute | solution.py:381
  199.1 11.2 %collective-permute-done.16.refs_6_ = bf16[2,256,512]{2,1,0:T(8,128)(2,1)S(1)} collective-permute-done((bf16[2,256,512]{2,1,0:T(8,128)(2,1)S(1)}, bf16[2,256,512]{2,1,0:T(8,128)(2,1)S(1)}, u32[]{:S(2)}, u32[]{:S(2)}) %collective-permute-start.16) | collective-permute-done | bytes 524320 | tf_op jit(solution)/shard_map/ppermute | solution.py:381
  210.3 11.2 %collective-permute-done.19.refs_10_ = bf16[2,128,1024]{2,1,0:T(8,128)(2,1)S(1)} collective-permute-done((bf16[2,128,1024]{2,1,0:T(8,128)(2,1)S(1)}, bf16[2,128,1024]{2,1,0:T(8,128)(2,1)S(1)}, u32[]{:S(2)}, u32[]{:S(2)}) %collective-permute-start.19) | collective-permute-done | bytes 524320 | tf_op jit(solution)/shard_map/ppermute | solution.py:381
  221.5 9.4 %all-gather = bf16[128,256]{1,0:T(8,128)(2,1)S(1)} all-gather(bf16[16,256]{1,0:T(8,128)(2,1)S(1)} %convert_bitcast_fusion), channel_id=2, replica_groups=mesh['hi'=1,'yx'=4,'cr'=2,'shard'=4] {'yx','cr'}, dimensions={0}, use_global_device_ids=true | all-gather | bytes 73728 | tf_op jit(solution)/shard_map/all_gather | solution.py:427
  232.9 11.2 %collective-permute-done.17.refs_7_ = bf16[2,256,512]{2,1,0:T(8,128)(2,1)} collective-permute-done((bf16[2,256,512]{2,1,0:T(8,128)(2,1)S(1)}, bf16[2,256,512]{2,1,0:T(8,128)(2,1)}, u32[]{:S(2)}, u32[]{:S(2)}) %collective-permute-start.17) | collective-permute-done | bytes 524320 | tf_op jit(solution)/shard_map/ppermute | solution.py:381
  244.1 10.9 %collective-permute-done.20.refs_11_ = bf16[2,128,1024]{2,1,0:T(8,128)(2,1)} collective-permute-done((bf16[2,128,1024]{2,1,0:T(8,128)(2,1)S(1)}, bf16[2,128,1024]{2,1,0:T(8,128)(2,1)}, u32[]{:S(2)}, u32[]{:S(2)}) %collective-permute-start.20) | collective-permute-done | bytes 524320 | tf_op jit(solution)/shard_map/ppermute | solution.py:381
  255.0 23.0 %experts.3 = (bf16[1024,1024]{1,0:T(8,128)(2,1)}, bf16[1024,1152]{1,0:T(8,128)(2,1)}, f32[1024,128]{1,0:T(8,128)}, bf16[2,1024,512]{2,1,0:T(8,128)(2,1)}, bf16[2...) custom-call(s32[2]{0:T(128)} %pad_add_fusion.place_ref, ...), custom_call_target="tpu_custom_call" | custom-call | flops 12884901888 | bytes 70000000 | tf_op jit(solution)/shard_map/experts/pallas_call | solution.py:488
  279.1 23.4 %experts.2 = (bf16[1024,1024]{1,0:T(8,128)(2,1)}, bf16[1024,1152]{1,0:T(8,128)(2,1)}, f32[1024,128]{1,0:T(8,128)}, bf16[2,1024,512]{2,1,0:T(8,128)(2,1)}, bf16[2...) custom-call(s32[2]{0:T(128)} %pad_add_fusion.place_ref, ...), custom_call_target="tpu_custom_call" | custom-call | flops 12884901888 | bytes 70000000 | tf_op jit(solution)/shard_map/experts/pallas_call | solution.py:488
  302.5 3.7 add_convert_fusion
  306.2 24.2 %expert_grads.1 = (bf16[4,2,256,512]{3,2,1,0:T(8,128)(2,1)}, bf16[4,2,256,512]{3,2,1,0:T(8,128)(2,1)}, bf16[4,2,128,1024]{3,2,1,0:T(8,128)(2,1)}) custom-call(s32[2]{0:T(128)} %pad_add_fusion.place_ref, bf16[1024,1024]{1,0:T(8,128)(2,1)} %collective-permute-done.21.n2_ref.refs_0_, bf16[1024,1024]{1,0:T(8,128)(2,1)} %collective-permute-done.22.dy_ref.refs_1_, ...), custom_call_target="tpu_custom_call" | custom-call | flops 12884901888 | bytes 80000000 | tf_op jit(solution)/shard_map/expert_grads/pallas_call | solution.py:549
  331.7 15.9 %collective-permute-done.29 = bf16[2,256,512]{2,1,0:T(8,128)(2,1)S(1)} collective-permute-done((bf16[2,256,512]{2,1,0:T(8,128)(2,1)S(1)}, bf16[2,256,512]{2,1,0:T(8,128)(2,1)S(1)}, u32[]{:S(2)}, u32[]{:S(2)}) %collective-permute-start.29) | collective-permute-done | bytes 524320 | tf_op jit(solution)/shard_map/ppermute | solution.py:381
  349.1 15.1 %collective-permute-done.30 = bf16[2,256,512]{2,1,0:T(8,128)(2,1)S(1)} collective-permute-done((bf16[2,256,512]{2,1,0:T(8,128)(2,1)S(1)}, bf16[2,256,512]{2,1,0:T(8,128)(2,1)S(1)}, u32[]{:S(2)}, u32[]{:S(2)}) %collective-permute-start.30) | collective-permute-done | bytes 524320 | tf_op jit(solution)/shard_map/ppermute | solution.py:381
  364.4 14.2 %collective-permute-done.31 = bf16[2,256,512]{2,1,0:T(8,128)(2,1)S(1)} collective-permute-done((bf16[2,256,512]{2,1,0:T(8,128)(2,1)S(1)}, bf16[2,256,512]{2,1,0:T(8,128)(2,1)S(1)}, u32[]{:S(2)}, u32[]{:S(2)}) %collective-permute-start.31) | collective-permute-done | bytes 524320 | tf_op jit(solution)/shard_map/ppermute | solution.py:381
  379.8 13.3 %collective-permute-done.33 = bf16[2,256,512]{2,1,0:T(8,128)(2,1)S(1)} collective-permute-done((bf16[2,256,512]{2,1,0:T(8,128)(2,1)S(1)}, bf16[2,256,512]{2,1,0:T(8,128)(2,1)S(1)}, u32[]{:S(2)}, u32[]{:S(2)}) %collective-permute-start.33) | collective-permute-done | bytes 524320 | tf_op jit(solution)/shard_map/ppermute | solution.py:381
  393.3 12.4 %collective-permute-done.34 = bf16[2,256,512]{2,1,0:T(8,128)(2,1)S(1)} collective-permute-done((bf16[2,256,512]{2,1,0:T(8,128)(2,1)S(1)}, bf16[2,256,512]{2,1,0:T(8,128)(2,1)S(1)}, u32[]{:S(2)}, u32[]{:S(2)}) %collective-permute-start.34) | collective-permute-done | bytes 524320 | tf_op jit(solution)/shard_map/ppermute | solution.py:381
  405.9 11.5 %collective-permute-done.35 = bf16[2,256,512]{2,1,0:T(8,128)(2,1)S(1)} collective-permute-done((bf16[2,256,512]{2,1,0:T(8,128)(2,1)S(1)}, bf16[2,256,512]{2,1,0:T(8,128)(2,1)S(1)}, u32[]{:S(2)}, u32[]{:S(2)}) %collective-permute-start.35) | collective-permute-done | bytes 524320 | tf_op jit(solution)/shard_map/ppermute | solution.py:381
  418.5 12.5 %collective-permute-done.37 = bf16[2,128,1024]{2,1,0:T(8,128)(2,1)S(1)} collective-permute-done((bf16[2,128,1024]{2,1,0:T(8,128)(2,1)S(1)}, bf16[2,128,1024]{2,1,0:T(8,128)(2,1)S(1)}, u32[]{:S(2)}, u32[]{:S(2)}) %collective-permute-start.37) | collective-permute-done | bytes 524320 | tf_op jit(solution)/shard_map/ppermute | solution.py:381
  431.2 13.6 %collective-permute-done.38 = bf16[2,128,1024]{2,1,0:T(8,128)(2,1)S(1)} collective-permute-done((bf16[2,128,1024]{2,1,0:T(8,128)(2,1)S(1)}, bf16[2,128,1024]{2,1,0:T(8,128)(2,1)S(1)}, u32[]{:S(2)}, u32[]{:S(2)}) %collective-permute-start.38) | collective-permute-done | bytes 524320 | tf_op jit(solution)/shard_map/ppermute | solution.py:381
  445.1 11.0 %collective-permute-done.39 = bf16[2,128,1024]{2,1,0:T(8,128)(2,1)S(1)} collective-permute-done((bf16[2,128,1024]{2,1,0:T(8,128)(2,1)S(1)}, bf16[2,128,1024]{2,1,0:T(8,128)(2,1)S(1)}, u32[]{:S(2)}, u32[]{:S(2)}) %collective-permute-start.39) | collective-permute-done | bytes 524320 | tf_op jit(solution)/shard_map/ppermute | solution.py:381
  457.2 4.4 collective-permute-done.23
  463.9 6.6 %mid_back.1 = (f32[256,1024]{1,0:T(8,128)}, bf16[4,256,256]{2,1,0:T(8,128)(2,1)}, bf16[4,1024,256]{2,1,0:T(8,128)(2,1)}, f32[1,1024]{1,0:T(1,128)}, f32[128,1024]{1,0:T(8,128)}) custom-call(s32[2]{0:T(128)} %pad_add_fusion.place_ref, f32[256,1024]{1,0:T(8,128)} %get-tuple-element.58.hidden_ref, bf16[256,1152]{1,0:T(8,128)(2,1)} %reduce-scatter.6.cloned.1.call-done.nb_ref, ...), custom_call_target="tpu_custom_call" | custom-call | flops 1073741824 | bytes 20000000 | tf_op jit(solution)/shard_map/mid_back/pallas_call | solution.py:594
  475.5 13.4 %all-to-all-done.1 = bf16[4,256,256]{2,1,0:T(8,128)(2,1)S(1)} async-done(((bf16[4,256,256]{2,1,0:T(8,128)(2,1)}), bf16[4,256,256]{2,1,0:T(8,128)(2,1)S(1)}, u32[]{:S(2)}, u32[]{:S(2)}) %all-to-all-start.1) | async-done | bytes 524320 | tf_op jit(solution)/shard_map/all_to_all | solution.py:610
  489.8 22.1 %back.1 = (bf16[4,256,1024]{2,1,0:T(8,128)(2,1)}, bf16[1024,512]{1,0:T(8,128)(2,1)}, f32[1,1024]{1,0:T(1,128)}) custom-call(s32[2]{0:T(128)} %pad_add_fusion.place_ref, bf16[4,1024,64]{2,1,0:T(8,128)(2,1)} %get-tuple-element.69.q_ref, bf16[2,1024,64]{2,1,0:T(8,128)(2,1)} %get-tuple-element.70.k_ref, bf16[2,1024,64]{2,1,0:T(8,128)(2,1)} %get-tuple-element.71.v_ref, ...), custom_call_target="tpu_custom_call" | custom-call | flops 2147483648 | bytes 80000000 | tf_op jit(solution)/shard_map/back/pallas_call | solution.py:611
  517.3 3.6 collective-permute-done.28
  523.6 5.0 reduce-scatter.4.cloned.1.call-done
  530.6 33.7 %reduce-scatter.8.cloned.1.call-done = bf16[832,256]{1,0:T(8,128)(2,1)} async-done(((bf16[3328,256]{1,0:T(8,128)(2,1)}), bf16[832,256]{1,0:T(8,128)(2,1)}) %reduce-scatter.8.cloned.1.call-update) | async-done | bytes 426000 | tf_op jit(solution)/shard_map/reduce_scatter | solution.py:653
  564.3 4.6 all-to-all-start.2
  568.9 3.8 select_bitcast_fusion.5
  576.6 15.9 %all-to-all-done.2 = bf16[4,208,256]{2,1,0:T(8,128)(2,1)S(1)} async-done(((bf16[4,208,256]{2,1,0:T(8,128)(2,1)}), bf16[4,208,256]{2,1,0:T(8,128)(2,1)S(1)}, u32[]{:S(2)}, u32[]{:S(2)}) %all-to-all-start.2) | async-done | bytes 426016 | tf_op jit(solution)/shard_map/all_to_all | solution.py:656
  598.0 4.5 copy.118
  604.7 7.5 %collective-permute-done.26 = bf16[256,1024]{1,0:T(8,128)(2,1)S(1)} collective-permute-done((bf16[256,1024]{1,0:T(8,128)(2,1)S(1)}, bf16[256,1024]{1,0:T(8,128)(2,1)S(1)}, u32[]{:S(2)}, u32[]{:S(2)}) %collective-permute-start.26) | collective-permute-done | bytes 524320 | tf_op jit(solution)/shard_map/ppermute | solution.py:381
  613.2 4.5 copy.119
  618.2 4.2 copy.120
  622.4 3.9 collective-permute-done.27
  (262 shorter events, 88.7 us)
Async XLA Ops:
  7.2 59.8 %all-gather.14.cloned.1.call-start = ((), (), s32[]{:S(2)}) async-start(), calls=%async_computation.6 | async-start | bytes 1179648 | tf_op jit(solution)/shard_map/all_gather | solution.py:414
  9.5 6.7 %collective-permute-start.8 = (bf16[32,512]{1,0:T(8,128)(2,1)S(1)}, bf16[32,512]{1,0:T(8,128)(2,1)S(1)}, u32[]{:S(2)}, u32[]{:S(2)}) collective-permute-start(bf16[32,512]{1,0:T(8,128)(2,1)S(1)} %bitcast.224), channel_id=1, source_target_pairs={{0,3},{1,0},{2,1},{3,2},{4,7},{5,4},{6,5},{7,6},{8,11},{9,8},{10,9... | collective-permute-start | bytes 98312 | tf_op jit(solution)/shard_map/ppermute | solution.py:381
  21.2 78.6 %all-gather.16.cloned.1.call-start = ((), (), s32[]{:S(2)}) async-start(), calls=%async_computation.7 | async-start | bytes 2359296 | tf_op jit(solution)/shard_map/all_gather | solution.py:418
  29.5 81.7 %all-gather.20.cloned.1.call-start = ((), (), s32[]{:S(2)}) async-start(), calls=%async_computation.9 | async-start | bytes 2621440 | tf_op jit(solution)/shard_map/all_gather | solution.py:478
  30.2 13.7 %collective-permute-start = (bf16[256,1024]{1,0:T(8,128)(2,1)S(1)}, bf16[256,1024]{1,0:T(8,128)(2,1)S(1)}, u32[]{:S(2)}, u32[]{:S(2)}) collective-permute-start(bf16[256,1024]{1,0:T(8,128)(2,1)S(1)} %copy-done.2), channel_id=1, source_target_pairs={{0,1},{1,2},{2,3},{3,0},{4,5},{5,6},{6,7},{7,4},{8,9},{9,10},{10,1... | collective-permute-start | bytes 1572872 | tf_op jit(solution)/shard_map/ppermute | solution.py:381
  30.4 27.6 %collective-permute-start.5 = (bf16[19,256]{1,0:T(8,128)(2,1)S(1)}, bf16[19,256]{1,0:T(8,128)(2,1)S(1)}, u32[]{:S(2)}, u32[]{:S(2)}) collective-permute-start(bf16[19,256]{1,0:T(8,128)(2,1)S(1)} %get-tuple-element.122), channel_id=1, source_target_pairs={{0,3},{1,0},{2,1},{3,2},{4,7},{5,4},{6,5},{7,6},{8,11},{9,8},{10,9... | collective-permute-start | bytes 29192 | tf_op jit(solution)/shard_map/ppermute | solution.py:381
  34.2 23.7 %collective-permute-start.4 = (bf16[19,256]{1,0:T(8,128)(2,1)S(1)}, bf16[19,256]{1,0:T(8,128)(2,1)S(1)}, u32[]{:S(2)}, u32[]{:S(2)}) collective-permute-start(bf16[19,256]{1,0:T(8,128)(2,1)S(1)} %get-tuple-element.122), channel_id=1, source_target_pairs={{0,2},{1,3},{2,0},{3,1},{4,6},{5,7},{6,4},{7,5},{8,10},{9,11},{10,... | collective-permute-start | bytes 29192 | tf_op jit(solution)/shard_map/ppermute | solution.py:381
  34.2 23.7 %collective-permute-start.3 = (bf16[19,256]{1,0:T(8,128)(2,1)S(1)}, bf16[19,256]{1,0:T(8,128)(2,1)S(1)}, u32[]{:S(2)}, u32[]{:S(2)}) collective-permute-start(bf16[19,256]{1,0:T(8,128)(2,1)S(1)} %get-tuple-element.122), channel_id=1, source_target_pairs={{0,1},{1,2},{2,3},{3,0},{4,5},{5,6},{6,7},{7,4},{8,9},{9,10},{10,1... | collective-permute-start | bytes 29192 | tf_op jit(solution)/shard_map/ppermute | solution.py:381
  43.9 12.1 %collective-permute-start.1 = (bf16[256,1024]{1,0:T(8,128)(2,1)S(1)}, bf16[256,1024]{1,0:T(8,128)(2,1)S(1)}, u32[]{:S(2)}, u32[]{:S(2)}) collective-permute-start(bf16[256,1024]{1,0:T(8,128)(2,1)S(1)} %collective-permute-done.refs_1_), channel_id=1, source_target_pairs={{0,1},{1,2},{2,3},{3,0},{4,5},{5,6},{6,7},{7,4},{8,9},{9,10},{10,1... | collective-permute-start | bytes 1572872 | tf_op jit(solution)/shard_map/ppermute | solution.py:381
  56.0 11.0 %collective-permute-start.2 = (bf16[256,1024]{1,0:T(8,128)(2,1)S(1)}, bf16[256,1024]{1,0:T(8,128)(2,1)S(1)}, u32[]{:S(2)}, u32[]{:S(2)}) collective-permute-start(bf16[256,1024]{1,0:T(8,128)(2,1)S(1)} %collective-permute-done.1.refs_2_), channel_id=1, source_target_pairs={{0,1},{1,2},{2,3},{3,0},{4,5},{5,6},{6,7},{7,4},{8,9},{9,10},{10,1... | collective-permute-start | bytes 1572872 | tf_op jit(solution)/shard_map/ppermute | solution.py:381
  86.0 13.7 %all-to-all-start = ((bf16[4,256,256]{2,1,0:T(8,128)(2,1)}), bf16[4,256,256]{2,1,0:T(8,128)(2,1)S(1)}, u32[]{:S(2)}, u32[]{:S(2)}) async-start(bf16[4,256,256]{2,1,0:T(8,128)(2,1)} %bitcast.209), calls=%async_computation | async-start | bytes 1048576 | tf_op jit(solution)/shard_map/all_to_all | solution.py:468
  89.5 59.3 %all-gather.18.cloned.1.call-start = ((), (), s32[]{:S(2)}) async-start(), calls=%async_computation.8 | async-start | bytes 2621440 | tf_op jit(solution)/shard_map/all_gather | solution.py:480
  104.6 359.3 %reduce-scatter.6.cloned.1.call-start = ((), (), s32[]{:S(2)}) async-start(), calls=%async_computation.11 | async-start | bytes 2949120 | tf_op jit(solution)/shard_map/reduce_scatter | solution.py:534
  111.2 143.7 %collective-permute-start.22 = (bf16[1024,1024]{1,0:T(8,128)(2,1)}, bf16[1024,1024]{1,0:T(8,128)(2,1)}, u32[]{:S(2)}, u32[]{:S(2)}) collective-permute-start(bf16[1024,1024]{1,0:T(8,128)(2,1)} %all-gather.20.cloned.1.call-done.dy_ref.refs_7_), channel_id=1, source_target_pairs={{0,4},{4,0},{1,5},{5,1},{2,6},{6,2},{3,7},{7,3},{8,12},{12,8},{9,1... | collective-permute-start | bytes 6291464 | tf_op jit(solution)/shard_map/ppermute | solution.py:384
  148.8 106.1 %collective-permute-start.21 = (bf16[1024,1024]{1,0:T(8,128)(2,1)}, bf16[1024,1024]{1,0:T(8,128)(2,1)}, u32[]{:S(2)}, u32[]{:S(2)}) collective-permute-start(bf16[1024,1024]{1,0:T(8,128)(2,1)} %all-gather.18.cloned.1.call-done.n2_ref.refs_6_), channel_id=1, source_target_pairs={{0,4},{4,0},{1,5},{5,1},{2,6},{6,2},{3,7},{7,3},{8,12},{12,8},{9,1... | collective-permute-start | bytes 6291464 | tf_op jit(solution)/shard_map/ppermute | solution.py:384
  148.8 16.5 %collective-permute-start.12 = (bf16[2,256,512]{2,1,0:T(8,128)(2,1)S(1)}, bf16[2,256,512]{2,1,0:T(8,128)(2,1)S(1)}, u32[]{:S(2)}, u32[]{:S(2)}) collective-permute-start(bf16[2,256,512]{2,1,0:T(8,128)(2,1)S(1)} %get-tuple-element.60.refs_0_), channel_id=1, source_target_pairs={{0,1},{1,2},{2,3},{3,0},{4,5},{5,6},{6,7},{7,4},{8,9},{9,10},{10,1... | collective-permute-start | bytes 1572872 | tf_op jit(solution)/shard_map/ppermute | solution.py:381
  150.3 26.3 %collective-permute-start.15 = (bf16[2,256,512]{2,1,0:T(8,128)(2,1)S(1)}, bf16[2,256,512]{2,1,0:T(8,128)(2,1)S(1)}, u32[]{:S(2)}, u32[]{:S(2)}) collective-permute-start(bf16[2,256,512]{2,1,0:T(8,128)(2,1)S(1)} %get-tuple-element.61.refs_4_), channel_id=1, source_target_pairs={{0,1},{1,2},{2,3},{3,0},{4,5},{5,6},{6,7},{7,4},{8,9},{9,10},{10,1... | collective-permute-start | bytes 1572872 | tf_op jit(solution)/shard_map/ppermute | solution.py:381
  151.8 36.0 %collective-permute-start.18 = (bf16[2,128,1024]{2,1,0:T(8,128)(2,1)S(1)}, bf16[2,128,1024]{2,1,0:T(8,128)(2,1)S(1)}, u32[]{:S(2)}, u32[]{:S(2)}) collective-permute-start(bf16[2,128,1024]{2,1,0:T(8,128)(2,1)S(1)} %constant_dynamic-slice_fusion.14.refs_8_), channel_id=1, source_target_pairs={{0,1},{1,2},{2,3},{3,0},{4,5},{5,6},{6,7},{7,4},{8,9},{9,10},{10,1... | collective-permute-start | bytes 1572872 | tf_op jit(solution)/shard_map/ppermute | solution.py:381
  165.3 33.7 %collective-permute-start.13 = (bf16[2,256,512]{2,1,0:T(8,128)(2,1)S(1)}, bf16[2,256,512]{2,1,0:T(8,128)(2,1)S(1)}, u32[]{:S(2)}, u32[]{:S(2)}) collective-permute-start(bf16[2,256,512]{2,1,0:T(8,128)(2,1)S(1)} %collective-permute-done.12.refs_1_), channel_id=1, source_target_pairs={{0,1},{1,2},{2,3},{3,0},{4,5},{5,6},{6,7},{7,4},{8,9},{9,10},{10,1... | collective-permute-start | bytes 1572872 | tf_op jit(solution)/shard_map/ppermute | solution.py:381
  176.6 33.7 %collective-permute-start.16 = (bf16[2,256,512]{2,1,0:T(8,128)(2,1)S(1)}, bf16[2,256,512]{2,1,0:T(8,128)(2,1)S(1)}, u32[]{:S(2)}, u32[]{:S(2)}) collective-permute-start(bf16[2,256,512]{2,1,0:T(8,128)(2,1)S(1)} %collective-permute-done.15.refs_5_), channel_id=1, source_target_pairs={{0,1},{1,2},{2,3},{3,0},{4,5},{5,6},{6,7},{7,4},{8,9},{9,10},{10,1... | collective-permute-start | bytes 1572872 | tf_op jit(solution)/shard_map/ppermute | solution.py:381
  187.8 33.7 %collective-permute-start.19 = (bf16[2,128,1024]{2,1,0:T(8,128)(2,1)S(1)}, bf16[2,128,1024]{2,1,0:T(8,128)(2,1)S(1)}, u32[]{:S(2)}, u32[]{:S(2)}) collective-permute-start(bf16[2,128,1024]{2,1,0:T(8,128)(2,1)S(1)} %collective-permute-done.18.refs_9_), channel_id=1, source_target_pairs={{0,1},{1,2},{2,3},{3,0},{4,5},{5,6},{6,7},{7,4},{8,9},{9,10},{10,1... | collective-permute-start | bytes 1572872 | tf_op jit(solution)/shard_map/ppermute | solution.py:381
  199.1 33.8 %collective-permute-start.14 = (bf16[2,256,512]{2,1,0:T(8,128)(2,1)S(1)}, bf16[2,256,512]{2,1,0:T(8,128)(2,1)}, u32[]{:S(2)}, u32[]{:S(2)}) collective-permute-start(bf16[2,256,512]{2,1,0:T(8,128)(2,1)S(1)} %collective-permute-done.13.refs_2_), channel_id=1, source_target_pairs={{0,1},{1,2},{2,3},{3,0},{4,5},{5,6},{6,7},{7,4},{8,9},{9,10},{10,1... | collective-permute-start | bytes 1572872 | tf_op jit(solution)/shard_map/ppermute | solution.py:381
  210.3 33.8 %collective-permute-start.17 = (bf16[2,256,512]{2,1,0:T(8,128)(2,1)S(1)}, bf16[2,256,512]{2,1,0:T(8,128)(2,1)}, u32[]{:S(2)}, u32[]{:S(2)}) collective-permute-start(bf16[2,256,512]{2,1,0:T(8,128)(2,1)S(1)} %collective-permute-done.16.refs_6_), channel_id=1, source_target_pairs={{0,1},{1,2},{2,3},{3,0},{4,5},{5,6},{6,7},{7,4},{8,9},{9,10},{10,1... | collective-permute-start | bytes 1572872 | tf_op jit(solution)/shard_map/ppermute | solution.py:381
  221.5 33.4 %collective-permute-start.20 = (bf16[2,128,1024]{2,1,0:T(8,128)(2,1)S(1)}, bf16[2,128,1024]{2,1,0:T(8,128)(2,1)}, u32[]{:S(2)}, u32[]{:S(2)}) collective-permute-start(bf16[2,128,1024]{2,1,0:T(8,128)(2,1)S(1)} %collective-permute-done.19.refs_10_), channel_id=1, source_target_pairs={{0,1},{1,2},{2,3},{3,0},{4,5},{5,6},{6,7},{7,4},{8,9},{9,10},{10,1... | collective-permute-start | bytes 1572872 | tf_op jit(solution)/shard_map/ppermute | solution.py:381
  278.0 24.5 %collective-permute-start.24 = (bf16[1024,1152]{1,0:T(8,128)(2,1)}, bf16[1024,1152]{1,0:T(8,128)(2,1)S(1)}, u32[]{:S(2)}, u32[]{:S(2)}) collective-permute-start(bf16[1024,1152]{1,0:T(8,128)(2,1)} %get-tuple-element.66), channel_id=1, source_target_pairs={{0,4},{4,0},{1,5},{5,1},{2,6},{6,2},{3,7},{7,3},{8,12},{12,8},{9,1... | collective-permute-start | bytes 7077896 | tf_op jit(solution)/shard_map/ppermute | solution.py:384
  306.2 216.4 %all-gather.24.cloned.1.call-start = ((), (), s32[]{:S(2)}) async-start(), calls=%async_computation.14 | async-start | bytes 2621440 | tf_op jit(solution)/shard_map/all_gather | solution.py:587
  331.7 16.0 %collective-permute-start.29 = (bf16[2,256,512]{2,1,0:T(8,128)(2,1)S(1)}, bf16[2,256,512]{2,1,0:T(8,128)(2,1)S(1)}, u32[]{:S(2)}, u32[]{:S(2)}) collective-permute-start(bf16[2,256,512]{2,1,0:T(8,128)(2,1)S(1)} %slice_bitcast_fusion.2), channel_id=1, source_target_pairs={{0,1},{1,2},{2,3},{3,0},{4,5},{5,6},{6,7},{7,4},{8,9},{9,10},{10,1... | collective-permute-start | bytes 1572872 | tf_op jit(solution)/shard_map/ppermute | solution.py:381
  348.9 15.4 %collective-permute-start.30 = (bf16[2,256,512]{2,1,0:T(8,128)(2,1)S(1)}, bf16[2,256,512]{2,1,0:T(8,128)(2,1)S(1)}, u32[]{:S(2)}, u32[]{:S(2)}) collective-permute-start(bf16[2,256,512]{2,1,0:T(8,128)(2,1)S(1)} %fusion.16), channel_id=1, source_target_pairs={{0,1},{1,2},{2,3},{3,0},{4,5},{5,6},{6,7},{7,4},{8,9},{9,10},{10,1... | collective-permute-start | bytes 1572872 | tf_op jit(solution)/shard_map/ppermute | solution.py:381
  364.4 14.3 %collective-permute-start.31 = (bf16[2,256,512]{2,1,0:T(8,128)(2,1)S(1)}, bf16[2,256,512]{2,1,0:T(8,128)(2,1)S(1)}, u32[]{:S(2)}, u32[]{:S(2)}) collective-permute-start(bf16[2,256,512]{2,1,0:T(8,128)(2,1)S(1)} %fusion.15), channel_id=1, source_target_pairs={{0,1},{1,2},{2,3},{3,0},{4,5},{5,6},{6,7},{7,4},{8,9},{9,10},{10,1... | collective-permute-start | bytes 1572872 | tf_op jit(solution)/shard_map/ppermute | solution.py:381
  379.6 143.2 %all-gather.26.cloned.1.call-start = ((), (), s32[]{:S(2)}) async-start(), calls=%async_computation.15 | async-start | bytes 2621440 | tf_op jit(solution)/shard_map/all_gather | solution.py:587
  379.7 13.4 %collective-permute-start.33 = (bf16[2,256,512]{2,1,0:T(8,128)(2,1)S(1)}, bf16[2,256,512]{2,1,0:T(8,128)(2,1)S(1)}, u32[]{:S(2)}, u32[]{:S(2)}) collective-permute-start(bf16[2,256,512]{2,1,0:T(8,128)(2,1)S(1)} %slice_bitcast_fusion.1), channel_id=1, source_target_pairs={{0,1},{1,2},{2,3},{3,0},{4,5},{5,6},{6,7},{7,4},{8,9},{9,10},{10,1... | collective-permute-start | bytes 1572872 | tf_op jit(solution)/shard_map/ppermute | solution.py:381
  393.3 12.4 %collective-permute-start.34 = (bf16[2,256,512]{2,1,0:T(8,128)(2,1)S(1)}, bf16[2,256,512]{2,1,0:T(8,128)(2,1)S(1)}, u32[]{:S(2)}, u32[]{:S(2)}) collective-permute-start(bf16[2,256,512]{2,1,0:T(8,128)(2,1)S(1)} %fusion.13), channel_id=1, source_target_pairs={{0,1},{1,2},{2,3},{3,0},{4,5},{5,6},{6,7},{7,4},{8,9},{9,10},{10,1... | collective-permute-start | bytes 1572872 | tf_op jit(solution)/shard_map/ppermute | solution.py:381
  405.8 11.5 %collective-permute-start.35 = (bf16[2,256,512]{2,1,0:T(8,128)(2,1)S(1)}, bf16[2,256,512]{2,1,0:T(8,128)(2,1)S(1)}, u32[]{:S(2)}, u32[]{:S(2)}) collective-permute-start(bf16[2,256,512]{2,1,0:T(8,128)(2,1)S(1)} %fusion.12), channel_id=1, source_target_pairs={{0,1},{1,2},{2,3},{3,0},{4,5},{5,6},{6,7},{7,4},{8,9},{9,10},{10,1... | collective-permute-start | bytes 1572872 | tf_op jit(solution)/shard_map/ppermute | solution.py:381
  418.3 105.1 %all-gather.28.cloned.1.call-start = ((), (), s32[]{:S(2)}) async-start(), calls=%async_computation.16 | async-start | bytes 2621440 | tf_op jit(solution)/shard_map/all_gather | solution.py:587
  418.4 12.5 %collective-permute-start.37 = (bf16[2,128,1024]{2,1,0:T(8,128)(2,1)S(1)}, bf16[2,128,1024]{2,1,0:T(8,128)(2,1)S(1)}, u32[]{:S(2)}, u32[]{:S(2)}) collective-permute-start(bf16[2,128,1024]{2,1,0:T(8,128)(2,1)S(1)} %slice_bitcast_fusion), channel_id=1, source_target_pairs={{0,1},{1,2},{2,3},{3,0},{4,5},{5,6},{6,7},{7,4},{8,9},{9,10},{10,1... | collective-permute-start | bytes 1572872 | tf_op jit(solution)/shard_map/ppermute | solution.py:381
  431.2 13.6 %collective-permute-start.38 = (bf16[2,128,1024]{2,1,0:T(8,128)(2,1)S(1)}, bf16[2,128,1024]{2,1,0:T(8,128)(2,1)S(1)}, u32[]{:S(2)}, u32[]{:S(2)}) collective-permute-start(bf16[2,128,1024]{2,1,0:T(8,128)(2,1)S(1)} %fusion.10), channel_id=1, source_target_pairs={{0,1},{1,2},{2,3},{3,0},{4,5},{5,6},{6,7},{7,4},{8,9},{9,10},{10,1... | collective-permute-start | bytes 1572872 | tf_op jit(solution)/shard_map/ppermute | solution.py:381
  445.0 11.0 %collective-permute-start.39 = (bf16[2,128,1024]{2,1,0:T(8,128)(2,1)S(1)}, bf16[2,128,1024]{2,1,0:T(8,128)(2,1)S(1)}, u32[]{:S(2)}, u32[]{:S(2)}) collective-permute-start(bf16[2,128,1024]{2,1,0:T(8,128)(2,1)S(1)} %fusion.9), channel_id=1, source_target_pairs={{0,1},{1,2},{2,3},{3,0},{4,5},{5,6},{6,7},{7,4},{8,9},{9,10},{10,1... | collective-permute-start | bytes 1572872 | tf_op jit(solution)/shard_map/ppermute | solution.py:381
  457.0 71.6 %reduce-scatter.4.cloned.1.call-start = ((), (), s32[]{:S(2)}) async-start(), calls=%async_computation.10 | async-start | bytes 2621440 | tf_op jit(solution)/shard_map/reduce_scatter | solution.py:535
  470.4 18.5 %all-to-all-start.1 = ((bf16[4,256,256]{2,1,0:T(8,128)(2,1)}), bf16[4,256,256]{2,1,0:T(8,128)(2,1)S(1)}, u32[]{:S(2)}, u32[]{:S(2)}) async-start(bf16[4,256,256]{2,1,0:T(8,128)(2,1)} %get-tuple-element.72), calls=%async_computation.3 | async-start | bytes 1048576 | tf_op jit(solution)/shard_map/all_to_all | solution.py:610
  473.9 90.4 %reduce-scatter.8.cloned.1.call-start = ((), (), s32[]{:S(2)}) async-start(), calls=%async_computation.12 | async-start | bytes 2129920 | tf_op jit(solution)/shard_map/reduce_scatter | solution.py:653
  522.6 46.3 %collective-permute-start.32 = (bf16[4,2,256,512]{3,2,1,0:T(8,128)(2,1)}, bf16[4,2,256,512]{3,2,1,0:T(8,128)(2,1)}, u32[]{:S(2)}, u32[]{:S(2)}) collective-permute-start(bf16[4,2,256,512]{3,2,1,0:T(8,128)(2,1)} %bitcast.189), channel_id=1, source_target_pairs={{0,4},{4,0},{1,5},{5,1},{2,6},{6,2},{3,7},{7,3},{8,12},{12,8},{9,1... | collective-permute-start | bytes 6291464 | tf_op jit(solution)/shard_map/ppermute | solution.py:384
  522.8 70.5 %collective-permute-start.36 = (bf16[4,2,256,512]{3,2,1,0:T(8,128)(2,1)}, bf16[4,2,256,512]{3,2,1,0:T(8,128)(2,1)}, u32[]{:S(2)}, u32[]{:S(2)}) collective-permute-start(bf16[4,2,256,512]{3,2,1,0:T(8,128)(2,1)} %bitcast.191), channel_id=1, source_target_pairs={{0,4},{4,0},{1,5},{5,1},{2,6},{6,2},{3,7},{7,3},{8,12},{12,8},{9,1... | collective-permute-start | bytes 6291464 | tf_op jit(solution)/shard_map/ppermute | solution.py:384
  523.4 79.1 %collective-permute-start.40 = (bf16[4,2,128,1024]{3,2,1,0:T(8,128)(2,1)}, bf16[4,2,128,1024]{3,2,1,0:T(8,128)(2,1)}, u32[]{:S(2)}, u32[]{:S(2)}) collective-permute-start(bf16[4,2,128,1024]{3,2,1,0:T(8,128)(2,1)} %bitcast.193), channel_id=1, source_target_pairs={{0,4},{4,0},{1,5},{5,1},{2,6},{6,2},{3,7},{7,3},{8,12},{12,8},{9,1... | collective-permute-start | bytes 6291464 | tf_op jit(solution)/shard_map/ppermute | solution.py:384
  564.3 28.2 %all-to-all-start.2 = ((bf16[4,208,256]{2,1,0:T(8,128)(2,1)}), bf16[4,208,256]{2,1,0:T(8,128)(2,1)S(1)}, u32[]{:S(2)}, u32[]{:S(2)}) async-start(bf16[4,208,256]{2,1,0:T(8,128)(2,1)} %bitcast.212), calls=%async_computation.5 | async-start | bytes 851968 | tf_op jit(solution)/shard_map/all_to_all | solution.py:656
  568.9 59.2 %all-gather.22.cloned.1.call-start = ((), (), s32[]{:S(2)}) async-start(), calls=%async_computation.13 | async-start | bytes 1843200 | tf_op jit(solution)/shard_map/all_gather | solution.py:660
  574.6 21.4 %collective-permute-start.25 = (bf16[256,1024]{1,0:T(8,128)(2,1)}, bf16[256,1024]{1,0:T(8,128)(2,1)}, u32[]{:S(2)}, u32[]{:S(2)}) collective-permute-start(bf16[256,1024]{1,0:T(8,128)(2,1)} %slice_bitcast_fusion.3), channel_id=1, source_target_pairs={{0,1},{1,2},{2,3},{3,0},{4,5},{5,6},{6,7},{7,4},{8,9},{9,10},{10,1... | collective-permute-start | bytes 1572872 | tf_op jit(solution)/shard_map/ppermute | solution.py:381
  597.4 14.7 %collective-permute-start.26 = (bf16[256,1024]{1,0:T(8,128)(2,1)S(1)}, bf16[256,1024]{1,0:T(8,128)(2,1)S(1)}, u32[]{:S(2)}, u32[]{:S(2)}) collective-permute-start(bf16[256,1024]{1,0:T(8,128)(2,1)S(1)} %fusion.19), channel_id=1, source_target_pairs={{0,1},{1,2},{2,3},{3,0},{4,5},{5,6},{6,7},{7,4},{8,9},{9,10},{10,1... | collective-permute-start | bytes 1572872 | tf_op jit(solution)/shard_map/ppermute | solution.py:381
  612.3 14.0 %collective-permute-start.27 = (bf16[256,1024]{1,0:T(8,128)(2,1)S(1)}, bf16[256,1024]{1,0:T(8,128)(2,1)S(1)}, u32[]{:S(2)}, u32[]{:S(2)}) collective-permute-start(bf16[256,1024]{1,0:T(8,128)(2,1)S(1)} %fusion.18), channel_id=1, source_target_pairs={{0,1},{1,2},{2,3},{3,0},{4,5},{5,6},{6,7},{7,4},{8,9},{9,10},{10,1... | collective-permute-start | bytes 1572872 | tf_op jit(solution)/shard_map/ppermute | solution.py:381
  (44 other events, 1080.2 us)
Sparse Core Ops, SparseCore 0:
  21.3 22.2 all-gather.13
  46.1 27.8 all-gather.15
  75.8 35.3 all-gather.19
  113.5 35.2 all-gather.17
  306.3 35.7 reduce-scatter.5
  379.7 32.5 all-gather.23
  418.4 32.6 all-gather.25
  457.2 32.6 all-gather.27
  493.4 35.1 reduce-scatter.3
  532.3 31.9 reduce-scatter.7
  593.4 23.1 all-gather.21

commit v3 on v2

--- a/solution.py
+++ b/solution.py
@@ -76,26 +76,35 @@
     return pl.ds(pl.multiple_of(index * size, size), size)
 
 
+def peer(place_ref, c, j):
+    return lax.bitwise_xor(place_ref[2], jnp.int32(j)) * 2 + lax.bitwise_xor(place_ref[3], jnp.int32(c))
+
+
 def front_kernel(
     block, heads, kv_heads, parts, place_ref, *refs
 ):
     chunks = refs[:parts]
-    (gain_ref, wrel_ref, cos_ref, sin_ref, segc_ref, segr_ref,
+    (gain_ref, mine_ref, mate_ref, cos_ref, sin_ref, segc_ref, segr_ref,
      x_ref, w_ref, normed_ref, q_ref, k_ref, v_ref, att_ref, lse_ref, out_s, sems) = refs[parts:]
     seq = x_ref.shape[0]
     blocks = seq // block
     group = heads // kv_heads
     qw, kw = heads * HEAD, kv_heads * HEAD
     z = place_ref[0]
-    slab = wrel_ref.shape[1]
+    slab = w_ref.shape[0] // parts
+    part = slab // (2 * mine_ref.shape[0])
     copies = []
     for i in range(parts):
         at = chunk_of(ring_chunk(z, i, parts), block)
         copies.append(pltpu.make_async_copy(chunks[i], x_ref.at[at, :], sems.at[i]))
     for copy in copies:
         copy.start()
-    for i in range(parts):
-        w_ref[chunk_of(ring_chunk(z, i, parts), slab), :] = wrel_ref[i]
+    for c, piece_ref in enumerate((mine_ref, mate_ref)):
+        for j in range(piece_ref.shape[0]):
+            at = peer(place_ref, c, j) * part
+            for i in range(parts):
+                start = pl.multiple_of(ring_chunk(z, i, parts) * slab + at, part)
+                w_ref[pl.ds(start, part), :] = piece_ref[j, i, :part, :]
     for copy in copies:
         copy.wait()
 
@@ -201,8 +210,22 @@
     return e * (1.0 / jnp.sum(e, axis=-1, keepdims=True))
 
 
-def mid_kernel(place_ref, x_ref, att_ref, ow_ref, gain_ref, router_ref, mask_ref, hidden_ref, normed_ref, gates_ref):
+def mid_kernel(
+    place_ref, x_ref, att_ref, mine_ref, mate_ref, gain_ref, router_ref, mask_ref,
+    hidden_ref, normed_ref, gates_ref, ow_ref,
+):
     parts, width = ow_ref.shape[0], ow_ref.shape[2]
+    share = ow_ref.shape[1] // (2 * mine_ref.shape[0])
+    fold = mine_ref.shape[3] // width
+    lines = share // fold
+    skip = mine_ref.shape[2] - lines
+    for c, piece_ref in enumerate((mine_ref, mate_ref)):
+        for j in range(piece_ref.shape[0]):
+            at = peer(place_ref, c, j) * share
+            for k in range(parts):
+                for f in range(fold):
+                    start = pl.multiple_of(at + f * lines, lines)
+                    ow_ref[k, pl.ds(start, lines), :] = piece_ref[j, k, skip:, f * width : (f + 1) * width]
     depth = att_ref.shape[2]
     for j in range(parts):
         cols = chunk_of(ring_chunk(place_ref[0], j, parts), width)
@@ -217,19 +240,20 @@
 
 
 def mid_back_kernel(
-    place_ref, hidden_ref, nb_ref, dy_ref, gates_ref, normed_ref, router_ref, gain_ref, ow_ref, att_ref,
+    place_ref, hidden_ref, nb0_ref, nb1_ref, nb2_ref, nb3_ref, dy_ref, gates_ref, normed_ref, router_ref, gain_ref, ow_ref, att_ref,
     hg_ref, ag_ref, owg_ref, fg_ref, rg_ref, aog_s,
 ):
     gates = gates_ref[...]
     width_all = hidden_ref.shape[1]
-    mix = nb_ref[:, width_all:].astype(F32)
+    nb = sum(ref[...].astype(F32) for ref in (nb1_ref, nb2_ref, nb3_ref)) + nb0_ref[...].astype(F32)
+    mix = nb[:, width_all:]
     mix = mix + pltpu.roll(mix, LANES - MIX_LOW, 1)
     lg = gates * (mix - jnp.sum(gates * mix, axis=-1, keepdims=True))
     high, low = split_hi_lo(lg)
     normed = normed_ref[...]
     rg_ref[...] = dot_tn(high, normed) + dot_tn(low, normed)
     router = router_ref[...]
-    ng = nb_ref[:, :width_all].astype(F32) + dot_nt(high, router) + dot_nt(low, router)
+    ng = nb[:, :width_all] + dot_nt(high, router) + dot_nt(low, router)
     hidden = hidden_ref[...]
     inv = inverse_rms(hidden)
     scaled = hidden * inv
@@ -252,68 +276,69 @@
             owg_ref[j, rows, :] = dot_tn(att_ref[i], aog_s[:, j * width : (j + 1) * width]).astype(BF16)
 
 
-def expert_kernel(
-    experts, parts, place_ref, n2_ref, dy_ref, mask_ref, router_ref, *refs
-):
-    weights = refs[: 3 * parts]
-    moe_ref, nb_ref, g_ref, inner_ref, gg_ref, ug_ref = refs[3 * parts : 3 * parts + 6]
-    wg_s, wu_s, wd_s, sems = refs[3 * parts + 6 :]
-    z = place_ref[0]
-    first = place_ref[1]
+def expert_kernel(parts, e, place_ref, n2_ref, dyx_ref, router_ref, w_ref, *refs):
+    previous = refs[:2] if e else ()
+    moe_ref, nb_ref, g_ref, inner_ref, gg_ref, ug_ref, wg_s, wu_s, wd_s, sems = refs[len(previous) :]
+    width, ff = wg_s.shape
+    slab, ff_slab = width // parts, ff // parts
 
     @pl.when(pl.program_id(0) == 0)
     def load():
         copies = []
-        for m, target in enumerate((wg_s, wu_s, wd_s)):
-            for k in range(parts):
-                source = weights[m * parts + k]
-                size = source.shape[1]
-                at = chunk_of(ring_chunk(z, k, parts), size)
-                copies.append(pltpu.make_async_copy(source, target.at[:, at, :], sems.at[m * parts + k]))
+
+        def move(start, count, target):
+            copies.append(pltpu.make_async_copy(w_ref.at[start : start + count, :], target, sems.at[len(copies)]))
+
+        for k in range(parts):
+            start = k * 3 * slab
+            move(start, slab, wg_s.at[k * slab : (k + 1) * slab, :])
+            move(start + slab, slab, wu_s.at[k * slab : (k + 1) * slab, :])
+            for c in range(width // ff):
+                at = start + 2 * slab + c * ff_slab
+                move(at, ff_slab, wd_s.at[k * ff_slab : (k + 1) * ff_slab, c * ff : (c + 1) * ff])
         for copy in copies:
             copy.start()
         for copy in copies:
             copy.wait()
 
     x = n2_ref[...]
-    dy = dy_ref[...].astype(F32)
-    gates = softmax_gates(dot(x, router_ref[...]), mask_ref[...])
+    dy = dyx_ref[:, :width].astype(F32)
+    gates = softmax_gates(dot(x, router_ref[...]), dyx_ref[:, width:].astype(F32))
     lane = lax.broadcasted_iota(jnp.int32, gates.shape, 1)
-    moe = nb = mix_out = None
-    for e in range(experts):
-        g = jnp.sum(jnp.where(lane == first + e, gates, 0.0), axis=-1, keepdims=True)
-        ga = dot(x, wg_s[e])
-        ua = dot(x, wu_s[e])
-        sg = jax.nn.sigmoid(ga)
-        act = ga * sg
-        inner = (act * ua).astype(BF16)
-        inner_ref[e] = inner
-        eo = dot(inner, wd_s[e]).astype(BF16).astype(F32)
-        mix = jnp.sum(dy * eo, axis=-1, keepdims=True)
-        part = g * eo
-        moe = part if moe is None else moe + part
-        high, low = split_hi_lo(mix)
-        row = jnp.where(lane == first + e, high.astype(F32), 0.0)
-        row = row + jnp.where(lane == MIX_LOW + first + e, low.astype(F32), 0.0)
-        mix_out = row if mix_out is None else mix_out + row
-        g_ref[...] = jnp.where(lane == e, g, g_ref[...] if e else 0.0)
-        ig = dot_nt((g * dy).astype(BF16), wd_s[e])
-        gg = (ig * ua * sg * (1.0 + ga * (1.0 - sg))).astype(BF16)
-        ug = (ig * act).astype(BF16)
-        gg_ref[e] = gg
-        ug_ref[e] = ug
-        back = dot_nt(gg, wg_s[e]) + dot_nt(ug, wu_s[e])
-        nb = back if nb is None else nb + back
+    at = place_ref[1] + e
+    g = jnp.sum(jnp.where(lane == at, gates, 0.0), axis=-1, keepdims=True)
+    ga = dot(x, wg_s[...])
+    ua = dot(x, wu_s[...])
+    sg = jax.nn.sigmoid(ga)
+    act = ga * sg
+    inner = (act * ua).astype(BF16)
+    inner_ref[...] = inner
+    eo = dot(inner, wd_s[...]).astype(BF16).astype(F32)
+    moe = g * eo
+    high, low = split_hi_lo(jnp.sum(dy * eo, axis=-1, keepdims=True))
+    mix = jnp.where(lane == at, high.astype(F32), 0.0) + jnp.where(lane == MIX_LOW + at, low.astype(F32), 0.0)
+    g_ref[...] = jnp.where(lane == 0, g, 0.0)
+    ig = dot_nt((g * dy).astype(BF16), wd_s[...])
+    gg = (ig * ua * sg * (1.0 + ga * (1.0 - sg))).astype(BF16)
+    ug = (ig * act).astype(BF16)
+    gg_ref[...] = gg
+    ug_ref[...] = ug
+    nb = dot_nt(gg, wg_s[...]) + dot_nt(ug, wu_s[...])
+    if e:
+        moe = moe + previous[0][...].astype(F32)
+        nb = nb + previous[1][:, :width].astype(F32)
+        mix = mix + previous[1][:, width:].astype(F32)
     moe_ref[...] = moe.astype(BF16)
-    width = n2_ref.shape[1]
     nb_ref[:, :width] = nb.astype(BF16)
-    nb_ref[:, width:] = mix_out.astype(BF16)
-
-
-def expert_grad_kernel(experts, parts, half, place_ref, *refs):
+    nb_ref[:, width:] = mix.astype(BF16)
+
+
+def expert_grad_kernel(parts, half, *refs):
     halves = (refs[:6], refs[6:12])
-    dg_ref, du_ref, dd_ref, g_s, u_s, d_s = refs[12:]
-    e, step = pl.program_id(0), pl.program_id(1)
+    out_ref, g_s, u_s, d_s = refs[12:]
+    step = pl.program_id(0)
+    width, ff = g_s.shape
+    slab, ff_slab = width // parts, ff // parts
 
     @pl.when(step == 0)
     def clear():
@@ -321,25 +346,41 @@
         u_s[...] = jnp.zeros_like(u_s)
         d_s[...] = jnp.zeros_like(d_s)
 
-    def add(n2_ref, dy_ref, g_ref, inner_ref, gg_ref, ug_ref):
+    def add(n2_ref, dyx_ref, g_ref, inner_ref, gg_ref, ug_ref):
         x = n2_ref[...]
-        lane = lax.broadcasted_iota(jnp.int32, g_ref.shape, 1)
-        g = jnp.sum(jnp.where(lane == e, g_ref[...], 0.0), axis=-1, keepdims=True)
-        og = (g * dy_ref[...].astype(F32)).astype(BF16)
-        g_s[...] += dot_tn(x, gg_ref[0])
-        u_s[...] += dot_tn(x, ug_ref[0])
-        d_s[...] += dot_tn(inner_ref[0], og)
+        g = jnp.sum(g_ref[...], axis=-1, keepdims=True)
+        og = (g * dyx_ref[:, :width].astype(F32)).astype(BF16)
+        g_s[...] += dot_tn(x, gg_ref[...])
+        u_s[...] += dot_tn(x, ug_ref[...])
+        d_s[...] += dot_tn(inner_ref[...], og)
 
     pl.when(step < half)(lambda: add(*halves[0]))
     pl.when(step >= half)(lambda: add(*halves[1]))
 
-    @pl.when(step == pl.num_programs(1) - 1)
+    @pl.when(step == pl.num_programs(0) - 1)
     def store():
-        z = place_ref[0]
-        for total, out in ((g_s, dg_ref), (u_s, du_ref), (d_s, dd_ref)):
-            size = out.shape[2]
-            for k in range(parts):
-                out[k, 0] = total[chunk_of(ring_chunk(z, k, parts), size), :].astype(BF16)
+        for k in range(parts):
+            start = k * 3 * slab
+            out_ref[start : start + slab, :] = g_s[k * slab : (k + 1) * slab, :].astype(BF16)
+            out_ref[start + slab : start + 2 * slab, :] = u_s[k * slab : (k + 1) * slab, :].astype(BF16)
+            for c in range(width // ff):
+                at = start + 2 * slab + c * ff_slab
+                out_ref[at : at + ff_slab, :] = d_s[k * ff_slab : (k + 1) * ff_slab, c * ff : (c + 1) * ff].astype(BF16)
+
+
+def share_kernel(count, place_ref, *refs):
+    gate_ref, up_ref, down_ref = refs[-3:]
+    _, _, slab, ff = gate_ref.shape
+    ff_slab, width = down_ref.shape[2:]
+    for i in range(count):
+
+        @pl.when(pl.program_id(0) == i)
+        def copy(piece_ref=refs[i]):
+            gate_ref[0, 0] = piece_ref[:slab, :].astype(F32)
+            up_ref[0, 0] = piece_ref[slab : 2 * slab, :].astype(F32)
+            for c in range(width // ff):
+                at = 2 * slab + c * ff_slab
+                down_ref[0, 0, :, c * ff : (c + 1) * ff] = piece_ref[at : at + ff_slab, :].astype(F32)
 
 
 def sds(shape, dtype):
@@ -370,9 +411,9 @@
     ff = gate_weight.shape[2]
     z = lax.axis_index("shard").astype(jnp.int32)
     core = lax.axis_index("cr").astype(jnp.int32)
-    r = lax.axis_index("yx").astype(jnp.int32) * 2 + core
-    place = jnp.stack([z, r * own])
-    plane = ("yx", "cr")
+    chip = lax.axis_index("yx").astype(jnp.int32)
+    r = chip * 2 + core
+    place = jnp.stack([z, r * own, chip, core])
     smem = pl.BlockSpec(memory_space=pltpu.SMEM)
     vmem = pl.BlockSpec(memory_space=pltpu.VMEM)
     hbm = pl.BlockSpec(memory_space=pl.ANY)
@@ -383,12 +424,25 @@
     def swap(value):
         return lax.ppermute(value, "cr", [(0, 1), (1, 0)])
 
+    def flip(value, j):
+        return lax.ppermute(value, "yx", [(i, i ^ j) for i in range(yx)])
+
     def pick(value, index, axis):
         return lax.dynamic_index_in_dim(value, index, axis, keepdims=False)
 
     def absolute(parts):
         stacked = jnp.stack(parts)
         return jnp.stack([pick(stacked, lax.rem(z - j + n, n), 0) for j in range(n)])
+
+    def around(value):
+        return [value] + [flip(value, j) for j in range(1, yx)]
+
+    def plus(one, other):
+        return (one.astype(F32) + other.astype(F32)).astype(BF16)
+
+    chunks = [tokens]
+    for _ in range(n - 1):
+        chunks.append(shift(chunks[-1]))
 
     pack = jnp.concatenate(
         [attn_gain[None], ffn_gain[None], segment_ids.astype(BF16)[None], router_weight.T], axis=0
@@ -408,27 +462,23 @@
         ],
         axis=2,
     )
-    w_rel = jnp.stack(
-        [pick(by_dest, z, 1)] + [shift(pick(by_dest, lax.rem(z + k, n), 1), k) for k in range(1, n)]
-    )
-    w_rel = lax.all_gather(w_rel, plane, axis=1, tiled=True)
     ow_rows = out_weight.shape[0] // ep
+    fold = cols // slab
     ow_mine = lax.dynamic_slice_in_dim(out_weight, r * ow_rows, ow_rows, axis=0)
-    ow = jnp.stack([ow_mine] + [shift(ow_mine, k) for k in range(1, n)])
-    ow = lax.all_gather(ow, plane, axis=1, tiled=True)
-
-    chunks = [tokens]
-    for _ in range(n - 1):
-        chunks.append(shift(chunks[-1]))
+    ow_mine = ow_mine.reshape(fold, ow_rows // fold, slab).transpose(1, 0, 2).reshape(ow_rows // fold, cols)
+
+    def piece(k):
+        return jnp.concatenate([pick(by_dest, lax.rem(z + k, n), 1), ow_mine], axis=0)
+
+    dense_mine = jnp.stack([piece(0)] + [shift(piece(k), k) for k in range(1, n)])
+    dense_mine = jnp.stack(around(dense_mine))
+    dense_mate = swap(dense_mine)
 
     ids = jnp.arange(experts, dtype=jnp.int32)
     routed = jnp.any(routes[:, :, None] == ids[None, None, :], axis=1)
     mask_own = jnp.pad(routed.astype(F32), ((0, 0), (0, LANES - experts)))
-    mask_all = lax.all_gather(routed.T.astype(BF16), plane, axis=0, tiled=False).reshape(yx, 2, experts, rows)
-
-    def mask_of(which):
-        mask = pick(mask_all, which, 1).transpose(0, 2, 1).reshape(yx * rows, experts).astype(F32)
-        return jnp.pad(mask, ((0, 0), (0, LANES - experts)))
+    dyx_mine = jnp.concatenate(around(jnp.concatenate([cotangent, mask_own.astype(BF16)], axis=1)), axis=0)
+    dyx_mate = swap(dyx_mine)
 
     positions = jnp.arange(seq, dtype=jnp.int32).astype(F32)
     frequency = ROPE_BASE ** (-jnp.arange(HEAD // 2, dtype=F32) / (HEAD // 2))
@@ -437,18 +487,18 @@
     cosine = jnp.concatenate([cosine] * 4, axis=1)
     sine = jnp.concatenate([-sine, sine] * 2, axis=1)
 
-    mine = [lax.dynamic_slice_in_dim(w, r * own, own, axis=0) for w in (gate_weight, up_weight, down_weight)]
-    mine, chunks = lax.optimization_barrier((mine, chunks))
-    slabs = []
-    for w in mine:
-        slabs.append(w)
-        for _ in range(n - 1):
-            w = shift(w)
-            slabs.append(w)
+    folds = width // ff
+    packed = []
+    for e in range(own):
+        gate, up, down = (pick(w, r * own + e, 0) for w in (gate_weight, up_weight, down_weight))
+        down = [down[:, c * ff : (c + 1) * ff] for c in range(folds)]
+        packed.append(jnp.concatenate([gate, up] + down, axis=0))
+    packed, chunks = lax.optimization_barrier((packed, chunks))
+    weights = [lax.all_gather(w, "shard", axis=0, tiled=True) for w in packed]
 
     x_all, w_qkv, normed, q, k, v, att, lse = pl.pallas_call(
         functools.partial(front_kernel, rows, heads, kv_heads, n),
-        in_specs=[smem] + [hbm] * n + [vmem] * 6,
+        in_specs=[smem] + [hbm] * n + [vmem] * 7,
         out_shape=(
             sds((seq, width), BF16),
             sds((width, cols), BF16),
@@ -463,137 +513,122 @@
         compiler_params=params(),
         cost_estimate=cost(2 * seq * width * cols, 60e6),
         name="front",
-    )(place, *chunks, gain1, w_rel, cosine, sine, seg_col, seg_row)
+    )(place, *chunks, gain1, dense_mine, dense_mate, cosine, sine, seg_col, seg_row)
 
     att = lax.all_to_all(att.reshape(n, rows, qw), "shard", 0, 0)
-    hidden, normed2, gates_own = pl.pallas_call(
+    hidden, normed2, gates_own, ow = pl.pallas_call(
         mid_kernel,
-        in_specs=[smem] + [vmem] * 6,
-        out_shape=(sds((rows, width), F32), sds((rows, width), BF16), sds((rows, LANES), F32)),
+        in_specs=[smem] + [vmem] * 7,
+        out_shape=(
+            sds((rows, width), F32),
+            sds((rows, width), BF16),
+            sds((rows, LANES), F32),
+            sds((n, ep * ow_rows, slab), BF16),
+        ),
         compiler_params=params(),
         cost_estimate=cost(2 * rows * width * width, 14e6),
         name="mid",
-    )(place, tokens, att, ow, gain2, router, mask_own)
-
-    dy_mine = lax.all_gather(cotangent, "yx", axis=0, tiled=True)
-    dy_mate = swap(dy_mine)
-    n2_mine = lax.all_gather(normed2, "yx", axis=0, tiled=True)
+    )(place, tokens, att, dense_mine, dense_mate, gain2, router, mask_own)
+
+    n2_mine = jnp.concatenate(around(normed2), axis=0)
     n2_mate = swap(n2_mine)
 
     total = yx * rows
     block = min(512, total)
     steps = total // block
 
-    def run_experts(n2, dy, mask):
+    def by_block(size):
+        return pl.BlockSpec((block, size), lambda i: (i, 0))
+
+    def run_expert(e, n2, dyx, previous):
         return pl.pallas_call(
-            functools.partial(expert_kernel, own, n),
+            functools.partial(expert_kernel, n, e),
             grid=(steps,),
             in_specs=[
                 smem,
-                pl.BlockSpec((block, width), lambda i: (i, 0)),
-                pl.BlockSpec((block, width), lambda i: (i, 0)),
-                pl.BlockSpec((block, LANES), lambda i: (i, 0)),
+                by_block(width),
+                by_block(width + LANES),
                 pl.BlockSpec((width, LANES), lambda i: (0, 0)),
+                hbm,
             ]
-            + [hbm] * (3 * n),
+            + ([by_block(width), by_block(width + LANES)] if e else []),
             out_specs=(
-                pl.BlockSpec((block, width), lambda i: (i, 0)),
-                pl.BlockSpec((block, width + LANES), lambda i: (i, 0)),
-                pl.BlockSpec((block, LANES), lambda i: (i, 0)),
-                pl.BlockSpec((own, block, ff), lambda i: (0, i, 0)),
-                pl.BlockSpec((own, block, ff), lambda i: (0, i, 0)),
-                pl.BlockSpec((own, block, ff), lambda i: (0, i, 0)),
+                by_block(width),
+                by_block(width + LANES),
+                by_block(LANES),
+                by_block(ff),
+                by_block(ff),
+                by_block(ff),
             ),
             out_shape=(
                 sds((total, width), BF16),
                 sds((total, width + LANES), BF16),
                 sds((total, LANES), F32),
-                sds((own, total, ff), BF16),
-                sds((own, total, ff), BF16),
-                sds((own, total, ff), BF16),
+                sds((total, ff), BF16),
+                sds((total, ff), BF16),
+                sds((total, ff), BF16),
             ),
             scratch_shapes=[
-                pltpu.VMEM((own, width, ff), BF16),
-                pltpu.VMEM((own, width, ff), BF16),
-                pltpu.VMEM((own, ff, width), BF16),
-                pltpu.SemaphoreType.DMA((3 * n,)),
+                pltpu.VMEM((width, ff), BF16),
+                pltpu.VMEM((width, ff), BF16),
+                pltpu.VMEM((ff, width), BF16),
+                pltpu.SemaphoreType.DMA(((2 + folds) * n,)),
             ],
             compiler_params=params(),
-            cost_estimate=cost(12 * own * total * width * ff, 70e6),
-            name="experts",
-        )(place, n2, dy, mask, router, *slabs)
-
-    moe_mate, nb_mate, *saved_mate = run_experts(n2_mate, dy_mate, mask_of(1 - core))
-    nb_got = swap(nb_mate)
-    moe_got = swap(moe_mate)
-    moe, nb, *saved_mine = run_experts(n2_mine, dy_mine, mask_of(core))
-
-    def plus(one, other):
-        return (one.astype(F32) + other.astype(F32)).astype(BF16)
-
-    nb_own = lax.psum_scatter(plus(nb, nb_got), "yx", scatter_dimension=0, tiled=True)
-    moe_own = lax.psum_scatter(plus(moe, moe_got), "yx", scatter_dimension=0, tiled=True)
-
-    ff_slab = ff // n
+            cost_estimate=cost(12 * total * width * ff, 36e6),
+            name="expert",
+        )(place, n2, dyx, router, weights[e], *previous)
 
     def half_specs(at):
-        return [
-            pl.BlockSpec((block, width), lambda e, i: (at(i), 0)),
-            pl.BlockSpec((block, width), lambda e, i: (at(i), 0)),
-            pl.BlockSpec((block, LANES), lambda e, i: (at(i), 0)),
-            pl.BlockSpec((1, block, ff), lambda e, i: (e, at(i), 0)),
-            pl.BlockSpec((1, block, ff), lambda e, i: (e, at(i), 0)),
-            pl.BlockSpec((1, block, ff), lambda e, i: (e, at(i), 0)),
-        ]
-
-    dg, du, dd = pl.pallas_call(
-        functools.partial(expert_grad_kernel, own, n, steps),
-        grid=(own, 2 * steps),
-        in_specs=[smem]
-        + half_specs(lambda i: jnp.minimum(i, steps - 1))
-        + half_specs(lambda i: jnp.maximum(i - steps, 0)),
-        out_specs=(
-            pl.BlockSpec((n, 1, slab, ff), lambda e, i: (0, e, 0, 0)),
-            pl.BlockSpec((n, 1, slab, ff), lambda e, i: (0, e, 0, 0)),
-            pl.BlockSpec((n, 1, ff_slab, width), lambda e, i: (0, e, 0, 0)),
-        ),
-        out_shape=(
-            sds((n, own, slab, ff), BF16),
-            sds((n, own, slab, ff), BF16),
-            sds((n, own, ff_slab, width), BF16),
-        ),
-        scratch_shapes=[
-            pltpu.VMEM((width, ff), F32),
-            pltpu.VMEM((width, ff), F32),
-            pltpu.VMEM((ff, width), F32),
-        ],
-        compiler_params=params(),
-        cost_estimate=cost(6 * own * 2 * total * width * ff, 80e6),
-        name="expert_grads",
-    )(place, n2_mate, dy_mate, *saved_mate, n2_mine, dy_mine, *saved_mine)
-
-    def ring_sum(parts):
-        part = parts[1]
-        for step in list(range(2, n)) + [0]:
-            part = shift(part).astype(F32) + parts[step].astype(F32)
-            if step:
-                part = part.astype(BF16)
-        return part
-
-    def expert_sum(parts):
-        part = ring_sum(parts)
+        sizes = (width, width + LANES, LANES, ff, ff, ff)
+        return [pl.BlockSpec((block, size), lambda i: (at(i), 0)) for size in sizes]
+
+    def weight_grads(mate, mine):
+        return pl.pallas_call(
+            functools.partial(expert_grad_kernel, n, steps),
+            grid=(2 * steps,),
+            in_specs=half_specs(lambda i: jnp.minimum(i, steps - 1))
+            + half_specs(lambda i: jnp.maximum(i - steps, 0)),
+            out_specs=pl.BlockSpec((3 * width, ff), lambda i: (0, 0)),
+            out_shape=sds((3 * width, ff), BF16),
+            scratch_shapes=[
+                pltpu.VMEM((width, ff), F32),
+                pltpu.VMEM((width, ff), F32),
+                pltpu.VMEM((ff, width), F32),
+            ],
+            compiler_params=params(),
+            cost_estimate=cost(12 * total * width * ff, 40e6),
+            name="expert_grads",
+        )(n2_mate, dyx_mate, *mate, n2_mine, dyx_mine, *mine)
+
+    def spread(value):
+        return [value[j * rows : (j + 1) * rows] for j in range(yx)]
+
+    def exchanged(blocks):
+        return [blocks[0]] + [flip(blocks[j], j) for j in range(1, yx)]
+
+    previous_mate = previous_mine = ()
+    owned = []
+    for e in range(own):
+        *previous_mate, g_mate, in_mate, gg_mate, ug_mate = run_expert(e, n2_mate, dyx_mate, previous_mate)
+        if e == own - 1:
+            moe_got, nb_got = swap(previous_mate[0]), swap(previous_mate[1])
+        *previous_mine, g_mine, in_mine, gg_mine, ug_mine = run_expert(e, n2_mine, dyx_mine, previous_mine)
+        grads = weight_grads((g_mate, in_mate, gg_mate, ug_mate), (g_mine, in_mine, gg_mine, ug_mine))
+        if e < own - 1:
+            grads, weights[e + 1] = lax.optimization_barrier((grads, weights[e + 1]))
+        else:
+            nb_parts = exchanged(spread(plus(previous_mine[1], nb_got)))
+            moe_sum = plus(previous_mine[0], moe_got)
+            nb_parts, moe_sum, grads = lax.optimization_barrier((nb_parts, moe_sum, grads))
+        grads = lax.psum_scatter(grads, "shard", scatter_dimension=0, tiled=True)
         if hi > 1:
-            part = lax.psum(part, "hi")
-        mine = lax.all_gather(part.astype(BF16), "yx", axis=0, tiled=False)
-        mate = swap(mine)
-        even, odd = jnp.where(core == 0, mine, mate), jnp.where(core == 0, mate, mine)
-        return jnp.stack([even, odd], axis=1).reshape((experts,) + part.shape[1:]).astype(F32)
-
-    gate_grad, up_grad, down_grad = expert_sum(dg), expert_sum(du), expert_sum(dd)
+            grads = lax.psum(grads.astype(F32), "hi").astype(BF16)
+        owned.append(grads)
 
     hidden_grad, att_grad, ow_grad, ffn_grad, router_grad = pl.pallas_call(
         mid_back_kernel,
-        in_specs=[smem] + [vmem] * 9,
+        in_specs=[smem] + [vmem] * 12,
         out_shape=(
             sds((rows, width), F32),
             sds((n, rows, qw), BF16),
@@ -605,7 +640,7 @@
         compiler_params=params(),
         cost_estimate=cost(4 * rows * width * width, 20e6),
         name="mid_back",
-    )(place, hidden, nb_own, cotangent, gates_own, normed2, router, gain2, ow, att)
+    )(place, hidden, *nb_parts, cotangent, gates_own, normed2, router, gain2, ow, att)
 
     att_grad = lax.all_to_all(att_grad, "shard", 0, 0).reshape(seq, qw)
     ng, qkv_grad, gain_grad = pl.pallas_call(
@@ -625,14 +660,51 @@
         name="back",
     )(place, q, k, v, att_grad, lse, seg_col, seg_row, x_all, normed, w_qkv, cosine, sine)
 
-    ng_own = ring_sum(ng)
-    output = (hidden + moe_own.astype(F32)).astype(BF16)
-
+    part = ng[1]
+    for step in list(range(2, n)) + [0]:
+        part = shift(part).astype(F32) + ng[step].astype(F32)
+        if step:
+            part = part.astype(BF16)
     x = tokens.astype(F32)
     inv = inverse_rms(x)
     scaled = x * inv
-    w1 = ng_own * gain1
+    w1 = part * gain1
     input_grad = hidden_grad + inv * (w1 - scaled * jnp.mean(w1 * scaled, axis=-1, keepdims=True))
+
+    moe_parts = exchanged(spread(moe_sum))
+    output = (hidden + sum(p.astype(F32) for p in moe_parts)).astype(BF16)
+
+    shared = ()
+    for e in range(own):
+        mine = around(owned[e])
+        pieces = [p for one in mine for p in (one, swap(one))]
+
+        def out_index(j, place_ref, e=e):
+            return (peer(place_ref, j % 2, j // 2), e, 0, 0)
+
+        shared = pl.pallas_call(
+            functools.partial(share_kernel, ep),
+            grid_spec=pltpu.PrefetchScalarGridSpec(
+                num_scalar_prefetch=1,
+                grid=(ep,),
+                in_specs=[pl.BlockSpec((3 * slab, ff), lambda j, place_ref: (0, 0))] * ep + [hbm] * len(shared),
+                out_specs=(
+                    pl.BlockSpec((1, 1, slab, ff), out_index),
+                    pl.BlockSpec((1, 1, slab, ff), out_index),
+                    pl.BlockSpec((1, 1, ff // n, width), out_index),
+                ),
+            ),
+            out_shape=(
+                sds((ep, own, slab, ff), F32),
+                sds((ep, own, slab, ff), F32),
+                sds((ep, own, ff // n, width), F32),
+            ),
+            input_output_aliases={1 + ep + i: i for i in range(len(shared))},
+            compiler_params=params(),
+            cost_estimate=cost(0, 20e6),
+            name="share",
+        )(place, *pieces, *shared)
+    gate_grad, up_grad, down_grad = (g.reshape((experts,) + g.shape[2:]) for g in shared)
 
     kvw = 2 * kw
     small = jnp.concatenate([gain_grad, ffn_grad, router_grad[:experts]], axis=0)
@@ -649,15 +721,18 @@
     dense = jnp.concatenate(pieces, axis=2)
     dense = dense.reshape(n, yx, 2, dense.shape[2], wide).transpose(2, 1, 0, 3, 4)
     dense = plus(pick(dense, core, 0), swap(pick(dense, 1 - core, 0)))
-    piece = dense.shape[1:]
-    dense = lax.psum_scatter(dense.reshape(-1, wide), "yx", scatter_dimension=0, tiled=True).reshape(piece)
+    dense = exchanged([pick(dense, lax.bitwise_xor(chip, jnp.int32(j)), 0) for j in range(yx)])
+    dense = sum(p.astype(F32) for p in dense)
     if hi > 1:
-        dense = lax.psum(dense.astype(F32), "hi").astype(BF16)
-    dense = lax.all_to_all(dense, "shard", 0, 0)
+        dense = lax.psum(dense, "hi")
+    dense = dense.astype(BF16)
+    dense = [pick(dense, z, 0)] + [shift(pick(dense, lax.rem(z + k, n), 0), k) for k in range(1, n)]
     cut = ow_rows + small_rows
-    summed = jnp.sum(dense[:, :cut].astype(F32), axis=0).astype(BF16)
-    kept = dense[:, cut:].reshape(n * 2 * part_rows, wide)
-    full = lax.all_gather(jnp.concatenate([summed, kept], axis=0), plane, axis=0, tiled=False)
+    summed = sum(p[:cut].astype(F32) for p in dense).astype(BF16)
+    kept = absolute([p[cut:] for p in dense]).reshape(n * 2 * part_rows, wide)
+    mine = jnp.stack(around(jnp.concatenate([summed, kept], axis=0)))
+    both = jnp.stack([mine, swap(mine)], axis=1).reshape((ep,) + mine.shape[1:])
+    full = jnp.stack([pick(both, lax.bitwise_xor(r, jnp.int32(i)), 0) for i in range(ep)])
     ow_full = full[:, :ow_rows, :slab].reshape(-1, slab).astype(F32)
     small_full = full[:, ow_rows:cut, :slab].reshape(-1, slab).astype(F32)
     kept = full[:, cut:].reshape(ep, n, 2, part_rows, wide)

time: 654 us -> 566 us (0.87)
  waiting for transfers between devices: 383 us -> 239 us
  starting transfers between devices: 34.4 us -> 78.6 us
  Pallas kernels: 121 us -> 156 us
  blocking collectives: 9.36 us -> 0 us
  local copies, waits for them, and re-layouts: 37.5 us -> 30.1 us
    ppermute x33 -> x15, waiting for transfers between devices: 254 us -> 102 us  [shift(): return lax.ppermute(value, 'shard', [(i, (i + k) % n) for i in range(n)])]
    ppermute x0 -> x27, waiting for transfers between devices: none -> 114 us  [flip(): return lax.ppermute(value, 'yx', [(i, i ^ j) for i in range(yx)])]
    all_gather x8 -> x2, waiting for transfers between devices: 44.2 us -> 0.01 us  [per_device(): weights = [lax.all_gather(w, 'shard', axis=0, tiled=True) for w in packed]]
    reduce_scatter x3 -> x2, waiting for transfers between devices: 38.7 us -> 0.02 us  [per_device(): grads = lax.psum_scatter(grads, 'shard', scatter_dimension=0, tiled=True)]
    pallas_call x5 -> x10, Pallas kernels: 81.1 us -> 115 us  [the longest x4 57.4 us: run_expert(): pl.pallas_call(functools.partial(expert_kernel, n, e), grid=(steps,), in_...]
    ppermute x0 -> x27, starting transfers between devices: none -> 31.1 us  [flip(): return lax.ppermute(value, 'yx', [(i, i ^ j) for i in range(yx)])]
    ppermute x33 -> x15, starting transfers between devices: 21.5 us -> 37.7 us  [shift(): return lax.ppermute(value, 'shard', [(i, (i + k) % n) for i in range(n)])]
    all_to_all x1 -> x0, waiting for transfers between devices: 15.9 us -> none  [per_device(): dense = lax.all_to_all(dense, 'shard', 0, 0)]
  transfers between devices with their start and end apart: 55 -> 63, of which waited for: 38 -> 24; matrix products, arithmetic and copies ran while one was open for 10% -> 11% of each run, Pallas kernels for 15% -> 24%
where the time goes in v3:
time: 566 us; the launch traced here: 556 us
  waiting for transfers between devices  239 us (42%)
  Pallas kernels  156 us (28%)
  starting transfers between devices  78.6 us (14%)
  other arithmetic  37.3 us (7%)
  local copies, waits for them, and re-layouts  30.1 us (5%)
  between operations  15 us (3%)
    ppermute x27, waiting for transfers between devices, flip(): return lax.ppermute(value, 'yx', [(i, i ^ j) for i in range(yx)])  114 us
    ppermute x15, waiting for transfers between devices, shift(): return lax.ppermute(value, 'shard', [(i, (i + k) % n) for i in range(n)])  102 us
    pallas_call x4, Pallas kernels, run_expert(): pl.pallas_call(functools.partial(expert_kernel, n, e), grid=(steps,), in_...  57.4 us
    ppermute x15, starting transfers between devices, shift(): return lax.ppermute(value, 'shard', [(i, (i + k) % n) for i in range(n)])  37.7 us
    ppermute x27, starting transfers between devices, flip(): return lax.ppermute(value, 'yx', [(i, i ^ j) for i in range(yx)])  31.1 us
    pallas_call x2, Pallas kernels, weight_grads(): pl.pallas_call(functools.partial(expert_grad_kernel, n, steps), grid=(2 *...  27.8 us
    pallas_call x1, Pallas kernels, per_device(): pl.pallas_call(functools.partial(back_kernel, rows, heads, kv_heads), in_...  22.3 us
    pallas_call x1, Pallas kernels, per_device(): pl.pallas_call(functools.partial(front_kernel, rows, heads, kv_heads, n),...  18.8 us
  transfers between devices with their start and end apart: 63, of which 24 were waited for; matrix products, arithmetic and copies ran while one was open for 11% of the time, Pallas kernels for 24%

profile of v3, /device:TPU:0, one launch (start us, length us, event | category | flops | bytes accessed | tf_op | source)
XLA Modules:
  0.0 556.2 jit_solution(18398575892869028412)
XLA Ops:
  7.2 3.1 collective-permute-start
  10.3 14.2 %collective-permute-done.refs_1_ = bf16[256,1024]{1,0:T(8,128)(2,1)S(1)} collective-permute-done((bf16[256,1024]{1,0:T(8,128)(2,1)}, bf16[256,1024]{1,0:T(8,128)(2,1)S(1)}, u32[]{:S(2)}, u32[]{:S(2)}) %collective-permute-start) | collective-permute-done | bytes 524320 | tf_op jit(solution)/shard_map/ppermute | solution.py:422
  25.9 13.5 %collective-permute-done.1.refs_2_ = bf16[256,1024]{1,0:T(8,128)(2,1)S(1)} collective-permute-done((bf16[256,1024]{1,0:T(8,128)(2,1)S(1)}, bf16[256,1024]{1,0:T(8,128)(2,1)S(1)}, u32[]{:S(2)}, u32[]{:S(2)}) %collective-permute-start.1) | collective-permute-done | bytes 524320 | tf_op jit(solution)/shard_map/ppermute | solution.py:422
  42.6 10.8 %collective-permute-done.2.refs_3_ = bf16[256,1024]{1,0:T(8,128)(2,1)S(1)} collective-permute-done((bf16[256,1024]{1,0:T(8,128)(2,1)S(1)}, bf16[256,1024]{1,0:T(8,128)(2,1)S(1)}, u32[]{:S(2)}, u32[]{:S(2)}) %collective-permute-start.2) | collective-permute-done | bytes 524320 | tf_op jit(solution)/shard_map/ppermute | solution.py:422
  55.9 3.7 collective-permute-start.8
  59.7 2.7 collective-permute-done.6
  62.4 5.1 collective-permute-done.7
  71.2 5.2 collective-permute-done.10
  76.4 4.8 collective-permute-done.11
  81.6 4.8 collective-permute-start.4
  87.5 2.7 collective-permute-start.5
  98.3 18.8 %front.1 = (bf16[1024,1024]{1,0:T(8,128)(2,1)}, bf16[1024,512]{1,0:T(8,128)(2,1)}, bf16[1024,1024]{1,0:T(8,128)(2,1)}, bf16[4,1024,64]{2,1,0:T(8,128)(2,1)}, bf1...) custom-call(s32[4]{0:T(128)} %pad_add_fusion.place_ref, ...), custom_call_target="tpu_custom_call" | custom-call | flops 1073741824 | bytes 60000000 | tf_op jit(solution)/shard_map/front/pallas_call | solution.py:499
  117.2 3.5 all-to-all-start
  126.8 8.4 %all-to-all-done.att_ref = bf16[4,256,256]{2,1,0:T(8,128)(2,1)S(1)} async-done(((bf16[4,256,256]{2,1,0:T(8,128)(2,1)}), bf16[4,256,256]{2,1,0:T(8,128)(2,1)S(1)}, u32[]{:S(2)}, u32[]{:S(2)}) %all-to-all-start) | async-done | bytes 524320 | tf_op jit(solution)/shard_map/all_to_all | solution.py:518
  136.0 4.5 mid.1
  143.9 16.3 %collective-permute-done.17 = bf16[256,1152]{1,0:T(8,128)(2,1)S(1)} collective-permute-done((bf16[256,1152]{1,0:T(8,128)(2,1)}, bf16[256,1152]{1,0:T(8,128)(2,1)S(1)}, u32[]{:S(2)}, u32[]{:S(2)}) %collective-permute-start.17) | collective-permute-done | bytes 589856 | tf_op jit(solution)/shard_map/ppermute | solution.py:428
  163.8 7.6 %collective-permute-done.13 = bf16[256,1024]{1,0:T(8,128)(2,1)S(1)} collective-permute-done((bf16[256,1024]{1,0:T(8,128)(2,1)}, bf16[256,1024]{1,0:T(8,128)(2,1)S(1)}, u32[]{:S(2)}, u32[]{:S(2)}) %collective-permute-start.13) | collective-permute-done | bytes 524320 | tf_op jit(solution)/shard_map/ppermute | solution.py:428
  174.0 13.9 %expert.5 = (bf16[1024,1024]{1,0:T(8,128)(2,1)}, bf16[1024,1152]{1,0:T(8,128)(2,1)}, f32[1024,128]{1,0:T(8,128)}, bf16[1024,512]{1,0:T(8,128)(2,1)}, bf16[1024,5...) custom-call(s32[4]{0:T(128)} %pad_add_fusion.place_ref, bf16[1024,1024]{1,0:T(8,128)(2,1)} %constant_dynamic-update-slice_fusion.3.n2_ref.refs_6_, ...), custom_call_target="tpu_custom_call" | custom-call | flops 6442450944 | bytes 36000000 | tf_op jit(solution)/shard_map/expert/pallas_call | solution.py:544
  187.9 13.7 %expert.4 = (bf16[1024,1024]{1,0:T(8,128)(2,1)}, bf16[1024,1152]{1,0:T(8,128)(2,1)}, f32[1024,128]{1,0:T(8,128)}, bf16[1024,512]{1,0:T(8,128)(2,1)}, bf16[1024,5...) custom-call(s32[4]{0:T(128)} %pad_add_fusion.place_ref, bf16[1024,1024]{1,0:T(8,128)(2,1)} %collective-permute-done.19.n2_ref.refs_0_, ...), custom_call_target="tpu_custom_call" | custom-call | flops 6442450944 | bytes 36000000 | tf_op jit(solution)/shard_map/expert/pallas_call | solution.py:544
  201.5 13.6 %expert_grads.2 = bf16[3072,512]{1,0:T(8,128)(2,1)} custom-call(bf16[1024,1024]{1,0:T(8,128)(2,1)} %collective-permute-done.19.n2_ref.refs_0_, bf16[1024,1152]{1,0:T(8,128)(2,1)} %collective-permute-done.20.dyx_ref.refs_1_, f32[1024,128]{1,0:T(8,128)} %get-tuple-element.84.refs_2_, bf16[1024,512]{1,0:T(8,128)(2,1)} %get-tuple-element.85.refs_3_, ...), custom_call_target="tpu_custom_call" | custom-call | flops 6442450944 | bytes 40000000 | tf_op jit(solution)/shard_map/expert_grads/pallas_call | solution.py:587
  215.1 15.1 %expert.7 = (bf16[1024,1024]{1,0:T(8,128)(2,1)}, bf16[1024,1152]{1,0:T(8,128)(2,1)}, f32[1024,128]{1,0:T(8,128)}, bf16[1024,512]{1,0:T(8,128)(2,1)}, bf16[1024,5...) custom-call(s32[4]{0:T(128)} %pad_add_fusion.place_ref, bf16[1024,1024]{1,0:T(8,128)(2,1)} %collective-permute-done.19.n2_ref.refs_0_, ...), custom_call_target="tpu_custom_call" | custom-call | flops 6442450944 | bytes 36000000 | tf_op jit(solution)/shard_map/expert/pallas_call | solution.py:544
  230.9 14.8 %expert.6 = (bf16[1024,1024]{1,0:T(8,128)(2,1)}, bf16[1024,1152]{1,0:T(8,128)(2,1)}, f32[1024,128]{1,0:T(8,128)}, bf16[1024,512]{1,0:T(8,128)(2,1)}, bf16[1024,5...) custom-call(s32[4]{0:T(128)} %pad_add_fusion.place_ref, bf16[1024,1024]{1,0:T(8,128)(2,1)} %constant_dynamic-update-slice_fusion.3.n2_ref.refs_6_, ...), custom_call_target="tpu_custom_call" | custom-call | flops 6442450944 | bytes 36000000 | tf_op jit(solution)/shard_map/expert/pallas_call | solution.py:544
  245.7 2.2 add_convert_fusion
  252.9 14.2 %expert_grads.3 = bf16[3072,512]{1,0:T(8,128)(2,1)} custom-call(bf16[1024,1024]{1,0:T(8,128)(2,1)} %collective-permute-done.19.n2_ref.refs_0_, bf16[1024,1152]{1,0:T(8,128)(2,1)} %collective-permute-done.20.dyx_ref.refs_1_, f32[1024,128]{1,0:T(8,128)} %get-tuple-element.102.refs_2_, bf16[1024,512]{1,0:T(8,128)(2,1)} %get-tuple-element.103.refs_3_, ...), custom_call_target="tpu_custom_call" | custom-call | flops 6442450944 | bytes 40000000 | tf_op jit(solution)/shard_map/expert_grads/pallas_call | solution.py:587
  267.1 3.9 add_convert_fusion.1
  271.0 7.8 %collective-permute-done.23.nb2_ref = bf16[256,1152]{1,0:T(8,128)(2,1)S(1)} collective-permute-done((bf16[256,1152]{1,0:T(8,128)(2,1)}, bf16[256,1152]{1,0:T(8,128)(2,1)S(1)}, u32[]{:S(2)}, u32[]{:S(2)}) %collective-permute-start.23) | collective-permute-done | bytes 589856 | tf_op jit(solution)/shard_map/ppermute | solution.py:428
  279.7 7.2 %mid_back.1 = (f32[256,1024]{1,0:T(8,128)}, bf16[4,256,256]{2,1,0:T(8,128)(2,1)}, bf16[4,1024,256]{2,1,0:T(8,128)(2,1)}, f32[1,1024]{1,0:T(1,128)}, f32[128,1024]{1,0:T(8,128)}) custom-call(s32[4]{0:T(128)} %pad_add_fusion.place_ref, f32[256,1024]{1,0:T(8,128)} %get-tuple-element.81.hidden_ref, bf16[256,1152]{1,0:T(8,128)(2,1)} %get-tuple-element.111.nb0_ref, ...), custom_call_target="tpu_custom_call" | custom-call | flops 1073741824 | bytes 20000000 | tf_op jit(solution)/shard_map/mid_back/pallas_call | solution.py:629
  286.9 4.8 all-to-all-start.1
  293.2 13.3 %all-to-all-done.1 = bf16[4,256,256]{2,1,0:T(8,128)(2,1)S(1)} async-done(((bf16[4,256,256]{2,1,0:T(8,128)(2,1)}), bf16[4,256,256]{2,1,0:T(8,128)(2,1)S(1)}, u32[]{:S(2)}, u32[]{:S(2)}) %all-to-all-start.1) | async-done | bytes 524320 | tf_op jit(solution)/shard_map/all_to_all | solution.py:645
  307.3 22.3 %back.1 = (bf16[4,256,1024]{2,1,0:T(8,128)(2,1)}, bf16[1024,512]{1,0:T(8,128)(2,1)}, f32[1,1024]{1,0:T(1,128)}) custom-call(s32[4]{0:T(128)} %pad_add_fusion.place_ref, bf16[4,1024,64]{2,1,0:T(8,128)(2,1)} %get-tuple-element.118.q_ref, bf16[2,1024,64]{2,1,0:T(8,128)(2,1)} %get-tuple-element.119.k_ref, bf16[2,1024,64]{2,1,0:T(8,128)(2,1)} %get-tuple-element.120.v_ref, ...), custom_call_target="tpu_custom_call" | custom-call | flops 2147483648 | bytes 80000000 | tf_op jit(solution)/shard_map/back/pallas_call | solution.py:646
  347.2 17.2 %collective-permute-done.29 = bf16[256,1024]{1,0:T(8,128)(2,1)S(1)} collective-permute-done((bf16[256,1024]{1,0:T(8,128)(2,1)S(1)}, bf16[256,1024]{1,0:T(8,128)(2,1)S(1)}, u32[]{:S(2)}, u32[]{:S(2)}) %collective-permute-start.29) | collective-permute-done | bytes 524320 | tf_op jit(solution)/shard_map/ppermute | solution.py:422
  364.8 2.3 collective-permute-start.27
  367.4 3.3 collective-permute-start.36
  370.7 30.7 %collective-permute-done.36 = bf16[208,256]{1,0:T(8,128)(2,1)S(1)} collective-permute-done((bf16[208,256]{1,0:T(8,128)(2,1)S(1)}, bf16[208,256]{1,0:T(8,128)(2,1)S(1)}, u32[]{:S(2)}, u32[]{:S(2)}) %collective-permute-start.36) | collective-permute-done | bytes 106528 | tf_op jit(solution)/shard_map/ppermute | solution.py:422
  401.4 13.7 %collective-permute-start.38 = (bf16[208,256]{1,0:T(8,128)(2,1)S(1)}, bf16[208,256]{1,0:T(8,128)(2,1)S(1)}, u32[]{:S(2)}, u32[]{:S(2)}) collective-permute-start(bf16[208,256]{1,0:T(8,128)(2,1)S(1)} %get-tuple-element.163), channel_id=1, source_target_pairs={{0,3},{1,0},{2,1},{3,2},{4,7},{5,4},{6,5},{7,6},{8,11},{9,8},{10,9... | collective-permute-start | bytes 319496 | tf_op jit(solution)/shard_map/ppermute | solution.py:422
  415.1 3.6 collective-permute-done.38
  420.7 3.7 collective-permute-done.37
  427.4 3.0 collective-permute-done.40
  430.4 3.1 collective-permute-start.31
  434.4 5.8 %collective-permute-done.41 = bf16[400,256]{1,0:T(8,128)(2,1)S(1)} collective-permute-done((bf16[400,256]{1,0:T(8,128)(2,1)S(1)}, bf16[400,256]{1,0:T(8,128)(2,1)S(1)}, u32[]{:S(2)}, u32[]{:S(2)}) %collective-permute-start.41) | collective-permute-done | bytes 204832 | tf_op jit(solution)/shard_map/ppermute | solution.py:428
  443.0 2.9 add_convert_fusion.2
  451.1 2.8 fusion.6
  455.5 13.7 %collective-permute-done.55.refs_6_ = bf16[768,512]{1,0:T(8,128)(2,1)} collective-permute-done((bf16[768,512]{1,0:T(8,128)(2,1)}, bf16[768,512]{1,0:T(8,128)(2,1)}, u32[]{:S(2)}, u32[]{:S(2)}) %collective-permute-start.55) | collective-permute-done | bytes 786464 | tf_op jit(solution)/shard_map/ppermute | solution.py:428
  469.2 16.3 %collective-permute-done.53.refs_4_ = bf16[768,512]{1,0:T(8,128)(2,1)} collective-permute-done((bf16[768,512]{1,0:T(8,128)(2,1)}, bf16[768,512]{1,0:T(8,128)(2,1)}, u32[]{:S(2)}, u32[]{:S(2)}) %collective-permute-start.53) | collective-permute-done | bytes 786464 | tf_op jit(solution)/shard_map/ppermute | solution.py:428
  490.4 16.8 %collective-permute-done.48.refs_6_ = bf16[768,512]{1,0:T(8,128)(2,1)} collective-permute-done((bf16[768,512]{1,0:T(8,128)(2,1)}, bf16[768,512]{1,0:T(8,128)(2,1)}, u32[]{:S(2)}, u32[]{:S(2)}) %collective-permute-start.48) | collective-permute-done | bytes 786464 | tf_op jit(solution)/shard_map/ppermute | solution.py:428
  507.2 16.0 %collective-permute-done.46.refs_4_ = bf16[768,512]{1,0:T(8,128)(2,1)} collective-permute-done((bf16[768,512]{1,0:T(8,128)(2,1)}, bf16[768,512]{1,0:T(8,128)(2,1)}, u32[]{:S(2)}, u32[]{:S(2)}) %collective-permute-start.46) | collective-permute-done | bytes 786464 | tf_op jit(solution)/shard_map/ppermute | solution.py:428
  531.2 9.0 %share.2 = (f32[8,2,256,512]{3,2,1,0:T(8,128)}, f32[8,2,256,512]{3,2,1,0:T(8,128)}, f32[8,2,128,1024]{3,2,1,0:T(8,128)}) custom-call(s32[4]{0:T(128)} %pad_add_fusion.place_ref, bf16[768,512]{1,0:T(8,128)(2,1)} %reduce-scatter.5.cloned.1.call-done.refs_0_, bf16[768,512]{1,0:T(8,128)(2,1)} %collective-permute-done.50.refs_1_, ...), custom_call_target="tpu_custom_call" | custom-call | bytes 20000000 | tf_op jit(solution)/shard_map/share/pallas_call | solution.py:685
  540.3 9.2 %share.3 = (f32[8,2,256,512]{3,2,1,0:T(8,128)}, f32[8,2,256,512]{3,2,1,0:T(8,128)}, f32[8,2,128,1024]{3,2,1,0:T(8,128)}) custom-call(s32[4]{0:T(128)} %pad_add_fusion.place_ref, bf16[768,512]{1,0:T(8,128)(2,1)} %reduce-scatter.3.cloned.1.call-done.refs_0_, ...), custom_call_target="tpu_custom_call", output_to_operand_aliasing={{0}: (9, {}), {1}: (10, {}), {2}: (11, {})} | custom-call | bytes 20000000 | tf_op jit(solution)/shard_map/share/pallas_call | solution.py:685
  (267 shorter events, 91.3 us)
Async XLA Ops:
  7.2 166.8 %all-gather.3.cloned.1.call-start = ((), (), s32[]{:S(2)}) async-start(), calls=%async_computation.4 | async-start | bytes 3932160 | tf_op jit(solution)/shard_map/all_gather | solution.py:497
  7.2 17.2 %collective-permute-start = (bf16[256,1024]{1,0:T(8,128)(2,1)}, bf16[256,1024]{1,0:T(8,128)(2,1)S(1)}, u32[]{:S(2)}, u32[]{:S(2)}) collective-permute-start(bf16[256,1024]{1,0:T(8,128)(2,1)} %x_ref.1), channel_id=1, source_target_pairs={{0,1},{1,2},{2,3},{3,0},{4,5},{5,6},{6,7},{7,4},{8,9},{9,10},{10,1... | collective-permute-start | bytes 1572872 | tf_op jit(solution)/shard_map/ppermute | solution.py:422
  24.5 14.9 %collective-permute-start.1 = (bf16[256,1024]{1,0:T(8,128)(2,1)S(1)}, bf16[256,1024]{1,0:T(8,128)(2,1)S(1)}, u32[]{:S(2)}, u32[]{:S(2)}) collective-permute-start(bf16[256,1024]{1,0:T(8,128)(2,1)S(1)} %collective-permute-done.refs_1_), channel_id=1, source_target_pairs={{0,1},{1,2},{2,3},{3,0},{4,5},{5,6},{6,7},{7,4},{8,9},{9,10},{10,1... | collective-permute-start | bytes 1572872 | tf_op jit(solution)/shard_map/ppermute | solution.py:422
  39.4 14.0 %collective-permute-start.2 = (bf16[256,1024]{1,0:T(8,128)(2,1)S(1)}, bf16[256,1024]{1,0:T(8,128)(2,1)S(1)}, u32[]{:S(2)}, u32[]{:S(2)}) collective-permute-start(bf16[256,1024]{1,0:T(8,128)(2,1)S(1)} %collective-permute-done.1.refs_2_), channel_id=1, source_target_pairs={{0,1},{1,2},{2,3},{3,0},{4,5},{5,6},{6,7},{7,4},{8,9},{9,10},{10,1... | collective-permute-start | bytes 1572872 | tf_op jit(solution)/shard_map/ppermute | solution.py:422
  81.4 15.8 %collective-permute-start.12 = (bf16[4,4,96,512]{3,2,1,0:T(8,128)(2,1)S(1)}, bf16[4,4,96,512]{3,2,1,0:T(8,128)(2,1)S(1)}, u32[]{:S(2)}, u32[]{:S(2)}) collective-permute-start(bf16[4,4,96,512]{3,2,1,0:T(8,128)(2,1)S(1)} %pad_maximum_fusion.3.refs_5_.mine_ref), channel_id=1, source_target_pairs={{0,4},{4,0},{1,5},{5,1},{2,6},{6,2},{3,7},{7,3},{8,12},{12,8},{9,1... | collective-permute-start | bytes 4718600 | tf_op jit(solution)/shard_map/ppermute | solution.py:425
  81.6 13.9 %collective-permute-start.4 = (bf16[19,256]{1,0:T(8,128)(2,1)S(1)}, bf16[19,256]{1,0:T(8,128)(2,1)S(1)}, u32[]{:S(2)}, u32[]{:S(2)}) collective-permute-start(bf16[19,256]{1,0:T(8,128)(2,1)S(1)} %get-tuple-element.197), channel_id=1, source_target_pairs={{0,2},{1,3},{2,0},{3,1},{4,6},{5,7},{6,4},{7,5},{8,10},{9,11},{10,... | collective-permute-start | bytes 29192 | tf_op jit(solution)/shard_map/ppermute | solution.py:422
  117.2 18.0 %all-to-all-start = ((bf16[4,256,256]{2,1,0:T(8,128)(2,1)}), bf16[4,256,256]{2,1,0:T(8,128)(2,1)S(1)}, u32[]{:S(2)}, u32[]{:S(2)}) async-start(bf16[4,256,256]{2,1,0:T(8,128)(2,1)} %bitcast.199), calls=%async_computation | async-start | bytes 1048576 | tf_op jit(solution)/shard_map/all_to_all | solution.py:518
  120.6 94.4 %all-gather.5.cloned.1.call-start = ((), (), s32[]{:S(2)}) async-start(), calls=%async_computation.5 | async-start | bytes 3932160 | tf_op jit(solution)/shard_map/all_gather | solution.py:497
  121.6 20.2 %collective-permute-start.18 = (bf16[256,1152]{1,0:T(8,128)(2,1)}, bf16[256,1152]{1,0:T(8,128)(2,1)S(1)}, u32[]{:S(2)}, u32[]{:S(2)}) collective-permute-start(bf16[256,1152]{1,0:T(8,128)(2,1)} %pad_maximum_fusion.7), channel_id=1, source_target_pairs={{0,24},{8,16},{16,8},{24,0},{1,25},{9,17},{17,9},{25,1},{2,26},{10... | collective-permute-start | bytes 1769480 | tf_op jit(solution)/shard_map/ppermute | solution.py:428
  122.1 38.2 %collective-permute-start.17 = (bf16[256,1152]{1,0:T(8,128)(2,1)}, bf16[256,1152]{1,0:T(8,128)(2,1)S(1)}, u32[]{:S(2)}, u32[]{:S(2)}) collective-permute-start(bf16[256,1152]{1,0:T(8,128)(2,1)} %pad_maximum_fusion.7), channel_id=1, source_target_pairs={{0,16},{8,24},{16,0},{24,8},{1,17},{9,25},{17,1},{25,9},{2,18},{10... | collective-permute-start | bytes 1769480 | tf_op jit(solution)/shard_map/ppermute | solution.py:428
  123.1 38.0 %collective-permute-start.16 = (bf16[256,1152]{1,0:T(8,128)(2,1)}, bf16[256,1152]{1,0:T(8,128)(2,1)}, u32[]{:S(2)}, u32[]{:S(2)}) collective-permute-start(bf16[256,1152]{1,0:T(8,128)(2,1)} %pad_maximum_fusion.7), channel_id=1, source_target_pairs={{0,8},{8,0},{16,24},{24,16},{1,9},{9,1},{17,25},{25,17},{2,10},{10... | collective-permute-start | bytes 1769480 | tf_op jit(solution)/shard_map/ppermute | solution.py:428
  125.2 322.4 %reduce-scatter.5.cloned.1.call-start = ((), (), s32[]{:S(2)}) async-start(), calls=%async_computation.7 | async-start | bytes 3932160 | tf_op jit(solution)/shard_map/reduce_scatter | solution.py:624
  140.4 32.7 %collective-permute-start.15 = (bf16[256,1024]{1,0:T(8,128)(2,1)}, bf16[256,1024]{1,0:T(8,128)(2,1)S(1)}, u32[]{:S(2)}, u32[]{:S(2)}) collective-permute-start(bf16[256,1024]{1,0:T(8,128)(2,1)} %get-tuple-element.82.normed_ref), channel_id=1, source_target_pairs={{0,24},{8,16},{16,8},{24,0},{1,25},{9,17},{17,9},{25,1},{2,26},{10... | collective-permute-start | bytes 1572872 | tf_op jit(solution)/shard_map/ppermute | solution.py:428
  141.2 31.1 %collective-permute-start.14 = (bf16[256,1024]{1,0:T(8,128)(2,1)}, bf16[256,1024]{1,0:T(8,128)(2,1)S(1)}, u32[]{:S(2)}, u32[]{:S(2)}) collective-permute-start(bf16[256,1024]{1,0:T(8,128)(2,1)} %get-tuple-element.82.normed_ref), channel_id=1, source_target_pairs={{0,16},{8,24},{16,0},{24,8},{1,17},{9,25},{17,1},{25,9},{2,18},{10... | collective-permute-start | bytes 1572872 | tf_op jit(solution)/shard_map/ppermute | solution.py:428
  141.9 29.5 %collective-permute-start.13 = (bf16[256,1024]{1,0:T(8,128)(2,1)}, bf16[256,1024]{1,0:T(8,128)(2,1)S(1)}, u32[]{:S(2)}, u32[]{:S(2)}) collective-permute-start(bf16[256,1024]{1,0:T(8,128)(2,1)} %get-tuple-element.82.normed_ref), channel_id=1, source_target_pairs={{0,8},{8,0},{16,24},{24,16},{1,9},{9,1},{17,25},{25,17},{2,10},{10... | collective-permute-start | bytes 1572872 | tf_op jit(solution)/shard_map/ppermute | solution.py:428
  162.7 25.1 %collective-permute-start.20 = (bf16[1024,1152]{1,0:T(8,128)(2,1)S(1)}, bf16[1024,1152]{1,0:T(8,128)(2,1)}, u32[]{:S(2)}, u32[]{:S(2)}) collective-permute-start(bf16[1024,1152]{1,0:T(8,128)(2,1)S(1)} %pad_maximum_fusion.1.dyx_ref.refs_7_), channel_id=1, source_target_pairs={{0,4},{4,0},{1,5},{5,1},{2,6},{6,2},{3,7},{7,3},{8,12},{12,8},{9,1... | collective-permute-start | bytes 7077896 | tf_op jit(solution)/shard_map/ppermute | solution.py:425
  174.0 13.9 %collective-permute-start.19 = (bf16[1024,1024]{1,0:T(8,128)(2,1)}, bf16[1024,1024]{1,0:T(8,128)(2,1)}, u32[]{:S(2)}, u32[]{:S(2)}) collective-permute-start(bf16[1024,1024]{1,0:T(8,128)(2,1)} %constant_dynamic-update-slice_fusion.3.n2_ref.refs_6_), channel_id=1, source_target_pairs={{0,4},{4,0},{1,5},{5,1},{2,6},{6,2},{3,7},{7,3},{8,12},{12,8},{9,1... | collective-permute-start | bytes 6291464 | tf_op jit(solution)/shard_map/ppermute | solution.py:425
  230.2 15.5 %collective-permute-start.21 = (bf16[1024,1152]{1,0:T(8,128)(2,1)}, bf16[1024,1152]{1,0:T(8,128)(2,1)S(1)}, u32[]{:S(2)}, u32[]{:S(2)}) collective-permute-start(bf16[1024,1152]{1,0:T(8,128)(2,1)} %get-tuple-element.99), channel_id=1, source_target_pairs={{0,4},{4,0},{1,5},{5,1},{2,6},{6,2},{3,7},{7,3},{8,12},{12,8},{9,1... | collective-permute-start | bytes 7077896 | tf_op jit(solution)/shard_map/ppermute | solution.py:425
  230.8 36.3 %collective-permute-start.25 = (bf16[1024,1024]{1,0:T(8,128)(2,1)}, bf16[1024,1024]{1,0:T(8,128)(2,1)}, u32[]{:S(2)}, u32[]{:S(2)}) collective-permute-start(bf16[1024,1024]{1,0:T(8,128)(2,1)} %get-tuple-element.101), channel_id=1, source_target_pairs={{0,4},{4,0},{1,5},{5,1},{2,6},{6,2},{3,7},{7,3},{8,12},{12,8},{9,1... | collective-permute-start | bytes 6291464 | tf_op jit(solution)/shard_map/ppermute | solution.py:425
  249.4 21.6 %collective-permute-start.24 = (bf16[256,1152]{1,0:T(8,128)(2,1)}, bf16[256,1152]{1,0:T(8,128)(2,1)S(1)}, u32[]{:S(2)}, u32[]{:S(2)}) collective-permute-start(bf16[256,1152]{1,0:T(8,128)(2,1)} %get-tuple-element.146), channel_id=1, source_target_pairs={{0,24},{8,16},{16,8},{24,0},{1,25},{9,17},{17,9},{25,1},{2,26},{10... | collective-permute-start | bytes 1769480 | tf_op jit(solution)/shard_map/ppermute | solution.py:428
  250.8 28.0 %collective-permute-start.23 = (bf16[256,1152]{1,0:T(8,128)(2,1)}, bf16[256,1152]{1,0:T(8,128)(2,1)S(1)}, u32[]{:S(2)}, u32[]{:S(2)}) collective-permute-start(bf16[256,1152]{1,0:T(8,128)(2,1)} %get-tuple-element.147), channel_id=1, source_target_pairs={{0,16},{8,24},{16,0},{24,8},{1,17},{9,25},{17,1},{25,9},{2,18},{10... | collective-permute-start | bytes 1769480 | tf_op jit(solution)/shard_map/ppermute | solution.py:428
  252.1 27.5 %collective-permute-start.22 = (bf16[256,1152]{1,0:T(8,128)(2,1)}, bf16[256,1152]{1,0:T(8,128)(2,1)}, u32[]{:S(2)}, u32[]{:S(2)}) collective-permute-start(bf16[256,1152]{1,0:T(8,128)(2,1)} %get-tuple-element.148), channel_id=1, source_target_pairs={{0,8},{8,0},{16,24},{24,16},{1,9},{9,1},{17,25},{25,17},{2,10},{10... | collective-permute-start | bytes 1769480 | tf_op jit(solution)/shard_map/ppermute | solution.py:428
  286.9 19.6 %all-to-all-start.1 = ((bf16[4,256,256]{2,1,0:T(8,128)(2,1)}), bf16[4,256,256]{2,1,0:T(8,128)(2,1)S(1)}, u32[]{:S(2)}, u32[]{:S(2)}) async-start(bf16[4,256,256]{2,1,0:T(8,128)(2,1)} %get-tuple-element.121), calls=%async_computation.1 | async-start | bytes 1048576 | tf_op jit(solution)/shard_map/all_to_all | solution.py:645
  291.7 193.9 %reduce-scatter.3.cloned.1.call-start = ((), (), s32[]{:S(2)}) async-start(), calls=%async_computation.6 | async-start | bytes 3932160 | tf_op jit(solution)/shard_map/reduce_scatter | solution.py:624
  337.3 27.1 %collective-permute-start.29 = (bf16[256,1024]{1,0:T(8,128)(2,1)S(1)}, bf16[256,1024]{1,0:T(8,128)(2,1)S(1)}, u32[]{:S(2)}, u32[]{:S(2)}) collective-permute-start(bf16[256,1024]{1,0:T(8,128)(2,1)S(1)} %slice_bitcast_fusion), channel_id=1, source_target_pairs={{0,1},{1,2},{2,3},{3,0},{4,5},{5,6},{6,7},{7,4},{8,9},{9,10},{10,1... | collective-permute-start | bytes 1572872 | tf_op jit(solution)/shard_map/ppermute | solution.py:422
  341.2 23.6 %collective-permute-start.33 = (bf16[4,208,256]{2,1,0:T(8,128)(2,1)S(1)}, bf16[4,208,256]{2,1,0:T(8,128)(2,1)S(1)}, u32[]{:S(2)}, u32[]{:S(2)}) collective-permute-start(bf16[4,208,256]{2,1,0:T(8,128)(2,1)S(1)} %get-tuple-element.153), channel_id=1, source_target_pairs={{0,8},{8,0},{16,24},{24,16},{1,9},{9,1},{17,25},{25,17},{2,10},{10... | collective-permute-start | bytes 1277960 | tf_op jit(solution)/shard_map/ppermute | solution.py:428
  342.5 24.6 %collective-permute-start.35 = (bf16[4,208,256]{2,1,0:T(8,128)(2,1)S(1)}, bf16[4,208,256]{2,1,0:T(8,128)(2,1)S(1)}, u32[]{:S(2)}, u32[]{:S(2)}) collective-permute-start(bf16[4,208,256]{2,1,0:T(8,128)(2,1)S(1)} %get-tuple-element.154), channel_id=1, source_target_pairs={{0,24},{8,16},{16,8},{24,0},{1,25},{9,17},{17,9},{25,1},{2,26},{10... | collective-permute-start | bytes 1277960 | tf_op jit(solution)/shard_map/ppermute | solution.py:428
  343.5 23.6 %collective-permute-start.34 = (bf16[4,208,256]{2,1,0:T(8,128)(2,1)S(1)}, bf16[4,208,256]{2,1,0:T(8,128)(2,1)S(1)}, u32[]{:S(2)}, u32[]{:S(2)}) collective-permute-start(bf16[4,208,256]{2,1,0:T(8,128)(2,1)S(1)} %get-tuple-element.155), channel_id=1, source_target_pairs={{0,16},{8,24},{16,0},{24,8},{1,17},{9,25},{17,1},{25,9},{2,18},{10... | collective-permute-start | bytes 1277960 | tf_op jit(solution)/shard_map/ppermute | solution.py:428
  345.9 97.0 %collective-permute-start.26 = (bf16[256,1024]{1,0:T(8,128)(2,1)}, bf16[256,1024]{1,0:T(8,128)(2,1)}, u32[]{:S(2)}, u32[]{:S(2)}) collective-permute-start(bf16[256,1024]{1,0:T(8,128)(2,1)} %get-tuple-element.150), channel_id=1, source_target_pairs={{0,8},{8,0},{16,24},{24,16},{1,9},{9,1},{17,25},{25,17},{2,10},{10... | collective-permute-start | bytes 1572872 | tf_op jit(solution)/shard_map/ppermute | solution.py:428
  364.4 78.6 %collective-permute-start.28 = (bf16[256,1024]{1,0:T(8,128)(2,1)}, bf16[256,1024]{1,0:T(8,128)(2,1)}, u32[]{:S(2)}, u32[]{:S(2)}) collective-permute-start(bf16[256,1024]{1,0:T(8,128)(2,1)} %get-tuple-element.151), channel_id=1, source_target_pairs={{0,24},{8,16},{16,8},{24,0},{1,25},{9,17},{17,9},{25,1},{2,26},{10... | collective-permute-start | bytes 1572872 | tf_op jit(solution)/shard_map/ppermute | solution.py:428
  364.8 78.2 %collective-permute-start.27 = (bf16[256,1024]{1,0:T(8,128)(2,1)}, bf16[256,1024]{1,0:T(8,128)(2,1)}, u32[]{:S(2)}, u32[]{:S(2)}) collective-permute-start(bf16[256,1024]{1,0:T(8,128)(2,1)} %get-tuple-element.152), channel_id=1, source_target_pairs={{0,16},{8,24},{16,0},{24,8},{1,17},{9,25},{17,1},{25,9},{2,18},{10... | collective-permute-start | bytes 1572872 | tf_op jit(solution)/shard_map/ppermute | solution.py:428
  367.1 58.3 %collective-permute-start.30 = (bf16[256,1024]{1,0:T(8,128)(2,1)S(1)}, bf16[256,1024]{1,0:T(8,128)(2,1)S(1)}, u32[]{:S(2)}, u32[]{:S(2)}) collective-permute-start(bf16[256,1024]{1,0:T(8,128)(2,1)S(1)} %fusion.10), channel_id=1, source_target_pairs={{0,1},{1,2},{2,3},{3,0},{4,5},{5,6},{6,7},{7,4},{8,9},{9,10},{10,1... | collective-permute-start | bytes 1572872 | tf_op jit(solution)/shard_map/ppermute | solution.py:422
  367.4 34.0 %collective-permute-start.36 = (bf16[208,256]{1,0:T(8,128)(2,1)S(1)}, bf16[208,256]{1,0:T(8,128)(2,1)S(1)}, u32[]{:S(2)}, u32[]{:S(2)}) collective-permute-start(bf16[208,256]{1,0:T(8,128)(2,1)S(1)} %get-tuple-element.162), channel_id=1, source_target_pairs={{0,1},{1,2},{2,3},{3,0},{4,5},{5,6},{6,7},{7,4},{8,9},{9,10},{10,1... | collective-permute-start | bytes 319496 | tf_op jit(solution)/shard_map/ppermute | solution.py:422
  401.4 17.4 %collective-permute-start.38 = (bf16[208,256]{1,0:T(8,128)(2,1)S(1)}, bf16[208,256]{1,0:T(8,128)(2,1)S(1)}, u32[]{:S(2)}, u32[]{:S(2)}) collective-permute-start(bf16[208,256]{1,0:T(8,128)(2,1)S(1)} %get-tuple-element.163), channel_id=1, source_target_pairs={{0,3},{1,0},{2,1},{3,2},{4,7},{5,4},{6,5},{7,6},{8,11},{9,8},{10,9... | collective-permute-start | bytes 319496 | tf_op jit(solution)/shard_map/ppermute | solution.py:422
  430.4 15.5 %collective-permute-start.31 = (bf16[256,1024]{1,0:T(8,128)(2,1)}, bf16[256,1024]{1,0:T(8,128)(2,1)}, u32[]{:S(2)}, u32[]{:S(2)}) collective-permute-start(bf16[256,1024]{1,0:T(8,128)(2,1)} %fusion.9), channel_id=1, source_target_pairs={{0,1},{1,2},{2,3},{3,0},{4,5},{5,6},{6,7},{7,4},{8,9},{9,10},{10,1... | collective-permute-start | bytes 1572872 | tf_op jit(solution)/shard_map/ppermute | solution.py:422
  447.5 21.7 %collective-permute-start.55 = (bf16[768,512]{1,0:T(8,128)(2,1)}, bf16[768,512]{1,0:T(8,128)(2,1)}, u32[]{:S(2)}, u32[]{:S(2)}) collective-permute-start(bf16[768,512]{1,0:T(8,128)(2,1)} %reduce-scatter.5.cloned.1.call-done.refs_0_), channel_id=1, source_target_pairs={{0,24},{8,16},{16,8},{24,0},{1,25},{9,17},{17,9},{25,1},{2,26},{10... | collective-permute-start | bytes 2359304 | tf_op jit(solution)/shard_map/ppermute | solution.py:428
  448.5 37.1 %collective-permute-start.53 = (bf16[768,512]{1,0:T(8,128)(2,1)}, bf16[768,512]{1,0:T(8,128)(2,1)}, u32[]{:S(2)}, u32[]{:S(2)}) collective-permute-start(bf16[768,512]{1,0:T(8,128)(2,1)} %reduce-scatter.5.cloned.1.call-done.refs_0_), channel_id=1, source_target_pairs={{0,16},{8,24},{16,0},{24,8},{1,17},{9,25},{17,1},{25,9},{2,18},{10... | collective-permute-start | bytes 2359304 | tf_op jit(solution)/shard_map/ppermute | solution.py:428
  450.7 35.8 %collective-permute-start.51 = (bf16[768,512]{1,0:T(8,128)(2,1)}, bf16[768,512]{1,0:T(8,128)(2,1)}, u32[]{:S(2)}, u32[]{:S(2)}) collective-permute-start(bf16[768,512]{1,0:T(8,128)(2,1)} %reduce-scatter.5.cloned.1.call-done.refs_0_), channel_id=1, source_target_pairs={{0,8},{8,0},{16,24},{24,16},{1,9},{9,1},{17,25},{25,17},{2,10},{10... | collective-permute-start | bytes 2359304 | tf_op jit(solution)/shard_map/ppermute | solution.py:428
  451.1 36.9 %collective-permute-start.50 = (bf16[768,512]{1,0:T(8,128)(2,1)}, bf16[768,512]{1,0:T(8,128)(2,1)}, u32[]{:S(2)}, u32[]{:S(2)}) collective-permute-start(bf16[768,512]{1,0:T(8,128)(2,1)} %reduce-scatter.5.cloned.1.call-done.refs_0_), channel_id=1, source_target_pairs={{0,4},{4,0},{1,5},{5,1},{2,6},{6,2},{3,7},{7,3},{8,12},{12,8},{9,1... | collective-permute-start | bytes 2359304 | tf_op jit(solution)/shard_map/ppermute | solution.py:425
  469.2 20.4 %collective-permute-start.56 = (bf16[768,512]{1,0:T(8,128)(2,1)}, bf16[768,512]{1,0:T(8,128)(2,1)}, u32[]{:S(2)}, u32[]{:S(2)}) collective-permute-start(bf16[768,512]{1,0:T(8,128)(2,1)} %collective-permute-done.55.refs_6_), channel_id=1, source_target_pairs={{0,4},{4,0},{1,5},{5,1},{2,6},{6,2},{3,7},{7,3},{8,12},{12,8},{9,1... | collective-permute-start | bytes 2359304 | tf_op jit(solution)/shard_map/ppermute | solution.py:425
  485.6 21.6 %collective-permute-start.48 = (bf16[768,512]{1,0:T(8,128)(2,1)}, bf16[768,512]{1,0:T(8,128)(2,1)}, u32[]{:S(2)}, u32[]{:S(2)}) collective-permute-start(bf16[768,512]{1,0:T(8,128)(2,1)} %reduce-scatter.3.cloned.1.call-done.refs_0_), channel_id=1, source_target_pairs={{0,24},{8,16},{16,8},{24,0},{1,25},{9,17},{17,9},{25,1},{2,26},{10... | collective-permute-start | bytes 2359304 | tf_op jit(solution)/shard_map/ppermute | solution.py:428
  486.5 36.8 %collective-permute-start.46 = (bf16[768,512]{1,0:T(8,128)(2,1)}, bf16[768,512]{1,0:T(8,128)(2,1)}, u32[]{:S(2)}, u32[]{:S(2)}) collective-permute-start(bf16[768,512]{1,0:T(8,128)(2,1)} %reduce-scatter.3.cloned.1.call-done.refs_0_), channel_id=1, source_target_pairs={{0,16},{8,24},{16,0},{24,8},{1,17},{9,25},{17,1},{25,9},{2,18},{10... | collective-permute-start | bytes 2359304 | tf_op jit(solution)/shard_map/ppermute | solution.py:428
  488.0 35.3 %collective-permute-start.44 = (bf16[768,512]{1,0:T(8,128)(2,1)}, bf16[768,512]{1,0:T(8,128)(2,1)}, u32[]{:S(2)}, u32[]{:S(2)}) collective-permute-start(bf16[768,512]{1,0:T(8,128)(2,1)} %reduce-scatter.3.cloned.1.call-done.refs_0_), channel_id=1, source_target_pairs={{0,8},{8,0},{16,24},{24,16},{1,9},{9,1},{17,25},{25,17},{2,10},{10... | collective-permute-start | bytes 2359304 | tf_op jit(solution)/shard_map/ppermute | solution.py:428
  489.6 40.7 %collective-permute-start.52 = (bf16[768,512]{1,0:T(8,128)(2,1)}, bf16[768,512]{1,0:T(8,128)(2,1)S(1)}, u32[]{:S(2)}, u32[]{:S(2)}) collective-permute-start(bf16[768,512]{1,0:T(8,128)(2,1)} %collective-permute-done.51.refs_2_), channel_id=1, source_target_pairs={{0,4},{4,0},{1,5},{5,1},{2,6},{6,2},{3,7},{7,3},{8,12},{12,8},{9,1... | collective-permute-start | bytes 2359304 | tf_op jit(solution)/shard_map/ppermute | solution.py:425
  490.4 49.8 %collective-permute-start.43 = (bf16[768,512]{1,0:T(8,128)(2,1)S(1)}, bf16[768,512]{1,0:T(8,128)(2,1)}, u32[]{:S(2)}, u32[]{:S(2)}) collective-permute-start(bf16[768,512]{1,0:T(8,128)(2,1)S(1)} %copy-done.14), channel_id=1, source_target_pairs={{0,4},{4,0},{1,5},{5,1},{2,6},{6,2},{3,7},{7,3},{8,12},{12,8},{9,1... | collective-permute-start | bytes 2359304 | tf_op jit(solution)/shard_map/ppermute | solution.py:425
  507.2 33.0 %collective-permute-start.49 = (bf16[768,512]{1,0:T(8,128)(2,1)}, bf16[768,512]{1,0:T(8,128)(2,1)}, u32[]{:S(2)}, u32[]{:S(2)}) collective-permute-start(bf16[768,512]{1,0:T(8,128)(2,1)} %collective-permute-done.48.refs_6_), channel_id=1, source_target_pairs={{0,4},{4,0},{1,5},{5,1},{2,6},{6,2},{3,7},{7,3},{8,12},{12,8},{9,1... | collective-permute-start | bytes 2359304 | tf_op jit(solution)/shard_map/ppermute | solution.py:425
  523.3 17.0 %collective-permute-start.47 = (bf16[768,512]{1,0:T(8,128)(2,1)}, bf16[768,512]{1,0:T(8,128)(2,1)}, u32[]{:S(2)}, u32[]{:S(2)}) collective-permute-start(bf16[768,512]{1,0:T(8,128)(2,1)} %collective-permute-done.46.refs_4_), channel_id=1, source_target_pairs={{0,4},{4,0},{1,5},{5,1},{2,6},{6,2},{3,7},{7,3},{8,12},{12,8},{9,1... | collective-permute-start | bytes 2359304 | tf_op jit(solution)/shard_map/ppermute | solution.py:425
  523.3 17.0 %collective-permute-start.45 = (bf16[768,512]{1,0:T(8,128)(2,1)}, bf16[768,512]{1,0:T(8,128)(2,1)}, u32[]{:S(2)}, u32[]{:S(2)}) collective-permute-start(bf16[768,512]{1,0:T(8,128)(2,1)} %collective-permute-done.44.refs_2_), channel_id=1, source_target_pairs={{0,4},{4,0},{1,5},{5,1},{2,6},{6,2},{3,7},{7,3},{8,12},{12,8},{9,1... | collective-permute-start | bytes 2359304 | tf_op jit(solution)/shard_map/ppermute | solution.py:425
  (46 other events, 447.8 us)
Sparse Core Ops, SparseCore 0:
  53.5 64.0 all-gather.2
  125.3 62.9 all-gather.4
  230.9 60.8 reduce-scatter.4
  335.1 84.9 reduce-scatter.2

commit v4 on v3

--- a/solution.py
+++ b/solution.py
@@ -148,10 +148,10 @@
 
 
 def back_kernel(
-    block, heads, kv_heads, place_ref, q_ref, k_ref, v_ref, do_ref, lse_ref, segc_ref, segr_ref, x_ref,
-    normed_ref, w_ref, cos_ref, sin_ref, ng_ref, dw_ref, gain_ref, do_s, dq_s, dk_s, dv_s, raw_s, g_s,
+    block, heads, kv_heads, q_ref, k_ref, v_ref, do_ref, lse_ref, segc_ref, segr_ref,
+    raw_ref, do_s, dq_s, dk_s, dv_s,
 ):
-    seq = x_ref.shape[0]
+    seq = do_ref.shape[0]
     blocks = seq // block
     group = heads // kv_heads
     qw, kw = heads * HEAD, kv_heads * HEAD
@@ -182,16 +182,23 @@
 
     lax.fori_loop(0, heads, one_head, 0)
     for h in range(heads):
-        raw_s[:, h * HEAD : (h + 1) * HEAD] = dq_s[h]
+        raw_ref[:, h * HEAD : (h + 1) * HEAD] = dq_s[h]
     for h in range(kv_heads):
-        raw_s[:, qw + h * HEAD : qw + (h + 1) * HEAD] = dk_s[h]
-        raw_s[:, qw + kw + h * HEAD : qw + kw + (h + 1) * HEAD] = dv_s[h]
+        raw_ref[:, qw + h * HEAD : qw + (h + 1) * HEAD] = dk_s[h]
+        raw_ref[:, qw + kw + h * HEAD : qw + kw + (h + 1) * HEAD] = dv_s[h]
+
+
+def finish_kernel(
+    block, turned, place_ref, raw_ref, x_ref, normed_ref, w_ref, cos_ref, sin_ref, ng_ref, dw_ref, gain_ref, g_s,
+):
+    seq = x_ref.shape[0]
+    blocks = seq // block
     gain_ref[...] = jnp.zeros_like(gain_ref)
 
     def finish(i, carry):
         rows = pl.ds(pl.multiple_of(i * block, block), block)
-        g_s[rows, : qw + kw] = rotate(raw_s[rows, : qw + kw], cos_ref[rows, :], -sin_ref[rows, :]).astype(BF16)
-        g_s[rows, qw + kw :] = raw_s[rows, qw + kw :].astype(BF16)
+        g_s[rows, :turned] = rotate(raw_ref[rows, :turned], cos_ref[rows, :], -sin_ref[rows, :]).astype(BF16)
+        g_s[rows, turned:] = raw_ref[rows, turned:].astype(BF16)
         ng = dot_nt(g_s[rows, :], w_ref[...])
         x = x_ref[rows, :].astype(F32)
         gain_ref[...] += jnp.sum(ng * (x * inverse_rms(x)), axis=0, keepdims=True)
@@ -240,12 +247,12 @@
 
 
 def mid_back_kernel(
-    place_ref, hidden_ref, nb0_ref, nb1_ref, nb2_ref, nb3_ref, dy_ref, gates_ref, normed_ref, router_ref, gain_ref, ow_ref, att_ref,
+    place_ref, hidden_ref, nb0_ref, nb1_ref, nb2_ref, dy_ref, gates_ref, normed_ref, router_ref, gain_ref, ow_ref, att_ref,
     hg_ref, ag_ref, owg_ref, fg_ref, rg_ref, aog_s,
 ):
     gates = gates_ref[...]
     width_all = hidden_ref.shape[1]
-    nb = sum(ref[...].astype(F32) for ref in (nb1_ref, nb2_ref, nb3_ref)) + nb0_ref[...].astype(F32)
+    nb = sum(ref[...].astype(F32) for ref in (nb1_ref, nb2_ref)) + nb0_ref[...].astype(F32)
     mix = nb[:, width_all:]
     mix = mix + pltpu.roll(mix, LANES - MIX_LOW, 1)
     lg = gates * (mix - jnp.sum(gates * mix, axis=-1, keepdims=True))
@@ -434,26 +441,30 @@
         stacked = jnp.stack(parts)
         return jnp.stack([pick(stacked, lax.rem(z - j + n, n), 0) for j in range(n)])
 
-    def around(value):
-        return [value] + [flip(value, j) for j in range(1, yx)]
-
     def plus(one, other):
         return (one.astype(F32) + other.astype(F32)).astype(BF16)
 
-    chunks = [tokens]
-    for _ in range(n - 1):
-        chunks.append(shift(chunks[-1]))
+    def around(value):
+        return across_too(value, flip(value, 1), flip(value, 2))
+
+    def across_too(value, by_x, by_y):
+        half = value.shape[0] // 2
+        across = jnp.concatenate([flip(by_x[:half], 2), flip(by_y[half:], 1)], axis=0)
+        return [value, by_x, by_y, across]
+
+    def plane_sum(blocks):
+        half = blocks[0].shape[0] // 2
+        low, high = flip(blocks[3][:half], 1), flip(blocks[3][half:], 2)
+        to_y = jnp.concatenate([plus(blocks[2][:half], low), blocks[2][half:]], axis=0)
+        to_x = jnp.concatenate([blocks[1][:half], plus(blocks[1][half:], high)], axis=0)
+        return [blocks[0], flip(to_x, 1), flip(to_y, 2)]
+
+    chunks = [tokens, shift(tokens)]
 
     pack = jnp.concatenate(
         [attn_gain[None], ffn_gain[None], segment_ids.astype(BF16)[None], router_weight.T], axis=0
     )
-    packs = absolute([pack] + [shift(pack, k) for k in range(1, n)])
-    gain1 = packs[:, 0, :].reshape(1, width).astype(F32)
-    gain2 = packs[:, 1, :].reshape(1, width).astype(F32)
-    segments = packs[:, 2, :].reshape(seq).astype(F32)
-    seg_col, seg_row = segments[:, None], segments[None, :]
-    router = jnp.pad(packs[:, 3:, :].transpose(0, 2, 1).reshape(width, experts), ((0, 0), (0, LANES - experts)))
-
+    packs = [pack] + [shift(pack, k) for k in range(1, n)]
     part_rows = slab // ep
     by_dest = jnp.concatenate(
         [
@@ -470,14 +481,27 @@
     def piece(k):
         return jnp.concatenate([pick(by_dest, lax.rem(z + k, n), 1), ow_mine], axis=0)
 
-    dense_mine = jnp.stack([piece(0)] + [shift(piece(k), k) for k in range(1, n)])
-    dense_mine = jnp.stack(around(dense_mine))
-    dense_mate = swap(dense_mine)
-
+    dense_mine = [piece(0)] + [shift(piece(k), k) for k in range(1, n)]
     ids = jnp.arange(experts, dtype=jnp.int32)
     routed = jnp.any(routes[:, :, None] == ids[None, None, :], axis=1)
     mask_own = jnp.pad(routed.astype(F32), ((0, 0), (0, LANES - experts)))
-    dyx_mine = jnp.concatenate(around(jnp.concatenate([cotangent, mask_own.astype(BF16)], axis=1)), axis=0)
+    dyx_mine = around(jnp.concatenate([cotangent, mask_own.astype(BF16)], axis=1))
+    chunks[1], packs, dense_mine = lax.optimization_barrier((chunks[1], packs, dense_mine))
+    chunks.append(shift(chunks[1]))
+    dense_mine = around(jnp.stack(dense_mine))
+    chunks[2], dense_mine, dyx_mine = lax.optimization_barrier((chunks[2], dense_mine, dyx_mine))
+    for _ in range(n - 3):
+        chunks.append(shift(chunks[-1]))
+    dense_mine = jnp.stack(dense_mine)
+    dense_mate = swap(dense_mine)
+    packs = absolute(packs)
+    gain1 = packs[:, 0, :].reshape(1, width).astype(F32)
+    gain2 = packs[:, 1, :].reshape(1, width).astype(F32)
+    segments = packs[:, 2, :].reshape(seq).astype(F32)
+    seg_col, seg_row = segments[:, None], segments[None, :]
+    router = jnp.pad(packs[:, 3:, :].transpose(0, 2, 1).reshape(width, experts), ((0, 0), (0, LANES - experts)))
+
+    dyx_mine = jnp.concatenate(dyx_mine, axis=0)
     dyx_mate = swap(dyx_mine)
 
     positions = jnp.arange(seq, dtype=jnp.int32).astype(F32)
@@ -604,9 +628,6 @@
     def spread(value):
         return [value[j * rows : (j + 1) * rows] for j in range(yx)]
 
-    def exchanged(blocks):
-        return [blocks[0]] + [flip(blocks[j], j) for j in range(1, yx)]
-
     previous_mate = previous_mine = ()
     owned = []
     for e in range(own):
@@ -618,7 +639,7 @@
         if e < own - 1:
             grads, weights[e + 1] = lax.optimization_barrier((grads, weights[e + 1]))
         else:
-            nb_parts = exchanged(spread(plus(previous_mine[1], nb_got)))
+            nb_parts = plane_sum(spread(plus(previous_mine[1], nb_got)))
             moe_sum = plus(previous_mine[0], moe_got)
             nb_parts, moe_sum, grads = lax.optimization_barrier((nb_parts, moe_sum, grads))
         grads = lax.psum_scatter(grads, "shard", scatter_dimension=0, tiled=True)
@@ -628,7 +649,7 @@
 
     hidden_grad, att_grad, ow_grad, ffn_grad, router_grad = pl.pallas_call(
         mid_back_kernel,
-        in_specs=[smem] + [vmem] * 12,
+        in_specs=[smem] + [vmem] * 11,
         out_shape=(
             sds((rows, width), F32),
             sds((n, rows, qw), BF16),
@@ -642,47 +663,61 @@
         name="mid_back",
     )(place, hidden, *nb_parts, cotangent, gates_own, normed2, router, gain2, ow, att)
 
+    kvw = 2 * kw
+    wide = max(slab, qw, kvw)
+    small_rows = 16
+
+    def widen(part):
+        return jnp.pad(part, ((0, 0),) * 3 + ((0, wide - part.shape[3]),))
+
+    def rows_of(small):
+        small = jnp.pad(small, ((0, ep * small_rows - small.shape[0]), (0, 0)))
+        return widen(small.reshape(ep, small_rows, n, slab).transpose(2, 0, 1, 3).astype(BF16))
+
+    def dense_sum(pieces):
+        dense = jnp.concatenate(pieces, axis=2)
+        depth = dense.shape[2]
+        dense = dense.reshape(n, yx, 2, depth, wide).transpose(2, 1, 0, 3, 4)
+        dense = plus(pick(dense, core, 0), swap(pick(dense, 1 - core, 0)))
+        parts = plane_sum([pick(dense, lax.bitwise_xor(chip, jnp.int32(j)), 0) for j in range(yx)])
+        return sum(p.astype(F32) for p in parts).astype(BF16)
+
     att_grad = lax.all_to_all(att_grad, "shard", 0, 0).reshape(seq, qw)
-    ng, qkv_grad, gain_grad = pl.pallas_call(
+    att_grad, owned[0] = lax.optimization_barrier((att_grad, owned[0]))
+    early = around(owned[0])
+    small = rows_of(jnp.concatenate([ffn_grad, router_grad[:experts]], axis=0))
+    dense_early = dense_sum([widen(ow_grad.reshape(n, ep, ow_rows, slab)), small])
+    raw = pl.pallas_call(
         functools.partial(back_kernel, rows, heads, kv_heads),
-        in_specs=[smem] + [vmem] * 12,
-        out_shape=(sds((n, rows, width), BF16), sds((width, cols), BF16), sds((1, width), F32)),
+        out_shape=sds((seq, cols), F32),
         scratch_shapes=[
             pltpu.VMEM((heads, seq, HEAD), BF16),
             pltpu.VMEM((heads, seq, HEAD), F32),
             pltpu.VMEM((kv_heads, seq, HEAD), F32),
             pltpu.VMEM((kv_heads, seq, HEAD), F32),
-            pltpu.VMEM((seq, cols), F32),
-            pltpu.VMEM((seq, cols), BF16),
         ],
         compiler_params=params(),
-        cost_estimate=cost(4 * seq * width * cols, 80e6),
+        cost_estimate=cost(2 * seq * width * cols, 52e6),
         name="back",
-    )(place, q, k, v, att_grad, lse, seg_col, seg_row, x_all, normed, w_qkv, cosine, sine)
-
-    part = ng[1]
-    for step in list(range(2, n)) + [0]:
-        part = shift(part).astype(F32) + ng[step].astype(F32)
-        if step:
-            part = part.astype(BF16)
-    x = tokens.astype(F32)
-    inv = inverse_rms(x)
-    scaled = x * inv
-    w1 = part * gain1
-    input_grad = hidden_grad + inv * (w1 - scaled * jnp.mean(w1 * scaled, axis=-1, keepdims=True))
-
-    moe_parts = exchanged(spread(moe_sum))
-    output = (hidden + sum(p.astype(F32) for p in moe_parts)).astype(BF16)
-
-    shared = ()
-    for e in range(own):
-        mine = around(owned[e])
+    )(q, k, v, att_grad, lse, seg_col, seg_row)
+    raw, owned, early, dense_early = lax.optimization_barrier((raw, owned, early, dense_early))
+    ng, qkv_grad, gain_grad = pl.pallas_call(
+        functools.partial(finish_kernel, rows, qw + kw),
+        in_specs=[smem] + [vmem] * 6,
+        out_shape=(sds((n, rows, width), BF16), sds((width, cols), BF16), sds((1, width), F32)),
+        scratch_shapes=[pltpu.VMEM((seq, cols), BF16)],
+        compiler_params=params(),
+        cost_estimate=cost(4 * seq * width * cols, 30e6),
+        name="finish",
+    )(place, raw, x_all, normed, w_qkv, cosine, sine)
+    qkv_rows = qkv_grad.reshape(n, ep, part_rows, cols)
+    def share(e, mine, shared):
         pieces = [p for one in mine for p in (one, swap(one))]
 
-        def out_index(j, place_ref, e=e):
+        def out_index(j, place_ref):
             return (peer(place_ref, j % 2, j // 2), e, 0, 0)
 
-        shared = pl.pallas_call(
+        return pl.pallas_call(
             functools.partial(share_kernel, ep),
             grid_spec=pltpu.PrefetchScalarGridSpec(
                 num_scalar_prefetch=1,
@@ -704,37 +739,41 @@
             cost_estimate=cost(0, 20e6),
             name="share",
         )(place, *pieces, *shared)
+
+    dense = dense_sum([rows_of(gain_grad), widen(qkv_rows[..., :qw]), widen(qkv_rows[..., qw:])])
+    dense = jnp.concatenate([dense_early, dense], axis=1)
+    if hi > 1:
+        dense = lax.psum(dense.astype(F32), "hi").astype(BF16)
+    got = shift(ng[1])
+    shared = share(0, early, ())
+    last = [(value, flip(value, 1), flip(value, 2)) for value in owned[1:]]
+    dense, got, shared, last = lax.optimization_barrier((dense, got, shared, last))
+    for e in range(1, own):
+        shared = share(e, across_too(*last[e - 1]), shared)
+    for step in range(2, n):
+        got = shift((got.astype(F32) + ng[step].astype(F32)).astype(BF16))
+    part = got.astype(F32) + ng[0].astype(F32)
+    x = tokens.astype(F32)
+    inv = inverse_rms(x)
+    scaled = x * inv
+    w1 = part * gain1
+    input_grad = hidden_grad + inv * (w1 - scaled * jnp.mean(w1 * scaled, axis=-1, keepdims=True))
+
+    moe_parts = plane_sum(spread(moe_sum))
+    output = (hidden + sum(p.astype(F32) for p in moe_parts)).astype(BF16)
+
     gate_grad, up_grad, down_grad = (g.reshape((experts,) + g.shape[2:]) for g in shared)
 
-    kvw = 2 * kw
-    small = jnp.concatenate([gain_grad, ffn_grad, router_grad[:experts]], axis=0)
-    small_rows = 16
-    small = jnp.pad(small, ((0, ep * small_rows - small.shape[0]), (0, 0)))
-    small = small.reshape(ep, small_rows, n, slab).transpose(2, 0, 1, 3).astype(BF16)
-    qkv_rows = qkv_grad.reshape(n, ep, part_rows, cols)
-    wide = max(slab, qw, kvw)
-
-    def widen(part):
-        return jnp.pad(part, ((0, 0),) * 3 + ((0, wide - part.shape[3]),))
-
-    pieces = [widen(ow_grad.reshape(n, ep, ow_rows, slab)), widen(small), widen(qkv_rows[..., :qw]), widen(qkv_rows[..., qw:])]
-    dense = jnp.concatenate(pieces, axis=2)
-    dense = dense.reshape(n, yx, 2, dense.shape[2], wide).transpose(2, 1, 0, 3, 4)
-    dense = plus(pick(dense, core, 0), swap(pick(dense, 1 - core, 0)))
-    dense = exchanged([pick(dense, lax.bitwise_xor(chip, jnp.int32(j)), 0) for j in range(yx)])
-    dense = sum(p.astype(F32) for p in dense)
-    if hi > 1:
-        dense = lax.psum(dense, "hi")
-    dense = dense.astype(BF16)
     dense = [pick(dense, z, 0)] + [shift(pick(dense, lax.rem(z + k, n), 0), k) for k in range(1, n)]
-    cut = ow_rows + small_rows
+    cut = ow_rows + 2 * small_rows
     summed = sum(p[:cut].astype(F32) for p in dense).astype(BF16)
     kept = absolute([p[cut:] for p in dense]).reshape(n * 2 * part_rows, wide)
     mine = jnp.stack(around(jnp.concatenate([summed, kept], axis=0)))
     both = jnp.stack([mine, swap(mine)], axis=1).reshape((ep,) + mine.shape[1:])
     full = jnp.stack([pick(both, lax.bitwise_xor(r, jnp.int32(i)), 0) for i in range(ep)])
     ow_full = full[:, :ow_rows, :slab].reshape(-1, slab).astype(F32)
-    small_full = full[:, ow_rows:cut, :slab].reshape(-1, slab).astype(F32)
+    small_full = full[:, ow_rows : ow_rows + small_rows, :slab].reshape(-1, slab).astype(F32)
+    gain_full = full[0, ow_rows + small_rows, :slab].astype(F32)
     kept = full[:, cut:].reshape(ep, n, 2, part_rows, wide)
 
     def columns(which, start, size):
@@ -744,13 +783,13 @@
     return (
         output,
         input_grad,
-        small_full[0],
+        gain_full,
         columns(0, 0, qw),
         columns(1, 0, kw),
         columns(1, kw, kw),
         ow_full,
-        small_full[1],
-        small_full[2 : 2 + experts].T,
+        small_full[0],
+        small_full[1 : 1 + experts].T,
         gate_grad,
         up_grad,
         down_grad,

time: 566 us -> 517 us (0.913)
  waiting for transfers between devices: 239 us -> 164 us
  other arithmetic: 37.3 us -> 48.7 us
  local copies, waits for them, and re-layouts: 30.1 us -> 40.6 us
    ppermute x15, waiting for transfers between devices: 102 us -> 33.9 us  [shift(): return lax.ppermute(value, 'shard', [(i, (i + k) % n) for i in range(n)])]
    ppermute x27 -> x40, waiting for transfers between devices: 114 us -> 72.2 us  [flip(): return lax.ppermute(value, 'yx', [(i, i ^ j) for i in range(yx)])]
    ppermute x27 -> x40, starting transfers between devices: 31.1 us -> 55.9 us  [flip(): return lax.ppermute(value, 'yx', [(i, i ^ j) for i in range(yx)])]
    ppermute x15, starting transfers between devices: 37.7 us -> 12.9 us  [shift(): return lax.ppermute(value, 'shard', [(i, (i + k) % n) for i in range(n)])]
    all_to_all x1, waiting for transfers between devices: 8.4 us -> 27.2 us  [per_device(): att = lax.all_to_all(att.reshape(n, rows, qw), 'shard', 0, 0)]
    all_to_all x1, waiting for transfers between devices: 13.3 us -> 26.1 us  [per_device(): att_grad = lax.all_to_all(att_grad, 'shard', 0, 0).reshape(seq, qw)]
    unnamed x84 -> x136, local copies, waits for them, and re-layouts: 13.2 us -> 19.2 us
    pallas_call x4 -> x5, Pallas kernels: 47.7 us -> 50.7 us  [the longest x2 18.2 us: share(): pl.pallas_call(functools.partial(share_kernel, ep), grid_spec=pltpu.Prefe...]
  transfers between devices with their start and end apart: 63 -> 77, of which waited for: 24 -> 30; matrix products, arithmetic and copies ran while one was open for 11% -> 13% of each run, Pallas kernels for 24% -> 30%
where the time goes in v4:
time: 517 us; the launch traced here: 507 us
  waiting for transfers between devices  164 us (32%)
  Pallas kernels  159 us (31%)
  starting transfers between devices  79.3 us (15%)
  other arithmetic  48.7 us (9%)
  local copies, waits for them, and re-layouts  40.6 us (8%)
  between operations  15.6 us (3%)
    ppermute x40, waiting for transfers between devices, flip(): return lax.ppermute(value, 'yx', [(i, i ^ j) for i in range(yx)])  72.2 us
    pallas_call x4, Pallas kernels, run_expert(): pl.pallas_call(functools.partial(expert_kernel, n, e), grid=(steps,), in_...  57.8 us
    ppermute x40, starting transfers between devices, flip(): return lax.ppermute(value, 'yx', [(i, i ^ j) for i in range(yx)])  55.9 us
    ppermute x15, waiting for transfers between devices, shift(): return lax.ppermute(value, 'shard', [(i, (i + k) % n) for i in range(n)])  33.9 us
    pallas_call x2, Pallas kernels, weight_grads(): pl.pallas_call(functools.partial(expert_grad_kernel, n, steps), grid=(2 *...  27.4 us
    all_to_all x1, waiting for transfers between devices, per_device(): att = lax.all_to_all(att.reshape(n, rows, qw), 'shard', 0, 0)  27.2 us
    all_to_all x1, waiting for transfers between devices, per_device(): att_grad = lax.all_to_all(att_grad, 'shard', 0, 0).reshape(seq, qw)  26.1 us
    unnamed x136, local copies, waits for them, and re-layouts  19.2 us
  transfers between devices with their start and end apart: 77, of which 30 were waited for; matrix products, arithmetic and copies ran while one was open for 13% of the time, Pallas kernels for 30%

profile of v4, /device:TPU:0, one launch (start us, length us, event | category | flops | bytes accessed | tf_op | source)
XLA Modules:
  0.0 506.9 jit_solution(15152589006656787368)
XLA Ops:
  10.0 3.0 collective-permute-start.13
  18.3 2.3 collective-permute-start.6
  22.6 9.5 %collective-permute-done.3 = bf16[19,256]{1,0:T(8,128)(2,1)S(1)} collective-permute-done((bf16[19,256]{1,0:T(8,128)(2,1)S(1)}, bf16[19,256]{1,0:T(8,128)(2,1)S(1)}, u32[]{:S(2)}, u32[]{:S(2)}) %collective-permute-start.3) | collective-permute-done | bytes 9760 | tf_op jit(solution)/shard_map/ppermute | solution.py:429
  32.6 4.1 collective-permute-done.2
  37.2 5.0 collective-permute-done.1
  42.6 6.2 %collective-permute-done.4 = bf16[96,512]{1,0:T(8,128)(2,1)S(1)} collective-permute-done((bf16[96,512]{1,0:T(8,128)(2,1)S(1)}, bf16[96,512]{1,0:T(8,128)(2,1)S(1)}, u32[]{:S(2)}, u32[]{:S(2)}) %collective-permute-start.4) | collective-permute-done | bytes 98336 | tf_op jit(solution)/shard_map/ppermute | solution.py:429
  58.2 4.7 collective-permute-done.9
  65.0 2.0 collective-permute-done.15
  67.0 1.9 pad_maximum_fusion.8
  72.9 7.8 %collective-permute-done.16.refs_3_ = bf16[256,1024]{1,0:T(8,128)(2,1)} collective-permute-done((bf16[256,1024]{1,0:T(8,128)(2,1)}, bf16[256,1024]{1,0:T(8,128)(2,1)}, u32[]{:S(2)}, u32[]{:S(2)}) %collective-permute-start.16) | collective-permute-done | bytes 524320 | tf_op jit(solution)/shard_map/ppermute | solution.py:429
  81.8 1.9 fusion.25
  88.5 18.7 %front.1 = (bf16[1024,1024]{1,0:T(8,128)(2,1)}, bf16[1024,512]{1,0:T(8,128)(2,1)}, bf16[1024,1024]{1,0:T(8,128)(2,1)}, bf16[4,1024,64]{2,1,0:T(8,128)(2,1)}, bf1...) custom-call(s32[4]{0:T(128)} %pad_add_fusion.place_ref, ...), custom_call_target="tpu_custom_call" | custom-call | flops 1073741824 | bytes 60000000 | tf_op jit(solution)/shard_map/front/pallas_call | solution.py:523
  107.2 3.6 all-to-all-start
  113.4 27.2 %all-to-all-done.att_ref = bf16[4,256,256]{2,1,0:T(8,128)(2,1)S(1)} async-done(((bf16[4,256,256]{2,1,0:T(8,128)(2,1)}), bf16[4,256,256]{2,1,0:T(8,128)(2,1)S(1)}, u32[]{:S(2)}, u32[]{:S(2)}) %all-to-all-start) | async-done | bytes 524320 | tf_op jit(solution)/shard_map/all_to_all | solution.py:542
  141.4 4.6 mid.1
  150.7 9.0 %collective-permute-done.18 = bf16[256,1024]{1,0:T(8,128)(2,1)S(1)} collective-permute-done((bf16[256,1024]{1,0:T(8,128)(2,1)}, bf16[256,1024]{1,0:T(8,128)(2,1)S(1)}, u32[]{:S(2)}, u32[]{:S(2)}) %collective-permute-start.18) | collective-permute-done | bytes 524320 | tf_op jit(solution)/shard_map/ppermute | solution.py:435
  164.1 3.2 collective-permute-done.20
  169.5 14.0 %expert.5 = (bf16[1024,1024]{1,0:T(8,128)(2,1)}, bf16[1024,1152]{1,0:T(8,128)(2,1)}, f32[1024,128]{1,0:T(8,128)}, bf16[1024,512]{1,0:T(8,128)(2,1)}, bf16[1024,5...) custom-call(s32[4]{0:T(128)} %pad_add_fusion.place_ref, bf16[1024,1024]{1,0:T(8,128)(2,1)} %constant_dynamic-update-slice_fusion.3.n2_ref.refs_6_, ...), custom_call_target="tpu_custom_call" | custom-call | flops 6442450944 | bytes 36000000 | tf_op jit(solution)/shard_map/expert/pallas_call | solution.py:568
  184.9 13.7 %expert.4 = (bf16[1024,1024]{1,0:T(8,128)(2,1)}, bf16[1024,1152]{1,0:T(8,128)(2,1)}, f32[1024,128]{1,0:T(8,128)}, bf16[1024,512]{1,0:T(8,128)(2,1)}, bf16[1024,5...) custom-call(s32[4]{0:T(128)} %pad_add_fusion.place_ref, bf16[1024,1024]{1,0:T(8,128)(2,1)} %copy-done.50, ...), custom_call_target="tpu_custom_call" | custom-call | flops 6442450944 | bytes 36000000 | tf_op jit(solution)/shard_map/expert/pallas_call | solution.py:568
  198.6 13.6 %expert_grads.2 = bf16[3072,512]{1,0:T(8,128)(2,1)} custom-call(bf16[1024,1024]{1,0:T(8,128)(2,1)} %copy-done.50, bf16[1024,1152]{1,0:T(8,128)(2,1)} %collective-permute-done.23.dyx_ref.refs_1_, f32[1024,128]{1,0:T(8,128)} %get-tuple-element.136.refs_2_, bf16[1024,512]{1,0:T(8,128)(2,1)} %get-tuple-element.137.refs_3_, ...), custom_call_target="tpu_custom_call" | custom-call | flops 6442450944 | bytes 40000000 | tf_op jit(solution)/shard_map/expert_grads/pallas_call | solution.py:611
  212.2 4.1 all-gather.5.cloned.1.call-done.w_ref
  216.4 15.2 %expert.7 = (bf16[1024,1024]{1,0:T(8,128)(2,1)}, bf16[1024,1152]{1,0:T(8,128)(2,1)}, f32[1024,128]{1,0:T(8,128)}, bf16[1024,512]{1,0:T(8,128)(2,1)}, bf16[1024,5...) custom-call(s32[4]{0:T(128)} %pad_add_fusion.place_ref, bf16[1024,1024]{1,0:T(8,128)(2,1)} %copy-done.50, ...), custom_call_target="tpu_custom_call" | custom-call | flops 6442450944 | bytes 36000000 | tf_op jit(solution)/shard_map/expert/pallas_call | solution.py:568
  232.2 14.9 %expert.6 = (bf16[1024,1024]{1,0:T(8,128)(2,1)}, bf16[1024,1152]{1,0:T(8,128)(2,1)}, f32[1024,128]{1,0:T(8,128)}, bf16[1024,512]{1,0:T(8,128)(2,1)}, bf16[1024,5...) custom-call(s32[4]{0:T(128)} %pad_add_fusion.place_ref, bf16[1024,1024]{1,0:T(8,128)(2,1)} %constant_dynamic-update-slice_fusion.3.n2_ref.refs_6_, ...), custom_call_target="tpu_custom_call" | custom-call | flops 6442450944 | bytes 36000000 | tf_op jit(solution)/shard_map/expert/pallas_call | solution.py:568
  247.1 3.0 add_convert_fusion
  253.2 6.0 %collective-permute-done.27 = bf16[128,1152]{1,0:T(8,128)(2,1)S(1)} collective-permute-done((bf16[128,1152]{1,0:T(8,128)(2,1)S(1)}, bf16[128,1152]{1,0:T(8,128)(2,1)S(1)}, u32[]{:S(2)}, u32[]{:S(2)}) %collective-permute-start.27) | collective-permute-done | bytes 294944 | tf_op jit(solution)/shard_map/ppermute | solution.py:435
  264.3 13.8 %expert_grads.3 = bf16[3072,512]{1,0:T(8,128)(2,1)} custom-call(bf16[1024,1024]{1,0:T(8,128)(2,1)} %copy-done.50, bf16[1024,1152]{1,0:T(8,128)(2,1)} %collective-permute-done.23.dyx_ref.refs_1_, f32[1024,128]{1,0:T(8,128)} %get-tuple-element.154.refs_2_, bf16[1024,512]{1,0:T(8,128)(2,1)} %get-tuple-element.155.refs_3_, ...), custom_call_target="tpu_custom_call" | custom-call | flops 6442450944 | bytes 40000000 | tf_op jit(solution)/shard_map/expert_grads/pallas_call | solution.py:611
  278.1 4.5 add_convert_fusion.1
  284.6 7.1 %mid_back.1 = (f32[256,1024]{1,0:T(8,128)}, bf16[4,256,256]{2,1,0:T(8,128)(2,1)}, bf16[4,1024,256]{2,1,0:T(8,128)(2,1)}, f32[1,1024]{1,0:T(1,128)}, f32[128,1024]{1,0:T(8,128)}) custom-call(s32[4]{0:T(128)} %pad_add_fusion.place_ref, f32[256,1024]{1,0:T(8,128)} %get-tuple-element.129.hidden_ref, bf16[256,1152]{1,0:T(8,128)(2,1)} %slice.347.nb0_ref, ...), custom_call_target="tpu_custom_call" | custom-call | flops 1073741824 | bytes 20000000 | tf_op jit(solution)/shard_map/mid_back/pallas_call | solution.py:650
  295.0 4.4 all-to-all-start.1
  303.1 26.1 %all-to-all-done.1 = bf16[4,256,256]{2,1,0:T(8,128)(2,1)} async-done(((bf16[4,256,256]{2,1,0:T(8,128)(2,1)}), bf16[4,256,256]{2,1,0:T(8,128)(2,1)}, u32[]{:S(2)}, u32[]{:S(2)}) %all-to-all-start.1) | async-done | bytes 524320 | tf_op jit(solution)/shard_map/all_to_all | solution.py:685
  334.1 15.7 %collective-permute-done.35.refs_4_ = bf16[768,512]{1,0:T(8,128)(2,1)S(1)} collective-permute-done((bf16[768,512]{1,0:T(8,128)(2,1)}, bf16[768,512]{1,0:T(8,128)(2,1)S(1)}, u32[]{:S(2)}, u32[]{:S(2)}) %collective-permute-start.35) | collective-permute-done | bytes 786464 | tf_op jit(solution)/shard_map/ppermute | solution.py:435
  353.7 2.5 collective-permute-done.42
  356.7 1.9 fusion.17
  358.6 16.9 %back.1.raw_ref = f32[1024,512]{1,0:T(8,128)} custom-call(bf16[4,1024,64]{2,1,0:T(8,128)(2,1)} %get-tuple-element.169.q_ref, bf16[2,1024,64]{2,1,0:T(8,128)(2,1)} %get-tuple-element.170.k_ref, bf16[2,1024,64]{2,1,0:T(8,128)(2,1)} %get-tuple-element.171.v_ref, bf16[1024,256]{1,0:T(8,128)(2,1)} %bitcast.33.do_ref, f32[4,1024,1]{2,1,0:T(8,128)} %get-tuple-element.175.lse_ref, ...), custom_call_target="tpu_custom_call" | custom-call | flops 1073741824 | bytes 52000000 | tf_op jit(solution)/shard_map/back/pallas_call | solution.py:690
  375.7 8.4 %finish.1 = (bf16[4,256,1024]{2,1,0:T(8,128)(2,1)}, bf16[1024,512]{1,0:T(8,128)(2,1)}, f32[1,1024]{1,0:T(1,128)}) custom-call(s32[4]{0:T(128)} %pad_add_fusion.place_ref, f32[1024,512]{1,0:T(8,128)} %back.1.raw_ref, bf16[1024,1024]{1,0:T(8,128)(2,1)} %get-tuple-element.183.x_ref, bf16[1024,1024]{1,0:T(8,128)(2,1)} %get-tuple-element.184.normed_ref, ...), custom_call_target="tpu_custom_call" | custom-call | flops 2147483648 | bytes 30000000 | tf_op jit(solution)/shard_map/finish/pallas_call | solution.py:704
  393.5 3.9 collective-permute-done.32
  400.2 2.8 collective-permute-done.44
  405.6 1.9 collective-permute-done.46
  414.2 9.1 %share.2 = (f32[8,2,256,512]{3,2,1,0:T(8,128)}, f32[8,2,256,512]{3,2,1,0:T(8,128)}, f32[8,2,128,1024]{3,2,1,0:T(8,128)}) custom-call(s32[4]{0:T(128)} %pad_add_fusion.place_ref, bf16[768,512]{1,0:T(8,128)(2,1)} %reduce-scatter.3.cloned.1.call-done.refs_0_, bf16[768,512]{1,0:T(8,128)(2,1)} %copy-done.32, bf16[768,512]{1,0:T(8,128)(2,1)} %copy-done.20, ...), custom_call_target="tpu_custom_call" | custom-call | bytes 20000000 | tf_op jit(solution)/shard_map/share/pallas_call | solution.py:720
  423.3 5.3 %collective-permute-done.47 = bf16[4,80,256]{2,1,0:T(8,128)(2,1)} collective-permute-done((bf16[4,80,256]{2,1,0:T(8,128)(2,1)}, bf16[4,80,256]{2,1,0:T(8,128)(2,1)}, u32[]{:S(2)}, u32[]{:S(2)}) %collective-permute-start.47) | collective-permute-done | bytes 163872 | tf_op jit(solution)/shard_map/ppermute | solution.py:435
  432.6 3.9 collective-permute-start.59
  443.4 12.3 %collective-permute-start.60 = (bf16[416,256]{1,0:T(8,128)(2,1)S(1)}, bf16[416,256]{1,0:T(8,128)(2,1)S(1)}, u32[]{:S(2)}, u32[]{:S(2)}) collective-permute-start(bf16[416,256]{1,0:T(8,128)(2,1)S(1)} %get-tuple-element.252), channel_id=1, source_target_pairs={{0,8},{8,0},{16,24},{24,16},{1,9},{9,1},{17,25},{25,17},{2,10},{10... | collective-permute-start | bytes 638984 | tf_op jit(solution)/shard_map/ppermute | solution.py:435
  457.4 4.4 collective-permute-done.60
  467.5 4.8 collective-permute-done.63
  472.4 2.1 fusion.36
  475.6 2.3 add_convert_fusion.2
  479.4 2.4 fusion.11
  481.8 9.0 %share.3 = (f32[8,2,256,512]{3,2,1,0:T(8,128)}, f32[8,2,256,512]{3,2,1,0:T(8,128)}, f32[8,2,128,1024]{3,2,1,0:T(8,128)}) custom-call(s32[4]{0:T(128)} %pad_add_fusion.place_ref, bf16[768,512]{1,0:T(8,128)(2,1)} %reduce-scatter.5.cloned.1.call-done.refs_0_, ...), custom_call_target="tpu_custom_call", output_to_operand_aliasing={{0}: (9, {}), {1}: (10, {}), {2}: (11, {})} | custom-call | bytes 20000000 | tf_op jit(solution)/shard_map/share/pallas_call | solution.py:720
  (389 shorter events, 126.6 us)
Async XLA Ops:
  7.2 162.3 %all-gather.3.cloned.1.call-start = ((), (), s32[]{:S(2)}) async-start(), calls=%async_computation.4 | async-start | bytes 3932160 | tf_op jit(solution)/shard_map/all_gather | solution.py:521
  10.0 42.0 %collective-permute-start.13 = (bf16[256,1152]{1,0:T(8,128)(2,1)S(1)}, bf16[256,1152]{1,0:T(8,128)(2,1)S(1)}, u32[]{:S(2)}, u32[]{:S(2)}) collective-permute-start(bf16[256,1152]{1,0:T(8,128)(2,1)S(1)} %pad_maximum_fusion.7), channel_id=1, source_target_pairs={{0,16},{8,24},{16,0},{24,8},{1,17},{9,25},{17,1},{25,9},{2,18},{10... | collective-permute-start | bytes 1769480 | tf_op jit(solution)/shard_map/ppermute | solution.py:435
  13.0 41.2 %collective-permute-start.12 = (bf16[256,1152]{1,0:T(8,128)(2,1)S(1)}, bf16[256,1152]{1,0:T(8,128)(2,1)S(1)}, u32[]{:S(2)}, u32[]{:S(2)}) collective-permute-start(bf16[256,1152]{1,0:T(8,128)(2,1)S(1)} %pad_maximum_fusion.7), channel_id=1, source_target_pairs={{0,8},{8,0},{16,24},{24,16},{1,9},{9,1},{17,25},{25,17},{2,10},{10... | collective-permute-start | bytes 1769480 | tf_op jit(solution)/shard_map/ppermute | solution.py:435
  14.5 35.5 %collective-permute-start = (bf16[256,1024]{1,0:T(8,128)(2,1)}, bf16[256,1024]{1,0:T(8,128)(2,1)S(1)}, u32[]{:S(2)}, u32[]{:S(2)}) collective-permute-start(bf16[256,1024]{1,0:T(8,128)(2,1)} %x_ref.1), channel_id=1, source_target_pairs={{0,1},{1,2},{2,3},{3,0},{4,5},{5,6},{6,7},{7,4},{8,9},{9,10},{10,1... | collective-permute-start | bytes 1572872 | tf_op jit(solution)/shard_map/ppermute | solution.py:429
  18.3 23.9 %collective-permute-start.6 = (bf16[96,512]{1,0:T(8,128)(2,1)S(1)}, bf16[96,512]{1,0:T(8,128)(2,1)S(1)}, u32[]{:S(2)}, u32[]{:S(2)}) collective-permute-start(bf16[96,512]{1,0:T(8,128)(2,1)S(1)} %get-tuple-element.261), channel_id=1, source_target_pairs={{0,3},{1,0},{2,1},{3,2},{4,7},{5,4},{6,5},{7,6},{8,11},{9,8},{10,9... | collective-permute-start | bytes 294920 | tf_op jit(solution)/shard_map/ppermute | solution.py:429
  50.8 12.1 %collective-permute-start.9 = (bf16[4,96,512]{2,1,0:T(8,128)(2,1)S(1)}, bf16[4,96,512]{2,1,0:T(8,128)(2,1)S(1)}, u32[]{:S(2)}, u32[]{:S(2)}) collective-permute-start(bf16[4,96,512]{2,1,0:T(8,128)(2,1)S(1)} %pad_maximum_fusion.16), channel_id=1, source_target_pairs={{0,16},{8,24},{16,0},{24,8},{1,17},{9,25},{17,1},{25,9},{2,18},{10... | collective-permute-start | bytes 1179656 | tf_op jit(solution)/shard_map/ppermute | solution.py:435
  51.4 12.2 %collective-permute-start.8 = (bf16[4,96,512]{2,1,0:T(8,128)(2,1)S(1)}, bf16[4,96,512]{2,1,0:T(8,128)(2,1)S(1)}, u32[]{:S(2)}, u32[]{:S(2)}) collective-permute-start(bf16[4,96,512]{2,1,0:T(8,128)(2,1)S(1)} %pad_maximum_fusion.16), channel_id=1, source_target_pairs={{0,8},{8,0},{16,24},{24,16},{1,9},{9,1},{17,25},{25,17},{2,10},{10... | collective-permute-start | bytes 1179656 | tf_op jit(solution)/shard_map/ppermute | solution.py:435
  52.7 14.4 %collective-permute-start.15 = (bf16[128,1152]{1,0:T(8,128)(2,1)}, bf16[128,1152]{1,0:T(8,128)(2,1)}, u32[]{:S(2)}, u32[]{:S(2)}) collective-permute-start(bf16[128,1152]{1,0:T(8,128)(2,1)} %slice.344), channel_id=1, source_target_pairs={{0,8},{8,0},{16,24},{24,16},{1,9},{9,1},{17,25},{25,17},{2,10},{10... | collective-permute-start | bytes 884744 | tf_op jit(solution)/shard_map/ppermute | solution.py:435
  56.5 12.8 %collective-permute-start.7 = (bf16[256,1024]{1,0:T(8,128)(2,1)}, bf16[256,1024]{1,0:T(8,128)(2,1)}, u32[]{:S(2)}, u32[]{:S(2)}) collective-permute-start(bf16[256,1024]{1,0:T(8,128)(2,1)} %copy-done.38), channel_id=1, source_target_pairs={{0,1},{1,2},{2,3},{3,0},{4,5},{5,6},{6,7},{7,4},{8,9},{9,10},{10,1... | collective-permute-start | bytes 1572872 | tf_op jit(solution)/shard_map/ppermute | solution.py:429
  107.2 33.4 %all-to-all-start = ((bf16[4,256,256]{2,1,0:T(8,128)(2,1)}), bf16[4,256,256]{2,1,0:T(8,128)(2,1)S(1)}, u32[]{:S(2)}, u32[]{:S(2)}) async-start(bf16[4,256,256]{2,1,0:T(8,128)(2,1)} %bitcast.260), calls=%async_computation | async-start | bytes 1048576 | tf_op jit(solution)/shard_map/all_to_all | solution.py:542
  110.8 105.5 %all-gather.5.cloned.1.call-start = ((), (), s32[]{:S(2)}) async-start(), calls=%async_computation.5 | async-start | bytes 3932160 | tf_op jit(solution)/shard_map/all_gather | solution.py:521
  113.3 215.8 %reduce-scatter.3.cloned.1.call-start = ((), (), s32[]{:S(2)}) async-start(), calls=%async_computation.6 | async-start | bytes 3932160 | tf_op jit(solution)/shard_map/reduce_scatter | solution.py:645
  145.9 13.7 %collective-permute-start.18 = (bf16[256,1024]{1,0:T(8,128)(2,1)}, bf16[256,1024]{1,0:T(8,128)(2,1)S(1)}, u32[]{:S(2)}, u32[]{:S(2)}) collective-permute-start(bf16[256,1024]{1,0:T(8,128)(2,1)} %get-tuple-element.130.normed_ref), channel_id=1, source_target_pairs={{0,8},{8,0},{16,24},{24,16},{1,9},{9,1},{17,25},{25,17},{2,10},{10... | collective-permute-start | bytes 1572872 | tf_op jit(solution)/shard_map/ppermute | solution.py:435
  148.3 14.0 %collective-permute-start.19 = (bf16[256,1024]{1,0:T(8,128)(2,1)}, bf16[256,1024]{1,0:T(8,128)(2,1)S(1)}, u32[]{:S(2)}, u32[]{:S(2)}) collective-permute-start(bf16[256,1024]{1,0:T(8,128)(2,1)} %get-tuple-element.130.normed_ref), channel_id=1, source_target_pairs={{0,16},{8,24},{16,0},{24,8},{1,17},{9,25},{17,1},{25,9},{2,18},{10... | collective-permute-start | bytes 1572872 | tf_op jit(solution)/shard_map/ppermute | solution.py:435
  150.7 32.8 %collective-permute-start.23 = (bf16[1024,1152]{1,0:T(8,128)(2,1)}, bf16[1024,1152]{1,0:T(8,128)(2,1)}, u32[]{:S(2)}, u32[]{:S(2)}) collective-permute-start(bf16[1024,1152]{1,0:T(8,128)(2,1)} %constant_dynamic-update-slice_fusion.8.dyx_ref.refs_7_), channel_id=1, source_target_pairs={{0,4},{4,0},{1,5},{5,1},{2,6},{6,2},{3,7},{7,3},{8,12},{12,8},{9,1... | collective-permute-start | bytes 7077896 | tf_op jit(solution)/shard_map/ppermute | solution.py:432
  169.5 14.0 %collective-permute-start.22 = (bf16[1024,1024]{1,0:T(8,128)(2,1)}, bf16[1024,1024]{1,0:T(8,128)(2,1)S(1)}, u32[]{:S(2)}, u32[]{:S(2)}) collective-permute-start(bf16[1024,1024]{1,0:T(8,128)(2,1)} %constant_dynamic-update-slice_fusion.3.n2_ref.refs_6_), channel_id=1, source_target_pairs={{0,4},{4,0},{1,5},{5,1},{2,6},{6,2},{3,7},{7,3},{8,12},{12,8},{9,1... | collective-permute-start | bytes 6291464 | tf_op jit(solution)/shard_map/ppermute | solution.py:432
  216.4 159.3 %reduce-scatter.5.cloned.1.call-start = ((), (), s32[]{:S(2)}) async-start(), calls=%async_computation.7 | async-start | bytes 3932160 | tf_op jit(solution)/shard_map/reduce_scatter | solution.py:645
  231.6 15.5 %collective-permute-start.24 = (bf16[1024,1152]{1,0:T(8,128)(2,1)}, bf16[1024,1152]{1,0:T(8,128)(2,1)}, u32[]{:S(2)}, u32[]{:S(2)}) collective-permute-start(bf16[1024,1152]{1,0:T(8,128)(2,1)} %get-tuple-element.151), channel_id=1, source_target_pairs={{0,4},{4,0},{1,5},{5,1},{2,6},{6,2},{3,7},{7,3},{8,12},{12,8},{9,1... | collective-permute-start | bytes 7077896 | tf_op jit(solution)/shard_map/ppermute | solution.py:432
  231.7 46.4 %collective-permute-start.29 = (bf16[1024,1024]{1,0:T(8,128)(2,1)}, bf16[1024,1024]{1,0:T(8,128)(2,1)}, u32[]{:S(2)}, u32[]{:S(2)}) collective-permute-start(bf16[1024,1024]{1,0:T(8,128)(2,1)} %get-tuple-element.153), channel_id=1, source_target_pairs={{0,4},{4,0},{1,5},{5,1},{2,6},{6,2},{3,7},{7,3},{8,12},{12,8},{9,1... | collective-permute-start | bytes 6291464 | tf_op jit(solution)/shard_map/ppermute | solution.py:432
  261.4 22.1 %collective-permute-start.26 = (bf16[256,1152]{1,0:T(8,128)(2,1)}, bf16[256,1152]{1,0:T(8,128)(2,1)S(1)}, u32[]{:S(2)}, u32[]{:S(2)}) collective-permute-start(bf16[256,1152]{1,0:T(8,128)(2,1)} %pad_maximum_fusion.9), channel_id=1, source_target_pairs={{0,8},{8,0},{16,24},{24,16},{1,9},{9,1},{17,25},{25,17},{2,10},{10... | collective-permute-start | bytes 1769480 | tf_op jit(solution)/shard_map/ppermute | solution.py:435
  262.8 20.7 %collective-permute-start.28 = (bf16[256,1152]{1,0:T(8,128)(2,1)}, bf16[256,1152]{1,0:T(8,128)(2,1)S(1)}, u32[]{:S(2)}, u32[]{:S(2)}) collective-permute-start(bf16[256,1152]{1,0:T(8,128)(2,1)} %pad_maximum_fusion.10), channel_id=1, source_target_pairs={{0,16},{8,24},{16,0},{24,8},{1,17},{9,25},{17,1},{25,9},{2,18},{10... | collective-permute-start | bytes 1769480 | tf_op jit(solution)/shard_map/ppermute | solution.py:435
  295.0 34.1 %all-to-all-start.1 = ((bf16[4,256,256]{2,1,0:T(8,128)(2,1)}), bf16[4,256,256]{2,1,0:T(8,128)(2,1)}, u32[]{:S(2)}, u32[]{:S(2)}) async-start(bf16[4,256,256]{2,1,0:T(8,128)(2,1)} %get-tuple-element.172), calls=%async_computation.1 | async-start | bytes 1048576 | tf_op jit(solution)/shard_map/all_to_all | solution.py:685
  301.1 30.0 %collective-permute-start.41 = (bf16[2,144,256]{2,1,0:T(8,128)(2,1)S(1)}, bf16[2,144,256]{2,1,0:T(8,128)(2,1)S(1)}, u32[]{:S(2)}, u32[]{:S(2)}) collective-permute-start(bf16[2,144,256]{2,1,0:T(8,128)(2,1)S(1)} %get-tuple-element.231), channel_id=1, source_target_pairs={{0,8},{8,0},{16,24},{24,16},{1,9},{9,1},{17,25},{25,17},{2,10},{10... | collective-permute-start | bytes 442376 | tf_op jit(solution)/shard_map/ppermute | solution.py:435
  302.4 30.2 %collective-permute-start.39 = (bf16[2,144,256]{2,1,0:T(8,128)(2,1)S(1)}, bf16[2,144,256]{2,1,0:T(8,128)(2,1)S(1)}, u32[]{:S(2)}, u32[]{:S(2)}) collective-permute-start(bf16[2,144,256]{2,1,0:T(8,128)(2,1)S(1)} %get-tuple-element.230), channel_id=1, source_target_pairs={{0,16},{8,24},{16,0},{24,8},{1,17},{9,25},{17,1},{25,9},{2,18},{10... | collective-permute-start | bytes 442376 | tf_op jit(solution)/shard_map/ppermute | solution.py:435
  329.1 20.6 %collective-permute-start.35 = (bf16[768,512]{1,0:T(8,128)(2,1)}, bf16[768,512]{1,0:T(8,128)(2,1)S(1)}, u32[]{:S(2)}, u32[]{:S(2)}) collective-permute-start(bf16[768,512]{1,0:T(8,128)(2,1)} %reduce-scatter.3.cloned.1.call-done.refs_0_), channel_id=1, source_target_pairs={{0,16},{8,24},{16,0},{24,8},{1,17},{9,25},{17,1},{25,9},{2,18},{10... | collective-permute-start | bytes 2359304 | tf_op jit(solution)/shard_map/ppermute | solution.py:435
  329.6 22.5 %collective-permute-start.34 = (bf16[768,512]{1,0:T(8,128)(2,1)}, bf16[768,512]{1,0:T(8,128)(2,1)S(1)}, u32[]{:S(2)}, u32[]{:S(2)}) collective-permute-start(bf16[768,512]{1,0:T(8,128)(2,1)} %reduce-scatter.3.cloned.1.call-done.refs_0_), channel_id=1, source_target_pairs={{0,8},{8,0},{16,24},{24,16},{1,9},{9,1},{17,25},{25,17},{2,10},{10... | collective-permute-start | bytes 2359304 | tf_op jit(solution)/shard_map/ppermute | solution.py:435
  331.2 25.0 %collective-permute-start.42 = (bf16[4,144,256]{2,1,0:T(8,128)(2,1)S(1)}, bf16[4,144,256]{2,1,0:T(8,128)(2,1)}, u32[]{:S(2)}, u32[]{:S(2)}) collective-permute-start(bf16[4,144,256]{2,1,0:T(8,128)(2,1)S(1)} %pad_maximum_fusion.19), channel_id=1, source_target_pairs={{0,16},{8,24},{16,0},{24,8},{1,17},{9,25},{17,1},{25,9},{2,18},{10... | collective-permute-start | bytes 884744 | tf_op jit(solution)/shard_map/ppermute | solution.py:435
  333.5 23.3 %collective-permute-start.40 = (bf16[4,144,256]{2,1,0:T(8,128)(2,1)}, bf16[4,144,256]{2,1,0:T(8,128)(2,1)}, u32[]{:S(2)}, u32[]{:S(2)}) collective-permute-start(bf16[4,144,256]{2,1,0:T(8,128)(2,1)} %pad_maximum_fusion.18), channel_id=1, source_target_pairs={{0,8},{8,0},{16,24},{24,16},{1,9},{9,1},{17,25},{25,17},{2,10},{10... | collective-permute-start | bytes 884744 | tf_op jit(solution)/shard_map/ppermute | solution.py:435
  350.7 24.9 %collective-permute-start.37 = (bf16[384,512]{1,0:T(8,128)(2,1)S(1)}, bf16[384,512]{1,0:T(8,128)(2,1)S(1)}, u32[]{:S(2)}, u32[]{:S(2)}) collective-permute-start(bf16[384,512]{1,0:T(8,128)(2,1)S(1)} %slice.355), channel_id=1, source_target_pairs={{0,8},{8,0},{16,24},{24,16},{1,9},{9,1},{17,25},{25,17},{2,10},{10... | collective-permute-start | bytes 1179656 | tf_op jit(solution)/shard_map/ppermute | solution.py:435
  353.1 22.5 %collective-permute-start.36 = (bf16[384,512]{1,0:T(8,128)(2,1)S(1)}, bf16[384,512]{1,0:T(8,128)(2,1)S(1)}, u32[]{:S(2)}, u32[]{:S(2)}) collective-permute-start(bf16[384,512]{1,0:T(8,128)(2,1)S(1)} %slice.354), channel_id=1, source_target_pairs={{0,16},{8,24},{16,0},{24,8},{1,17},{9,25},{17,1},{25,9},{2,18},{10... | collective-permute-start | bytes 1179656 | tf_op jit(solution)/shard_map/ppermute | solution.py:435
  391.6 17.4 %collective-permute-start.49 = (bf16[768,512]{1,0:T(8,128)(2,1)}, bf16[768,512]{1,0:T(8,128)(2,1)S(1)}, u32[]{:S(2)}, u32[]{:S(2)}) collective-permute-start(bf16[768,512]{1,0:T(8,128)(2,1)} %reduce-scatter.3.cloned.1.call-done.refs_0_), channel_id=1, source_target_pairs={{0,4},{4,0},{1,5},{5,1},{2,6},{6,2},{3,7},{7,3},{8,12},{12,8},{9,1... | collective-permute-start | bytes 2359304 | tf_op jit(solution)/shard_map/ppermute | solution.py:432
  391.6 18.9 %collective-permute-start.50 = (bf16[768,512]{1,0:T(8,128)(2,1)S(1)}, bf16[768,512]{1,0:T(8,128)(2,1)S(1)}, u32[]{:S(2)}, u32[]{:S(2)}) collective-permute-start(bf16[768,512]{1,0:T(8,128)(2,1)S(1)} %copy-done.21), channel_id=1, source_target_pairs={{0,4},{4,0},{1,5},{5,1},{2,6},{6,2},{3,7},{7,3},{8,12},{12,8},{9,1... | collective-permute-start | bytes 2359304 | tf_op jit(solution)/shard_map/ppermute | solution.py:432
  392.1 18.4 %collective-permute-start.51 = (bf16[768,512]{1,0:T(8,128)(2,1)S(1)}, bf16[768,512]{1,0:T(8,128)(2,1)S(1)}, u32[]{:S(2)}, u32[]{:S(2)}) collective-permute-start(bf16[768,512]{1,0:T(8,128)(2,1)S(1)} %copy-done.19), channel_id=1, source_target_pairs={{0,4},{4,0},{1,5},{5,1},{2,6},{6,2},{3,7},{7,3},{8,12},{12,8},{9,1... | collective-permute-start | bytes 2359304 | tf_op jit(solution)/shard_map/ppermute | solution.py:432
  397.4 13.8 %collective-permute-start.52 = (bf16[768,512]{1,0:T(8,128)(2,1)S(1)}, bf16[768,512]{1,0:T(8,128)(2,1)S(1)}, u32[]{:S(2)}, u32[]{:S(2)}) collective-permute-start(bf16[768,512]{1,0:T(8,128)(2,1)S(1)} %pad_maximum_fusion.6.refs_6_), channel_id=1, source_target_pairs={{0,4},{4,0},{1,5},{5,1},{2,6},{6,2},{3,7},{7,3},{8,12},{12,8},{9,1... | collective-permute-start | bytes 2359304 | tf_op jit(solution)/shard_map/ppermute | solution.py:432
  407.4 23.8 %collective-permute-start.54 = (bf16[768,512]{1,0:T(8,128)(2,1)}, bf16[768,512]{1,0:T(8,128)(2,1)}, u32[]{:S(2)}, u32[]{:S(2)}) collective-permute-start(bf16[768,512]{1,0:T(8,128)(2,1)} %reduce-scatter.5.cloned.1.call-done.refs_0_), channel_id=1, source_target_pairs={{0,16},{8,24},{16,0},{24,8},{1,17},{9,25},{17,1},{25,9},{2,18},{10... | collective-permute-start | bytes 2359304 | tf_op jit(solution)/shard_map/ppermute | solution.py:435
  408.9 22.3 %collective-permute-start.53 = (bf16[768,512]{1,0:T(8,128)(2,1)}, bf16[768,512]{1,0:T(8,128)(2,1)}, u32[]{:S(2)}, u32[]{:S(2)}) collective-permute-start(bf16[768,512]{1,0:T(8,128)(2,1)} %reduce-scatter.5.cloned.1.call-done.refs_0_), channel_id=1, source_target_pairs={{0,8},{8,0},{16,24},{24,16},{1,9},{9,1},{17,25},{25,17},{2,10},{10... | collective-permute-start | bytes 2359304 | tf_op jit(solution)/shard_map/ppermute | solution.py:435
  410.4 20.8 %collective-permute-start.48 = (bf16[256,1024]{1,0:T(8,128)(2,1)}, bf16[256,1024]{1,0:T(8,128)(2,1)}, u32[]{:S(2)}, u32[]{:S(2)}) collective-permute-start(bf16[256,1024]{1,0:T(8,128)(2,1)} %slice_bitcast_fusion), channel_id=1, source_target_pairs={{0,1},{1,2},{2,3},{3,0},{4,5},{5,6},{6,7},{7,4},{8,9},{9,10},{10,1... | collective-permute-start | bytes 1572872 | tf_op jit(solution)/shard_map/ppermute | solution.py:429
  410.5 18.1 %collective-permute-start.47 = (bf16[4,80,256]{2,1,0:T(8,128)(2,1)}, bf16[4,80,256]{2,1,0:T(8,128)(2,1)}, u32[]{:S(2)}, u32[]{:S(2)}) collective-permute-start(bf16[4,80,256]{2,1,0:T(8,128)(2,1)} %pad_maximum_fusion.22), channel_id=1, source_target_pairs={{0,16},{8,24},{16,0},{24,8},{1,17},{9,25},{17,1},{25,9},{2,18},{10... | collective-permute-start | bytes 491528 | tf_op jit(solution)/shard_map/ppermute | solution.py:435
  411.2 18.9 %collective-permute-start.45 = (bf16[4,80,256]{2,1,0:T(8,128)(2,1)S(1)}, bf16[4,80,256]{2,1,0:T(8,128)(2,1)S(1)}, u32[]{:S(2)}, u32[]{:S(2)}) collective-permute-start(bf16[4,80,256]{2,1,0:T(8,128)(2,1)S(1)} %pad_maximum_fusion.21), channel_id=1, source_target_pairs={{0,8},{8,0},{16,24},{24,16},{1,9},{9,1},{17,25},{25,17},{2,10},{10... | collective-permute-start | bytes 491528 | tf_op jit(solution)/shard_map/ppermute | solution.py:435
  428.7 45.8 %collective-permute-start.33 = (bf16[256,1024]{1,0:T(8,128)(2,1)}, bf16[256,1024]{1,0:T(8,128)(2,1)}, u32[]{:S(2)}, u32[]{:S(2)}) collective-permute-start(bf16[256,1024]{1,0:T(8,128)(2,1)} %pad_maximum_fusion.14), channel_id=1, source_target_pairs={{0,16},{8,24},{16,0},{24,8},{1,17},{9,25},{17,1},{25,9},{2,18},{10... | collective-permute-start | bytes 1572872 | tf_op jit(solution)/shard_map/ppermute | solution.py:435
  440.0 24.7 %collective-permute-start.69 = (bf16[384,512]{1,0:T(8,128)(2,1)}, bf16[384,512]{1,0:T(8,128)(2,1)S(1)}, u32[]{:S(2)}, u32[]{:S(2)}) collective-permute-start(bf16[384,512]{1,0:T(8,128)(2,1)} %slice.336), channel_id=1, source_target_pairs={{0,8},{8,0},{16,24},{24,16},{1,9},{9,1},{17,25},{25,17},{2,10},{10... | collective-permute-start | bytes 1179656 | tf_op jit(solution)/shard_map/ppermute | solution.py:435
  440.9 21.9 %collective-permute-start.68 = (bf16[384,512]{1,0:T(8,128)(2,1)}, bf16[384,512]{1,0:T(8,128)(2,1)}, u32[]{:S(2)}, u32[]{:S(2)}) collective-permute-start(bf16[384,512]{1,0:T(8,128)(2,1)} %slice.335), channel_id=1, source_target_pairs={{0,16},{8,24},{16,0},{24,8},{1,17},{9,25},{17,1},{25,9},{2,18},{10... | collective-permute-start | bytes 1179656 | tf_op jit(solution)/shard_map/ppermute | solution.py:435
  441.6 14.0 %collective-permute-start.55 = (bf16[256,1024]{1,0:T(8,128)(2,1)S(1)}, bf16[256,1024]{1,0:T(8,128)(2,1)S(1)}, u32[]{:S(2)}, u32[]{:S(2)}) collective-permute-start(bf16[256,1024]{1,0:T(8,128)(2,1)S(1)} %fusion.15), channel_id=1, source_target_pairs={{0,1},{1,2},{2,3},{3,0},{4,5},{5,6},{6,7},{7,4},{8,9},{9,10},{10,1... | collective-permute-start | bytes 1572872 | tf_op jit(solution)/shard_map/ppermute | solution.py:429
  443.4 18.4 %collective-permute-start.60 = (bf16[416,256]{1,0:T(8,128)(2,1)S(1)}, bf16[416,256]{1,0:T(8,128)(2,1)S(1)}, u32[]{:S(2)}, u32[]{:S(2)}) collective-permute-start(bf16[416,256]{1,0:T(8,128)(2,1)S(1)} %get-tuple-element.252), channel_id=1, source_target_pairs={{0,8},{8,0},{16,24},{24,16},{1,9},{9,1},{17,25},{25,17},{2,10},{10... | collective-permute-start | bytes 638984 | tf_op jit(solution)/shard_map/ppermute | solution.py:435
  461.8 13.2 %collective-permute-start.31 = (bf16[256,1024]{1,0:T(8,128)(2,1)}, bf16[256,1024]{1,0:T(8,128)(2,1)}, u32[]{:S(2)}, u32[]{:S(2)}) collective-permute-start(bf16[256,1024]{1,0:T(8,128)(2,1)} %pad_maximum_fusion.13), channel_id=1, source_target_pairs={{0,8},{8,0},{16,24},{24,16},{1,9},{9,1},{17,25},{25,17},{2,10},{10... | collective-permute-start | bytes 1572872 | tf_op jit(solution)/shard_map/ppermute | solution.py:435
  462.6 12.5 %collective-permute-start.56 = (bf16[256,1024]{1,0:T(8,128)(2,1)}, bf16[256,1024]{1,0:T(8,128)(2,1)}, u32[]{:S(2)}, u32[]{:S(2)}) collective-permute-start(bf16[256,1024]{1,0:T(8,128)(2,1)} %fusion.14), channel_id=1, source_target_pairs={{0,1},{1,2},{2,3},{3,0},{4,5},{5,6},{6,7},{7,4},{8,9},{9,10},{10,1... | collective-permute-start | bytes 1572872 | tf_op jit(solution)/shard_map/ppermute | solution.py:429
  467.5 14.2 %collective-permute-start.66 = (bf16[768,512]{1,0:T(8,128)(2,1)}, bf16[768,512]{1,0:T(8,128)(2,1)}, u32[]{:S(2)}, u32[]{:S(2)}) collective-permute-start(bf16[768,512]{1,0:T(8,128)(2,1)} %collective-permute-done.53.refs_2_), channel_id=1, source_target_pairs={{0,4},{4,0},{1,5},{5,1},{2,6},{6,2},{3,7},{7,3},{8,12},{12,8},{9,1... | collective-permute-start | bytes 2359304 | tf_op jit(solution)/shard_map/ppermute | solution.py:432
  475.2 15.7 %collective-permute-start.64 = (bf16[4,416,256]{2,1,0:T(8,128)(2,1)}, bf16[4,416,256]{2,1,0:T(8,128)(2,1)}, u32[]{:S(2)}, u32[]{:S(2)}) collective-permute-start(bf16[4,416,256]{2,1,0:T(8,128)(2,1)} %get-tuple-element.237), channel_id=1, source_target_pairs={{0,4},{4,0},{1,5},{5,1},{2,6},{6,2},{3,7},{7,3},{8,12},{12,8},{9,1... | collective-permute-start | bytes 2555912 | tf_op jit(solution)/shard_map/ppermute | solution.py:432
  (83 other events, 634.7 us)
Sparse Core Ops, SparseCore 0:
  80.8 71.7 all-gather.2
  154.2 62.1 all-gather.4
  219.2 58.8 reduce-scatter.2
  283.7 66.3 reduce-scatter.4

commit v5 on v4

--- a/solution.py
+++ b/solution.py
@@ -14,6 +14,7 @@
 HEAD = 64
 LANES = 128
 MIX_LOW = 64
+SCALE = 0.02
 
 EPS = 1e-06
 ROPE_BASE = 10000.0
@@ -81,32 +82,22 @@
 
 
 def front_kernel(
-    block, heads, kv_heads, parts, place_ref, *refs
+    block, heads, kv_heads, place_ref, x_ref, gain_ref, mine_ref, mate_ref, cos_ref, sin_ref, segc_ref, segr_ref,
+    w_ref, normed_ref, q_ref, k_ref, v_ref, att_ref, lse_ref, out_s,
 ):
-    chunks = refs[:parts]
-    (gain_ref, mine_ref, mate_ref, cos_ref, sin_ref, segc_ref, segr_ref,
-     x_ref, w_ref, normed_ref, q_ref, k_ref, v_ref, att_ref, lse_ref, out_s, sems) = refs[parts:]
     seq = x_ref.shape[0]
     blocks = seq // block
     group = heads // kv_heads
     qw, kw = heads * HEAD, kv_heads * HEAD
     z = place_ref[0]
-    slab = w_ref.shape[0] // parts
+    slab = w_ref.shape[0] // blocks
     part = slab // (2 * mine_ref.shape[0])
-    copies = []
-    for i in range(parts):
-        at = chunk_of(ring_chunk(z, i, parts), block)
-        copies.append(pltpu.make_async_copy(chunks[i], x_ref.at[at, :], sems.at[i]))
-    for copy in copies:
-        copy.start()
     for c, piece_ref in enumerate((mine_ref, mate_ref)):
         for j in range(piece_ref.shape[0]):
             at = peer(place_ref, c, j) * part
-            for i in range(parts):
-                start = pl.multiple_of(ring_chunk(z, i, parts) * slab + at, part)
+            for i in range(blocks):
+                start = pl.multiple_of(ring_chunk(z, i, blocks) * slab + at, part)
                 w_ref[pl.ds(start, part), :] = piece_ref[j, i, :part, :]
-    for copy in copies:
-        copy.wait()
 
     def project(i, carry):
         rows = pl.ds(pl.multiple_of(i * block, block), block)
@@ -143,20 +134,24 @@
         return carry
 
     lax.fori_loop(0, heads, one_head, 0)
-    for h in range(heads):
-        att_ref[:, h * HEAD : (h + 1) * HEAD] = out_s[h].astype(BF16)
+    for i in range(blocks):
+        k = lax.rem(i - z + blocks, blocks)
+        for h in range(heads):
+            att_ref[k, :, h * HEAD : (h + 1) * HEAD] = out_s[h, i * block : (i + 1) * block, :].astype(BF16)
 
 
 def back_kernel(
-    block, heads, kv_heads, q_ref, k_ref, v_ref, do_ref, lse_ref, segc_ref, segr_ref,
-    raw_ref, do_s, dq_s, dk_s, dv_s,
+    block, heads, kv_heads, place_ref, q_ref, k_ref, v_ref, lse_ref, segc_ref, segr_ref, *refs
 ):
-    seq = do_ref.shape[0]
+    seq = q_ref.shape[1]
     blocks = seq // block
+    raw_ref, do_s, dq_s, dk_s, dv_s = refs[blocks:]
     group = heads // kv_heads
     qw, kw = heads * HEAD, kv_heads * HEAD
-    for h in range(heads):
-        do_s[h] = do_ref[:, h * HEAD : (h + 1) * HEAD]
+    for k in range(blocks):
+        at = chunk_of(lax.rem(place_ref[0] + k, blocks), block)
+        for h in range(heads):
+            do_s[h, at, :] = refs[k][:, h * HEAD : (h + 1) * HEAD]
     dk_s[...] = jnp.zeros_like(dk_s)
     dv_s[...] = jnp.zeros_like(dv_s)
 
@@ -189,7 +184,7 @@
 
 
 def finish_kernel(
-    block, turned, place_ref, raw_ref, x_ref, normed_ref, w_ref, cos_ref, sin_ref, ng_ref, dw_ref, gain_ref, g_s,
+    block, turned, raw_ref, x_ref, normed_ref, w_ref, cos_ref, sin_ref, ng_ref, dw_ref, gain_ref, g_s,
 ):
     seq = x_ref.shape[0]
     blocks = seq // block
@@ -202,7 +197,7 @@
         ng = dot_nt(g_s[rows, :], w_ref[...])
         x = x_ref[rows, :].astype(F32)
         gain_ref[...] += jnp.sum(ng * (x * inverse_rms(x)), axis=0, keepdims=True)
-        ng_ref[ring_chunk(place_ref[0], i, blocks)] = ng.astype(BF16)
+        ng_ref[rows, :] = ng.astype(BF16)
         return carry
 
     lax.fori_loop(0, blocks, finish, 0)
@@ -218,27 +213,29 @@
 
 
 def mid_kernel(
-    place_ref, x_ref, att_ref, mine_ref, mate_ref, gain_ref, router_ref, mask_ref,
-    hidden_ref, normed_ref, gates_ref, ow_ref,
+    place_ref, x_ref, mine_ref, mate_ref, gain_ref, router_ref, mask_ref, *refs
 ):
+    hidden_ref, normed_ref, gates_ref, ow_ref = refs[-4:]
+    att_refs = refs[:-4]
     parts, width = ow_ref.shape[0], ow_ref.shape[2]
     share = ow_ref.shape[1] // (2 * mine_ref.shape[0])
     fold = mine_ref.shape[3] // width
     lines = share // fold
-    skip = mine_ref.shape[2] - lines
+    skip = ow_ref.shape[0] * width // (2 * parts * mine_ref.shape[0])
     for c, piece_ref in enumerate((mine_ref, mate_ref)):
         for j in range(piece_ref.shape[0]):
             at = peer(place_ref, c, j) * share
             for k in range(parts):
                 for f in range(fold):
                     start = pl.multiple_of(at + f * lines, lines)
-                    ow_ref[k, pl.ds(start, lines), :] = piece_ref[j, k, skip:, f * width : (f + 1) * width]
-    depth = att_ref.shape[2]
+                    ow_ref[k, pl.ds(start, lines), :] = piece_ref[j, k, skip : skip + lines, f * width : (f + 1) * width]
+    depth = att_refs[0].shape[1]
     for j in range(parts):
         cols = chunk_of(ring_chunk(place_ref[0], j, parts), width)
         total = x_ref[:, cols].astype(F32)
-        for i in range(att_ref.shape[0]):
-            total = total + dot(att_ref[i], ow_ref[j, i * depth : (i + 1) * depth, :])
+        for i in range(parts):
+            at = chunk_of(ring_chunk(place_ref[0], i, parts), depth)
+            total = total + dot(att_refs[i][...], ow_ref[j, at, :])
         hidden_ref[:, cols] = total
     hidden = hidden_ref[...]
     normed = (hidden * inverse_rms(hidden) * gain_ref[...]).astype(BF16)
@@ -247,12 +244,14 @@
 
 
 def mid_back_kernel(
-    place_ref, hidden_ref, nb0_ref, nb1_ref, nb2_ref, dy_ref, gates_ref, normed_ref, router_ref, gain_ref, ow_ref, att_ref,
-    hg_ref, ag_ref, owg_ref, fg_ref, rg_ref, aog_s,
+    place_ref, hidden_ref, dy_ref, gates_ref, normed_ref, router_ref, gain_ref, ow_ref, *refs
 ):
+    hg_ref, ag_ref, owg_ref, fg_ref, rg_ref, aog_s = refs[-6:]
+    att_refs = refs[: ow_ref.shape[0]]
+    nb_refs = refs[ow_ref.shape[0] : -6]
     gates = gates_ref[...]
     width_all = hidden_ref.shape[1]
-    nb = sum(ref[...].astype(F32) for ref in (nb1_ref, nb2_ref)) + nb0_ref[...].astype(F32)
+    nb = sum(ref[...].astype(F32) for ref in nb_refs)
     mix = nb[:, width_all:]
     mix = mix + pltpu.roll(mix, LANES - MIX_LOW, 1)
     lg = gates * (mix - jnp.sum(gates * mix, axis=-1, keepdims=True))
@@ -270,9 +269,9 @@
     hg_ref[...] = hg
     aog_s[...] = hg.astype(BF16)
     parts, width = ow_ref.shape[0], ow_ref.shape[2]
-    groups, _, depth = att_ref.shape
-    for i in range(groups):
-        rows = slice(i * depth, (i + 1) * depth)
+    depth = att_refs[0].shape[1]
+    for i in range(parts):
+        rows = chunk_of(ring_chunk(place_ref[0], i, parts), depth)
         total = None
         for j in range(parts):
             chunk = ring_chunk(place_ref[0], j, parts)
@@ -280,7 +279,7 @@
             total = part if total is None else total + part
         ag_ref[i] = total.astype(BF16)
         for j in range(parts):
-            owg_ref[j, rows, :] = dot_tn(att_ref[i], aog_s[:, j * width : (j + 1) * width]).astype(BF16)
+            owg_ref[j, rows, :] = dot_tn(att_refs[i][...], aog_s[:, j * width : (j + 1) * width]).astype(BF16)
 
 
 def expert_kernel(parts, e, place_ref, n2_ref, dyx_ref, router_ref, w_ref, *refs):
@@ -399,7 +398,7 @@
 
 
 def cost(flops, traffic):
-    return pl.CostEstimate(flops=int(flops), bytes_accessed=int(traffic), transcendentals=0)
+    return pl.CostEstimate(flops=int(flops * SCALE), bytes_accessed=int(traffic * SCALE), transcendentals=0)
 
 
 def per_device(
@@ -459,12 +458,14 @@
         to_x = jnp.concatenate([blocks[1][:half], plus(blocks[1][half:], high)], axis=0)
         return [blocks[0], flip(to_x, 1), flip(to_y, 2)]
 
-    chunks = [tokens, shift(tokens)]
+    x_all = lax.all_gather(tokens, "shard", axis=0, tiled=True)
 
     pack = jnp.concatenate(
         [attn_gain[None], ffn_gain[None], segment_ids.astype(BF16)[None], router_weight.T], axis=0
     )
-    packs = [pack] + [shift(pack, k) for k in range(1, n)]
+    pack_rows = 16
+    pack = jnp.pad(pack, ((0, 2 * pack_rows - pack.shape[0]), (0, 0)))
+    pack = jnp.concatenate([pack[:pack_rows], pack[pack_rows:]], axis=1)
     part_rows = slab // ep
     by_dest = jnp.concatenate(
         [
@@ -479,30 +480,33 @@
     ow_mine = ow_mine.reshape(fold, ow_rows // fold, slab).transpose(1, 0, 2).reshape(ow_rows // fold, cols)
 
     def piece(k):
-        return jnp.concatenate([pick(by_dest, lax.rem(z + k, n), 1), ow_mine], axis=0)
+        return jnp.concatenate([pick(by_dest, lax.rem(z + k, n), 1), ow_mine, pack], axis=0)
 
     dense_mine = [piece(0)] + [shift(piece(k), k) for k in range(1, n)]
     ids = jnp.arange(experts, dtype=jnp.int32)
     routed = jnp.any(routes[:, :, None] == ids[None, None, :], axis=1)
     mask_own = jnp.pad(routed.astype(F32), ((0, 0), (0, LANES - experts)))
     dyx_mine = around(jnp.concatenate([cotangent, mask_own.astype(BF16)], axis=1))
-    chunks[1], packs, dense_mine = lax.optimization_barrier((chunks[1], packs, dense_mine))
-    chunks.append(shift(chunks[1]))
-    dense_mine = around(jnp.stack(dense_mine))
-    chunks[2], dense_mine, dyx_mine = lax.optimization_barrier((chunks[2], dense_mine, dyx_mine))
-    for _ in range(n - 3):
-        chunks.append(shift(chunks[-1]))
-    dense_mine = jnp.stack(dense_mine)
+
+    folds = width // ff
+    packed = []
+    for e in range(own):
+        gate, up, down = (pick(w, r * own + e, 0) for w in (gate_weight, up_weight, down_weight))
+        down = [down[:, c * ff : (c + 1) * ff] for c in range(folds)]
+        packed.append(jnp.concatenate([gate, up] + down, axis=0))
+    packed, dense_mine = lax.optimization_barrier((packed, dense_mine))
+    weights = [lax.all_gather(w, "shard", axis=0, tiled=True) for w in packed]
+
+    packs = absolute([p[-pack_rows:] for p in dense_mine])
+    packs = jnp.concatenate([packs[:, :, :slab], packs[:, :, slab : 2 * slab]], axis=1)
+    dense_mine = jnp.stack(around(jnp.stack([p[:-pack_rows] for p in dense_mine])))
     dense_mate = swap(dense_mine)
-    packs = absolute(packs)
     gain1 = packs[:, 0, :].reshape(1, width).astype(F32)
     gain2 = packs[:, 1, :].reshape(1, width).astype(F32)
     segments = packs[:, 2, :].reshape(seq).astype(F32)
     seg_col, seg_row = segments[:, None], segments[None, :]
-    router = jnp.pad(packs[:, 3:, :].transpose(0, 2, 1).reshape(width, experts), ((0, 0), (0, LANES - experts)))
-
-    dyx_mine = jnp.concatenate(dyx_mine, axis=0)
-    dyx_mate = swap(dyx_mine)
+    router = jnp.pad(packs[:, 3 : 3 + experts, :].transpose(0, 2, 1).reshape(width, experts), ((0, 0), (0, LANES - experts)))
+
 
     positions = jnp.arange(seq, dtype=jnp.int32).astype(F32)
     frequency = ROPE_BASE ** (-jnp.arange(HEAD // 2, dtype=F32) / (HEAD // 2))
@@ -511,38 +515,31 @@
     cosine = jnp.concatenate([cosine] * 4, axis=1)
     sine = jnp.concatenate([-sine, sine] * 2, axis=1)
 
-    folds = width // ff
-    packed = []
-    for e in range(own):
-        gate, up, down = (pick(w, r * own + e, 0) for w in (gate_weight, up_weight, down_weight))
-        down = [down[:, c * ff : (c + 1) * ff] for c in range(folds)]
-        packed.append(jnp.concatenate([gate, up] + down, axis=0))
-    packed, chunks = lax.optimization_barrier((packed, chunks))
-    weights = [lax.all_gather(w, "shard", axis=0, tiled=True) for w in packed]
-
-    x_all, w_qkv, normed, q, k, v, att, lse = pl.pallas_call(
-        functools.partial(front_kernel, rows, heads, kv_heads, n),
-        in_specs=[smem] + [hbm] * n + [vmem] * 7,
+    x_all, dyx_mine = lax.optimization_barrier((x_all, dyx_mine))
+    dyx_mine = jnp.concatenate(dyx_mine, axis=0)
+    dyx_mate = swap(dyx_mine)
+    w_qkv, normed, q, k, v, att, lse = pl.pallas_call(
+        functools.partial(front_kernel, rows, heads, kv_heads),
+        in_specs=[smem] + [vmem] * 8,
         out_shape=(
-            sds((seq, width), BF16),
             sds((width, cols), BF16),
             sds((seq, width), BF16),
             sds((heads, seq, HEAD), BF16),
             sds((kv_heads, seq, HEAD), BF16),
             sds((kv_heads, seq, HEAD), BF16),
-            sds((seq, qw), BF16),
+            sds((n, rows, qw), BF16),
             sds((heads, seq, 1), F32),
         ),
-        scratch_shapes=[pltpu.VMEM((heads, seq, HEAD), F32), pltpu.SemaphoreType.DMA((n,))],
+        scratch_shapes=[pltpu.VMEM((heads, seq, HEAD), F32)],
         compiler_params=params(),
         cost_estimate=cost(2 * seq * width * cols, 60e6),
         name="front",
-    )(place, *chunks, gain1, dense_mine, dense_mate, cosine, sine, seg_col, seg_row)
-
-    att = lax.all_to_all(att.reshape(n, rows, qw), "shard", 0, 0)
+    )(place, x_all, gain1, dense_mine, dense_mate, cosine, sine, seg_col, seg_row)
+
+    att = [att[0]] + [shift(att[k], k) for k in range(1, n)]
     hidden, normed2, gates_own, ow = pl.pallas_call(
         mid_kernel,
-        in_specs=[smem] + [vmem] * 7,
+        in_specs=[smem] + [vmem] * (6 + n),
         out_shape=(
             sds((rows, width), F32),
             sds((rows, width), BF16),
@@ -552,7 +549,7 @@
         compiler_params=params(),
         cost_estimate=cost(2 * rows * width * width, 14e6),
         name="mid",
-    )(place, tokens, att, dense_mine, dense_mate, gain2, router, mask_own)
+    )(place, tokens, dense_mine, dense_mate, gain2, router, mask_own, *att)
 
     n2_mine = jnp.concatenate(around(normed2), axis=0)
     n2_mate = swap(n2_mine)
@@ -639,9 +636,10 @@
         if e < own - 1:
             grads, weights[e + 1] = lax.optimization_barrier((grads, weights[e + 1]))
         else:
-            nb_parts = plane_sum(spread(plus(previous_mine[1], nb_got)))
+            nb_parts = spread(plus(previous_mine[1], nb_got))
+            nb_parts = [nb_parts[0]] + [flip(nb_parts[j], j) for j in range(1, yx)]
             moe_sum = plus(previous_mine[0], moe_got)
-            nb_parts, moe_sum, grads = lax.optimization_barrier((nb_parts, moe_sum, grads))
+            nb_parts, moe_sum, grads, owned = lax.optimization_barrier((nb_parts, moe_sum, grads, owned))
         grads = lax.psum_scatter(grads, "shard", scatter_dimension=0, tiled=True)
         if hi > 1:
             grads = lax.psum(grads.astype(F32), "hi").astype(BF16)
@@ -649,7 +647,7 @@
 
     hidden_grad, att_grad, ow_grad, ffn_grad, router_grad = pl.pallas_call(
         mid_back_kernel,
-        in_specs=[smem] + [vmem] * 11,
+        in_specs=[smem] + [vmem] * (7 + n + yx),
         out_shape=(
             sds((rows, width), F32),
             sds((n, rows, qw), BF16),
@@ -661,7 +659,7 @@
         compiler_params=params(),
         cost_estimate=cost(4 * rows * width * width, 20e6),
         name="mid_back",
-    )(place, hidden, *nb_parts, cotangent, gates_own, normed2, router, gain2, ow, att)
+    )(place, hidden, cotangent, gates_own, normed2, router, gain2, ow, *att, *nb_parts)
 
     kvw = 2 * kw
     wide = max(slab, qw, kvw)
@@ -682,35 +680,12 @@
         parts = plane_sum([pick(dense, lax.bitwise_xor(chip, jnp.int32(j)), 0) for j in range(yx)])
         return sum(p.astype(F32) for p in parts).astype(BF16)
 
-    att_grad = lax.all_to_all(att_grad, "shard", 0, 0).reshape(seq, qw)
-    att_grad, owned[0] = lax.optimization_barrier((att_grad, owned[0]))
-    early = around(owned[0])
+    att_grad = [att_grad[0]] + [shift(att_grad[k], n - k) for k in range(1, n)]
+    early = (owned[0], flip(owned[0], 1), flip(owned[0], 2))
+    att_grad, early = lax.optimization_barrier((att_grad, early))
+    early = across_too(*early)
     small = rows_of(jnp.concatenate([ffn_grad, router_grad[:experts]], axis=0))
     dense_early = dense_sum([widen(ow_grad.reshape(n, ep, ow_rows, slab)), small])
-    raw = pl.pallas_call(
-        functools.partial(back_kernel, rows, heads, kv_heads),
-        out_shape=sds((seq, cols), F32),
-        scratch_shapes=[
-            pltpu.VMEM((heads, seq, HEAD), BF16),
-            pltpu.VMEM((heads, seq, HEAD), F32),
-            pltpu.VMEM((kv_heads, seq, HEAD), F32),
-            pltpu.VMEM((kv_heads, seq, HEAD), F32),
-        ],
-        compiler_params=params(),
-        cost_estimate=cost(2 * seq * width * cols, 52e6),
-        name="back",
-    )(q, k, v, att_grad, lse, seg_col, seg_row)
-    raw, owned, early, dense_early = lax.optimization_barrier((raw, owned, early, dense_early))
-    ng, qkv_grad, gain_grad = pl.pallas_call(
-        functools.partial(finish_kernel, rows, qw + kw),
-        in_specs=[smem] + [vmem] * 6,
-        out_shape=(sds((n, rows, width), BF16), sds((width, cols), BF16), sds((1, width), F32)),
-        scratch_shapes=[pltpu.VMEM((seq, cols), BF16)],
-        compiler_params=params(),
-        cost_estimate=cost(4 * seq * width * cols, 30e6),
-        name="finish",
-    )(place, raw, x_all, normed, w_qkv, cosine, sine)
-    qkv_rows = qkv_grad.reshape(n, ep, part_rows, cols)
     def share(e, mine, shared):
         pieces = [p for one in mine for p in (one, swap(one))]
 
@@ -740,31 +715,52 @@
             name="share",
         )(place, *pieces, *shared)
 
+    raw = pl.pallas_call(
+        functools.partial(back_kernel, rows, heads, kv_heads),
+        in_specs=[smem] + [vmem] * (6 + n),
+        out_shape=sds((seq, cols), F32),
+        scratch_shapes=[
+            pltpu.VMEM((heads, seq, HEAD), BF16),
+            pltpu.VMEM((heads, seq, HEAD), F32),
+            pltpu.VMEM((kv_heads, seq, HEAD), F32),
+            pltpu.VMEM((kv_heads, seq, HEAD), F32),
+        ],
+        compiler_params=params(),
+        cost_estimate=cost(2 * seq * width * cols, 52e6),
+        name="back",
+    )(place, q, k, v, lse, seg_col, seg_row, *att_grad)
+    raw, early, dense_early, owned = lax.optimization_barrier((raw, early, dense_early, owned))
+    moe_parts = plane_sum(spread(moe_sum))
+    shared = share(0, early, ())
+    ng, qkv_grad, gain_grad = pl.pallas_call(
+        functools.partial(finish_kernel, rows, qw + kw),
+        out_shape=(sds((seq, width), BF16), sds((width, cols), BF16), sds((1, width), F32)),
+        scratch_shapes=[pltpu.VMEM((seq, cols), BF16)],
+        compiler_params=params(),
+        cost_estimate=cost(4 * seq * width * cols, 30e6),
+        name="finish",
+    )(raw, x_all, normed, w_qkv, cosine, sine)
+    qkv_rows = qkv_grad.reshape(n, ep, part_rows, cols)
+    part = lax.psum_scatter(ng, "shard", scatter_dimension=0, tiled=True).astype(F32)
+    last = [(value, flip(value, 1), flip(value, 2)) for value in owned[1:]]
     dense = dense_sum([rows_of(gain_grad), widen(qkv_rows[..., :qw]), widen(qkv_rows[..., qw:])])
     dense = jnp.concatenate([dense_early, dense], axis=1)
     if hi > 1:
         dense = lax.psum(dense.astype(F32), "hi").astype(BF16)
-    got = shift(ng[1])
-    shared = share(0, early, ())
-    last = [(value, flip(value, 1), flip(value, 2)) for value in owned[1:]]
-    dense, got, shared, last = lax.optimization_barrier((dense, got, shared, last))
+    dense, last, shared, moe_parts = lax.optimization_barrier((dense, last, shared, moe_parts))
     for e in range(1, own):
         shared = share(e, across_too(*last[e - 1]), shared)
-    for step in range(2, n):
-        got = shift((got.astype(F32) + ng[step].astype(F32)).astype(BF16))
-    part = got.astype(F32) + ng[0].astype(F32)
+    output = (hidden + sum(p.astype(F32) for p in moe_parts)).astype(BF16)
+
+
+    dense = [pick(dense, z, 0)] + [shift(pick(dense, lax.rem(z + k, n), 0), k) for k in range(1, n)]
+    part, dense, shared = lax.optimization_barrier((part, dense, shared))
     x = tokens.astype(F32)
     inv = inverse_rms(x)
     scaled = x * inv
     w1 = part * gain1
     input_grad = hidden_grad + inv * (w1 - scaled * jnp.mean(w1 * scaled, axis=-1, keepdims=True))
 
-    moe_parts = plane_sum(spread(moe_sum))
-    output = (hidden + sum(p.astype(F32) for p in moe_parts)).astype(BF16)
-
-    gate_grad, up_grad, down_grad = (g.reshape((experts,) + g.shape[2:]) for g in shared)
-
-    dense = [pick(dense, z, 0)] + [shift(pick(dense, lax.rem(z + k, n), 0), k) for k in range(1, n)]
     cut = ow_rows + 2 * small_rows
     summed = sum(p[:cut].astype(F32) for p in dense).astype(BF16)
     kept = absolute([p[cut:] for p in dense]).reshape(n * 2 * part_rows, wide)
@@ -775,6 +771,8 @@
     small_full = full[:, ow_rows : ow_rows + small_rows, :slab].reshape(-1, slab).astype(F32)
     gain_full = full[0, ow_rows + small_rows, :slab].astype(F32)
     kept = full[:, cut:].reshape(ep, n, 2, part_rows, wide)
+
+    gate_grad, up_grad, down_grad = (g.reshape((experts,) + g.shape[2:]) for g in shared)
 
     def columns(which, start, size):
         part = kept[:, :, which, :, start : start + size]

time: 517 us -> 501 us (0.969)
  waiting for transfers between devices: 164 us -> 148 us
  other arithmetic: 48.7 us -> 41.8 us
  local copies, waits for them, and re-layouts: 40.6 us -> 46.9 us
    all_to_all x2 -> x0, waiting for transfers between devices: 53.3 us -> none  [the longest x1 27.2 us: per_device(): att = lax.all_to_all(att.reshape(n, rows, qw), 'shard', 0, 0)]
    ppermute x40 -> x39, waiting for transfers between devices: 72.2 us -> 99.6 us  [flip(): return lax.ppermute(value, 'yx', [(i, i ^ j) for i in range(yx)])]
    ppermute x15 -> x12, starting transfers between devices: 12.9 us -> 30.7 us  [shift(): return lax.ppermute(value, 'shard', [(i, (i + k) % n) for i in range(n)])]
    ppermute x15 -> x12, waiting for transfers between devices: 33.9 us -> 43.5 us  [shift(): return lax.ppermute(value, 'shard', [(i, (i + k) % n) for i in range(n)])]
    ppermute x40 -> x39, starting transfers between devices: 55.9 us -> 46.4 us  [flip(): return lax.ppermute(value, 'yx', [(i, i ^ j) for i in range(yx)])]
    all_to_all x2 -> x0, starting transfers between devices: 7.97 us -> none  [the longest x1 4.36 us: per_device(): att_grad = lax.all_to_all(att_grad, 'shard', 0, 0).reshape(seq, qw)]
    convert_element_type x9 -> x8, other arithmetic: 10.7 us -> 7.85 us  [plus(): return (one.astype(F32) + other.astype(F32)).astype(BF16)]
    unnamed x136 -> x110, local copies, waits for them, and re-layouts: 19.2 us -> 16.5 us
  transfers between devices with their start and end apart: 77 -> 73, of which waited for: 30 -> 29; matrix products, arithmetic and copies ran while one was open for 13% -> 14% of each run, Pallas kernels for 30% -> 31%
where the time goes in v5:
time: 501 us; the launch traced here: 491 us
  Pallas kernels  159 us (32%)
  waiting for transfers between devices  148 us (30%)
  starting transfers between devices  79.4 us (16%)
  local copies, waits for them, and re-layouts  46.9 us (9%)
  other arithmetic  41.8 us (8%)
  between operations  15.9 us (3%)
    ppermute x39, waiting for transfers between devices, flip(): return lax.ppermute(value, 'yx', [(i, i ^ j) for i in range(yx)])  99.6 us
    pallas_call x4, Pallas kernels, run_expert(): pl.pallas_call(functools.partial(expert_kernel, n, e), grid=(steps,), in_...  57.7 us
    ppermute x39, starting transfers between devices, flip(): return lax.ppermute(value, 'yx', [(i, i ^ j) for i in range(yx)])  46.4 us
    ppermute x12, waiting for transfers between devices, shift(): return lax.ppermute(value, 'shard', [(i, (i + k) % n) for i in range(n)])  43.5 us
    ppermute x12, starting transfers between devices, shift(): return lax.ppermute(value, 'shard', [(i, (i + k) % n) for i in range(n)])  30.7 us
    pallas_call x2, Pallas kernels, weight_grads(): pl.pallas_call(functools.partial(expert_grad_kernel, n, steps), grid=(2 *...  27.3 us
    pallas_call x1, Pallas kernels, per_device(): pl.pallas_call(functools.partial(front_kernel, rows, heads, kv_heads), in...  19.1 us
    pallas_call x2, Pallas kernels, share(): pl.pallas_call(functools.partial(share_kernel, ep), grid_spec=pltpu.Prefe...  18.4 us
  transfers between devices with their start and end apart: 73, of which 29 were waited for; matrix products, arithmetic and copies ran while one was open for 14% of the time, Pallas kernels for 31%

profile of v5, /device:TPU:0, one launch (start us, length us, event | category | flops | bytes accessed | tf_op | source)
XLA Modules:
  0.0 491.2 jit_solution(15857262142768131045)
XLA Ops:
  12.5 3.1 collective-permute-start
  15.6 2.6 collective-permute-start.1
  23.9 6.4 %collective-permute-done.1 = bf16[112,512]{1,0:T(8,128)(2,1)S(1)} collective-permute-done((bf16[112,512]{1,0:T(8,128)(2,1)S(1)}, bf16[112,512]{1,0:T(8,128)(2,1)S(1)}, u32[]{:S(2)}, u32[]{:S(2)}) %collective-permute-start.1) | collective-permute-done | bytes 114720 | tf_op jit(solution)/shard_map/ppermute | solution.py:428
  40.7 14.7 %collective-permute-done.4 = bf16[4,96,512]{2,1,0:T(8,128)(2,1)S(1)} collective-permute-done((bf16[4,96,512]{2,1,0:T(8,128)(2,1)S(1)}, bf16[4,96,512]{2,1,0:T(8,128)(2,1)S(1)}, u32[]{:S(2)}, u32[]{:S(2)}) %collective-permute-start.4) | collective-permute-done | bytes 393248 | tf_op jit(solution)/shard_map/ppermute | solution.py:434
  57.6 3.5 collective-permute-done.6
  72.1 2.9 collective-permute-done.11
  75.0 2.8 collective-permute-done.10
  77.8 1.9 pad_maximum_fusion.8
  80.9 19.1 %front.1 = (bf16[1024,512]{1,0:T(8,128)(2,1)}, bf16[1024,1024]{1,0:T(8,128)(2,1)}, bf16[4,1024,64]{2,1,0:T(8,128)(2,1)}, bf16[2,1024,64]{2,1,0:T(8,128)(2,1)}, b...) custom-call(s32[4]{0:T(128)} %pad_add_fusion.place_ref, ...), custom_call_target="tpu_custom_call" | custom-call | flops 21474836 | bytes 1200000 | tf_op jit(solution)/shard_map/front/pallas_call | solution.py:521
  101.7 11.2 %collective-permute-start.12 = (bf16[256,256]{1,0:T(8,128)(2,1)S(1)}, bf16[256,256]{1,0:T(8,128)(2,1)S(1)}, u32[]{:S(2)}, u32[]{:S(2)}) collective-permute-start(bf16[256,256]{1,0:T(8,128)(2,1)S(1)} %get-tuple-element.254), channel_id=1, source_target_pairs={{0,1},{1,2},{2,3},{3,0},{4,5},{5,6},{6,7},{7,4},{8,9},{9,10},{10,1... | collective-permute-start | bytes 393224 | tf_op jit(solution)/shard_map/ppermute | solution.py:428
  112.9 2.4 collective-permute-start.14
  116.4 3.2 collective-permute-done.12.refs_1_
  119.5 7.4 %collective-permute-done.13.refs_2_ = bf16[256,256]{1,0:T(8,128)(2,1)S(1)} collective-permute-done((bf16[256,256]{1,0:T(8,128)(2,1)S(1)}, bf16[256,256]{1,0:T(8,128)(2,1)S(1)}, u32[]{:S(2)}, u32[]{:S(2)}) %collective-permute-start.13) | collective-permute-done | bytes 131104 | tf_op jit(solution)/shard_map/ppermute | solution.py:428
  126.9 3.2 collective-permute-done.14.refs_3_
  130.8 4.6 mid.1
  140.0 7.8 %collective-permute-done.15 = bf16[256,1024]{1,0:T(8,128)(2,1)S(1)} collective-permute-done((bf16[256,1024]{1,0:T(8,128)(2,1)}, bf16[256,1024]{1,0:T(8,128)(2,1)S(1)}, u32[]{:S(2)}, u32[]{:S(2)}) %collective-permute-start.15) | collective-permute-done | bytes 524320 | tf_op jit(solution)/shard_map/ppermute | solution.py:434
  150.7 2.5 collective-permute-start.18
  158.2 13.9 %expert.5 = (bf16[1024,1024]{1,0:T(8,128)(2,1)}, bf16[1024,1152]{1,0:T(8,128)(2,1)}, f32[1024,128]{1,0:T(8,128)}, bf16[1024,512]{1,0:T(8,128)(2,1)}, bf16[1024,5...) custom-call(s32[4]{0:T(128)} %pad_add_fusion.place_ref, bf16[1024,1024]{1,0:T(8,128)(2,1)} %constant_dynamic-update-slice_fusion.3.n2_ref.refs_6_, ...), custom_call_target="tpu_custom_call" | custom-call | flops 128849016 | bytes 720000 | tf_op jit(solution)/shard_map/expert/pallas_call | solution.py:565
  172.1 13.7 %expert.4 = (bf16[1024,1024]{1,0:T(8,128)(2,1)}, bf16[1024,1152]{1,0:T(8,128)(2,1)}, f32[1024,128]{1,0:T(8,128)}, bf16[1024,512]{1,0:T(8,128)(2,1)}, bf16[1024,5...) custom-call(s32[4]{0:T(128)} %pad_add_fusion.place_ref, bf16[1024,1024]{1,0:T(8,128)(2,1)} %collective-permute-done.19.n2_ref.refs_0_, ...), custom_call_target="tpu_custom_call" | custom-call | flops 128849016 | bytes 720000 | tf_op jit(solution)/shard_map/expert/pallas_call | solution.py:565
  185.8 13.6 %expert_grads.2 = bf16[3072,512]{1,0:T(8,128)(2,1)} custom-call(bf16[1024,1024]{1,0:T(8,128)(2,1)} %collective-permute-done.19.n2_ref.refs_0_, bf16[1024,1152]{1,0:T(8,128)(2,1)} %collective-permute-done.20.dyx_ref.refs_1_, f32[1024,128]{1,0:T(8,128)} %get-tuple-element.132.refs_2_, bf16[1024,512]{1,0:T(8,128)(2,1)} %get-tuple-element.133.refs_3_, ...), custom_call_target="tpu_custom_call" | custom-call | flops 128849016 | bytes 800000 | tf_op jit(solution)/shard_map/expert_grads/pallas_call | solution.py:608
  199.4 2.9 all-gather.8.cloned.1.call-done.w_ref
  202.4 15.2 %expert.7 = (bf16[1024,1024]{1,0:T(8,128)(2,1)}, bf16[1024,1152]{1,0:T(8,128)(2,1)}, f32[1024,128]{1,0:T(8,128)}, bf16[1024,512]{1,0:T(8,128)(2,1)}, bf16[1024,5...) custom-call(s32[4]{0:T(128)} %pad_add_fusion.place_ref, bf16[1024,1024]{1,0:T(8,128)(2,1)} %collective-permute-done.19.n2_ref.refs_0_, ...), custom_call_target="tpu_custom_call" | custom-call | flops 128849016 | bytes 720000 | tf_op jit(solution)/shard_map/expert/pallas_call | solution.py:565
  218.2 14.9 %expert.6 = (bf16[1024,1024]{1,0:T(8,128)(2,1)}, bf16[1024,1152]{1,0:T(8,128)(2,1)}, f32[1024,128]{1,0:T(8,128)}, bf16[1024,512]{1,0:T(8,128)(2,1)}, bf16[1024,5...) custom-call(s32[4]{0:T(128)} %pad_add_fusion.place_ref, bf16[1024,1024]{1,0:T(8,128)(2,1)} %constant_dynamic-update-slice_fusion.3.n2_ref.refs_6_, ...), custom_call_target="tpu_custom_call" | custom-call | flops 128849016 | bytes 720000 | tf_op jit(solution)/shard_map/expert/pallas_call | solution.py:565
  233.0 2.2 add_convert_fusion
  240.2 13.7 %expert_grads.3 = bf16[3072,512]{1,0:T(8,128)(2,1)} custom-call(bf16[1024,1024]{1,0:T(8,128)(2,1)} %collective-permute-done.19.n2_ref.refs_0_, bf16[1024,1152]{1,0:T(8,128)(2,1)} %collective-permute-done.20.dyx_ref.refs_1_, f32[1024,128]{1,0:T(8,128)} %get-tuple-element.150.refs_2_, bf16[1024,512]{1,0:T(8,128)(2,1)} %get-tuple-element.151.refs_3_, ...), custom_call_target="tpu_custom_call" | custom-call | flops 128849016 | bytes 800000 | tf_op jit(solution)/shard_map/expert_grads/pallas_call | solution.py:608
  253.9 3.2 add_convert_fusion.1
  257.2 8.9 %collective-permute-done.23.refs_6_ = bf16[256,1152]{1,0:T(8,128)(2,1)S(1)} collective-permute-done((bf16[256,1152]{1,0:T(8,128)(2,1)}, bf16[256,1152]{1,0:T(8,128)(2,1)S(1)}, u32[]{:S(2)}, u32[]{:S(2)}) %collective-permute-start.23) | collective-permute-done | bytes 589856 | tf_op jit(solution)/shard_map/ppermute | solution.py:434
  267.3 7.2 %mid_back.1 = (f32[256,1024]{1,0:T(8,128)}, bf16[4,256,256]{2,1,0:T(8,128)(2,1)}, bf16[4,1024,256]{2,1,0:T(8,128)(2,1)}, f32[1,1024]{1,0:T(1,128)}, f32[128,1024]{1,0:T(8,128)}) custom-call(s32[4]{0:T(128)} %pad_add_fusion.place_ref, f32[256,1024]{1,0:T(8,128)} %get-tuple-element.119.hidden_ref, bf16[256,1024]{1,0:T(8,128)(2,1)} %dy_ref.1, ...), custom_call_target="tpu_custom_call" | custom-call | flops 21474836 | bytes 400000 | tf_op jit(solution)/shard_map/mid_back/pallas_call | solution.py:648
  276.3 2.4 fusion.5
  283.5 5.4 %collective-permute-start.26 = (bf16[256,256]{1,0:T(8,128)(2,1)S(1)}, bf16[256,256]{1,0:T(8,128)(2,1)S(1)}, u32[]{:S(2)}, u32[]{:S(2)}) collective-permute-start(bf16[256,256]{1,0:T(8,128)(2,1)S(1)} %get-tuple-element.250), channel_id=1, source_target_pairs={{0,3},{1,0},{2,1},{3,2},{4,7},{5,4},{6,5},{7,6},{8,11},{9,8},{10,9... | collective-permute-start | bytes 393224 | tf_op jit(solution)/shard_map/ppermute | solution.py:428
  292.5 4.6 collective-permute-done.26.refs_1_
  297.5 18.8 %collective-permute-done.27.refs_2_ = bf16[256,256]{1,0:T(8,128)(2,1)S(1)} collective-permute-done((bf16[256,256]{1,0:T(8,128)(2,1)S(1)}, bf16[256,256]{1,0:T(8,128)(2,1)S(1)}, u32[]{:S(2)}, u32[]{:S(2)}) %collective-permute-start.27) | collective-permute-done | bytes 131104 | tf_op jit(solution)/shard_map/ppermute | solution.py:428
  324.1 11.3 %collective-permute-done.34 = bf16[2,144,256]{2,1,0:T(8,128)(2,1)S(1)} collective-permute-done((bf16[2,144,256]{2,1,0:T(8,128)(2,1)S(1)}, bf16[2,144,256]{2,1,0:T(8,128)(2,1)S(1)}, u32[]{:S(2)}, u32[]{:S(2)}) %collective-permute-start.34) | collective-permute-done | bytes 147488 | tf_op jit(solution)/shard_map/ppermute | solution.py:434
  337.7 17.0 %back.1.raw_ref = f32[1024,512]{1,0:T(8,128)} custom-call(s32[4]{0:T(128)} %pad_add_fusion.place_ref, bf16[4,1024,64]{2,1,0:T(8,128)(2,1)} %get-tuple-element.120.q_ref, bf16[2,1024,64]{2,1,0:T(8,128)(2,1)} %get-tuple-element.121.k_ref, bf16[2,1024,64]{2,1,0:T(8,128)(2,1)} %get-tuple-element.122.v_ref, f32[4,1024,1]{2,1,0:T(8,128)} %get-tuple-element.123.lse_ref, ...), custom_call_target="tpu_custom_call" | custom-call | flops 21474836 | bytes 1040000 | tf_op jit(solution)/shard_map/back/pallas_call | solution.py:718
  354.7 2.0 pad_maximum_fusion.6.refs_6_
  358.6 8.2 %finish.1 = (bf16[1024,1024]{1,0:T(8,128)(2,1)}, bf16[1024,512]{1,0:T(8,128)(2,1)}, f32[1,1024]{1,0:T(1,128)}) custom-call(f32[1024,512]{1,0:T(8,128)} %back.1.raw_ref, bf16[1024,1024]{1,0:T(8,128)(2,1)} %all-gather.4.cloned.1.call-done.x_ref, bf16[1024,1024]{1,0:T(8,128)(2,1)} %get-tuple-element.178.normed_ref, bf16[1024,512]{1,0:T(8,128)(2,1)} %get-tuple-element.179.w_ref, ...), custom_call_target="tpu_custom_call" | custom-call | flops 42949672 | bytes 600000 | tf_op jit(solution)/shard_map/finish/pallas_call | solution.py:735
  373.1 6.1 %collective-permute-done.51 = bf16[128,1024]{1,0:T(8,128)(2,1)S(1)} collective-permute-done((bf16[128,1024]{1,0:T(8,128)(2,1)S(1)}, bf16[128,1024]{1,0:T(8,128)(2,1)S(1)}, u32[]{:S(2)}, u32[]{:S(2)}) %collective-permute-start.51) | collective-permute-done | bytes 262176 | tf_op jit(solution)/shard_map/ppermute | solution.py:434
  381.1 3.0 collective-permute-done.39
  386.3 2.3 collective-permute-done.41
  395.3 19.0 %collective-permute-done.42 = bf16[4,80,256]{2,1,0:T(8,128)(2,1)S(1)} collective-permute-done((bf16[4,80,256]{2,1,0:T(8,128)(2,1)S(1)}, bf16[4,80,256]{2,1,0:T(8,128)(2,1)S(1)}, u32[]{:S(2)}, u32[]{:S(2)}) %collective-permute-start.42) | collective-permute-done | bytes 163872 | tf_op jit(solution)/shard_map/ppermute | solution.py:434
  415.0 9.2 %share.2 = (f32[8,2,256,512]{3,2,1,0:T(8,128)}, f32[8,2,256,512]{3,2,1,0:T(8,128)}, f32[8,2,128,1024]{3,2,1,0:T(8,128)}) custom-call(s32[4]{0:T(128)} %pad_add_fusion.place_ref, bf16[768,512]{1,0:T(8,128)(2,1)} %reduce-scatter.4.cloned.1.call-done.refs_0_, bf16[768,512]{1,0:T(8,128)(2,1)} %copy-done.16, bf16[768,512]{1,0:T(8,128)(2,1)} %collective-permute-done.29.refs_2_, ...), custom_call_target="tpu_custom_call" | custom-call | bytes 400000 | tf_op jit(solution)/shard_map/share/pallas_call | solution.py:695
  431.0 3.3 collective-permute-done.59
  434.3 2.6 collective-permute-done.60
  438.5 2.8 collective-permute-start.55
  442.2 9.3 %share.3 = (f32[8,2,256,512]{3,2,1,0:T(8,128)}, f32[8,2,256,512]{3,2,1,0:T(8,128)}, f32[8,2,128,1024]{3,2,1,0:T(8,128)}) custom-call(s32[4]{0:T(128)} %pad_add_fusion.place_ref, bf16[768,512]{1,0:T(8,128)(2,1)} %reduce-scatter.6.cloned.1.call-done.refs_0_, ...), custom_call_target="tpu_custom_call", output_to_operand_aliasing={{0}: (9, {}), {1}: (10, {}), {2}: (11, {})} | custom-call | bytes 400000 | tf_op jit(solution)/shard_map/share/pallas_call | solution.py:695
  457.3 4.2 collective-permute-done.63
  467.0 2.9 collective-permute-done.64
  472.2 2.2 add_convert_fusion.2
  (365 shorter events, 130.4 us)
Async XLA Ops:
  7.2 72.5 %all-gather.4.cloned.1.call-start = ((), (), s32[]{:S(2)}) async-start(), calls=%async_computation.3 | async-start | bytes 2621440 | tf_op jit(solution)/shard_map/all_gather | solution.py:461
  7.9 150.3 %all-gather.6.cloned.1.call-start = ((), (), s32[]{:S(2)}) async-start(), calls=%async_computation.4 | async-start | bytes 3932160 | tf_op jit(solution)/shard_map/all_gather | solution.py:498
  15.6 14.7 %collective-permute-start.1 = (bf16[112,512]{1,0:T(8,128)(2,1)S(1)}, bf16[112,512]{1,0:T(8,128)(2,1)S(1)}, u32[]{:S(2)}, u32[]{:S(2)}) collective-permute-start(bf16[112,512]{1,0:T(8,128)(2,1)S(1)} %get-tuple-element.278), channel_id=1, source_target_pairs={{0,2},{1,3},{2,0},{3,1},{4,6},{5,7},{6,4},{7,5},{8,10},{9,11},{10,... | collective-permute-start | bytes 344072 | tf_op jit(solution)/shard_map/ppermute | solution.py:428
  18.2 12.1 %collective-permute-start.2 = (bf16[112,512]{1,0:T(8,128)(2,1)S(1)}, bf16[112,512]{1,0:T(8,128)(2,1)S(1)}, u32[]{:S(2)}, u32[]{:S(2)}) collective-permute-start(bf16[112,512]{1,0:T(8,128)(2,1)S(1)} %get-tuple-element.276), channel_id=1, source_target_pairs={{0,3},{1,0},{2,1},{3,2},{4,7},{5,4},{6,5},{7,6},{8,11},{9,8},{10,9... | collective-permute-start | bytes 344072 | tf_op jit(solution)/shard_map/ppermute | solution.py:428
  30.3 172.0 %all-gather.8.cloned.1.call-start = ((), (), s32[]{:S(2)}) async-start(), calls=%async_computation.5 | async-start | bytes 3932160 | tf_op jit(solution)/shard_map/all_gather | solution.py:498
  32.1 34.8 %collective-permute-start.8 = (bf16[256,1152]{1,0:T(8,128)(2,1)}, bf16[256,1152]{1,0:T(8,128)(2,1)}, u32[]{:S(2)}, u32[]{:S(2)}) collective-permute-start(bf16[256,1152]{1,0:T(8,128)(2,1)} %pad_maximum_fusion.7), channel_id=1, source_target_pairs={{0,8},{8,0},{16,24},{24,16},{1,9},{9,1},{17,25},{25,17},{2,10},{10... | collective-permute-start | bytes 1769480 | tf_op jit(solution)/shard_map/ppermute | solution.py:434
  33.5 30.3 %collective-permute-start.9 = (bf16[256,1152]{1,0:T(8,128)(2,1)}, bf16[256,1152]{1,0:T(8,128)(2,1)}, u32[]{:S(2)}, u32[]{:S(2)}) collective-permute-start(bf16[256,1152]{1,0:T(8,128)(2,1)} %pad_maximum_fusion.7), channel_id=1, source_target_pairs={{0,16},{8,24},{16,0},{24,8},{1,17},{9,25},{17,1},{25,9},{2,18},{10... | collective-permute-start | bytes 1769480 | tf_op jit(solution)/shard_map/ppermute | solution.py:434
  35.8 19.6 %collective-permute-start.4 = (bf16[4,96,512]{2,1,0:T(8,128)(2,1)S(1)}, bf16[4,96,512]{2,1,0:T(8,128)(2,1)S(1)}, u32[]{:S(2)}, u32[]{:S(2)}) collective-permute-start(bf16[4,96,512]{2,1,0:T(8,128)(2,1)S(1)} %get-tuple-element.261), channel_id=1, source_target_pairs={{0,16},{8,24},{16,0},{24,8},{1,17},{9,25},{17,1},{25,9},{2,18},{10... | collective-permute-start | bytes 1179656 | tf_op jit(solution)/shard_map/ppermute | solution.py:434
  36.3 19.8 %collective-permute-start.3 = (bf16[4,96,512]{2,1,0:T(8,128)(2,1)S(1)}, bf16[4,96,512]{2,1,0:T(8,128)(2,1)S(1)}, u32[]{:S(2)}, u32[]{:S(2)}) collective-permute-start(bf16[4,96,512]{2,1,0:T(8,128)(2,1)S(1)} %get-tuple-element.261), channel_id=1, source_target_pairs={{0,8},{8,0},{16,24},{24,16},{1,9},{9,1},{17,25},{25,17},{2,10},{10... | collective-permute-start | bytes 1179656 | tf_op jit(solution)/shard_map/ppermute | solution.py:434
  62.1 17.6 %collective-permute-start.7 = (bf16[4,4,96,512]{3,2,1,0:T(8,128)(2,1)S(1)}, bf16[4,4,96,512]{3,2,1,0:T(8,128)(2,1)S(1)}, u32[]{:S(2)}, u32[]{:S(2)}) collective-permute-start(bf16[4,4,96,512]{3,2,1,0:T(8,128)(2,1)S(1)} %pad_maximum_fusion.1.mine_ref), channel_id=1, source_target_pairs={{0,4},{4,0},{1,5},{5,1},{2,6},{6,2},{3,7},{7,3},{8,12},{12,8},{9,1... | collective-permute-start | bytes 4718600 | tf_op jit(solution)/shard_map/ppermute | solution.py:431
  62.2 205.0 %reduce-scatter.4.cloned.1.call-start = ((), (), s32[]{:S(2)}) async-start(), calls=%async_computation.6 | async-start | bytes 3932160 | tf_op jit(solution)/shard_map/reduce_scatter | solution.py:643
  101.7 17.8 %collective-permute-start.12 = (bf16[256,256]{1,0:T(8,128)(2,1)S(1)}, bf16[256,256]{1,0:T(8,128)(2,1)S(1)}, u32[]{:S(2)}, u32[]{:S(2)}) collective-permute-start(bf16[256,256]{1,0:T(8,128)(2,1)S(1)} %get-tuple-element.254), channel_id=1, source_target_pairs={{0,1},{1,2},{2,3},{3,0},{4,5},{5,6},{6,7},{7,4},{8,9},{9,10},{10,1... | collective-permute-start | bytes 393224 | tf_op jit(solution)/shard_map/ppermute | solution.py:428
  112.9 14.0 %collective-permute-start.13 = (bf16[256,256]{1,0:T(8,128)(2,1)S(1)}, bf16[256,256]{1,0:T(8,128)(2,1)S(1)}, u32[]{:S(2)}, u32[]{:S(2)}) collective-permute-start(bf16[256,256]{1,0:T(8,128)(2,1)S(1)} %get-tuple-element.253), channel_id=1, source_target_pairs={{0,2},{1,3},{2,0},{3,1},{4,6},{5,7},{6,4},{7,5},{8,10},{9,11},{10,... | collective-permute-start | bytes 393224 | tf_op jit(solution)/shard_map/ppermute | solution.py:428
  112.9 17.3 %collective-permute-start.14 = (bf16[256,256]{1,0:T(8,128)(2,1)S(1)}, bf16[256,256]{1,0:T(8,128)(2,1)S(1)}, u32[]{:S(2)}, u32[]{:S(2)}) collective-permute-start(bf16[256,256]{1,0:T(8,128)(2,1)S(1)} %get-tuple-element.252), channel_id=1, source_target_pairs={{0,3},{1,0},{2,1},{3,2},{4,7},{5,4},{6,5},{7,6},{8,11},{9,8},{10,9... | collective-permute-start | bytes 393224 | tf_op jit(solution)/shard_map/ppermute | solution.py:428
  135.4 12.4 %collective-permute-start.15 = (bf16[256,1024]{1,0:T(8,128)(2,1)}, bf16[256,1024]{1,0:T(8,128)(2,1)S(1)}, u32[]{:S(2)}, u32[]{:S(2)}) collective-permute-start(bf16[256,1024]{1,0:T(8,128)(2,1)} %get-tuple-element.125.normed_ref), channel_id=1, source_target_pairs={{0,8},{8,0},{16,24},{24,16},{1,9},{9,1},{17,25},{25,17},{2,10},{10... | collective-permute-start | bytes 1572872 | tf_op jit(solution)/shard_map/ppermute | solution.py:434
  137.2 13.5 %collective-permute-start.16 = (bf16[256,1024]{1,0:T(8,128)(2,1)}, bf16[256,1024]{1,0:T(8,128)(2,1)S(1)}, u32[]{:S(2)}, u32[]{:S(2)}) collective-permute-start(bf16[256,1024]{1,0:T(8,128)(2,1)} %get-tuple-element.125.normed_ref), channel_id=1, source_target_pairs={{0,16},{8,24},{16,0},{24,8},{1,17},{9,25},{17,1},{25,9},{2,18},{10... | collective-permute-start | bytes 1572872 | tf_op jit(solution)/shard_map/ppermute | solution.py:434
  139.9 32.2 %collective-permute-start.20 = (bf16[1024,1152]{1,0:T(8,128)(2,1)S(1)}, bf16[1024,1152]{1,0:T(8,128)(2,1)}, u32[]{:S(2)}, u32[]{:S(2)}) collective-permute-start(bf16[1024,1152]{1,0:T(8,128)(2,1)S(1)} %constant_dynamic-update-slice_fusion.8.dyx_ref.refs_7_), channel_id=1, source_target_pairs={{0,4},{4,0},{1,5},{5,1},{2,6},{6,2},{3,7},{7,3},{8,12},{12,8},{9,1... | collective-permute-start | bytes 7077896 | tf_op jit(solution)/shard_map/ppermute | solution.py:431
  158.2 13.9 %collective-permute-start.19 = (bf16[1024,1024]{1,0:T(8,128)(2,1)}, bf16[1024,1024]{1,0:T(8,128)(2,1)}, u32[]{:S(2)}, u32[]{:S(2)}) collective-permute-start(bf16[1024,1024]{1,0:T(8,128)(2,1)} %constant_dynamic-update-slice_fusion.3.n2_ref.refs_6_), channel_id=1, source_target_pairs={{0,4},{4,0},{1,5},{5,1},{2,6},{6,2},{3,7},{7,3},{8,12},{12,8},{9,1... | collective-permute-start | bytes 6291464 | tf_op jit(solution)/shard_map/ppermute | solution.py:431
  202.3 156.3 %reduce-scatter.6.cloned.1.call-start = ((), (), s32[]{:S(2)}) async-start(), calls=%async_computation.7 | async-start | bytes 3932160 | tf_op jit(solution)/shard_map/reduce_scatter | solution.py:643
  217.6 15.4 %collective-permute-start.21 = (bf16[1024,1152]{1,0:T(8,128)(2,1)}, bf16[1024,1152]{1,0:T(8,128)(2,1)S(1)}, u32[]{:S(2)}, u32[]{:S(2)}) collective-permute-start(bf16[1024,1152]{1,0:T(8,128)(2,1)} %get-tuple-element.147), channel_id=1, source_target_pairs={{0,4},{4,0},{1,5},{5,1},{2,6},{6,2},{3,7},{7,3},{8,12},{12,8},{9,1... | collective-permute-start | bytes 7077896 | tf_op jit(solution)/shard_map/ppermute | solution.py:431
  217.7 36.3 %collective-permute-start.25 = (bf16[1024,1024]{1,0:T(8,128)(2,1)}, bf16[1024,1024]{1,0:T(8,128)(2,1)}, u32[]{:S(2)}, u32[]{:S(2)}) collective-permute-start(bf16[1024,1024]{1,0:T(8,128)(2,1)} %get-tuple-element.149), channel_id=1, source_target_pairs={{0,4},{4,0},{1,5},{5,1},{2,6},{6,2},{3,7},{7,3},{8,12},{12,8},{9,1... | collective-permute-start | bytes 6291464 | tf_op jit(solution)/shard_map/ppermute | solution.py:431
  236.7 20.4 %collective-permute-start.22 = (bf16[256,1152]{1,0:T(8,128)(2,1)}, bf16[256,1152]{1,0:T(8,128)(2,1)S(1)}, u32[]{:S(2)}, u32[]{:S(2)}) collective-permute-start(bf16[256,1152]{1,0:T(8,128)(2,1)} %get-tuple-element.222), channel_id=1, source_target_pairs={{0,8},{8,0},{16,24},{24,16},{1,9},{9,1},{17,25},{25,17},{2,10},{10... | collective-permute-start | bytes 1769480 | tf_op jit(solution)/shard_map/ppermute | solution.py:434
  238.2 27.9 %collective-permute-start.23 = (bf16[256,1152]{1,0:T(8,128)(2,1)}, bf16[256,1152]{1,0:T(8,128)(2,1)S(1)}, u32[]{:S(2)}, u32[]{:S(2)}) collective-permute-start(bf16[256,1152]{1,0:T(8,128)(2,1)} %get-tuple-element.221), channel_id=1, source_target_pairs={{0,16},{8,24},{16,0},{24,8},{1,17},{9,25},{17,1},{25,9},{2,18},{10... | collective-permute-start | bytes 1769480 | tf_op jit(solution)/shard_map/ppermute | solution.py:434
  239.7 26.4 %collective-permute-start.24 = (bf16[256,1152]{1,0:T(8,128)(2,1)}, bf16[256,1152]{1,0:T(8,128)(2,1)}, u32[]{:S(2)}, u32[]{:S(2)}) collective-permute-start(bf16[256,1152]{1,0:T(8,128)(2,1)} %get-tuple-element.220), channel_id=1, source_target_pairs={{0,24},{8,16},{16,8},{24,0},{1,25},{9,17},{17,9},{25,1},{2,26},{10... | collective-permute-start | bytes 1769480 | tf_op jit(solution)/shard_map/ppermute | solution.py:434
  267.2 184.3 %reduce-scatter.8.cloned.1.call-start = ((), (), s32[]{:S(2)}) async-start(), calls=%async_computation.8 | async-start | bytes 2621440 | tf_op jit(solution)/shard_map/reduce_scatter | solution.py:744
  278.6 37.7 %collective-permute-start.29 = (bf16[768,512]{1,0:T(8,128)(2,1)}, bf16[768,512]{1,0:T(8,128)(2,1)}, u32[]{:S(2)}, u32[]{:S(2)}) collective-permute-start(bf16[768,512]{1,0:T(8,128)(2,1)} %reduce-scatter.4.cloned.1.call-done.refs_0_), channel_id=1, source_target_pairs={{0,8},{8,0},{16,24},{24,16},{1,9},{9,1},{17,25},{25,17},{2,10},{10... | collective-permute-start | bytes 2359304 | tf_op jit(solution)/shard_map/ppermute | solution.py:434
  280.3 36.1 %collective-permute-start.30 = (bf16[768,512]{1,0:T(8,128)(2,1)}, bf16[768,512]{1,0:T(8,128)(2,1)}, u32[]{:S(2)}, u32[]{:S(2)}) collective-permute-start(bf16[768,512]{1,0:T(8,128)(2,1)} %reduce-scatter.4.cloned.1.call-done.refs_0_), channel_id=1, source_target_pairs={{0,16},{8,24},{16,0},{24,8},{1,17},{9,25},{17,1},{25,9},{2,18},{10... | collective-permute-start | bytes 2359304 | tf_op jit(solution)/shard_map/ppermute | solution.py:434
  283.5 13.5 %collective-permute-start.26 = (bf16[256,256]{1,0:T(8,128)(2,1)S(1)}, bf16[256,256]{1,0:T(8,128)(2,1)S(1)}, u32[]{:S(2)}, u32[]{:S(2)}) collective-permute-start(bf16[256,256]{1,0:T(8,128)(2,1)S(1)} %get-tuple-element.250), channel_id=1, source_target_pairs={{0,3},{1,0},{2,1},{3,2},{4,7},{5,4},{6,5},{7,6},{8,11},{9,8},{10,9... | collective-permute-start | bytes 393224 | tf_op jit(solution)/shard_map/ppermute | solution.py:428
  289.0 27.3 %collective-permute-start.27 = (bf16[256,256]{1,0:T(8,128)(2,1)S(1)}, bf16[256,256]{1,0:T(8,128)(2,1)S(1)}, u32[]{:S(2)}, u32[]{:S(2)}) collective-permute-start(bf16[256,256]{1,0:T(8,128)(2,1)S(1)} %get-tuple-element.249), channel_id=1, source_target_pairs={{0,2},{1,3},{2,0},{3,1},{4,6},{5,7},{6,4},{7,5},{8,10},{9,11},{10,... | collective-permute-start | bytes 393224 | tf_op jit(solution)/shard_map/ppermute | solution.py:428
  290.5 25.8 %collective-permute-start.28 = (bf16[256,256]{1,0:T(8,128)(2,1)S(1)}, bf16[256,256]{1,0:T(8,128)(2,1)S(1)}, u32[]{:S(2)}, u32[]{:S(2)}) collective-permute-start(bf16[256,256]{1,0:T(8,128)(2,1)S(1)} %get-tuple-element.248), channel_id=1, source_target_pairs={{0,1},{1,2},{2,3},{3,0},{4,5},{5,6},{6,7},{7,4},{8,9},{9,10},{10,1... | collective-permute-start | bytes 393224 | tf_op jit(solution)/shard_map/ppermute | solution.py:428
  297.0 25.0 %collective-permute-start.36 = (bf16[2,144,256]{2,1,0:T(8,128)(2,1)S(1)}, bf16[2,144,256]{2,1,0:T(8,128)(2,1)S(1)}, u32[]{:S(2)}, u32[]{:S(2)}) collective-permute-start(bf16[2,144,256]{2,1,0:T(8,128)(2,1)S(1)} %get-tuple-element.235), channel_id=1, source_target_pairs={{0,8},{8,0},{16,24},{24,16},{1,9},{9,1},{17,25},{25,17},{2,10},{10... | collective-permute-start | bytes 442376 | tf_op jit(solution)/shard_map/ppermute | solution.py:434
  318.2 36.5 %collective-permute-start.32 = (bf16[384,512]{1,0:T(8,128)(2,1)}, bf16[384,512]{1,0:T(8,128)(2,1)}, u32[]{:S(2)}, u32[]{:S(2)}) collective-permute-start(bf16[384,512]{1,0:T(8,128)(2,1)} %slice.330), channel_id=1, source_target_pairs={{0,8},{8,0},{16,24},{24,16},{1,9},{9,1},{17,25},{25,17},{2,10},{10... | collective-permute-start | bytes 1179656 | tf_op jit(solution)/shard_map/ppermute | solution.py:434
  319.9 34.7 %collective-permute-start.31 = (bf16[384,512]{1,0:T(8,128)(2,1)}, bf16[384,512]{1,0:T(8,128)(2,1)}, u32[]{:S(2)}, u32[]{:S(2)}) collective-permute-start(bf16[384,512]{1,0:T(8,128)(2,1)} %slice.329), channel_id=1, source_target_pairs={{0,16},{8,24},{16,0},{24,8},{1,17},{9,25},{17,1},{25,9},{2,18},{10... | collective-permute-start | bytes 1179656 | tf_op jit(solution)/shard_map/ppermute | solution.py:434
  321.2 14.2 %collective-permute-start.34 = (bf16[2,144,256]{2,1,0:T(8,128)(2,1)S(1)}, bf16[2,144,256]{2,1,0:T(8,128)(2,1)S(1)}, u32[]{:S(2)}, u32[]{:S(2)}) collective-permute-start(bf16[2,144,256]{2,1,0:T(8,128)(2,1)S(1)} %get-tuple-element.234), channel_id=1, source_target_pairs={{0,16},{8,24},{16,0},{24,8},{1,17},{9,25},{17,1},{25,9},{2,18},{10... | collective-permute-start | bytes 442376 | tf_op jit(solution)/shard_map/ppermute | solution.py:434
  322.8 33.9 %collective-permute-start.37 = (bf16[4,144,256]{2,1,0:T(8,128)(2,1)}, bf16[4,144,256]{2,1,0:T(8,128)(2,1)}, u32[]{:S(2)}, u32[]{:S(2)}) collective-permute-start(bf16[4,144,256]{2,1,0:T(8,128)(2,1)} %pad_maximum_fusion.16), channel_id=1, source_target_pairs={{0,16},{8,24},{16,0},{24,8},{1,17},{9,25},{17,1},{25,9},{2,18},{10... | collective-permute-start | bytes 884744 | tf_op jit(solution)/shard_map/ppermute | solution.py:434
  336.2 20.6 %collective-permute-start.35 = (bf16[4,144,256]{2,1,0:T(8,128)(2,1)}, bf16[4,144,256]{2,1,0:T(8,128)(2,1)}, u32[]{:S(2)}, u32[]{:S(2)}) collective-permute-start(bf16[4,144,256]{2,1,0:T(8,128)(2,1)} %pad_maximum_fusion.15), channel_id=1, source_target_pairs={{0,8},{8,0},{16,24},{24,16},{1,9},{9,1},{17,25},{25,17},{2,10},{10... | collective-permute-start | bytes 884744 | tf_op jit(solution)/shard_map/ppermute | solution.py:434
  372.3 17.6 %collective-permute-start.45 = (bf16[768,512]{1,0:T(8,128)(2,1)}, bf16[768,512]{1,0:T(8,128)(2,1)S(1)}, u32[]{:S(2)}, u32[]{:S(2)}) collective-permute-start(bf16[768,512]{1,0:T(8,128)(2,1)} %reduce-scatter.4.cloned.1.call-done.refs_0_), channel_id=1, source_target_pairs={{0,4},{4,0},{1,5},{5,1},{2,6},{6,2},{3,7},{7,3},{8,12},{12,8},{9,1... | collective-permute-start | bytes 2359304 | tf_op jit(solution)/shard_map/ppermute | solution.py:431
  372.4 19.2 %collective-permute-start.46 = (bf16[768,512]{1,0:T(8,128)(2,1)}, bf16[768,512]{1,0:T(8,128)(2,1)S(1)}, u32[]{:S(2)}, u32[]{:S(2)}) collective-permute-start(bf16[768,512]{1,0:T(8,128)(2,1)} %collective-permute-done.29.refs_2_), channel_id=1, source_target_pairs={{0,4},{4,0},{1,5},{5,1},{2,6},{6,2},{3,7},{7,3},{8,12},{12,8},{9,1... | collective-permute-start | bytes 2359304 | tf_op jit(solution)/shard_map/ppermute | solution.py:431
  372.9 20.1 %collective-permute-start.47 = (bf16[768,512]{1,0:T(8,128)(2,1)}, bf16[768,512]{1,0:T(8,128)(2,1)S(1)}, u32[]{:S(2)}, u32[]{:S(2)}) collective-permute-start(bf16[768,512]{1,0:T(8,128)(2,1)} %collective-permute-done.30.refs_4_), channel_id=1, source_target_pairs={{0,4},{4,0},{1,5},{5,1},{2,6},{6,2},{3,7},{7,3},{8,12},{12,8},{9,1... | collective-permute-start | bytes 2359304 | tf_op jit(solution)/shard_map/ppermute | solution.py:431
  379.2 14.4 %collective-permute-start.48 = (bf16[768,512]{1,0:T(8,128)(2,1)S(1)}, bf16[768,512]{1,0:T(8,128)(2,1)S(1)}, u32[]{:S(2)}, u32[]{:S(2)}) collective-permute-start(bf16[768,512]{1,0:T(8,128)(2,1)S(1)} %copy-done.8), channel_id=1, source_target_pairs={{0,4},{4,0},{1,5},{5,1},{2,6},{6,2},{3,7},{7,3},{8,12},{12,8},{9,1... | collective-permute-start | bytes 2359304 | tf_op jit(solution)/shard_map/ppermute | solution.py:431
  388.6 36.7 %collective-permute-start.43 = (bf16[768,512]{1,0:T(8,128)(2,1)}, bf16[768,512]{1,0:T(8,128)(2,1)}, u32[]{:S(2)}, u32[]{:S(2)}) collective-permute-start(bf16[768,512]{1,0:T(8,128)(2,1)} %reduce-scatter.6.cloned.1.call-done.refs_0_), channel_id=1, source_target_pairs={{0,8},{8,0},{16,24},{24,16},{1,9},{9,1},{17,25},{25,17},{2,10},{10... | collective-permute-start | bytes 2359304 | tf_op jit(solution)/shard_map/ppermute | solution.py:434
  390.0 35.3 %collective-permute-start.44 = (bf16[768,512]{1,0:T(8,128)(2,1)}, bf16[768,512]{1,0:T(8,128)(2,1)}, u32[]{:S(2)}, u32[]{:S(2)}) collective-permute-start(bf16[768,512]{1,0:T(8,128)(2,1)} %reduce-scatter.6.cloned.1.call-done.refs_0_), channel_id=1, source_target_pairs={{0,16},{8,24},{16,0},{24,8},{1,17},{9,25},{17,1},{25,9},{2,18},{10... | collective-permute-start | bytes 2359304 | tf_op jit(solution)/shard_map/ppermute | solution.py:434
  391.6 22.6 %collective-permute-start.42 = (bf16[4,80,256]{2,1,0:T(8,128)(2,1)S(1)}, bf16[4,80,256]{2,1,0:T(8,128)(2,1)S(1)}, u32[]{:S(2)}, u32[]{:S(2)}) collective-permute-start(bf16[4,80,256]{2,1,0:T(8,128)(2,1)S(1)} %pad_maximum_fusion.19), channel_id=1, source_target_pairs={{0,16},{8,24},{16,0},{24,8},{1,17},{9,25},{17,1},{25,9},{2,18},{10... | collective-permute-start | bytes 491528 | tf_op jit(solution)/shard_map/ppermute | solution.py:434
  393.0 32.2 %collective-permute-start.50 = (bf16[256,1024]{1,0:T(8,128)(2,1)}, bf16[256,1024]{1,0:T(8,128)(2,1)}, u32[]{:S(2)}, u32[]{:S(2)}) collective-permute-start(bf16[256,1024]{1,0:T(8,128)(2,1)} %pad_maximum_fusion.11), channel_id=1, source_target_pairs={{0,8},{8,0},{16,24},{24,16},{1,9},{9,1},{17,25},{25,17},{2,10},{10... | collective-permute-start | bytes 1572872 | tf_op jit(solution)/shard_map/ppermute | solution.py:434
  393.7 31.5 %collective-permute-start.52 = (bf16[256,1024]{1,0:T(8,128)(2,1)}, bf16[256,1024]{1,0:T(8,128)(2,1)S(1)}, u32[]{:S(2)}, u32[]{:S(2)}) collective-permute-start(bf16[256,1024]{1,0:T(8,128)(2,1)} %pad_maximum_fusion.12), channel_id=1, source_target_pairs={{0,16},{8,24},{16,0},{24,8},{1,17},{9,25},{17,1},{25,9},{2,18},{10... | collective-permute-start | bytes 1572872 | tf_op jit(solution)/shard_map/ppermute | solution.py:434
  437.1 15.6 %collective-permute-start.53 = (bf16[224,256]{1,0:T(8,128)(2,1)S(1)}, bf16[224,256]{1,0:T(8,128)(2,1)S(1)}, u32[]{:S(2)}, u32[]{:S(2)}) collective-permute-start(bf16[224,256]{1,0:T(8,128)(2,1)S(1)} %get-tuple-element.258), channel_id=1, source_target_pairs={{0,1},{1,2},{2,3},{3,0},{4,5},{5,6},{6,7},{7,4},{8,9},{9,10},{10,1... | collective-permute-start | bytes 344072 | tf_op jit(solution)/shard_map/ppermute | solution.py:428
  437.2 15.5 %collective-permute-start.54 = (bf16[224,256]{1,0:T(8,128)(2,1)S(1)}, bf16[224,256]{1,0:T(8,128)(2,1)S(1)}, u32[]{:S(2)}, u32[]{:S(2)}) collective-permute-start(bf16[224,256]{1,0:T(8,128)(2,1)S(1)} %get-tuple-element.257), channel_id=1, source_target_pairs={{0,2},{1,3},{2,0},{3,1},{4,6},{5,7},{6,4},{7,5},{8,10},{9,11},{10,... | collective-permute-start | bytes 344072 | tf_op jit(solution)/shard_map/ppermute | solution.py:428
  438.5 14.2 %collective-permute-start.55 = (bf16[224,256]{1,0:T(8,128)(2,1)S(1)}, bf16[224,256]{1,0:T(8,128)(2,1)}, u32[]{:S(2)}, u32[]{:S(2)}) collective-permute-start(bf16[224,256]{1,0:T(8,128)(2,1)S(1)} %get-tuple-element.256), channel_id=1, source_target_pairs={{0,3},{1,0},{2,1},{3,2},{4,7},{5,4},{6,5},{7,6},{8,11},{9,8},{10,9... | collective-permute-start | bytes 344072 | tf_op jit(solution)/shard_map/ppermute | solution.py:428
  (67 other events, 725.6 us)
Sparse Core Ops, SparseCore 0:
  9.6 52.7 all-gather.3
  64.6 73.9 all-gather.5
  140.1 62.1 all-gather.7
  205.0 62.1 reduce-scatter.3
  269.9 68.7 reduce-scatter.5
  370.2 42.2 reduce-scatter.7
